TPU v7x, 256 devices: a whole 4x4x8 slice. The times are simulated.
256 devices in a mesh: tp: 128 (over y, x_lo, z, core), dp: 2 (over x_hi).
Axes of the slice: x: 4 (x_hi: 2, x_lo: 2; x = x_hi * 2 + x_lo), y: 4, z: 8, core: 2. Of those that a mesh axis runs over, the one named last changes fastest.
Arguments:
- tokens: bfloat16 [512, 8192], P('dp', 'tp'), parts along dimension 0, may hold values from -6 to 6
- grad_out: bfloat16 [512, 8192], P('dp', 'tp'), parts along dimension 0, may hold values from -6 to 6
- gate_blocks: bfloat16 [8192, 128, 128], P('tp'), may hold values from -0.09375 to 0.09375
- gate_index: int32 [128, 64], P('tp'), may hold values from 0 to 63, as said below
- gate_count: int32 [128], P('tp'), may hold values from 16 to 64, as said below
- up_blocks: bfloat16 [8192, 128, 128], P('tp'), may hold values from -0.09375 to 0.09375
- up_index: int32 [128, 64], P('tp'), may hold values from 0 to 63, as said below
- up_count: int32 [128], P('tp'), may hold values from 16 to 64, as said below
- down_blocks: bfloat16 [8192, 128, 128], P('tp'), may hold values from -0.0625 to 0.0625
- down_index: int32 [128, 64], P('tp'), may hold values from 0 to 63, as said below
- down_count: int32 [128], P('tp'), may hold values from 16 to 64, as said below
Outputs:
- outputs: bfloat16 [512, 8192], P('dp', 'tp'), parts along dimension 0
- grad_tokens: bfloat16 [512, 8192], P('dp', 'tp'), parts along dimension 0
There are 2 independent parts, one for each index of `dp`. A program takes and returns all parts, laid end to end along the dimension named above; an argument that names none is the same for every part. Nothing has to cross between parts.
Inputs may be any that keep to these rules, and one draw needn't show every extreme that they name: `gate_index`: each row is an ordering of the 64 block rows; entries at positions from gate_count onward are ignored. `gate_count`: both ends occur. `up_index`: each row is an ordering of the 64 block rows; entries at positions from up_count onward are ignored. `up_count`: both ends occur. `down_index`: each row is an ordering of the 64 block columns; entries at positions from down_count onward are ignored. `down_count`: both ends occur.
All inputs are finite; a program needn't handle non-finite values.
Results may differ from a plain program's by a relative error of at most 0.005.
Values may be sent and summed in bfloat16 or wider, within the bound.
No kernel may reach another device: no remote copies, remote signals or barrier semaphores. Data moves between devices by JAX's collectives and lax.ppermute only.
A program may use at most 128 MiB of HBM per device.

v0:
```python
import jax
import jax.numpy as jnp
from jax import lax
from jax.sharding import PartitionSpec as P


def densify(blocks, index, count):
    hidden_blocks, slots = index.shape
    block = blocks.shape[-1]
    live = lax.broadcasted_iota(jnp.int32, (hidden_blocks, slots), 1) < count[:, None]
    places = lax.broadcasted_iota(jnp.int32, (hidden_blocks, slots, slots), 2)
    onehot = ((index[:, :, None] == places) & live[:, :, None]).astype(jnp.bfloat16)
    shaped = blocks.reshape(hidden_blocks, slots, block, block)
    return jnp.einsum("hsr,hsab->hrab", onehot, shaped, preferred_element_type=jnp.float32).astype(
        jnp.bfloat16
    )


def column_matrix(dense):
    hidden_blocks, slots, block, _ = dense.shape
    return dense.transpose(1, 2, 0, 3).reshape(slots * block, hidden_blocks * block)


def row_matrix(dense):
    hidden_blocks, slots, block, _ = dense.shape
    return dense.transpose(0, 2, 1, 3).reshape(hidden_blocks * block, slots * block)


def contract_last(left, right):
    return lax.dot_general(
        left, right, (((1,), (1,)), ((), ())), preferred_element_type=jnp.float32
    )


def body(
    tokens,
    grad_out,
    gate_blocks,
    gate_index,
    gate_count,
    up_blocks,
    up_index,
    up_count,
    down_blocks,
    down_index,
    down_count,
):
    hidden_blocks, slots = gate_index.shape
    block = gate_blocks.shape[-1]
    width = hidden_blocks * block
    gate_weight = column_matrix(densify(gate_blocks, gate_index, gate_count))
    up_weight = column_matrix(densify(up_blocks, up_index, up_count))
    down_weight = row_matrix(densify(down_blocks, down_index, down_count))
    all_tokens = lax.all_gather(tokens, "tp", axis=1, tiled=True)
    projected = jnp.concatenate(
        [
            jnp.dot(all_tokens, gate_weight, preferred_element_type=jnp.float32),
            jnp.dot(all_tokens, up_weight, preferred_element_type=jnp.float32),
        ],
        axis=1,
    )
    gate = projected[:, :width]
    upper = projected[:, width:]
    hidden = (gate * jax.nn.sigmoid(gate) * upper).astype(jnp.bfloat16)
    outputs = lax.psum_scatter(
        jnp.dot(hidden, down_weight, preferred_element_type=jnp.float32),
        "tp",
        scatter_dimension=1,
        tiled=True,
    )
    all_grads = lax.all_gather(grad_out, "tp", axis=1, tiled=True)
    grad_hidden = contract_last(all_grads, down_weight)
    gate = projected[:, :width]
    upper = projected[:, width:]
    sigma = jax.nn.sigmoid(gate)
    grad_gate = (grad_hidden * upper * sigma * (1.0 + gate * (1.0 - sigma))).astype(jnp.bfloat16)
    grad_up = (grad_hidden * gate * sigma).astype(jnp.bfloat16)
    grad_gate, grad_up = (grad_gate, grad_up)
    grad_tokens = lax.psum_scatter(
        contract_last(grad_gate, gate_weight) + contract_last(grad_up, up_weight),
        "tp",
        scatter_dimension=1,
        tiled=True,
    )
    return (outputs.astype(jnp.bfloat16), grad_tokens.astype(jnp.bfloat16))


def solution(mesh):
    placed = (
        P("dp", "tp"),
        P("dp", "tp"),
        P("tp", None, None),
        P("tp", None),
        P("tp"),
        P("tp", None, None),
        P("tp", None),
        P("tp"),
        P("tp", None, None),
        P("tp", None),
        P("tp"),
    )
    return jax.shard_map(
        body, mesh=mesh, in_specs=placed, out_specs=(P("dp", "tp"), P("dp", "tp")), check_vma=False
    )
```

profile of v0, /device:TPU:1, one launch (start us, length us, event | category | flops | bytes accessed | tf_op | source)
XLA Modules:
  0.0 1595.6 jit_solution(4752452538050697444)
XLA Ops:
  7.2 0.0 copy-start
  7.2 0.0 all-gather.3.cloned.1.call-start
  7.2 0.7 all-gather.3.cloned.1.call-update
  7.9 0.0 all-gather.5.cloned.1.call-start
  8.0 0.7 all-gather.5.cloned.1.call-update
  8.7 0.0 reduce-scatter.3.cloned.1.call-start
  10.0 0.0 copy-done
  10.0 2.4 fusion.13
  12.4 0.0 copy-start.6
  12.4 0.0 copy-start.8
  12.5 2.7 copy.19
  15.8 0.0 copy-done.6
  15.8 0.0 copy-done.8
  15.8 1.7 fusion.10
  17.6 0.0 copy-start.7
  17.6 0.0 copy-start.9
  17.6 2.7 copy.17
  20.3 0.0 copy-done.7
  20.3 0.0 copy-done.9
  20.3 3.1 fusion.16
  23.4 205.5 %all-gather.3.cloned.1.call-done = bf16[256,8192]{0,1:T(8,128)(2,1)} async-done(((bf16[256,64]{0,1:T(8,128)(2,1)}), bf16[256,8192]{0,1:T(8,128)(2,1)}) %all-gather.3.cloned.1.call-update) | async-done | bytes 4194320 | tf_op jit(solution)/shard_map/all_gather | solution.py:54
  228.9 0.0 copy-start.2
  228.9 0.0 copy-start.4
  228.9 3.8 convolution_bitcast_fusion
  232.7 0.0 copy-done.2
  232.7 0.8 copy-done.4
  233.6 0.0 copy-start.5
  233.6 0.9 convolution_bitcast_fusion.1
  234.4 0.7 copy-done.5
  235.1 6.3 fusion.2
  241.4 0.0 reduce-scatter.3.cloned.1.call-update
  241.4 0.2 reduce-scatter.5.cloned.1.call-start
  241.7 203.5 %all-gather.5.cloned.1.call-done = bf16[256,8192]{0,1:T(8,128)(2,1)} async-done(((bf16[256,64]{0,1:T(8,128)(2,1)}), bf16[256,8192]{0,1:T(8,128)(2,1)}) %all-gather.5.cloned.1.call-update) | async-done | bytes 4194320 | tf_op jit(solution)/shard_map/all_gather | solution.py:71
  445.2 0.0 copy-start.3
  445.2 4.4 fusion.21
  449.6 0.0 copy-done.3
  449.6 0.0 copy-start.1
  449.6 1.3 fusion.24
  450.9 0.3 copy-done.1
  451.2 4.5 convolution_add_fusion
  455.7 0.0 reduce-scatter.5.cloned.1.call-update
  455.7 561.4 %reduce-scatter.3.cloned.1.call-done = f32[256,64]{0,1:T(8,128)} async-done(((f32[256,8192]{0,1:T(8,128)}), f32[256,64]{0,1:T(8,128)}) %reduce-scatter.3.cloned.1.call-update) | async-done | bytes 65552 | tf_op jit(solution)/shard_map/reduce_scatter | solution.py:65
  1017.1 1.5 convert_element_type.37
  1018.6 569.1 %reduce-scatter.5.cloned.1.call-done = f32[256,64]{0,1:T(8,128)} async-done(((f32[256,8192]{0,1:T(8,128)}), f32[256,64]{0,1:T(8,128)}) %reduce-scatter.5.cloned.1.call-update) | async-done | bytes 65552 | tf_op jit(solution)/shard_map/reduce_scatter | solution.py:79
  1587.6 1.5 convert_element_type.40
  (3 shorter events, 0.0 us)
Async XLA Ops:
  7.2 2.9 copy-start
  7.2 221.7 %all-gather.3.cloned.1.call-start = ((), (), s32[]{:S(2)}) async-start(), calls=%async_computation.2 | async-start | bytes 4227072 | tf_op jit(solution)/shard_map/all_gather | solution.py:54
  7.9 437.3 %all-gather.5.cloned.1.call-start = ((), (), s32[]{:S(2)}) async-start(), calls=%async_computation.4 | async-start | bytes 4227072 | tf_op jit(solution)/shard_map/all_gather | solution.py:71
  8.7 1008.5 %reduce-scatter.3.cloned.1.call-start = ((), (), s32[]{:S(2)}) async-start(), calls=%async_computation.3 | async-start | bytes 8454144 | tf_op jit(solution)/shard_map/reduce_scatter | solution.py:65
  12.4 3.4 copy-start.6
  12.4 3.4 copy-start.8
  17.6 2.7 copy-start.7
  17.6 2.7 copy-start.9
  228.9 3.8 copy-start.2
  228.9 4.7 copy-start.4
  233.6 1.6 copy-start.5
  241.4 1346.2 %reduce-scatter.5.cloned.1.call-start = ((), (), s32[]{:S(2)}) async-start(), calls=%async_computation.5 | async-start | bytes 8454144 | tf_op jit(solution)/shard_map/reduce_scatter | solution.py:79
  445.2 4.4 copy-start.3
  449.6 1.6 copy-start.1
Sparse Core Ops, SparseCore 0:
  9.9 218.9 all-gather.2
  230.8 214.3 all-gather.4
  447.7 569.3 reduce-scatter.2
  1019.7 567.9 reduce-scatter.4
where the time goes:
time: 1600 us
  waiting for transfers between devices  1540 us (96%)
  matrix products  28.3 us (2%)
    reduce_scatter x1, waiting for transfers between devices, body(): lax.psum_scatter(contract_last(grad_gate, gate_weight) + contract_last(gr...  569 us
    reduce_scatter x1, waiting for transfers between devices, body(): lax.psum_scatter(jnp.dot(hidden, down_weight, preferred_element_type=jnp....  561 us
    all_gather x1, waiting for transfers between devices, body(): all_tokens = lax.all_gather(tokens, 'tp', axis=1, tiled=True)  206 us
    all_gather x1, waiting for transfers between devices, body(): all_grads = lax.all_gather(grad_out, 'tp', axis=1, tiled=True)  204 us
  transfers between devices with their start and end apart: 4, of which 4 were waited for; matrix products, arithmetic and copies ran while one was open for 2% of the time, Pallas kernels for 0%

commit v1 on v0

v1 whole, which is shorter than its diff:
```python
import jax
import jax.numpy as jnp
from jax import lax
from jax.experimental import pallas as pl
from jax.experimental.pallas import tpu as pltpu
from jax.sharding import PartitionSpec as P

NY, NX, NZ, NC = 4, 2, 8, 2
SIZES = {"y": NY, "x": NX, "z": NZ, "c": NC}
BLOCK = 128
SLOTS = NY * NX * NZ
RING = 4
PART = SLOTS // RING
GROUP = 4
F32 = jnp.float32
BF16 = jnp.bfloat16


def permute(value, target):
    pairs = []
    for y in range(NY):
        for x in range(NX):
            for z in range(NZ):
                for c in range(NC):
                    at = {"y": y, "x": x, "z": z, "c": c}
                    to = target(dict(at))
                    numbers = [((k["y"] * NX + k["x"]) * NZ + k["z"]) * NC + k["c"] for k in (at, to)]
                    pairs.append(tuple(numbers))
    return lax.ppermute(value, "tp", pairs)


def shift(value, axis, step):
    def target(at):
        at[axis] = (at[axis] + step) % SIZES[axis]
        return at

    return permute(value, target)


def turn(value, axes, step):
    def target(at):
        axis = axes[at["c"]]
        at[axis] = (at[axis] + step) % SIZES[axis]
        return at

    return permute(value, target)


def ring_gather(value, axes):
    half = value.shape[0] // 2
    up, down = turn(value, axes, 1), turn(value, axes, -1)
    far_up, far_down = turn(up[:half], axes, 1), turn(down[half:], axes, -1)
    return jnp.concatenate([value, down, up, far_up, far_down])


def ring_reduce(parts, axes):
    here, ahead, behind, far = parts
    half = here.shape[0] // 2
    far = far.astype(BF16)
    down, up = turn(far[:half], axes, -1), turn(far[half:], axes, 1)
    behind = jnp.concatenate([behind[:half] + down.astype(F32), behind[half:]])
    ahead = jnp.concatenate([ahead[:half], ahead[half:] + up.astype(F32)])
    ahead, behind = turn(ahead.astype(BF16), axes, 1), turn(behind.astype(BF16), axes, -1)
    return here + ahead.astype(F32) + behind.astype(F32)


def read_block(maps_ref, which, blocks_ref, position):
    slot = maps_ref[which * SLOTS + position]
    return jnp.where(slot >= 0, blocks_ref[jnp.maximum(slot, 0)], jnp.zeros((), BF16))


def contract_last(left, right):
    return lax.dot_general(left, right, (((1,), (1,)), ((), ())), preferred_element_type=F32)


def inner_kernel(maps_ref, all_ref, g0, u0, g1, u1, d0, d1, sums_ref):
    core = maps_ref[6 * SLOTS]
    sums_ref[...] = jnp.zeros_like(sums_ref)
    wide = 2 * BLOCK

    def gathered(i):
        spots = [i * GROUP + j for j in range(GROUP)]
        return spots, jnp.concatenate([all_ref[p] for p in spots], axis=1)

    @pl.when(core == 0)
    def _():
        def step(i, carry):
            spots, left = gathered(i)
            for n, pair in enumerate((((0, g0), (1, u0)), ((3, g1), (4, u1)))):
                right = jnp.concatenate(
                    [
                        jnp.concatenate([read_block(maps_ref, k, ref, p) for k, ref in pair], axis=1)
                        for p in spots
                    ],
                    axis=0,
                )
                sums_ref[:, pl.ds(n * wide, wide)] += jnp.dot(left, right, preferred_element_type=F32)
            return carry

        lax.fori_loop(0, SLOTS // GROUP, step, 0, unroll=4)

    @pl.when(core == 1)
    def _():
        def step(i, carry):
            spots, left = gathered(i)
            right = jnp.concatenate(
                [
                    jnp.concatenate([read_block(maps_ref, k, ref, p) for p in spots], axis=1)
                    for k, ref in ((2, d0), (5, d1))
                ],
                axis=0,
            )
            sums_ref[:, pl.ds(0, wide)] += contract_last(left, right)
            return carry

        lax.fori_loop(0, SLOTS // GROUP, step, 0, unroll=4)


def outer_kernel(maps_ref, mine_ref, theirs_ref, g0, u0, g1, u1, d0, d1, *part_refs):
    core = maps_ref[6 * SLOTS]

    def columns(ref, n):
        return ref[:, pl.ds(n * BLOCK, BLOCK)]

    def emit(product):
        for rank, part_ref in enumerate(part_refs):

            def step(i, carry, rank=rank, part_ref=part_ref):
                spots = [i * 2 + j for j in range(2)]
                terms = product([rank * PART + p for p in spots]).astype(part_ref.dtype)
                for j, p in enumerate(spots):
                    part_ref[p] = terms[:, j * BLOCK : (j + 1) * BLOCK]
                return carry

            lax.fori_loop(0, PART // 2, step, 0, unroll=4)

    @pl.when(core == 0)
    def _():
        hidden = []
        for n in range(NC):
            gate, upper = columns(mine_ref, 2 * n), columns(mine_ref, 2 * n + 1)
            hidden.append((gate * jax.nn.sigmoid(gate) * upper).astype(BF16))
        hidden = jnp.concatenate(hidden, axis=1)

        def product(spots):
            right = jnp.concatenate(
                [
                    jnp.concatenate([read_block(maps_ref, k, ref, p) for p in spots], axis=1)
                    for k, ref in ((2, d0), (5, d1))
                ],
                axis=0,
            )
            return jnp.dot(hidden, right, preferred_element_type=F32)

        emit(product)

    @pl.when(core == 1)
    def _():
        grads = []
        for n in range(NC):
            gate, upper = columns(theirs_ref, 2 * (1 - n)), columns(theirs_ref, 2 * (1 - n) + 1)
            grad = columns(mine_ref, n)
            sigma = jax.nn.sigmoid(gate)
            grads.append((grad * upper * sigma * (1.0 + gate * (1.0 - sigma))).astype(BF16))
            grads.append((grad * gate * sigma).astype(BF16))
        grads = jnp.concatenate(grads, axis=1)

        def product(spots):
            right = jnp.concatenate(
                [
                    jnp.concatenate(
                        [read_block(maps_ref, k, ref, p) for k, ref in ((0, g0), (1, u0), (3, g1), (4, u1))],
                        axis=1,
                    )
                    for p in spots
                ],
                axis=0,
            )
            return contract_last(grads, right)

        emit(product)


def transpose_kernel(block_ref, turned_ref):
    turned_ref[...] = block_ref[...].T


def transpose(block):
    return pl.pallas_call(
        transpose_kernel,
        out_shape=jax.ShapeDtypeStruct(block.shape[::-1], block.dtype),
        compiler_params=pltpu.CompilerParams(vmem_limit_bytes=2 << 20),
    )(block)


def call(kernel, outs, flops, maps, *inputs):
    vmem = pl.BlockSpec(memory_space=pltpu.VMEM)
    return pl.pallas_call(
        kernel,
        out_shape=outs,
        in_specs=[pl.BlockSpec(memory_space=pltpu.SMEM)] + [vmem] * len(inputs),
        out_specs=jax.tree.map(lambda _: vmem, outs),
        cost_estimate=pl.CostEstimate(flops=flops, bytes_accessed=1 << 24, transcendentals=1 << 15),
        compiler_params=pltpu.CompilerParams(vmem_limit_bytes=21 << 20),
    )(maps, *inputs)


def body(
    tokens,
    grad_out,
    gate_blocks,
    gate_index,
    gate_count,
    up_blocks,
    up_index,
    up_count,
    down_blocks,
    down_index,
    down_count,
):
    me = lax.axis_index("tp")
    core, my_z, my_x, my_y = me & 1, (me >> 1) & 7, (me >> 4) & 1, me >> 5
    first = core == 0
    batch = tokens.shape[0]

    tokens, grad_out = tokens.T, grad_out.T
    own, other = jnp.where(first, tokens, grad_out), jnp.where(first, grad_out, tokens)
    other = shift(other, "c", 1)
    block = jnp.concatenate([jnp.where(first, own, other), jnp.where(first, other, own)])
    block = transpose(block).reshape(1, batch, BLOCK)
    block = jnp.concatenate([block, shift(block, "z", 4)])
    block = jnp.concatenate([block, shift(block, "x", 1)])
    block = ring_gather(block, "yz")
    block = ring_gather(block, "zy")

    lists = jnp.concatenate([gate_index, up_index, down_index])
    counts = jnp.stack([gate_count, up_count, down_count])
    lists = jnp.concatenate([lists, counts], axis=1)
    lists = jnp.concatenate([lists, shift(lists, "c", 1)])
    index, counts = lists[:, :SLOTS], lists[:, SLOTS:]
    y, x, z = ((index >> 4) - my_y) & 3, ((index >> 3) & 1) ^ my_x, ((index & 7) - my_z) & 7
    low, high = z & 3, z >> 2

    def ranked(k):
        return jnp.where(k >= 2, 5 - k, k)

    y_rank, z_rank = ranked(y), ranked(low)
    from_ahead = jnp.where(first, y_rank >= 2, x == 1)
    flipped = (low == 3) | ((low == 2) & jnp.logical_not(from_ahead))
    high = jnp.where(flipped, 1 - high, high)
    position = jnp.where(first, z_rank * RING + y_rank, y_rank * RING + z_rank) * 4 + x * 2 + high
    number = lax.broadcasted_iota(jnp.int32, (6, SLOTS, SLOTS), 2)
    places = lax.broadcasted_iota(jnp.int32, (6, SLOTS, SLOTS), 1)
    here = (position[:, None, :] == places) & (number < counts[:, :, None])
    maps = jnp.sum(jnp.where(here, number + 1, 0), axis=2) - 1
    maps = jnp.concatenate([maps.reshape(6 * SLOTS), core[None]])

    weights = (gate_blocks, up_blocks, shift(gate_blocks, "c", 1), shift(up_blocks, "c", 1))
    weights += (down_blocks, shift(down_blocks, "c", 1))
    flops = 4 * NC * SLOTS * BLOCK * BLOCK * batch
    mine = call(inner_kernel, jax.ShapeDtypeStruct((batch, 4 * BLOCK), F32), flops, maps, block, *weights)
    theirs = shift(mine, "c", 1)
    parts = tuple(
        jax.ShapeDtypeStruct((PART, batch, BLOCK), BF16 if rank == RING - 1 else F32) for rank in range(RING)
    )
    parts = call(outer_kernel, parts, flops, maps, mine, theirs, *weights)

    total = ring_reduce(parts, "zy")
    total = ring_reduce(jnp.split(total, RING), "yz")
    total = total[:2] + shift(total[2:].astype(BF16), "x", 1).astype(F32)
    total = total[0] + shift(total[1].astype(BF16), "z", 4).astype(F32)
    total = transpose(total).astype(BF16)
    low, high = jnp.split(total, 2)
    own, other = jnp.where(first, low, high), jnp.where(first, high, low)
    other = shift(other, "c", 1)
    return jnp.where(first, own, other).T, jnp.where(first, other, own).T


def solution(mesh):
    placed = (
        P("dp", "tp"),
        P("dp", "tp"),
        P("tp", None, None),
        P("tp", None),
        P("tp"),
        P("tp", None, None),
        P("tp", None),
        P("tp"),
        P("tp", None, None),
        P("tp", None),
        P("tp"),
    )
    return jax.shard_map(
        body, mesh=mesh, in_specs=placed, out_specs=(P("dp", "tp"), P("dp", "tp")), check_vma=False
    )
```

time: 1600 us -> 145 us (0.09)
  waiting for transfers between devices: 1540 us -> 57.1 us
  starting transfers between devices: 0.34 us -> 49.1 us
  matrix products: 28.3 us -> 0 us
    reduce_scatter x2 -> x0, waiting for transfers between devices: 1130 us -> none  [the longest x1 569 us: body(): lax.psum_scatter(contract_last(grad_gate, gate_weight) + contract_last(gr...]
    all_gather x2 -> x0, waiting for transfers between devices: 409 us -> none  [the longest x1 206 us: body(): all_tokens = lax.all_gather(tokens, 'tp', axis=1, tiled=True)]
    ppermute x0 -> x27, waiting for transfers between devices: none -> 57.1 us  [permute(): return lax.ppermute(value, 'tp', pairs)]
    ppermute x0 -> x27, starting transfers between devices: none -> 49.1 us  [permute(): return lax.ppermute(value, 'tp', pairs)]
    dot_general x9 -> x0, matrix products: 28.3 us -> none  [the longest x3 10.2 us: contract_last(): lax.dot_general(left, right, (((1,), (1,)), ((), ())), preferred_element_...]
  transfers between devices with their start and end apart: 4 -> 27, of which waited for: 4 -> 14; matrix products, arithmetic and copies ran while one was open for 2% -> 12% of each run, Pallas kernels for 0% -> 0%
where the time goes in v1:
time: 145 us; the launch traced here: 144 us
  waiting for transfers between devices  57.1 us (39%)
  starting transfers between devices  49.1 us (34%)
  local copies, waits for them, and re-layouts  16 us (11%)
  Pallas kernels  14.5 us (10%)
  other arithmetic  4.55 us (3%)
  between operations  2.92 us (2%)
    ppermute x27, waiting for transfers between devices, permute(): return lax.ppermute(value, 'tp', pairs)  57.1 us
    ppermute x27, starting transfers between devices, permute(): return lax.ppermute(value, 'tp', pairs)  49.1 us
    pallas_call x2, Pallas kernels, call(): pl.pallas_call(kernel, out_shape=outs, in_specs=[pl.BlockSpec(memory_spac...  14.4 us
    unnamed x19, local copies, waits for them, and re-layouts  9.94 us
  transfers between devices with their start and end apart: 27, of which 14 were waited for; matrix products, arithmetic and copies ran while one was open for 12% of the time, Pallas kernels for 0%

profile of v1, /device:TPU:1, one launch (start us, length us, event | category | flops | bytes accessed | tf_op | source)
XLA Modules:
  0.0 144.2 jit_solution(1052684560744499089)
XLA Ops:
  0.7 0.8 select_bitcast_fusion.2
  1.4 3.2 %collective-permute-start.1 = (bf16[64,256]{1,0:T(8,128)(2,1)S(1)}, bf16[64,256]{1,0:T(8,128)(2,1)S(1)}, u32[]{:S(2)}, u32[]{:S(2)}) collective-permute-start(bf16[64,256]{1,0:T(8,128)(2,1)S(1)} %select_bitcast_fusion.2), channel_id=1, source_target_pairs={{0,2},{2,0},{4,6},{6,4},{8,10},{10,8},{12,14},{14,12},{16,18},{18,... | collective-permute-start | bytes 98312 | tf_op jit(solution)/shard_map/ppermute | solution.py:29
  4.7 0.9 collective-permute-done.1
  5.5 0.8 bitcast_select_fusion.1
  6.4 5.3 %collective-permute-start.2 = (bf16[1,256,128]{2,1,0:T(8,128)(2,1)S(1)}, bf16[1,256,128]{2,1,0:T(8,128)(2,1)S(1)}, u32[]{:S(2)}, u32[]{:S(2)}) collective-permute-start(bf16[1,256,128]{2,1,0:T(8,128)(2,1)S(1)} %bitcast.25), channel_id=1, source_target_pairs={{0,16},{2,18},{4,20},{6,22},{8,24},{10,26},{12,28},{14,30},{16,0},... | collective-permute-start | bytes 196616 | tf_op jit(solution)/shard_map/ppermute | solution.py:29
  13.6 1.5 %collective-permute-start.3 = (bf16[2,256,128]{2,1,0:T(8,128)(2,1)S(1)}, bf16[2,256,128]{2,1,0:T(8,128)(2,1)S(1)}, u32[]{:S(2)}, u32[]{:S(2)}) collective-permute-start(bf16[2,256,128]{2,1,0:T(8,128)(2,1)S(1)} %pad_maximum_fusion.5), channel_id=1, source_target_pairs={{0,32},{2,34},{4,36},{6,38},{8,40},{10,42},{12,44},{14,46},{16,48}... | collective-permute-start | bytes 393224 | tf_op jit(solution)/shard_map/ppermute | solution.py:29
  15.2 0.1 copy.14
  15.3 0.8 pad_add_fusion.1
  16.1 1.3 collective-permute-start
  17.4 0.1 collective-permute-start.12
  17.5 0.4 collective-permute-start.13
  17.9 4.3 %collective-permute-start.4 = (bf16[4,256,128]{2,1,0:T(8,128)(2,1)S(1)}, bf16[4,256,128]{2,1,0:T(8,128)(2,1)S(1)}, u32[]{:S(2)}, u32[]{:S(2)}) collective-permute-start(bf16[4,256,128]{2,1,0:T(8,128)(2,1)S(1)} %pad_maximum_fusion.2), channel_id=1, source_target_pairs={{0,192},{2,30},{4,196},{6,2},{8,200},{10,6},{12,204},{14,10},{16,2... | collective-permute-start | bytes 786440 | tf_op jit(solution)/shard_map/ppermute | solution.py:29
  22.2 0.7 constant_dynamic-update-slice_fusion.6
  22.9 0.7 constant_dynamic-update-slice_fusion.5
  23.6 0.8 constant_dynamic-update-slice_fusion.4
  24.3 4.6 %collective-permute-done.5 = bf16[4,256,128]{2,1,0:T(8,128)(2,1)S(1)} collective-permute-done((bf16[4,256,128]{2,1,0:T(8,128)(2,1)S(1)}, bf16[4,256,128]{2,1,0:T(8,128)(2,1)S(1)}, u32[]{:S(2)}, u32[]{:S(2)}) %collective-permute-start.5) | collective-permute-done | bytes 262176 | tf_op jit(solution)/shard_map/ppermute | solution.py:29
  29.0 0.1 collective-permute-start.6
  29.1 2.7 %collective-permute-start.7 = (bf16[2,256,128]{2,1,0:T(8,128)(2,1)S(1)}, bf16[2,256,128]{2,1,0:T(8,128)(2,1)S(1)}, u32[]{:S(2)}, u32[]{:S(2)}) collective-permute-start(bf16[2,256,128]{2,1,0:T(8,128)(2,1)S(1)} %slice.101), channel_id=1, source_target_pairs={{0,192},{2,30},{4,196},{6,2},{8,200},{10,6},{12,204},{14,10},{16,2... | collective-permute-start | bytes 393224 | tf_op jit(solution)/shard_map/ppermute | solution.py:29
  31.8 0.9 constant_dynamic-update-slice_fusion.3
  32.7 0.9 constant_dynamic-update-slice_fusion.2
  33.5 0.5 collective-permute-done.6
  34.1 2.8 %collective-permute-start.14 = (bf16[64,128,128]{2,1,0:T(8,128)(2,1)}, bf16[64,128,128]{2,1,0:T(8,128)(2,1)}, u32[]{:S(2)}, u32[]{:S(2)}) collective-permute-start(bf16[64,128,128]{2,1,0:T(8,128)(2,1)} %d0.3), channel_id=1, source_target_pairs={{0,2},{2,0},{4,6},{6,4},{8,10},{10,8},{12,14},{14,12},{16,18},{18,... | collective-permute-start | bytes 6291464 | tf_op jit(solution)/shard_map/ppermute | solution.py:29
  36.9 0.7 constant_dynamic-update-slice_fusion.1
  37.6 0.7 constant_dynamic-update-slice_fusion
  38.3 2.7 %collective-permute-start.8 = (bf16[16,256,128]{2,1,0:T(8,128)(2,1)}, bf16[16,256,128]{2,1,0:T(8,128)(2,1)}, u32[]{:S(2)}, u32[]{:S(2)}) collective-permute-start(bf16[16,256,128]{2,1,0:T(8,128)(2,1)} %get-tuple-element.24), channel_id=1, source_target_pairs={{0,28},{2,194},{4,0},{6,198},{8,4},{10,202},{12,8},{14,206},{16,12... | collective-permute-start | bytes 3145736 | tf_op jit(solution)/shard_map/ppermute | solution.py:29
  41.1 0.2 slice_reduce_fusion
  41.3 0.3 select_reduce_fusion
  41.6 12.1 %collective-permute-done.9 = bf16[16,256,128]{2,1,0:T(8,128)(2,1)S(1)} collective-permute-done((bf16[16,256,128]{2,1,0:T(8,128)(2,1)}, bf16[16,256,128]{2,1,0:T(8,128)(2,1)S(1)}, u32[]{:S(2)}, u32[]{:S(2)}) %collective-permute-start.9) | collective-permute-done | bytes 1048608 | tf_op jit(solution)/shard_map/ppermute | solution.py:29
  53.7 0.8 slice.102
  54.5 1.9 %slice.103 = bf16[8,256,128]{2,1,0:T(8,128)(2,1)} slice(bf16[16,256,128]{2,1,0:T(8,128)(2,1)} %collective-permute-done.8), slice={[8:16], [0:256], [0:128]} | slice | bytes 1048576 | tf_op jit(solution)/shard_map/slice | solution.py:52
  56.4 2.7 %collective-permute-start.11 = (bf16[8,256,128]{2,1,0:T(8,128)(2,1)}, bf16[8,256,128]{2,1,0:T(8,128)(2,1)}, u32[]{:S(2)}, u32[]{:S(2)}) collective-permute-start(bf16[8,256,128]{2,1,0:T(8,128)(2,1)} %slice.103), channel_id=1, source_target_pairs={{0,28},{2,194},{4,0},{6,198},{8,4},{10,202},{12,8},{14,206},{16,12... | collective-permute-start | bytes 1572872 | tf_op jit(solution)/shard_map/ppermute | solution.py:29
  59.2 2.4 %constant_dynamic-update-slice_fusion.10 = bf16[64,256,128]{2,1,0:T(8,128)(2,1)} fusion(bf16[64,256,128]{2,1,0:T(8,128)(2,1)} %get-tuple-element.25, bf16[16,256,128]{2,1,0:T(8,128)(2,1)} %collective-permute-done.8), kind=kLoop, calls=%fused_computation.38 | loop fusion | bytes 2097152
  61.7 1.0 constant_dynamic-update-slice_fusion.9
  62.7 1.7 %collective-permute-done.10 = bf16[8,256,128]{2,1,0:T(8,128)(2,1)} collective-permute-done((bf16[8,256,128]{2,1,0:T(8,128)(2,1)}, bf16[8,256,128]{2,1,0:T(8,128)(2,1)}, u32[]{:S(2)}, u32[]{:S(2)}) %collective-permute-start.10) | collective-permute-done | bytes 524320 | tf_op jit(solution)/shard_map/ppermute | solution.py:29
  64.4 1.9 %constant_dynamic-update-slice_fusion.8 = bf16[64,256,128]{2,1,0:T(8,128)(2,1)} fusion(bf16[64,256,128]{2,1,0:T(8,128)(2,1)} %constant_dynamic-update-slice_fusion.9, bf16[8,256,128]{2,1,0:T(8,128)(2,1)} %collective-permute-done.10), kind=kLoop, calls=%fused_computation.36 | loop fusion | bytes 1048576
  66.3 1.9 %constant_dynamic-update-slice_fusion.7.all_ref = bf16[64,256,128]{2,1,0:T(8,128)(2,1)} fusion(bf16[64,256,128]{2,1,0:T(8,128)(2,1)} %constant_dynamic-update-slice_fusion.8, bf16[8,256,128]{2,1,0:T(8,128)(2,1)} %collective-permute-done.11), kind=kLoop, calls=%fused_computation.35 | loop fusion | bytes 1048576 | tf_op jit(solution)/shard_map/concatenate | solution.py:53
  68.2 6.8 %shard_map.123.mine_ref = f32[256,512]{1,0:T(8,128)S(1)} custom-call(s32[385]{0:T(512)S(1)} %pad_add_fusion.2.maps_ref, bf16[64,256,128]{2,1,0:T(8,128)(2,1)} %constant_dynamic-update-slice_fusion.7.all_ref, bf16[64,128,128]{2,1,0:T(8,128)(2,1)S(1)} %copy-done, bf16[64,128,128]{2,1,0:T(8,128)(2,1)S(1)} %copy-done.1, ...), custom_call_target="tpu_custom_call" | custom-call | flops 2147483648 | bytes 16777216 | tf_op jit(solution)/shard_map/pallas_call | solution.py:198
  75.0 4.1 %collective-permute-start.15 = (f32[256,512]{1,0:T(8,128)S(1)}, f32[256,512]{1,0:T(8,128)S(1)}, u32[]{:S(2)}, u32[]{:S(2)}) collective-permute-start(f32[256,512]{1,0:T(8,128)S(1)} %shard_map.123.mine_ref), channel_id=1, source_target_pairs={{0,2},{2,0},{4,6},{6,4},{8,10},{10,8},{12,14},{14,12},{16,18},{18,... | collective-permute-start | bytes 1572872 | tf_op jit(solution)/shard_map/ppermute | solution.py:29
  79.1 1.5 %collective-permute-done.15.theirs_ref = f32[256,512]{1,0:T(8,128)S(1)} collective-permute-done((f32[256,512]{1,0:T(8,128)S(1)}, f32[256,512]{1,0:T(8,128)S(1)}, u32[]{:S(2)}, u32[]{:S(2)}) %collective-permute-start.15) | collective-permute-done | bytes 524320 | tf_op jit(solution)/shard_map/ppermute | solution.py:29
  80.7 7.5 %shard_map.124 = (f32[16,256,128]{2,1,0:T(8,128)S(1)}, f32[16,256,128]{2,1,0:T(8,128)S(1)}, f32[16,256,128]{2,1,0:T(8,128)S(1)}, bf16[16,256,128]{2,1,0:T(8,128)(2,1)S(1)}) custom-call(s32[385]{0:T(512)S(1)} %pad_add_fusion.2.maps_ref, f32[256,512]{1,0:T(8,128)S(1)} %shard_map.123.mine_ref, f32[256,512]{1,0:T(8,128)S(1)} %collective-permute-done.15.theirs_ref, ...), custom_call_target="tpu_custom_call" | custom-call | flops 2147483648 | bytes 16777216 | tf_op jit(solution)/shard_map/pallas_call | solution.py:198
  88.3 0.1 collective-permute-start.16
  88.4 2.7 %collective-permute-start.18 = (bf16[8,256,128]{2,1,0:T(8,128)(2,1)S(1)}, bf16[8,256,128]{2,1,0:T(8,128)(2,1)S(1)}, u32[]{:S(2)}, u32[]{:S(2)}) collective-permute-start(bf16[8,256,128]{2,1,0:T(8,128)(2,1)S(1)} %get-tuple-element.19), channel_id=1, source_target_pairs={{0,28},{2,194},{4,0},{6,198},{8,4},{10,202},{12,8},{14,206},{16,12... | collective-permute-start | bytes 1572872 | tf_op jit(solution)/shard_map/ppermute | solution.py:29
  91.2 6.4 %collective-permute-done.16 = bf16[8,256,128]{2,1,0:T(8,128)(2,1)S(1)} collective-permute-done((bf16[8,256,128]{2,1,0:T(8,128)(2,1)S(1)}, bf16[8,256,128]{2,1,0:T(8,128)(2,1)S(1)}, u32[]{:S(2)}, u32[]{:S(2)}) %collective-permute-start.16) | collective-permute-done | bytes 524320 | tf_op jit(solution)/shard_map/ppermute | solution.py:29
  97.6 0.1 add_convert_fusion.1
  97.8 0.1 pad_maximum_fusion
  97.9 0.1 collective-permute-start.17
  98.0 0.1 add_convert_fusion
  98.1 0.1 pad_maximum_fusion.1
  98.2 2.7 %collective-permute-start.19 = (bf16[16,256,128]{2,1,0:T(8,128)(2,1)S(1)}, bf16[16,256,128]{2,1,0:T(8,128)(2,1)S(1)}, u32[]{:S(2)}, u32[]{:S(2)}) collective-permute-start(bf16[16,256,128]{2,1,0:T(8,128)(2,1)S(1)} %pad_maximum_fusion.1), channel_id=1, source_target_pairs={{0,28},{2,194},{4,0},{6,198},{8,4},{10,202},{12,8},{14,206},{16,12... | collective-permute-start | bytes 3145736 | tf_op jit(solution)/shard_map/ppermute | solution.py:29
  100.9 12.2 %collective-permute-done.17 = bf16[16,256,128]{2,1,0:T(8,128)(2,1)S(1)} collective-permute-done((bf16[16,256,128]{2,1,0:T(8,128)(2,1)S(1)}, bf16[16,256,128]{2,1,0:T(8,128)(2,1)S(1)}, u32[]{:S(2)}, u32[]{:S(2)}) %collective-permute-start.17) | collective-permute-done | bytes 1048608 | tf_op jit(solution)/shard_map/ppermute | solution.py:29
  113.1 0.5 fusion.7
  113.7 3.1 %collective-permute-start.22 = (bf16[2,256,128]{2,1,0:T(8,128)(2,1)S(1)}, bf16[2,256,128]{2,1,0:T(8,128)(2,1)S(1)}, u32[]{:S(2)}, u32[]{:S(2)}) collective-permute-start(bf16[2,256,128]{2,1,0:T(8,128)(2,1)S(1)} %get-tuple-element.16), channel_id=1, source_target_pairs={{0,192},{2,30},{4,196},{6,2},{8,200},{10,6},{12,204},{14,10},{16,2... | collective-permute-start | bytes 393224 | tf_op jit(solution)/shard_map/ppermute | solution.py:29
  116.8 2.6 %collective-permute-done.20 = bf16[2,256,128]{2,1,0:T(8,128)(2,1)S(1)} collective-permute-done((bf16[2,256,128]{2,1,0:T(8,128)(2,1)S(1)}, bf16[2,256,128]{2,1,0:T(8,128)(2,1)S(1)}, u32[]{:S(2)}, u32[]{:S(2)}) %collective-permute-start.20) | collective-permute-done | bytes 131104 | tf_op jit(solution)/shard_map/ppermute | solution.py:29
  119.4 3.0 %collective-permute-start.21 = (bf16[4,256,128]{2,1,0:T(8,128)(2,1)S(1)}, bf16[4,256,128]{2,1,0:T(8,128)(2,1)S(1)}, u32[]{:S(2)}, u32[]{:S(2)}) collective-permute-start(bf16[4,256,128]{2,1,0:T(8,128)(2,1)S(1)} %pad_maximum_fusion.3), channel_id=1, source_target_pairs={{0,64},{2,6},{4,68},{6,10},{8,72},{10,14},{12,76},{14,18},{16,80},... | collective-permute-start | bytes 786440 | tf_op jit(solution)/shard_map/ppermute | solution.py:29
  122.5 3.7 %collective-permute-done.21 = bf16[4,256,128]{2,1,0:T(8,128)(2,1)S(1)} collective-permute-done((bf16[4,256,128]{2,1,0:T(8,128)(2,1)S(1)}, bf16[4,256,128]{2,1,0:T(8,128)(2,1)S(1)}, u32[]{:S(2)}, u32[]{:S(2)}) %collective-permute-start.21) | collective-permute-done | bytes 262176 | tf_op jit(solution)/shard_map/ppermute | solution.py:29
  126.2 1.8 %collective-permute-done.23 = bf16[4,256,128]{2,1,0:T(8,128)(2,1)S(1)} collective-permute-done((bf16[4,256,128]{2,1,0:T(8,128)(2,1)S(1)}, bf16[4,256,128]{2,1,0:T(8,128)(2,1)S(1)}, u32[]{:S(2)}, u32[]{:S(2)}) %collective-permute-start.23) | collective-permute-done | bytes 262176 | tf_op jit(solution)/shard_map/ppermute | solution.py:29
  128.2 1.3 collective-permute-start.24
  129.5 3.0 %collective-permute-done.24 = bf16[2,256,128]{2,1,0:T(8,128)(2,1)S(1)} collective-permute-done((bf16[2,256,128]{2,1,0:T(8,128)(2,1)S(1)}, bf16[2,256,128]{2,1,0:T(8,128)(2,1)S(1)}, u32[]{:S(2)}, u32[]{:S(2)}) %collective-permute-start.24) | collective-permute-done | bytes 131104 | tf_op jit(solution)/shard_map/ppermute | solution.py:29
  132.5 2.6 %collective-permute-start.25 = (bf16[256,128]{1,0:T(8,128)(2,1)S(1)}, bf16[256,128]{1,0:T(8,128)(2,1)S(1)}, u32[]{:S(2)}, u32[]{:S(2)}) collective-permute-start(bf16[256,128]{1,0:T(8,128)(2,1)S(1)} %fusion.5), channel_id=1, source_target_pairs={{0,16},{2,18},{4,20},{6,22},{8,24},{10,26},{12,28},{14,30},{16,0},... | collective-permute-start | bytes 196616 | tf_op jit(solution)/shard_map/ppermute | solution.py:29
  135.1 5.2 %collective-permute-done.25 = bf16[256,128]{1,0:T(8,128)(2,1)S(1)} collective-permute-done((bf16[256,128]{1,0:T(8,128)(2,1)S(1)}, bf16[256,128]{1,0:T(8,128)(2,1)S(1)}, u32[]{:S(2)}, u32[]{:S(2)}) %collective-permute-start.25) | collective-permute-done | bytes 65568 | tf_op jit(solution)/shard_map/ppermute | solution.py:29
  140.4 0.1 shard_map.125
  140.5 2.2 %collective-permute-start.26 = (bf16[64,256]{1,0:T(8,128)(2,1)S(1)}, bf16[64,256]{1,0:T(8,128)(2,1)S(1)}, u32[]{:S(2)}, u32[]{:S(2)}) collective-permute-start(bf16[64,256]{1,0:T(8,128)(2,1)S(1)} %broadcast_select_fusion.1), channel_id=1, source_target_pairs={{0,2},{2,0},{4,6},{6,4},{8,10},{10,8},{12,14},{14,12},{16,18},{18,... | collective-permute-start | bytes 98312 | tf_op jit(solution)/shard_map/ppermute | solution.py:29
  142.7 0.9 collective-permute-done.26
  143.6 0.6 select_bitcast_fusion
  (55 shorter events, 1.2 us)
Async XLA Ops:
  0.6 40.4 %copy-start.4 = (s32[1,64]{1,0:T(1,128)S(1)}, s32[1,64]{1,0:T(1,128)}, u32[]{:S(2)}) copy-start(s32[1,64]{1,0:T(1,128)} %param.14) | copy-start | bytes 772
  0.6 40.4 %copy-start.3 = (s32[1,64]{1,0:T(1,128)S(1)}, s32[1,64]{1,0:T(1,128)}, u32[]{:S(2)}) copy-start(s32[1,64]{1,0:T(1,128)} %param.17) | copy-start | bytes 772
  0.7 40.4 %copy-start.2 = (s32[1,64]{1,0:T(1,128)S(1)}, s32[1,64]{1,0:T(1,128)}, u32[]{:S(2)}) copy-start(s32[1,64]{1,0:T(1,128)} %param.20) | copy-start | bytes 772
  1.4 4.1 %collective-permute-start.1 = (bf16[64,256]{1,0:T(8,128)(2,1)S(1)}, bf16[64,256]{1,0:T(8,128)(2,1)S(1)}, u32[]{:S(2)}, u32[]{:S(2)}) collective-permute-start(bf16[64,256]{1,0:T(8,128)(2,1)S(1)} %select_bitcast_fusion.2), channel_id=1, source_target_pairs={{0,2},{2,0},{4,6},{6,4},{8,10},{10,8},{12,14},{14,12},{16,18},{18,... | collective-permute-start | bytes 98312 | tf_op jit(solution)/shard_map/ppermute | solution.py:29
  6.4 7.2 %collective-permute-start.2 = (bf16[1,256,128]{2,1,0:T(8,128)(2,1)S(1)}, bf16[1,256,128]{2,1,0:T(8,128)(2,1)S(1)}, u32[]{:S(2)}, u32[]{:S(2)}) collective-permute-start(bf16[1,256,128]{2,1,0:T(8,128)(2,1)S(1)} %bitcast.25), channel_id=1, source_target_pairs={{0,16},{2,18},{4,20},{6,22},{8,24},{10,26},{12,28},{14,30},{16,0},... | collective-permute-start | bytes 196616 | tf_op jit(solution)/shard_map/ppermute | solution.py:29
  13.6 4.2 %collective-permute-start.3 = (bf16[2,256,128]{2,1,0:T(8,128)(2,1)S(1)}, bf16[2,256,128]{2,1,0:T(8,128)(2,1)S(1)}, u32[]{:S(2)}, u32[]{:S(2)}) collective-permute-start(bf16[2,256,128]{2,1,0:T(8,128)(2,1)S(1)} %pad_maximum_fusion.5), channel_id=1, source_target_pairs={{0,32},{2,34},{4,36},{6,38},{8,40},{10,42},{12,44},{14,46},{16,48}... | collective-permute-start | bytes 393224 | tf_op jit(solution)/shard_map/ppermute | solution.py:29
  16.1 22.2 %collective-permute-start = (s32[3,65]{1,0:T(4,128)S(1)}, s32[3,65]{1,0:T(4,128)S(1)}, u32[]{:S(2)}, u32[]{:S(2)}) collective-permute-start(s32[3,65]{1,0:T(4,128)S(1)} %pad_add_fusion.1), channel_id=1, source_target_pairs={{0,2},{2,0},{4,6},{6,4},{8,10},{10,8},{12,14},{14,12},{16,18},{18,... | collective-permute-start | bytes 2348 | tf_op jit(solution)/shard_map/ppermute | solution.py:29
  17.4 50.8 %collective-permute-start.12 = (bf16[64,128,128]{2,1,0:T(8,128)(2,1)}, bf16[64,128,128]{2,1,0:T(8,128)(2,1)}, u32[]{:S(2)}, u32[]{:S(2)}) collective-permute-start(bf16[64,128,128]{2,1,0:T(8,128)(2,1)} %g0.3), channel_id=1, source_target_pairs={{0,2},{2,0},{4,6},{6,4},{8,10},{10,8},{12,14},{14,12},{16,18},{18,... | collective-permute-start | bytes 6291464 | tf_op jit(solution)/shard_map/ppermute | solution.py:29
  17.5 50.7 %collective-permute-start.13 = (bf16[64,128,128]{2,1,0:T(8,128)(2,1)}, bf16[64,128,128]{2,1,0:T(8,128)(2,1)}, u32[]{:S(2)}, u32[]{:S(2)}) collective-permute-start(bf16[64,128,128]{2,1,0:T(8,128)(2,1)} %u0.3), channel_id=1, source_target_pairs={{0,2},{2,0},{4,6},{6,4},{8,10},{10,8},{12,14},{14,12},{16,18},{18,... | collective-permute-start | bytes 6291464 | tf_op jit(solution)/shard_map/ppermute | solution.py:29
  17.9 11.2 %collective-permute-start.4 = (bf16[4,256,128]{2,1,0:T(8,128)(2,1)S(1)}, bf16[4,256,128]{2,1,0:T(8,128)(2,1)S(1)}, u32[]{:S(2)}, u32[]{:S(2)}) collective-permute-start(bf16[4,256,128]{2,1,0:T(8,128)(2,1)S(1)} %pad_maximum_fusion.2), channel_id=1, source_target_pairs={{0,192},{2,30},{4,196},{6,2},{8,200},{10,6},{12,204},{14,10},{16,2... | collective-permute-start | bytes 786440 | tf_op jit(solution)/shard_map/ppermute | solution.py:29
  22.2 6.7 %collective-permute-start.5 = (bf16[4,256,128]{2,1,0:T(8,128)(2,1)S(1)}, bf16[4,256,128]{2,1,0:T(8,128)(2,1)S(1)}, u32[]{:S(2)}, u32[]{:S(2)}) collective-permute-start(bf16[4,256,128]{2,1,0:T(8,128)(2,1)S(1)} %pad_maximum_fusion.2), channel_id=1, source_target_pairs={{0,64},{2,6},{4,68},{6,10},{8,72},{10,14},{12,76},{14,18},{16,80},... | collective-permute-start | bytes 786440 | tf_op jit(solution)/shard_map/ppermute | solution.py:29
  29.0 5.1 %collective-permute-start.6 = (bf16[2,256,128]{2,1,0:T(8,128)(2,1)S(1)}, bf16[2,256,128]{2,1,0:T(8,128)(2,1)S(1)}, u32[]{:S(2)}, u32[]{:S(2)}) collective-permute-start(bf16[2,256,128]{2,1,0:T(8,128)(2,1)S(1)} %slice.100), channel_id=1, source_target_pairs={{0,64},{2,6},{4,68},{6,10},{8,72},{10,14},{12,76},{14,18},{16,80},... | collective-permute-start | bytes 393224 | tf_op jit(solution)/shard_map/ppermute | solution.py:29
  29.1 8.5 %collective-permute-start.7 = (bf16[2,256,128]{2,1,0:T(8,128)(2,1)S(1)}, bf16[2,256,128]{2,1,0:T(8,128)(2,1)S(1)}, u32[]{:S(2)}, u32[]{:S(2)}) collective-permute-start(bf16[2,256,128]{2,1,0:T(8,128)(2,1)S(1)} %slice.101), channel_id=1, source_target_pairs={{0,192},{2,30},{4,196},{6,2},{8,200},{10,6},{12,204},{14,10},{16,2... | collective-permute-start | bytes 393224 | tf_op jit(solution)/shard_map/ppermute | solution.py:29
  34.1 34.1 %collective-permute-start.14 = (bf16[64,128,128]{2,1,0:T(8,128)(2,1)}, bf16[64,128,128]{2,1,0:T(8,128)(2,1)}, u32[]{:S(2)}, u32[]{:S(2)}) collective-permute-start(bf16[64,128,128]{2,1,0:T(8,128)(2,1)} %d0.3), channel_id=1, source_target_pairs={{0,2},{2,0},{4,6},{6,4},{8,10},{10,8},{12,14},{14,12},{16,18},{18,... | collective-permute-start | bytes 6291464 | tf_op jit(solution)/shard_map/ppermute | solution.py:29
  38.3 15.4 %collective-permute-start.9 = (bf16[16,256,128]{2,1,0:T(8,128)(2,1)}, bf16[16,256,128]{2,1,0:T(8,128)(2,1)S(1)}, u32[]{:S(2)}, u32[]{:S(2)}) collective-permute-start(bf16[16,256,128]{2,1,0:T(8,128)(2,1)} %get-tuple-element.24), channel_id=1, source_target_pairs={{0,4},{2,66},{4,8},{6,70},{8,12},{10,74},{12,16},{14,78},{16,20},{... | collective-permute-start | bytes 3145736 | tf_op jit(solution)/shard_map/ppermute | solution.py:29
  38.3 16.2 %collective-permute-start.8 = (bf16[16,256,128]{2,1,0:T(8,128)(2,1)}, bf16[16,256,128]{2,1,0:T(8,128)(2,1)}, u32[]{:S(2)}, u32[]{:S(2)}) collective-permute-start(bf16[16,256,128]{2,1,0:T(8,128)(2,1)} %get-tuple-element.24), channel_id=1, source_target_pairs={{0,28},{2,194},{4,0},{6,198},{8,4},{10,202},{12,8},{14,206},{16,12... | collective-permute-start | bytes 3145736 | tf_op jit(solution)/shard_map/ppermute | solution.py:29
  41.6 26.6 %copy-start = (bf16[64,128,128]{2,1,0:T(8,128)(2,1)S(1)}, bf16[64,128,128]{2,1,0:T(8,128)(2,1)}, u32[]{:S(2)}) copy-start(bf16[64,128,128]{2,1,0:T(8,128)(2,1)} %g0.3) | copy-start | bytes 6291460
  54.5 9.9 %collective-permute-start.10 = (bf16[8,256,128]{2,1,0:T(8,128)(2,1)}, bf16[8,256,128]{2,1,0:T(8,128)(2,1)}, u32[]{:S(2)}, u32[]{:S(2)}) collective-permute-start(bf16[8,256,128]{2,1,0:T(8,128)(2,1)} %slice.102), channel_id=1, source_target_pairs={{0,4},{2,66},{4,8},{6,70},{8,12},{10,74},{12,16},{14,78},{16,20},{... | collective-permute-start | bytes 1572872 | tf_op jit(solution)/shard_map/ppermute | solution.py:29
  56.4 9.8 %collective-permute-start.11 = (bf16[8,256,128]{2,1,0:T(8,128)(2,1)}, bf16[8,256,128]{2,1,0:T(8,128)(2,1)}, u32[]{:S(2)}, u32[]{:S(2)}) collective-permute-start(bf16[8,256,128]{2,1,0:T(8,128)(2,1)} %slice.103), channel_id=1, source_target_pairs={{0,28},{2,194},{4,0},{6,198},{8,4},{10,202},{12,8},{14,206},{16,12... | collective-permute-start | bytes 1572872 | tf_op jit(solution)/shard_map/ppermute | solution.py:29
  59.2 9.0 %copy-start.1 = (bf16[64,128,128]{2,1,0:T(8,128)(2,1)S(1)}, bf16[64,128,128]{2,1,0:T(8,128)(2,1)}, u32[]{:S(2)}) copy-start(bf16[64,128,128]{2,1,0:T(8,128)(2,1)} %u0.3) | copy-start | bytes 6291460
  75.0 5.7 %collective-permute-start.15 = (f32[256,512]{1,0:T(8,128)S(1)}, f32[256,512]{1,0:T(8,128)S(1)}, u32[]{:S(2)}, u32[]{:S(2)}) collective-permute-start(f32[256,512]{1,0:T(8,128)S(1)} %shard_map.123.mine_ref), channel_id=1, source_target_pairs={{0,2},{2,0},{4,6},{6,4},{8,10},{10,8},{12,14},{14,12},{16,18},{18,... | collective-permute-start | bytes 1572872 | tf_op jit(solution)/shard_map/ppermute | solution.py:29
  88.3 9.3 %collective-permute-start.16 = (bf16[8,256,128]{2,1,0:T(8,128)(2,1)S(1)}, bf16[8,256,128]{2,1,0:T(8,128)(2,1)S(1)}, u32[]{:S(2)}, u32[]{:S(2)}) collective-permute-start(bf16[8,256,128]{2,1,0:T(8,128)(2,1)S(1)} %get-tuple-element.18), channel_id=1, source_target_pairs={{0,4},{2,66},{4,8},{6,70},{8,12},{10,74},{12,16},{14,78},{16,20},{... | collective-permute-start | bytes 1572872 | tf_op jit(solution)/shard_map/ppermute | solution.py:29
  88.4 9.6 %collective-permute-start.18 = (bf16[8,256,128]{2,1,0:T(8,128)(2,1)S(1)}, bf16[8,256,128]{2,1,0:T(8,128)(2,1)S(1)}, u32[]{:S(2)}, u32[]{:S(2)}) collective-permute-start(bf16[8,256,128]{2,1,0:T(8,128)(2,1)S(1)} %get-tuple-element.19), channel_id=1, source_target_pairs={{0,28},{2,194},{4,0},{6,198},{8,4},{10,202},{12,8},{14,206},{16,12... | collective-permute-start | bytes 1572872 | tf_op jit(solution)/shard_map/ppermute | solution.py:29
  97.9 15.2 %collective-permute-start.17 = (bf16[16,256,128]{2,1,0:T(8,128)(2,1)S(1)}, bf16[16,256,128]{2,1,0:T(8,128)(2,1)S(1)}, u32[]{:S(2)}, u32[]{:S(2)}) collective-permute-start(bf16[16,256,128]{2,1,0:T(8,128)(2,1)S(1)} %pad_maximum_fusion), channel_id=1, source_target_pairs={{0,4},{2,66},{4,8},{6,70},{8,12},{10,74},{12,16},{14,78},{16,20},{... | collective-permute-start | bytes 3145736 | tf_op jit(solution)/shard_map/ppermute | solution.py:29
  98.2 14.9 %collective-permute-start.19 = (bf16[16,256,128]{2,1,0:T(8,128)(2,1)S(1)}, bf16[16,256,128]{2,1,0:T(8,128)(2,1)S(1)}, u32[]{:S(2)}, u32[]{:S(2)}) collective-permute-start(bf16[16,256,128]{2,1,0:T(8,128)(2,1)S(1)} %pad_maximum_fusion.1), channel_id=1, source_target_pairs={{0,28},{2,194},{4,0},{6,198},{8,4},{10,202},{12,8},{14,206},{16,12... | collective-permute-start | bytes 3145736 | tf_op jit(solution)/shard_map/ppermute | solution.py:29
  113.6 5.7 %collective-permute-start.20 = (bf16[2,256,128]{2,1,0:T(8,128)(2,1)S(1)}, bf16[2,256,128]{2,1,0:T(8,128)(2,1)S(1)}, u32[]{:S(2)}, u32[]{:S(2)}) collective-permute-start(bf16[2,256,128]{2,1,0:T(8,128)(2,1)S(1)} %get-tuple-element.17), channel_id=1, source_target_pairs={{0,64},{2,6},{4,68},{6,10},{8,72},{10,14},{12,76},{14,18},{16,80},... | collective-permute-start | bytes 393224 | tf_op jit(solution)/shard_map/ppermute | solution.py:29
  113.7 5.6 %collective-permute-start.22 = (bf16[2,256,128]{2,1,0:T(8,128)(2,1)S(1)}, bf16[2,256,128]{2,1,0:T(8,128)(2,1)S(1)}, u32[]{:S(2)}, u32[]{:S(2)}) collective-permute-start(bf16[2,256,128]{2,1,0:T(8,128)(2,1)S(1)} %get-tuple-element.16), channel_id=1, source_target_pairs={{0,192},{2,30},{4,196},{6,2},{8,200},{10,6},{12,204},{14,10},{16,2... | collective-permute-start | bytes 393224 | tf_op jit(solution)/shard_map/ppermute | solution.py:29
  119.4 6.8 %collective-permute-start.21 = (bf16[4,256,128]{2,1,0:T(8,128)(2,1)S(1)}, bf16[4,256,128]{2,1,0:T(8,128)(2,1)S(1)}, u32[]{:S(2)}, u32[]{:S(2)}) collective-permute-start(bf16[4,256,128]{2,1,0:T(8,128)(2,1)S(1)} %pad_maximum_fusion.3), channel_id=1, source_target_pairs={{0,64},{2,6},{4,68},{6,10},{8,72},{10,14},{12,76},{14,18},{16,80},... | collective-permute-start | bytes 786440 | tf_op jit(solution)/shard_map/ppermute | solution.py:29
  122.4 5.6 %collective-permute-start.23 = (bf16[4,256,128]{2,1,0:T(8,128)(2,1)S(1)}, bf16[4,256,128]{2,1,0:T(8,128)(2,1)S(1)}, u32[]{:S(2)}, u32[]{:S(2)}) collective-permute-start(bf16[4,256,128]{2,1,0:T(8,128)(2,1)S(1)} %pad_maximum_fusion.4), channel_id=1, source_target_pairs={{0,192},{2,30},{4,196},{6,2},{8,200},{10,6},{12,204},{14,10},{16,2... | collective-permute-start | bytes 786440 | tf_op jit(solution)/shard_map/ppermute | solution.py:29
  128.2 4.3 %collective-permute-start.24 = (bf16[2,256,128]{2,1,0:T(8,128)(2,1)S(1)}, bf16[2,256,128]{2,1,0:T(8,128)(2,1)S(1)}, u32[]{:S(2)}, u32[]{:S(2)}) collective-permute-start(bf16[2,256,128]{2,1,0:T(8,128)(2,1)S(1)} %slice.138), channel_id=1, source_target_pairs={{0,32},{2,34},{4,36},{6,38},{8,40},{10,42},{12,44},{14,46},{16,48}... | collective-permute-start | bytes 393224 | tf_op jit(solution)/shard_map/ppermute | solution.py:29
  132.5 7.8 %collective-permute-start.25 = (bf16[256,128]{1,0:T(8,128)(2,1)S(1)}, bf16[256,128]{1,0:T(8,128)(2,1)S(1)}, u32[]{:S(2)}, u32[]{:S(2)}) collective-permute-start(bf16[256,128]{1,0:T(8,128)(2,1)S(1)} %fusion.5), channel_id=1, source_target_pairs={{0,16},{2,18},{4,20},{6,22},{8,24},{10,26},{12,28},{14,30},{16,0},... | collective-permute-start | bytes 196616 | tf_op jit(solution)/shard_map/ppermute | solution.py:29
  140.5 3.1 %collective-permute-start.26 = (bf16[64,256]{1,0:T(8,128)(2,1)S(1)}, bf16[64,256]{1,0:T(8,128)(2,1)S(1)}, u32[]{:S(2)}, u32[]{:S(2)}) collective-permute-start(bf16[64,256]{1,0:T(8,128)(2,1)S(1)} %broadcast_select_fusion.1), channel_id=1, source_target_pairs={{0,2},{2,0},{4,6},{6,4},{8,10},{10,8},{12,14},{14,12},{16,18},{18,... | collective-permute-start | bytes 98312 | tf_op jit(solution)/shard_map/ppermute | solution.py:29

commit v2 on v1

--- a/solution.py
+++ b/solution.py
@@ -1,3 +1,5 @@
+import functools
+
 import jax
 import jax.numpy as jnp
 from jax import lax
@@ -10,7 +12,8 @@
 BLOCK = 128
 SLOTS = NY * NX * NZ
 RING = 4
-PART = SLOTS // RING
+PIECES = 2 * RING
+PART = SLOTS // PIECES
 GROUP = 4
 F32 = jnp.float32
 BF16 = jnp.bfloat16
@@ -46,15 +49,50 @@
     return permute(value, target)
 
 
-def ring_gather(value, axes):
+def near(value):
+    far = permute(value, lambda at: at | {"x": 1 - at["x"], "z": (at["z"] + 4) % NZ})
+    ahead, beside = shift(value, "z", 4), shift(value, "x", 1)
+    return jnp.concatenate([value, ahead, beside, far])
+
+
+def near_reduce(total):
+    sent = total.astype(BF16)
+    far = permute(sent[3], lambda at: at | {"x": 1 - at["x"], "z": (at["z"] + 4) % NZ})
+    ahead, beside = shift(sent[1], "z", 4), shift(sent[2], "x", 1)
+    return total[0] + ahead.astype(F32) + beside.astype(F32) + far.astype(F32)
+
+
+def small_gather(value, axes):
     half = value.shape[0] // 2
-    up, down = turn(value, axes, 1), turn(value, axes, -1)
+    down, up = turn(value, axes, -1), turn(value, axes, 1)
     far_up, far_down = turn(up[:half], axes, 1), turn(down[half:], axes, -1)
-    return jnp.concatenate([value, down, up, far_up, far_down])
-
-
-def ring_reduce(parts, axes):
-    here, ahead, behind, far = parts
+    return jnp.concatenate([value, down]), jnp.concatenate([up, far_up, far_down])
+
+
+def large_gather(first, second, axes):
+    first_up, first_down = turn(first, axes, 1), turn(first, axes, -1)
+    second_down, second_up = turn(second, axes, -1), turn(second, axes, 1)
+    first_far, second_far = turn(first_up, axes, 1), turn(second_down, axes, -1)
+    return first, second, first_down, second_down, first_up, second_up, first_far, second_far
+
+
+SENT = (False, False, True, False, False, True, True, True)
+
+
+def large_reduce(parts, axes):
+    first, second, first_ahead, second_ahead, first_behind, second_behind, first_far, second_far = parts
+    second_far, first_far = turn(second_far, axes, 1), turn(first_far, axes, -1)
+    first_ahead, second_behind = turn(first_ahead, axes, 1), turn(second_behind, axes, -1)
+    second_ahead = turn((second_ahead + second_far.astype(F32)).astype(BF16), axes, 1)
+    first_behind = turn((first_behind + first_far.astype(F32)).astype(BF16), axes, -1)
+    first = first + first_ahead.astype(F32) + first_behind.astype(F32)
+    second = second + second_ahead.astype(F32) + second_behind.astype(F32)
+    return first, second
+
+
+def small_reduce(first, second, axes):
+    here, ahead = jnp.split(first, 2)
+    behind, far = jnp.split(second, 2)
     half = here.shape[0] // 2
     far = far.astype(BF16)
     down, up = turn(far[:half], axes, -1), turn(far[half:], axes, 1)
@@ -73,19 +111,25 @@
     return lax.dot_general(left, right, (((1,), (1,)), ((), ())), preferred_element_type=F32)
 
 
-def inner_kernel(maps_ref, all_ref, g0, u0, g1, u1, d0, d1, sums_ref):
+def inner_kernel(base, maps_ref, *refs):
+    *piece_refs, g0, u0, g1, u1, d0, d1, sums_ref = refs
     core = maps_ref[6 * SLOTS]
-    sums_ref[...] = jnp.zeros_like(sums_ref)
     wide = 2 * BLOCK
-
-    def gathered(i):
-        spots = [i * GROUP + j for j in range(GROUP)]
-        return spots, jnp.concatenate([all_ref[p] for p in spots], axis=1)
+    if base:
+        start_ref, *piece_refs = piece_refs
+        sums_ref[...] = start_ref[...]
+    else:
+        sums_ref[...] = jnp.zeros_like(sums_ref)
+
+    def groups():
+        for rank, ref in enumerate(piece_refs):
+            for i in range(0, PART, GROUP):
+                spots = [(base + rank) * PART + i + j for j in range(GROUP)]
+                yield spots, jnp.concatenate([ref[i + j] for j in range(GROUP)], axis=1)
 
     @pl.when(core == 0)
     def _():
-        def step(i, carry):
-            spots, left = gathered(i)
+        for spots, left in groups():
             for n, pair in enumerate((((0, g0), (1, u0)), ((3, g1), (4, u1)))):
                 right = jnp.concatenate(
                     [
@@ -95,14 +139,10 @@
                     axis=0,
                 )
                 sums_ref[:, pl.ds(n * wide, wide)] += jnp.dot(left, right, preferred_element_type=F32)
-            return carry
-
-        lax.fori_loop(0, SLOTS // GROUP, step, 0, unroll=4)
 
     @pl.when(core == 1)
     def _():
-        def step(i, carry):
-            spots, left = gathered(i)
+        for spots, left in groups():
             right = jnp.concatenate(
                 [
                     jnp.concatenate([read_block(maps_ref, k, ref, p) for p in spots], axis=1)
@@ -111,9 +151,6 @@
                 axis=0,
             )
             sums_ref[:, pl.ds(0, wide)] += contract_last(left, right)
-            return carry
-
-        lax.fori_loop(0, SLOTS // GROUP, step, 0, unroll=4)
 
 
 def outer_kernel(maps_ref, mine_ref, theirs_ref, g0, u0, g1, u1, d0, d1, *part_refs):
@@ -228,10 +265,7 @@
     other = shift(other, "c", 1)
     block = jnp.concatenate([jnp.where(first, own, other), jnp.where(first, other, own)])
     block = transpose(block).reshape(1, batch, BLOCK)
-    block = jnp.concatenate([block, shift(block, "z", 4)])
-    block = jnp.concatenate([block, shift(block, "x", 1)])
-    block = ring_gather(block, "yz")
-    block = ring_gather(block, "zy")
+    pieces = large_gather(*small_gather(near(block), "yz"), "zy")
 
     lists = jnp.concatenate([gate_index, up_index, down_index])
     counts = jnp.stack([gate_count, up_count, down_count])
@@ -257,18 +291,14 @@
 
     weights = (gate_blocks, up_blocks, shift(gate_blocks, "c", 1), shift(up_blocks, "c", 1))
     weights += (down_blocks, shift(down_blocks, "c", 1))
-    flops = 4 * NC * SLOTS * BLOCK * BLOCK * batch
-    mine = call(inner_kernel, jax.ShapeDtypeStruct((batch, 4 * BLOCK), F32), flops, maps, block, *weights)
+    flops = NC * SLOTS * BLOCK * BLOCK * batch
+    sums = jax.ShapeDtypeStruct((batch, 4 * BLOCK), F32)
+    mine = call(functools.partial(inner_kernel, 0), sums, 3 * flops, maps, *pieces[:6], *weights)
+    mine = call(functools.partial(inner_kernel, 6), sums, flops, maps, mine, *pieces[6:], *weights)
     theirs = shift(mine, "c", 1)
-    parts = tuple(
-        jax.ShapeDtypeStruct((PART, batch, BLOCK), BF16 if rank == RING - 1 else F32) for rank in range(RING)
-    )
-    parts = call(outer_kernel, parts, flops, maps, mine, theirs, *weights)
-
-    total = ring_reduce(parts, "zy")
-    total = ring_reduce(jnp.split(total, RING), "yz")
-    total = total[:2] + shift(total[2:].astype(BF16), "x", 1).astype(F32)
-    total = total[0] + shift(total[1].astype(BF16), "z", 4).astype(F32)
+    parts = tuple(jax.ShapeDtypeStruct((PART, batch, BLOCK), BF16 if sent else F32) for sent in SENT)
+    parts = call(outer_kernel, parts, 4 * flops, maps, mine, theirs, *weights)
+    total = near_reduce(small_reduce(*large_reduce(parts, "zy"), "yz"))
     total = transpose(total).astype(BF16)
     low, high = jnp.split(total, 2)
     own, other = jnp.where(first, low, high), jnp.where(first, high, low)

time: 145 us -> 138 us (0.952)
  local copies, waits for them, and re-layouts: 16 us -> 6.52 us
  starting transfers between devices: 49.1 us -> 51.6 us
    unnamed x19 -> x20, local copies, waits for them, and re-layouts: 9.94 us -> 5.12 us
    slice x9 -> x4, local copies, waits for them, and re-layouts: 3.05 us -> 0.07 us  [the longest x1 0.03 us: small_reduce(): down, up = (turn(far[:half], axes, -1), turn(far[half:], axes, 1))]
    ppermute x27 -> x33, starting transfers between devices: 49.1 us -> 51.6 us  [permute(): return lax.ppermute(value, 'tp', pairs)]
    concatenate x2, local copies, waits for them, and re-layouts: 2.62 us -> 0.96 us  [the longest x1 0.92 us: small_gather(): jnp.concatenate([up, far_up, far_down])]
    ppermute x27 -> x33, waiting for transfers between devices: 57.1 us -> 58.1 us  [permute(): return lax.ppermute(value, 'tp', pairs)]
    pallas_call x2 -> x3, Pallas kernels: 14.4 us -> 13.4 us  [call(): pl.pallas_call(kernel, out_shape=outs, in_specs=[pl.BlockSpec(memory_spac...]
  transfers between devices with their start and end apart: 27 -> 33, of which waited for: 14 -> 18; matrix products, arithmetic and copies ran while one was open for 12% -> 4% of each run, Pallas kernels for 0% -> 3%
where the time goes in v2:
time: 138 us
  waiting for transfers between devices  58.1 us (42%)
  starting transfers between devices  51.6 us (37%)
  Pallas kernels  13.6 us (10%)
  local copies, waits for them, and re-layouts  6.52 us (5%)
  other arithmetic  5.07 us (4%)
  between operations  2.95 us (2%)
    ppermute x33, waiting for transfers between devices, permute(): return lax.ppermute(value, 'tp', pairs)  58.1 us
    ppermute x33, starting transfers between devices, permute(): return lax.ppermute(value, 'tp', pairs)  51.6 us
    pallas_call x3, Pallas kernels, call(): pl.pallas_call(kernel, out_shape=outs, in_specs=[pl.BlockSpec(memory_spac...  13.4 us
    unnamed x20, local copies, waits for them, and re-layouts  5.12 us
  transfers between devices with their start and end apart: 33, of which 18 were waited for; matrix products, arithmetic and copies ran while one was open for 4% of the time, Pallas kernels for 3%

profile of v2, /device:TPU:1, one launch (start us, length us, event | category | flops | bytes accessed | tf_op | source)
XLA Modules:
  0.0 137.8 jit_solution(12468831693201624272)
XLA Ops:
  0.7 0.9 select_bitcast_fusion.2
  1.6 3.2 %collective-permute-start.1 = (bf16[64,256]{1,0:T(8,128)(2,1)S(1)}, bf16[64,256]{1,0:T(8,128)(2,1)S(1)}, u32[]{:S(2)}, u32[]{:S(2)}) collective-permute-start(bf16[64,256]{1,0:T(8,128)(2,1)S(1)} %select_bitcast_fusion.2), channel_id=1, source_target_pairs={{0,2},{2,0},{4,6},{6,4},{8,10},{10,8},{12,14},{14,12},{16,18},{18,... | collective-permute-start | bytes 98312 | tf_op jit(solution)/shard_map/ppermute | solution.py:32
  4.8 0.1 collective-permute-start.13
  4.9 0.4 collective-permute-start.14
  7.4 0.1 copy.14
  7.5 0.8 bitcast_select_fusion.1
  8.3 6.2 %collective-permute-start.4 = (bf16[1,256,128]{2,1,0:T(8,128)(2,1)S(1)}, bf16[1,256,128]{2,1,0:T(8,128)(2,1)S(1)}, u32[]{:S(2)}, u32[]{:S(2)}) collective-permute-start(bf16[1,256,128]{2,1,0:T(8,128)(2,1)S(1)} %bitcast.32), channel_id=1, source_target_pairs={{0,48},{2,50},{4,52},{6,54},{8,56},{10,58},{12,60},{14,62},{16,32}... | collective-permute-start | bytes 196616 | tf_op jit(solution)/shard_map/ppermute | solution.py:32
  14.5 0.3 collective-permute-start.3
  14.8 0.2 collective-permute-start.2
  15.0 0.8 pad_add_fusion.1
  15.7 1.6 %collective-permute-done.4 = bf16[1,256,128]{2,1,0:T(8,128)(2,1)S(1)} collective-permute-done((bf16[1,256,128]{2,1,0:T(8,128)(2,1)S(1)}, bf16[1,256,128]{2,1,0:T(8,128)(2,1)S(1)}, u32[]{:S(2)}, u32[]{:S(2)}) %collective-permute-start.4) | collective-permute-done | bytes 65568 | tf_op jit(solution)/shard_map/ppermute | solution.py:32
  17.3 1.1 collective-permute-start.15
  18.4 5.5 %collective-permute-done.2 = bf16[1,256,128]{2,1,0:T(8,128)(2,1)S(1)} collective-permute-done((bf16[1,256,128]{2,1,0:T(8,128)(2,1)S(1)}, bf16[1,256,128]{2,1,0:T(8,128)(2,1)S(1)}, u32[]{:S(2)}, u32[]{:S(2)}) %collective-permute-start.2) | collective-permute-done | bytes 65568 | tf_op jit(solution)/shard_map/ppermute | solution.py:32
  24.1 2.7 %collective-permute-start.5 = (bf16[4,256,128]{2,1,0:T(8,128)(2,1)S(1)}, bf16[4,256,128]{2,1,0:T(8,128)(2,1)S(1)}, u32[]{:S(2)}, u32[]{:S(2)}) collective-permute-start(bf16[4,256,128]{2,1,0:T(8,128)(2,1)S(1)} %pad_maximum_fusion), channel_id=1, source_target_pairs={{0,192},{2,30},{4,196},{6,2},{8,200},{10,6},{12,204},{14,10},{16,2... | collective-permute-start | bytes 786440 | tf_op jit(solution)/shard_map/ppermute | solution.py:32
  26.8 4.0 %collective-permute-done.6 = bf16[4,256,128]{2,1,0:T(8,128)(2,1)S(1)} collective-permute-done((bf16[4,256,128]{2,1,0:T(8,128)(2,1)S(1)}, bf16[4,256,128]{2,1,0:T(8,128)(2,1)S(1)}, u32[]{:S(2)}, u32[]{:S(2)}) %collective-permute-start.6) | collective-permute-done | bytes 262176 | tf_op jit(solution)/shard_map/ppermute | solution.py:32
  30.8 1.3 collective-permute-start
  32.2 1.1 collective-permute-start.7
  33.4 1.7 %collective-permute-start.8 = (bf16[2,256,128]{2,1,0:T(8,128)(2,1)S(1)}, bf16[2,256,128]{2,1,0:T(8,128)(2,1)}, u32[]{:S(2)}, u32[]{:S(2)}) collective-permute-start(bf16[2,256,128]{2,1,0:T(8,128)(2,1)S(1)} %slice.65), channel_id=1, source_target_pairs={{0,192},{2,30},{4,196},{6,2},{8,200},{10,6},{12,204},{14,10},{16,2... | collective-permute-start | bytes 393224 | tf_op jit(solution)/shard_map/ppermute | solution.py:32
  35.1 2.5 %collective-permute-done.7 = bf16[2,256,128]{2,1,0:T(8,128)(2,1)S(1)} collective-permute-done((bf16[2,256,128]{2,1,0:T(8,128)(2,1)S(1)}, bf16[2,256,128]{2,1,0:T(8,128)(2,1)S(1)}, u32[]{:S(2)}, u32[]{:S(2)}) %collective-permute-start.7) | collective-permute-done | bytes 131104 | tf_op jit(solution)/shard_map/ppermute | solution.py:32
  37.7 2.6 %collective-permute-start.9 = (bf16[8,256,128]{2,1,0:T(8,128)(2,1)S(1)}, bf16[8,256,128]{2,1,0:T(8,128)(2,1)}, u32[]{:S(2)}, u32[]{:S(2)}) collective-permute-start(bf16[8,256,128]{2,1,0:T(8,128)(2,1)S(1)} %constant_dynamic-update-slice_fusion.refs_0_), channel_id=1, source_target_pairs={{0,28},{2,194},{4,0},{6,198},{8,4},{10,202},{12,8},{14,206},{16,12... | collective-permute-start | bytes 1572872 | tf_op jit(solution)/shard_map/ppermute | solution.py:32
  40.3 0.9 constant_dynamic-update-slice_fusion.5.refs_1_
  41.2 6.0 %collective-permute-done.11.refs_4_ = bf16[8,256,128]{2,1,0:T(8,128)(2,1)} collective-permute-done((bf16[8,256,128]{2,1,0:T(8,128)(2,1)S(1)}, bf16[8,256,128]{2,1,0:T(8,128)(2,1)}, u32[]{:S(2)}, u32[]{:S(2)}) %collective-permute-start.11) | collective-permute-done | bytes 524320 | tf_op jit(solution)/shard_map/ppermute | solution.py:32
  47.2 2.7 %collective-permute-start.10 = (bf16[8,256,128]{2,1,0:T(8,128)(2,1)S(1)}, bf16[8,256,128]{2,1,0:T(8,128)(2,1)}, u32[]{:S(2)}, u32[]{:S(2)}) collective-permute-start(bf16[8,256,128]{2,1,0:T(8,128)(2,1)S(1)} %constant_dynamic-update-slice_fusion.5.refs_1_), channel_id=1, source_target_pairs={{0,28},{2,194},{4,0},{6,198},{8,4},{10,202},{12,8},{14,206},{16,12... | collective-permute-start | bytes 1572872 | tf_op jit(solution)/shard_map/ppermute | solution.py:32
  49.9 0.7 pad_add_fusion
  50.7 0.2 slice_reduce_fusion
  50.9 5.9 %collective-permute-done.12.refs_5_ = bf16[8,256,128]{2,1,0:T(8,128)(2,1)S(1)} collective-permute-done((bf16[8,256,128]{2,1,0:T(8,128)(2,1)S(1)}, bf16[8,256,128]{2,1,0:T(8,128)(2,1)S(1)}, u32[]{:S(2)}, u32[]{:S(2)}) %collective-permute-start.12) | collective-permute-done | bytes 524320 | tf_op jit(solution)/shard_map/ppermute | solution.py:32
  56.8 0.8 copy-done.3
  57.6 2.7 %collective-permute-start.17 = (bf16[8,256,128]{2,1,0:T(8,128)(2,1)}, bf16[8,256,128]{2,1,0:T(8,128)(2,1)}, u32[]{:S(2)}, u32[]{:S(2)}) collective-permute-start(bf16[8,256,128]{2,1,0:T(8,128)(2,1)} %collective-permute-done.10.refs_3_), channel_id=1, source_target_pairs={{0,28},{2,194},{4,0},{6,198},{8,4},{10,202},{12,8},{14,206},{16,12... | collective-permute-start | bytes 1572872 | tf_op jit(solution)/shard_map/ppermute | solution.py:32
  60.2 0.3 select_reduce_fusion
  60.7 1.6 %copy-done.1 = bf16[64,128,128]{2,1,0:T(8,128)(2,1)S(1)} copy-done((bf16[64,128,128]{2,1,0:T(8,128)(2,1)S(1)}, bf16[64,128,128]{2,1,0:T(8,128)(2,1)}, u32[]{:S(2)}) %copy-start.1) | copy-done | bytes 2097176
  62.2 1.6 %copy-done.2 = bf16[64,128,128]{2,1,0:T(8,128)(2,1)S(1)} copy-done((bf16[64,128,128]{2,1,0:T(8,128)(2,1)S(1)}, bf16[64,128,128]{2,1,0:T(8,128)(2,1)}, u32[]{:S(2)}) %copy-start.2) | copy-done | bytes 2097176
  63.8 1.0 copy-done.4
  64.9 4.4 %shard_map.123.refs_0_ = f32[256,512]{1,0:T(8,128)S(1)} custom-call(s32[385]{0:T(512)S(1)} %pad_add_fusion.2.maps_ref, bf16[8,256,128]{2,1,0:T(8,128)(2,1)S(1)} %constant_dynamic-update-slice_fusion.refs_0_, bf16[8,256,128]{2,1,0:T(8,128)(2,1)S(1)} %constant_dynamic-update-slice_fusion.5.refs_1_, bf16[8,256,128]{2,1,0:T(8,128)(2,1)} %collective-permute-done.9.refs_2_, ...), custom_call_target="tpu_custom_call" | custom-call | flops 1610612736 | bytes 16777216 | tf_op jit(solution)/shard_map/pallas_call | solution.py:235
  69.3 3.7 %shard_map.124.mine_ref = f32[256,512]{1,0:T(8,128)S(1)} custom-call(s32[385]{0:T(512)S(1)} %pad_add_fusion.2.maps_ref, f32[256,512]{1,0:T(8,128)S(1)} %shard_map.123.refs_0_, bf16[8,256,128]{2,1,0:T(8,128)(2,1)} %collective-permute-done.16.refs_1_, bf16[8,256,128]{2,1,0:T(8,128)(2,1)} %collective-permute-done.17.refs_2_, bf16[64,128,128]{2,1,0:T(8,128)(2,1)S(1)} %copy-done, ...), custom_call_target="tpu_custom_call" | custom-call | flops 536870912 | bytes 16777216 | tf_op jit(solution)/shard_map/pallas_call | solution.py:235
  73.1 4.5 %collective-permute-start.18 = (f32[256,512]{1,0:T(8,128)S(1)}, f32[256,512]{1,0:T(8,128)S(1)}, u32[]{:S(2)}, u32[]{:S(2)}) collective-permute-start(f32[256,512]{1,0:T(8,128)S(1)} %shard_map.124.mine_ref), channel_id=1, source_target_pairs={{0,2},{2,0},{4,6},{6,4},{8,10},{10,8},{12,14},{14,12},{16,18},{18,... | collective-permute-start | bytes 1572872 | tf_op jit(solution)/shard_map/ppermute | solution.py:32
  77.6 1.5 %collective-permute-done.18.theirs_ref = f32[256,512]{1,0:T(8,128)S(1)} collective-permute-done((f32[256,512]{1,0:T(8,128)S(1)}, f32[256,512]{1,0:T(8,128)S(1)}, u32[]{:S(2)}, u32[]{:S(2)}) %collective-permute-start.18) | collective-permute-done | bytes 524320 | tf_op jit(solution)/shard_map/ppermute | solution.py:32
  79.1 5.3 %shard_map.125 = (f32[8,256,128]{2,1,0:T(8,128)S(1)}, f32[8,256,128]{2,1,0:T(8,128)S(1)}, bf16[8,256,128]{2,1,0:T(8,128)(2,1)S(1)}, f32[8,256,128]{2,1,0:T(8,128...) custom-call(s32[385]{0:T(512)S(1)} %pad_add_fusion.2.maps_ref, ...), custom_call_target="tpu_custom_call" | custom-call | flops 2147483648 | bytes 16777216 | tf_op jit(solution)/shard_map/pallas_call | solution.py:235
  84.4 0.2 collective-permute-start.22
  84.6 2.6 %collective-permute-start.20 = (bf16[8,256,128]{2,1,0:T(8,128)(2,1)S(1)}, bf16[8,256,128]{2,1,0:T(8,128)(2,1)S(1)}, u32[]{:S(2)}, u32[]{:S(2)}) collective-permute-start(bf16[8,256,128]{2,1,0:T(8,128)(2,1)S(1)} %get-tuple-element.13), channel_id=1, source_target_pairs={{0,28},{2,194},{4,0},{6,198},{8,4},{10,202},{12,8},{14,206},{16,12... | collective-permute-start | bytes 1572872 | tf_op jit(solution)/shard_map/ppermute | solution.py:32
  87.1 0.2 collective-permute-start.24
  87.3 6.5 %collective-permute-done.22 = bf16[8,256,128]{2,1,0:T(8,128)(2,1)S(1)} collective-permute-done((bf16[8,256,128]{2,1,0:T(8,128)(2,1)S(1)}, bf16[8,256,128]{2,1,0:T(8,128)(2,1)S(1)}, u32[]{:S(2)}, u32[]{:S(2)}) %collective-permute-start.22) | collective-permute-done | bytes 524320 | tf_op jit(solution)/shard_map/ppermute | solution.py:32
  93.8 0.1 add_convert_fusion
  94.0 0.3 collective-permute-start.19
  94.3 0.1 add_convert_fusion.1
  94.4 2.7 %collective-permute-start.21 = (bf16[8,256,128]{2,1,0:T(8,128)(2,1)S(1)}, bf16[8,256,128]{2,1,0:T(8,128)(2,1)S(1)}, u32[]{:S(2)}, u32[]{:S(2)}) collective-permute-start(bf16[8,256,128]{2,1,0:T(8,128)(2,1)S(1)} %add_convert_fusion.1), channel_id=1, source_target_pairs={{0,28},{2,194},{4,0},{6,198},{8,4},{10,202},{12,8},{14,206},{16,12... | collective-permute-start | bytes 1572872 | tf_op jit(solution)/shard_map/ppermute | solution.py:32
  97.1 1.7 %collective-permute-done.24 = bf16[8,256,128]{2,1,0:T(8,128)(2,1)S(1)} collective-permute-done((bf16[8,256,128]{2,1,0:T(8,128)(2,1)S(1)}, bf16[8,256,128]{2,1,0:T(8,128)(2,1)S(1)}, u32[]{:S(2)}, u32[]{:S(2)}) %collective-permute-start.24) | collective-permute-done | bytes 524320 | tf_op jit(solution)/shard_map/ppermute | solution.py:32
  98.9 4.6 %collective-permute-done.23 = bf16[8,256,128]{2,1,0:T(8,128)(2,1)S(1)} collective-permute-done((bf16[8,256,128]{2,1,0:T(8,128)(2,1)S(1)}, bf16[8,256,128]{2,1,0:T(8,128)(2,1)S(1)}, u32[]{:S(2)}, u32[]{:S(2)}) %collective-permute-start.23) | collective-permute-done | bytes 524320 | tf_op jit(solution)/shard_map/ppermute | solution.py:32
  103.5 0.2 fusion.10
  103.8 0.9 collective-permute-start.27
  104.6 4.5 %collective-permute-done.19 = bf16[8,256,128]{2,1,0:T(8,128)(2,1)S(1)} collective-permute-done((bf16[8,256,128]{2,1,0:T(8,128)(2,1)S(1)}, bf16[8,256,128]{2,1,0:T(8,128)(2,1)S(1)}, u32[]{:S(2)}, u32[]{:S(2)}) %collective-permute-start.19) | collective-permute-done | bytes 524320 | tf_op jit(solution)/shard_map/ppermute | solution.py:32
  109.1 0.2 convert_add_fusion.1
  109.5 2.7 %collective-permute-start.28 = (bf16[4,256,128]{2,1,0:T(8,128)(2,1)S(1)}, bf16[4,256,128]{2,1,0:T(8,128)(2,1)S(1)}, u32[]{:S(2)}, u32[]{:S(2)}) collective-permute-start(bf16[4,256,128]{2,1,0:T(8,128)(2,1)S(1)} %pad_maximum_fusion.2), channel_id=1, source_target_pairs={{0,192},{2,30},{4,196},{6,2},{8,200},{10,6},{12,204},{14,10},{16,2... | collective-permute-start | bytes 786440 | tf_op jit(solution)/shard_map/ppermute | solution.py:32
  112.2 2.2 %collective-permute-done.25 = bf16[2,256,128]{2,1,0:T(8,128)(2,1)S(1)} collective-permute-done((bf16[2,256,128]{2,1,0:T(8,128)(2,1)S(1)}, bf16[2,256,128]{2,1,0:T(8,128)(2,1)S(1)}, u32[]{:S(2)}, u32[]{:S(2)}) %collective-permute-start.25) | collective-permute-done | bytes 131104 | tf_op jit(solution)/shard_map/ppermute | solution.py:32
  114.6 1.0 collective-permute-done.28
  115.5 5.5 %collective-permute-done.26 = bf16[4,256,128]{2,1,0:T(8,128)(2,1)S(1)} collective-permute-done((bf16[4,256,128]{2,1,0:T(8,128)(2,1)S(1)}, bf16[4,256,128]{2,1,0:T(8,128)(2,1)S(1)}, u32[]{:S(2)}, u32[]{:S(2)}) %collective-permute-start.26) | collective-permute-done | bytes 262176 | tf_op jit(solution)/shard_map/ppermute | solution.py:32
  121.1 1.4 %collective-permute-start.29 = (bf16[256,128]{1,0:T(8,128)(2,1)S(1)}, bf16[256,128]{1,0:T(8,128)(2,1)S(1)}, u32[]{:S(2)}, u32[]{:S(2)}) collective-permute-start(bf16[256,128]{1,0:T(8,128)(2,1)S(1)} %get-tuple-element.25), channel_id=1, source_target_pairs={{0,16},{2,18},{4,20},{6,22},{8,24},{10,26},{12,28},{14,30},{16,0},... | collective-permute-start | bytes 196616 | tf_op jit(solution)/shard_map/ppermute | solution.py:32
  122.5 4.5 %collective-permute-start.31 = (bf16[256,128]{1,0:T(8,128)(2,1)S(1)}, bf16[256,128]{1,0:T(8,128)(2,1)S(1)}, u32[]{:S(2)}, u32[]{:S(2)}) collective-permute-start(bf16[256,128]{1,0:T(8,128)(2,1)S(1)} %get-tuple-element.26), channel_id=1, source_target_pairs={{0,48},{2,50},{4,52},{6,54},{8,56},{10,58},{12,60},{14,62},{16,32}... | collective-permute-start | bytes 196616 | tf_op jit(solution)/shard_map/ppermute | solution.py:32
  127.0 0.8 collective-permute-start.30
  127.8 0.5 collective-permute-done.29
  128.2 3.7 %collective-permute-done.31 = bf16[256,128]{1,0:T(8,128)(2,1)S(1)} collective-permute-done((bf16[256,128]{1,0:T(8,128)(2,1)S(1)}, bf16[256,128]{1,0:T(8,128)(2,1)S(1)}, u32[]{:S(2)}, u32[]{:S(2)}) %collective-permute-start.31) | collective-permute-done | bytes 65568 | tf_op jit(solution)/shard_map/ppermute | solution.py:32
  132.0 0.1 shard_map.126
  132.1 4.3 %collective-permute-start.32 = (bf16[64,256]{1,0:T(8,128)(2,1)S(1)}, bf16[64,256]{1,0:T(8,128)(2,1)S(1)}, u32[]{:S(2)}, u32[]{:S(2)}) collective-permute-start(bf16[64,256]{1,0:T(8,128)(2,1)S(1)} %broadcast_select_fusion.1), channel_id=1, source_target_pairs={{0,2},{2,0},{4,6},{6,4},{8,10},{10,8},{12,14},{14,12},{16,18},{18,... | collective-permute-start | bytes 98312 | tf_op jit(solution)/shard_map/ppermute | solution.py:32
  136.4 0.9 collective-permute-done.32
  137.2 0.6 select_bitcast_fusion
  (62 shorter events, 1.2 us)
Async XLA Ops:
  0.6 60.0 %copy-start = (bf16[64,128,128]{2,1,0:T(8,128)(2,1)S(1)}, bf16[64,128,128]{2,1,0:T(8,128)(2,1)}, u32[]{:S(2)}) copy-start(bf16[64,128,128]{2,1,0:T(8,128)(2,1)} %g0.1) | copy-start | bytes 6291460
  0.6 49.3 %copy-start.5 = (s32[1,64]{1,0:T(1,128)S(1)}, s32[1,64]{1,0:T(1,128)}, u32[]{:S(2)}) copy-start(s32[1,64]{1,0:T(1,128)} %param.20) | copy-start | bytes 772
  0.7 49.3 %copy-start.6 = (s32[1,64]{1,0:T(1,128)S(1)}, s32[1,64]{1,0:T(1,128)}, u32[]{:S(2)}) copy-start(s32[1,64]{1,0:T(1,128)} %param.17) | copy-start | bytes 772
  1.6 5.9 %collective-permute-start.1 = (bf16[64,256]{1,0:T(8,128)(2,1)S(1)}, bf16[64,256]{1,0:T(8,128)(2,1)S(1)}, u32[]{:S(2)}, u32[]{:S(2)}) collective-permute-start(bf16[64,256]{1,0:T(8,128)(2,1)S(1)} %select_bitcast_fusion.2), channel_id=1, source_target_pairs={{0,2},{2,0},{4,6},{6,4},{8,10},{10,8},{12,14},{14,12},{16,18},{18,... | collective-permute-start | bytes 98312 | tf_op jit(solution)/shard_map/ppermute | solution.py:32
  4.8 55.8 %collective-permute-start.13 = (bf16[64,128,128]{2,1,0:T(8,128)(2,1)}, bf16[64,128,128]{2,1,0:T(8,128)(2,1)}, u32[]{:S(2)}, u32[]{:S(2)}) collective-permute-start(bf16[64,128,128]{2,1,0:T(8,128)(2,1)} %g0.1), channel_id=1, source_target_pairs={{0,2},{2,0},{4,6},{6,4},{8,10},{10,8},{12,14},{14,12},{16,18},{18,... | collective-permute-start | bytes 6291464 | tf_op jit(solution)/shard_map/ppermute | solution.py:32
  4.9 55.7 %collective-permute-start.14 = (bf16[64,128,128]{2,1,0:T(8,128)(2,1)}, bf16[64,128,128]{2,1,0:T(8,128)(2,1)}, u32[]{:S(2)}, u32[]{:S(2)}) collective-permute-start(bf16[64,128,128]{2,1,0:T(8,128)(2,1)} %u0.1), channel_id=1, source_target_pairs={{0,2},{2,0},{4,6},{6,4},{8,10},{10,8},{12,14},{14,12},{16,18},{18,... | collective-permute-start | bytes 6291464 | tf_op jit(solution)/shard_map/ppermute | solution.py:32
  8.3 9.0 %collective-permute-start.4 = (bf16[1,256,128]{2,1,0:T(8,128)(2,1)S(1)}, bf16[1,256,128]{2,1,0:T(8,128)(2,1)S(1)}, u32[]{:S(2)}, u32[]{:S(2)}) collective-permute-start(bf16[1,256,128]{2,1,0:T(8,128)(2,1)S(1)} %bitcast.32), channel_id=1, source_target_pairs={{0,48},{2,50},{4,52},{6,54},{8,56},{10,58},{12,60},{14,62},{16,32}... | collective-permute-start | bytes 196616 | tf_op jit(solution)/shard_map/ppermute | solution.py:32
  14.5 3.9 %collective-permute-start.3 = (bf16[1,256,128]{2,1,0:T(8,128)(2,1)S(1)}, bf16[1,256,128]{2,1,0:T(8,128)(2,1)S(1)}, u32[]{:S(2)}, u32[]{:S(2)}) collective-permute-start(bf16[1,256,128]{2,1,0:T(8,128)(2,1)S(1)} %bitcast.33), channel_id=1, source_target_pairs={{0,32},{2,34},{4,36},{6,38},{8,40},{10,42},{12,44},{14,46},{16,48}... | collective-permute-start | bytes 196616 | tf_op jit(solution)/shard_map/ppermute | solution.py:32
  14.8 9.2 %collective-permute-start.2 = (bf16[1,256,128]{2,1,0:T(8,128)(2,1)S(1)}, bf16[1,256,128]{2,1,0:T(8,128)(2,1)S(1)}, u32[]{:S(2)}, u32[]{:S(2)}) collective-permute-start(bf16[1,256,128]{2,1,0:T(8,128)(2,1)S(1)} %bitcast.34), channel_id=1, source_target_pairs={{0,16},{2,18},{4,20},{6,22},{8,24},{10,26},{12,28},{14,30},{16,0},... | collective-permute-start | bytes 196616 | tf_op jit(solution)/shard_map/ppermute | solution.py:32
  17.3 43.3 %collective-permute-start.15 = (bf16[64,128,128]{2,1,0:T(8,128)(2,1)}, bf16[64,128,128]{2,1,0:T(8,128)(2,1)}, u32[]{:S(2)}, u32[]{:S(2)}) collective-permute-start(bf16[64,128,128]{2,1,0:T(8,128)(2,1)} %d0.1), channel_id=1, source_target_pairs={{0,2},{2,0},{4,6},{6,4},{8,10},{10,8},{12,14},{14,12},{16,18},{18,... | collective-permute-start | bytes 6291464 | tf_op jit(solution)/shard_map/ppermute | solution.py:32
  24.0 6.8 %collective-permute-start.6 = (bf16[4,256,128]{2,1,0:T(8,128)(2,1)S(1)}, bf16[4,256,128]{2,1,0:T(8,128)(2,1)S(1)}, u32[]{:S(2)}, u32[]{:S(2)}) collective-permute-start(bf16[4,256,128]{2,1,0:T(8,128)(2,1)S(1)} %pad_maximum_fusion), channel_id=1, source_target_pairs={{0,64},{2,6},{4,68},{6,10},{8,72},{10,14},{12,76},{14,18},{16,80},... | collective-permute-start | bytes 786440 | tf_op jit(solution)/shard_map/ppermute | solution.py:32
  24.1 8.1 %collective-permute-start.5 = (bf16[4,256,128]{2,1,0:T(8,128)(2,1)S(1)}, bf16[4,256,128]{2,1,0:T(8,128)(2,1)S(1)}, u32[]{:S(2)}, u32[]{:S(2)}) collective-permute-start(bf16[4,256,128]{2,1,0:T(8,128)(2,1)S(1)} %pad_maximum_fusion), channel_id=1, source_target_pairs={{0,192},{2,30},{4,196},{6,2},{8,200},{10,6},{12,204},{14,10},{16,2... | collective-permute-start | bytes 786440 | tf_op jit(solution)/shard_map/ppermute | solution.py:32
  30.8 2.6 %collective-permute-start = (s32[3,65]{1,0:T(4,128)S(1)}, s32[3,65]{1,0:T(4,128)S(1)}, u32[]{:S(2)}, u32[]{:S(2)}) collective-permute-start(s32[3,65]{1,0:T(4,128)S(1)} %pad_add_fusion.1), channel_id=1, source_target_pairs={{0,2},{2,0},{4,6},{6,4},{8,10},{10,8},{12,14},{14,12},{16,18},{18,... | collective-permute-start | bytes 2348 | tf_op jit(solution)/shard_map/ppermute | solution.py:32
  32.2 5.4 %collective-permute-start.7 = (bf16[2,256,128]{2,1,0:T(8,128)(2,1)S(1)}, bf16[2,256,128]{2,1,0:T(8,128)(2,1)S(1)}, u32[]{:S(2)}, u32[]{:S(2)}) collective-permute-start(bf16[2,256,128]{2,1,0:T(8,128)(2,1)S(1)} %slice.64), channel_id=1, source_target_pairs={{0,64},{2,6},{4,68},{6,10},{8,72},{10,14},{12,76},{14,18},{16,80},... | collective-permute-start | bytes 393224 | tf_op jit(solution)/shard_map/ppermute | solution.py:32
  33.4 4.3 %collective-permute-start.8 = (bf16[2,256,128]{2,1,0:T(8,128)(2,1)S(1)}, bf16[2,256,128]{2,1,0:T(8,128)(2,1)}, u32[]{:S(2)}, u32[]{:S(2)}) collective-permute-start(bf16[2,256,128]{2,1,0:T(8,128)(2,1)S(1)} %slice.65), channel_id=1, source_target_pairs={{0,192},{2,30},{4,196},{6,2},{8,200},{10,6},{12,204},{14,10},{16,2... | collective-permute-start | bytes 393224 | tf_op jit(solution)/shard_map/ppermute | solution.py:32
  37.6 9.6 %collective-permute-start.11 = (bf16[8,256,128]{2,1,0:T(8,128)(2,1)S(1)}, bf16[8,256,128]{2,1,0:T(8,128)(2,1)}, u32[]{:S(2)}, u32[]{:S(2)}) collective-permute-start(bf16[8,256,128]{2,1,0:T(8,128)(2,1)S(1)} %constant_dynamic-update-slice_fusion.refs_0_), channel_id=1, source_target_pairs={{0,4},{2,66},{4,8},{6,70},{8,12},{10,74},{12,16},{14,78},{16,20},{... | collective-permute-start | bytes 1572872 | tf_op jit(solution)/shard_map/ppermute | solution.py:32
  37.7 9.6 %collective-permute-start.9 = (bf16[8,256,128]{2,1,0:T(8,128)(2,1)S(1)}, bf16[8,256,128]{2,1,0:T(8,128)(2,1)}, u32[]{:S(2)}, u32[]{:S(2)}) collective-permute-start(bf16[8,256,128]{2,1,0:T(8,128)(2,1)S(1)} %constant_dynamic-update-slice_fusion.refs_0_), channel_id=1, source_target_pairs={{0,28},{2,194},{4,0},{6,198},{8,4},{10,202},{12,8},{14,206},{16,12... | collective-permute-start | bytes 1572872 | tf_op jit(solution)/shard_map/ppermute | solution.py:32
  47.2 9.5 %collective-permute-start.12 = (bf16[8,256,128]{2,1,0:T(8,128)(2,1)S(1)}, bf16[8,256,128]{2,1,0:T(8,128)(2,1)S(1)}, u32[]{:S(2)}, u32[]{:S(2)}) collective-permute-start(bf16[8,256,128]{2,1,0:T(8,128)(2,1)S(1)} %constant_dynamic-update-slice_fusion.5.refs_1_), channel_id=1, source_target_pairs={{0,4},{2,66},{4,8},{6,70},{8,12},{10,74},{12,16},{14,78},{16,20},{... | collective-permute-start | bytes 1572872 | tf_op jit(solution)/shard_map/ppermute | solution.py:32
  47.2 10.3 %collective-permute-start.10 = (bf16[8,256,128]{2,1,0:T(8,128)(2,1)S(1)}, bf16[8,256,128]{2,1,0:T(8,128)(2,1)}, u32[]{:S(2)}, u32[]{:S(2)}) collective-permute-start(bf16[8,256,128]{2,1,0:T(8,128)(2,1)S(1)} %constant_dynamic-update-slice_fusion.5.refs_1_), channel_id=1, source_target_pairs={{0,28},{2,194},{4,0},{6,198},{8,4},{10,202},{12,8},{14,206},{16,12... | collective-permute-start | bytes 1572872 | tf_op jit(solution)/shard_map/ppermute | solution.py:32
  56.8 0.8 copy-start.3
  57.6 11.7 %collective-permute-start.16 = (bf16[8,256,128]{2,1,0:T(8,128)(2,1)}, bf16[8,256,128]{2,1,0:T(8,128)(2,1)}, u32[]{:S(2)}, u32[]{:S(2)}) collective-permute-start(bf16[8,256,128]{2,1,0:T(8,128)(2,1)} %collective-permute-done.11.refs_4_), channel_id=1, source_target_pairs={{0,4},{2,66},{4,8},{6,70},{8,12},{10,74},{12,16},{14,78},{16,20},{... | collective-permute-start | bytes 1572872 | tf_op jit(solution)/shard_map/ppermute | solution.py:32
  57.6 11.7 %collective-permute-start.17 = (bf16[8,256,128]{2,1,0:T(8,128)(2,1)}, bf16[8,256,128]{2,1,0:T(8,128)(2,1)}, u32[]{:S(2)}, u32[]{:S(2)}) collective-permute-start(bf16[8,256,128]{2,1,0:T(8,128)(2,1)} %collective-permute-done.10.refs_3_), channel_id=1, source_target_pairs={{0,28},{2,194},{4,0},{6,198},{8,4},{10,202},{12,8},{14,206},{16,12... | collective-permute-start | bytes 1572872 | tf_op jit(solution)/shard_map/ppermute | solution.py:32
  60.6 1.6 %copy-start.1 = (bf16[64,128,128]{2,1,0:T(8,128)(2,1)S(1)}, bf16[64,128,128]{2,1,0:T(8,128)(2,1)}, u32[]{:S(2)}) copy-start(bf16[64,128,128]{2,1,0:T(8,128)(2,1)} %u0.1) | copy-start | bytes 6291460
  62.2 1.6 %copy-start.2 = (bf16[64,128,128]{2,1,0:T(8,128)(2,1)S(1)}, bf16[64,128,128]{2,1,0:T(8,128)(2,1)}, u32[]{:S(2)}) copy-start(bf16[64,128,128]{2,1,0:T(8,128)(2,1)} %d0.1) | copy-start | bytes 6291460
  63.8 1.0 copy-start.4
  73.1 6.0 %collective-permute-start.18 = (f32[256,512]{1,0:T(8,128)S(1)}, f32[256,512]{1,0:T(8,128)S(1)}, u32[]{:S(2)}, u32[]{:S(2)}) collective-permute-start(f32[256,512]{1,0:T(8,128)S(1)} %shard_map.124.mine_ref), channel_id=1, source_target_pairs={{0,2},{2,0},{4,6},{6,4},{8,10},{10,8},{12,14},{14,12},{16,18},{18,... | collective-permute-start | bytes 1572872 | tf_op jit(solution)/shard_map/ppermute | solution.py:32
  84.4 9.4 %collective-permute-start.22 = (bf16[8,256,128]{2,1,0:T(8,128)(2,1)S(1)}, bf16[8,256,128]{2,1,0:T(8,128)(2,1)S(1)}, u32[]{:S(2)}, u32[]{:S(2)}) collective-permute-start(bf16[8,256,128]{2,1,0:T(8,128)(2,1)S(1)} %get-tuple-element.16), channel_id=1, source_target_pairs={{0,4},{2,66},{4,8},{6,70},{8,12},{10,74},{12,16},{14,78},{16,20},{... | collective-permute-start | bytes 1572872 | tf_op jit(solution)/shard_map/ppermute | solution.py:32
  84.6 9.7 %collective-permute-start.20 = (bf16[8,256,128]{2,1,0:T(8,128)(2,1)S(1)}, bf16[8,256,128]{2,1,0:T(8,128)(2,1)S(1)}, u32[]{:S(2)}, u32[]{:S(2)}) collective-permute-start(bf16[8,256,128]{2,1,0:T(8,128)(2,1)S(1)} %get-tuple-element.13), channel_id=1, source_target_pairs={{0,28},{2,194},{4,0},{6,198},{8,4},{10,202},{12,8},{14,206},{16,12... | collective-permute-start | bytes 1572872 | tf_op jit(solution)/shard_map/ppermute | solution.py:32
  87.1 11.7 %collective-permute-start.24 = (bf16[8,256,128]{2,1,0:T(8,128)(2,1)S(1)}, bf16[8,256,128]{2,1,0:T(8,128)(2,1)S(1)}, u32[]{:S(2)}, u32[]{:S(2)}) collective-permute-start(bf16[8,256,128]{2,1,0:T(8,128)(2,1)S(1)} %get-tuple-element.17), channel_id=1, source_target_pairs={{0,28},{2,194},{4,0},{6,198},{8,4},{10,202},{12,8},{14,206},{16,12... | collective-permute-start | bytes 1572872 | tf_op jit(solution)/shard_map/ppermute | solution.py:32
  93.9 9.6 %collective-permute-start.23 = (bf16[8,256,128]{2,1,0:T(8,128)(2,1)S(1)}, bf16[8,256,128]{2,1,0:T(8,128)(2,1)S(1)}, u32[]{:S(2)}, u32[]{:S(2)}) collective-permute-start(bf16[8,256,128]{2,1,0:T(8,128)(2,1)S(1)} %add_convert_fusion), channel_id=1, source_target_pairs={{0,4},{2,66},{4,8},{6,70},{8,12},{10,74},{12,16},{14,78},{16,20},{... | collective-permute-start | bytes 1572872 | tf_op jit(solution)/shard_map/ppermute | solution.py:32
  94.0 15.1 %collective-permute-start.19 = (bf16[8,256,128]{2,1,0:T(8,128)(2,1)S(1)}, bf16[8,256,128]{2,1,0:T(8,128)(2,1)S(1)}, u32[]{:S(2)}, u32[]{:S(2)}) collective-permute-start(bf16[8,256,128]{2,1,0:T(8,128)(2,1)S(1)} %get-tuple-element.11), channel_id=1, source_target_pairs={{0,4},{2,66},{4,8},{6,70},{8,12},{10,74},{12,16},{14,78},{16,20},{... | collective-permute-start | bytes 1572872 | tf_op jit(solution)/shard_map/ppermute | solution.py:32
  94.4 14.7 %collective-permute-start.21 = (bf16[8,256,128]{2,1,0:T(8,128)(2,1)S(1)}, bf16[8,256,128]{2,1,0:T(8,128)(2,1)S(1)}, u32[]{:S(2)}, u32[]{:S(2)}) collective-permute-start(bf16[8,256,128]{2,1,0:T(8,128)(2,1)S(1)} %add_convert_fusion.1), channel_id=1, source_target_pairs={{0,28},{2,194},{4,0},{6,198},{8,4},{10,202},{12,8},{14,206},{16,12... | collective-permute-start | bytes 1572872 | tf_op jit(solution)/shard_map/ppermute | solution.py:32
  103.8 5.7 %collective-permute-start.27 = (bf16[2,256,128]{2,1,0:T(8,128)(2,1)S(1)}, bf16[2,256,128]{2,1,0:T(8,128)(2,1)S(1)}, u32[]{:S(2)}, u32[]{:S(2)}) collective-permute-start(bf16[2,256,128]{2,1,0:T(8,128)(2,1)S(1)} %get-tuple-element.24), channel_id=1, source_target_pairs={{0,192},{2,30},{4,196},{6,2},{8,200},{10,6},{12,204},{14,10},{16,2... | collective-permute-start | bytes 393224 | tf_op jit(solution)/shard_map/ppermute | solution.py:32
  109.3 5.1 %collective-permute-start.25 = (bf16[2,256,128]{2,1,0:T(8,128)(2,1)S(1)}, bf16[2,256,128]{2,1,0:T(8,128)(2,1)S(1)}, u32[]{:S(2)}, u32[]{:S(2)}) collective-permute-start(bf16[2,256,128]{2,1,0:T(8,128)(2,1)S(1)} %get-tuple-element.22), channel_id=1, source_target_pairs={{0,64},{2,6},{4,68},{6,10},{8,72},{10,14},{12,76},{14,18},{16,80},... | collective-permute-start | bytes 393224 | tf_op jit(solution)/shard_map/ppermute | solution.py:32
  109.5 6.0 %collective-permute-start.28 = (bf16[4,256,128]{2,1,0:T(8,128)(2,1)S(1)}, bf16[4,256,128]{2,1,0:T(8,128)(2,1)S(1)}, u32[]{:S(2)}, u32[]{:S(2)}) collective-permute-start(bf16[4,256,128]{2,1,0:T(8,128)(2,1)S(1)} %pad_maximum_fusion.2), channel_id=1, source_target_pairs={{0,192},{2,30},{4,196},{6,2},{8,200},{10,6},{12,204},{14,10},{16,2... | collective-permute-start | bytes 786440 | tf_op jit(solution)/shard_map/ppermute | solution.py:32
  114.5 6.5 %collective-permute-start.26 = (bf16[4,256,128]{2,1,0:T(8,128)(2,1)S(1)}, bf16[4,256,128]{2,1,0:T(8,128)(2,1)S(1)}, u32[]{:S(2)}, u32[]{:S(2)}) collective-permute-start(bf16[4,256,128]{2,1,0:T(8,128)(2,1)S(1)} %pad_maximum_fusion.1), channel_id=1, source_target_pairs={{0,64},{2,6},{4,68},{6,10},{8,72},{10,14},{12,76},{14,18},{16,80},... | collective-permute-start | bytes 786440 | tf_op jit(solution)/shard_map/ppermute | solution.py:32
  121.1 7.1 %collective-permute-start.29 = (bf16[256,128]{1,0:T(8,128)(2,1)S(1)}, bf16[256,128]{1,0:T(8,128)(2,1)S(1)}, u32[]{:S(2)}, u32[]{:S(2)}) collective-permute-start(bf16[256,128]{1,0:T(8,128)(2,1)S(1)} %get-tuple-element.25), channel_id=1, source_target_pairs={{0,16},{2,18},{4,20},{6,22},{8,24},{10,26},{12,28},{14,30},{16,0},... | collective-permute-start | bytes 196616 | tf_op jit(solution)/shard_map/ppermute | solution.py:32
  122.5 9.4 %collective-permute-start.31 = (bf16[256,128]{1,0:T(8,128)(2,1)S(1)}, bf16[256,128]{1,0:T(8,128)(2,1)S(1)}, u32[]{:S(2)}, u32[]{:S(2)}) collective-permute-start(bf16[256,128]{1,0:T(8,128)(2,1)S(1)} %get-tuple-element.26), channel_id=1, source_target_pairs={{0,48},{2,50},{4,52},{6,54},{8,56},{10,58},{12,60},{14,62},{16,32}... | collective-permute-start | bytes 196616 | tf_op jit(solution)/shard_map/ppermute | solution.py:32
  127.0 4.9 %collective-permute-start.30 = (bf16[256,128]{1,0:T(8,128)(2,1)S(1)}, bf16[256,128]{1,0:T(8,128)(2,1)S(1)}, u32[]{:S(2)}, u32[]{:S(2)}) collective-permute-start(bf16[256,128]{1,0:T(8,128)(2,1)S(1)} %get-tuple-element.27), channel_id=1, source_target_pairs={{0,32},{2,34},{4,36},{6,38},{8,40},{10,42},{12,44},{14,46},{16,48}... | collective-permute-start | bytes 196616 | tf_op jit(solution)/shard_map/ppermute | solution.py:32
  132.1 5.1 %collective-permute-start.32 = (bf16[64,256]{1,0:T(8,128)(2,1)S(1)}, bf16[64,256]{1,0:T(8,128)(2,1)S(1)}, u32[]{:S(2)}, u32[]{:S(2)}) collective-permute-start(bf16[64,256]{1,0:T(8,128)(2,1)S(1)} %broadcast_select_fusion.1), channel_id=1, source_target_pairs={{0,2},{2,0},{4,6},{6,4},{8,10},{10,8},{12,14},{14,12},{16,18},{18,... | collective-permute-start | bytes 98312 | tf_op jit(solution)/shard_map/ppermute | solution.py:32

commit v3 on v2

--- a/solution.py
+++ b/solution.py
@@ -49,56 +49,37 @@
     return permute(value, target)
 
 
-def near(value):
-    far = permute(value, lambda at: at | {"x": 1 - at["x"], "z": (at["z"] + 4) % NZ})
-    ahead, beside = shift(value, "z", 4), shift(value, "x", 1)
-    return jnp.concatenate([value, ahead, beside, far])
-
-
-def near_reduce(total):
-    sent = total.astype(BF16)
-    far = permute(sent[3], lambda at: at | {"x": 1 - at["x"], "z": (at["z"] + 4) % NZ})
-    ahead, beside = shift(sent[1], "z", 4), shift(sent[2], "x", 1)
-    return total[0] + ahead.astype(F32) + beside.astype(F32) + far.astype(F32)
-
-
 def small_gather(value, axes):
-    half = value.shape[0] // 2
-    down, up = turn(value, axes, -1), turn(value, axes, 1)
-    far_up, far_down = turn(up[:half], axes, 1), turn(down[half:], axes, -1)
-    return jnp.concatenate([value, down]), jnp.concatenate([up, far_up, far_down])
-
-
-def large_gather(first, second, axes):
-    first_up, first_down = turn(first, axes, 1), turn(first, axes, -1)
-    second_down, second_up = turn(second, axes, -1), turn(second, axes, 1)
-    first_far, second_far = turn(first_up, axes, 1), turn(second_down, axes, -1)
-    return first, second, first_down, second_down, first_up, second_up, first_far, second_far
-
-
-SENT = (False, False, True, False, False, True, True, True)
-
-
-def large_reduce(parts, axes):
-    first, second, first_ahead, second_ahead, first_behind, second_behind, first_far, second_far = parts
-    second_far, first_far = turn(second_far, axes, 1), turn(first_far, axes, -1)
-    first_ahead, second_behind = turn(first_ahead, axes, 1), turn(second_behind, axes, -1)
-    second_ahead = turn((second_ahead + second_far.astype(F32)).astype(BF16), axes, 1)
-    first_behind = turn((first_behind + first_far.astype(F32)).astype(BF16), axes, -1)
-    first = first + first_ahead.astype(F32) + first_behind.astype(F32)
-    second = second + second_ahead.astype(F32) + second_behind.astype(F32)
-    return first, second
-
-
-def small_reduce(first, second, axes):
-    here, ahead = jnp.split(first, 2)
-    behind, far = jnp.split(second, 2)
-    half = here.shape[0] // 2
-    far = far.astype(BF16)
-    down, up = turn(far[:half], axes, -1), turn(far[half:], axes, 1)
-    behind = jnp.concatenate([behind[:half] + down.astype(F32), behind[half:]])
-    ahead = jnp.concatenate([ahead[:half], ahead[half:] + up.astype(F32)])
-    ahead, behind = turn(ahead.astype(BF16), axes, 1), turn(behind.astype(BF16), axes, -1)
+    up, down = turn(value, axes, 1), turn(value, axes, -1)
+    return jnp.concatenate([value, down, up, turn(up, axes, 1)])
+
+
+def large_gather(first, one, two, axes):
+    one_up, one_down = turn(one, axes, 1), turn(one, axes, -1)
+    two_up, two_down = turn(two, axes, 1), turn(two, axes, -1)
+    far_up, far_down = turn(one_up, axes, 1), turn(jnp.where(first, one_down, two_down), axes, -1)
+    return one, two, one_down, two_down, one_up, two_up, far_up, far_down
+
+
+SENT = (False, False, False, False, False, True, True, True)
+
+
+def large_reduce(first, parts, axes):
+    one, two, one_ahead, two_ahead, one_behind, two_behind, far_behind, far_ahead = parts
+    far_ahead, far_behind = turn(far_ahead, axes, 1).astype(F32), turn(far_behind, axes, -1).astype(F32)
+    two_behind = turn(two_behind, axes, -1)
+    two_ahead = turn((two_ahead + jnp.where(first, 0.0, far_ahead)).astype(BF16), axes, 1)
+    one_ahead = turn((one_ahead + jnp.where(first, far_ahead, 0.0)).astype(BF16), axes, 1)
+    one_behind = turn((one_behind + far_behind).astype(BF16), axes, -1)
+    one = one + one_ahead.astype(F32) + one_behind.astype(F32)
+    two = two + two_ahead.astype(F32) + two_behind.astype(F32)
+    return one, two
+
+
+def small_reduce(total, axes):
+    here, ahead, behind, far = jnp.split(total, RING)
+    ahead, far = turn(ahead.astype(BF16), axes, 1), turn(far.astype(BF16), axes, -1)
+    behind = turn((behind + far.astype(F32)).astype(BF16), axes, -1)
     return here + ahead.astype(F32) + behind.astype(F32)
 
 
@@ -265,7 +246,9 @@
     other = shift(other, "c", 1)
     block = jnp.concatenate([jnp.where(first, own, other), jnp.where(first, other, own)])
     block = transpose(block).reshape(1, batch, BLOCK)
-    pieces = large_gather(*small_gather(near(block), "yz"), "zy")
+    one = jnp.concatenate([block, shift(block, "x", 1)])
+    two = shift(one, "z", 4)
+    pieces = large_gather(first, small_gather(one, "yz"), small_gather(two, "yz"), "zy")
 
     lists = jnp.concatenate([gate_index, up_index, down_index])
     counts = jnp.stack([gate_count, up_count, down_count])
@@ -279,10 +262,9 @@
         return jnp.where(k >= 2, 5 - k, k)
 
     y_rank, z_rank = ranked(y), ranked(low)
-    from_ahead = jnp.where(first, y_rank >= 2, x == 1)
-    flipped = (low == 3) | ((low == 2) & jnp.logical_not(from_ahead))
-    high = jnp.where(flipped, 1 - high, high)
-    position = jnp.where(first, z_rank * RING + y_rank, y_rank * RING + z_rank) * 4 + x * 2 + high
+    chunk = jnp.where(low >= 2, 1 - high, high)
+    large, small = jnp.where(first, z_rank, y_rank), jnp.where(first, y_rank, z_rank)
+    position = (large * 2 + chunk) * PART + small * NX + x
     number = lax.broadcasted_iota(jnp.int32, (6, SLOTS, SLOTS), 2)
     places = lax.broadcasted_iota(jnp.int32, (6, SLOTS, SLOTS), 1)
     here = (position[:, None, :] == places) & (number < counts[:, :, None])
@@ -298,7 +280,10 @@
     theirs = shift(mine, "c", 1)
     parts = tuple(jax.ShapeDtypeStruct((PART, batch, BLOCK), BF16 if sent else F32) for sent in SENT)
     parts = call(outer_kernel, parts, 4 * flops, maps, mine, theirs, *weights)
-    total = near_reduce(small_reduce(*large_reduce(parts, "zy"), "yz"))
+    one, two = large_reduce(first, parts, "zy")
+    two = shift(small_reduce(two, "yz").astype(BF16), "z", 4)
+    one = small_reduce(one, "yz") + two.astype(F32)
+    total = one[0] + shift(one[1].astype(BF16), "x", 1).astype(F32)
     total = transpose(total).astype(BF16)
     low, high = jnp.split(total, 2)
     own, other = jnp.where(first, low, high), jnp.where(first, high, low)

time: 138 us -> 140 us (1.014)
  waiting for transfers between devices: 58.1 us -> 52.5 us
  local copies, waits for them, and re-layouts: 6.52 us -> 10.6 us
  starting transfers between devices: 51.6 us -> 54.9 us
    ppermute x33 -> x35, waiting for transfers between devices: 58.1 us -> 52.5 us  [permute(): return lax.ppermute(value, 'tp', pairs)]
    unnamed x20 -> x27, local copies, waits for them, and re-layouts: 5.12 us -> 9.51 us
    ppermute x33 -> x35, starting transfers between devices: 51.6 us -> 54.9 us  [permute(): return lax.ppermute(value, 'tp', pairs)]
  transfers between devices with their start and end apart: 33 -> 35, of which waited for: 18 -> 17; matrix products, arithmetic and copies ran while one was open for 4% -> 5% of each run, Pallas kernels for 3% -> 3%
where the time goes in v3:
time: 140 us
  starting transfers between devices  54.9 us (39%)
  waiting for transfers between devices  52.5 us (38%)
  Pallas kernels  13.4 us (10%)
  local copies, waits for them, and re-layouts  10.6 us (8%)
  other arithmetic  5.45 us (4%)
  between operations  2.93 us (2%)
    ppermute x35, starting transfers between devices, permute(): return lax.ppermute(value, 'tp', pairs)  54.9 us
    ppermute x35, waiting for transfers between devices, permute(): return lax.ppermute(value, 'tp', pairs)  52.5 us
    pallas_call x3, Pallas kernels, call(): pl.pallas_call(kernel, out_shape=outs, in_specs=[pl.BlockSpec(memory_spac...  13.3 us
    unnamed x27, local copies, waits for them, and re-layouts  9.51 us
  transfers between devices with their start and end apart: 35, of which 17 were waited for; matrix products, arithmetic and copies ran while one was open for 5% of the time, Pallas kernels for 3%

profile of v3, /device:TPU:1, one launch (start us, length us, event | category | flops | bytes accessed | tf_op | source)
XLA Modules:
  0.0 139.8 jit_solution(9798004121961592022)
XLA Ops:
  0.7 0.8 select_bitcast_fusion.2
  1.4 3.2 %collective-permute-start.1 = (bf16[64,256]{1,0:T(8,128)(2,1)S(1)}, bf16[64,256]{1,0:T(8,128)(2,1)S(1)}, u32[]{:S(2)}, u32[]{:S(2)}) collective-permute-start(bf16[64,256]{1,0:T(8,128)(2,1)S(1)} %select_bitcast_fusion.2), channel_id=1, source_target_pairs={{0,2},{2,0},{4,6},{6,4},{8,10},{10,8},{12,14},{14,12},{16,18},{18,... | collective-permute-start | bytes 98312 | tf_op jit(solution)/shard_map/ppermute | solution.py:32
  6.8 0.8 bitcast_select_fusion.1
  7.8 0.9 pad_add_fusion.1
  8.7 0.5 collective-permute-start.14
  9.2 2.3 %collective-permute-done.2 = bf16[1,256,128]{2,1,0:T(8,128)(2,1)S(1)} collective-permute-done((bf16[1,256,128]{2,1,0:T(8,128)(2,1)S(1)}, bf16[1,256,128]{2,1,0:T(8,128)(2,1)S(1)}, u32[]{:S(2)}, u32[]{:S(2)}) %collective-permute-start.2) | collective-permute-done | bytes 65568 | tf_op jit(solution)/shard_map/ppermute | solution.py:32
  11.6 3.9 %collective-permute-start.3 = (bf16[2,256,128]{2,1,0:T(8,128)(2,1)S(1)}, bf16[2,256,128]{2,1,0:T(8,128)(2,1)S(1)}, u32[]{:S(2)}, u32[]{:S(2)}) collective-permute-start(bf16[2,256,128]{2,1,0:T(8,128)(2,1)S(1)} %pad_maximum_fusion), channel_id=1, source_target_pairs={{0,192},{2,30},{4,196},{6,2},{8,200},{10,6},{12,204},{14,10},{16,2... | collective-permute-start | bytes 393224 | tf_op jit(solution)/shard_map/ppermute | solution.py:32
  15.5 0.6 constant_dynamic-update-slice_fusion.4
  16.1 3.9 %collective-permute-start.6 = (bf16[2,256,128]{2,1,0:T(8,128)(2,1)S(1)}, bf16[2,256,128]{2,1,0:T(8,128)(2,1)S(1)}, u32[]{:S(2)}, u32[]{:S(2)}) collective-permute-start(bf16[2,256,128]{2,1,0:T(8,128)(2,1)S(1)} %pad_maximum_fusion), channel_id=1, source_target_pairs={{0,16},{2,18},{4,20},{6,22},{8,24},{10,26},{12,28},{14,30},{16,0},... | collective-permute-start | bytes 393224 | tf_op jit(solution)/shard_map/ppermute | solution.py:32
  20.0 0.6 constant_dynamic-update-slice_fusion.3
  20.7 1.6 %collective-permute-start.15 = (bf16[64,128,128]{2,1,0:T(8,128)(2,1)}, bf16[64,128,128]{2,1,0:T(8,128)(2,1)}, u32[]{:S(2)}, u32[]{:S(2)}) collective-permute-start(bf16[64,128,128]{2,1,0:T(8,128)(2,1)} %u0.1), channel_id=1, source_target_pairs={{0,2},{2,0},{4,6},{6,4},{8,10},{10,8},{12,14},{14,12},{16,18},{18,... | collective-permute-start | bytes 6291464 | tf_op jit(solution)/shard_map/ppermute | solution.py:32
  22.4 0.7 collective-permute-start.5
  23.1 0.7 constant_dynamic-update-slice_fusion.2
  23.8 2.7 %collective-permute-done.6 = bf16[2,256,128]{2,1,0:T(8,128)(2,1)S(1)} collective-permute-done((bf16[2,256,128]{2,1,0:T(8,128)(2,1)S(1)}, bf16[2,256,128]{2,1,0:T(8,128)(2,1)S(1)}, u32[]{:S(2)}, u32[]{:S(2)}) %collective-permute-start.6) | collective-permute-done | bytes 131104 | tf_op jit(solution)/shard_map/ppermute | solution.py:32
  26.5 0.7 constant_dynamic-update-slice_fusion.1
  27.2 1.5 %collective-permute-done.5 = bf16[2,256,128]{2,1,0:T(8,128)(2,1)S(1)} collective-permute-done((bf16[2,256,128]{2,1,0:T(8,128)(2,1)S(1)}, bf16[2,256,128]{2,1,0:T(8,128)(2,1)S(1)}, u32[]{:S(2)}, u32[]{:S(2)}) %collective-permute-start.5) | collective-permute-done | bytes 131104 | tf_op jit(solution)/shard_map/ppermute | solution.py:32
  28.6 1.2 collective-permute-start.7
  29.8 0.7 constant_dynamic-update-slice_fusion.refs_0_
  30.5 1.0 collective-permute-done.8
  31.5 1.5 %collective-permute-start.12 = (bf16[8,256,128]{2,1,0:T(8,128)(2,1)}, bf16[8,256,128]{2,1,0:T(8,128)(2,1)}, u32[]{:S(2)}, u32[]{:S(2)}) collective-permute-start(bf16[8,256,128]{2,1,0:T(8,128)(2,1)} %constant_dynamic-update-slice_fusion.refs_0_), channel_id=1, source_target_pairs={{0,4},{2,66},{4,8},{6,70},{8,12},{10,74},{12,16},{14,78},{16,20},{... | collective-permute-start | bytes 1572872 | tf_op jit(solution)/shard_map/ppermute | solution.py:32
  33.0 5.0 %collective-permute-done.9 = bf16[2,256,128]{2,1,0:T(8,128)(2,1)S(1)} collective-permute-done((bf16[2,256,128]{2,1,0:T(8,128)(2,1)S(1)}, bf16[2,256,128]{2,1,0:T(8,128)(2,1)S(1)}, u32[]{:S(2)}, u32[]{:S(2)}) %collective-permute-start.9) | collective-permute-done | bytes 131104 | tf_op jit(solution)/shard_map/ppermute | solution.py:32
  38.0 4.2 %collective-permute-start.10 = (bf16[8,256,128]{2,1,0:T(8,128)(2,1)}, bf16[8,256,128]{2,1,0:T(8,128)(2,1)S(1)}, u32[]{:S(2)}, u32[]{:S(2)}) collective-permute-start(bf16[8,256,128]{2,1,0:T(8,128)(2,1)} %constant_dynamic-update-slice_fusion.refs_0_), channel_id=1, source_target_pairs={{0,28},{2,194},{4,0},{6,198},{8,4},{10,202},{12,8},{14,206},{16,12... | collective-permute-start | bytes 1572872 | tf_op jit(solution)/shard_map/ppermute | solution.py:32
  42.3 0.7 collective-permute-done.12.refs_4_
  43.0 1.5 %collective-permute-start.11 = (bf16[8,256,128]{2,1,0:T(8,128)(2,1)S(1)}, bf16[8,256,128]{2,1,0:T(8,128)(2,1)S(1)}, u32[]{:S(2)}, u32[]{:S(2)}) collective-permute-start(bf16[8,256,128]{2,1,0:T(8,128)(2,1)S(1)} %constant_dynamic-update-slice_fusion.5.refs_1_), channel_id=1, source_target_pairs={{0,28},{2,194},{4,0},{6,198},{8,4},{10,202},{12,8},{14,206},{16,12... | collective-permute-start | bytes 1572872 | tf_op jit(solution)/shard_map/ppermute | solution.py:32
  44.6 4.1 %collective-permute-done.10.refs_2_ = bf16[8,256,128]{2,1,0:T(8,128)(2,1)S(1)} collective-permute-done((bf16[8,256,128]{2,1,0:T(8,128)(2,1)}, bf16[8,256,128]{2,1,0:T(8,128)(2,1)S(1)}, u32[]{:S(2)}, u32[]{:S(2)}) %collective-permute-start.10) | collective-permute-done | bytes 524320 | tf_op jit(solution)/shard_map/ppermute | solution.py:32
  48.6 0.9 collective-permute-start.13
  49.6 0.8 copy-done.3
  50.6 3.6 %collective-permute-done.11.refs_3_ = bf16[8,256,128]{2,1,0:T(8,128)(2,1)S(1)} collective-permute-done((bf16[8,256,128]{2,1,0:T(8,128)(2,1)S(1)}, bf16[8,256,128]{2,1,0:T(8,128)(2,1)S(1)}, u32[]{:S(2)}, u32[]{:S(2)}) %collective-permute-start.11) | collective-permute-done | bytes 524320 | tf_op jit(solution)/shard_map/ppermute | solution.py:32
  54.2 0.9 collective-permute-start.17
  55.0 0.9 broadcast_select_fusion
  55.9 2.6 %collective-permute-done.13.refs_5_ = bf16[8,256,128]{2,1,0:T(8,128)(2,1)S(1)} collective-permute-done((bf16[8,256,128]{2,1,0:T(8,128)(2,1)S(1)}, bf16[8,256,128]{2,1,0:T(8,128)(2,1)S(1)}, u32[]{:S(2)}, u32[]{:S(2)}) %collective-permute-start.13) | collective-permute-done | bytes 524320 | tf_op jit(solution)/shard_map/ppermute | solution.py:32
  58.5 0.8 copy-done.5
  59.3 1.5 %collective-permute-start.18 = (bf16[8,256,128]{2,1,0:T(8,128)(2,1)}, bf16[8,256,128]{2,1,0:T(8,128)(2,1)}, u32[]{:S(2)}, u32[]{:S(2)}) collective-permute-start(bf16[8,256,128]{2,1,0:T(8,128)(2,1)} %broadcast_select_fusion), channel_id=1, source_target_pairs={{0,28},{2,194},{4,0},{6,198},{8,4},{10,202},{12,8},{14,206},{16,12... | collective-permute-start | bytes 1572872 | tf_op jit(solution)/shard_map/ppermute | solution.py:32
  60.8 0.3 select_reduce_fusion
  61.2 1.6 %copy-done.1 = bf16[64,128,128]{2,1,0:T(8,128)(2,1)S(1)} copy-done((bf16[64,128,128]{2,1,0:T(8,128)(2,1)S(1)}, bf16[64,128,128]{2,1,0:T(8,128)(2,1)}, u32[]{:S(2)}) %copy-start.1) | copy-done | bytes 2097176
  62.8 1.6 %copy-done.2 = bf16[64,128,128]{2,1,0:T(8,128)(2,1)S(1)} copy-done((bf16[64,128,128]{2,1,0:T(8,128)(2,1)S(1)}, bf16[64,128,128]{2,1,0:T(8,128)(2,1)}, u32[]{:S(2)}) %copy-start.2) | copy-done | bytes 2097176
  64.4 1.0 copy-done.4
  65.4 1.0 copy-done.6
  66.5 4.3 %shard_map.123.refs_0_ = f32[256,512]{1,0:T(8,128)S(1)} custom-call(s32[385]{0:T(512)S(1)} %pad_add_fusion.2.maps_ref, bf16[8,256,128]{2,1,0:T(8,128)(2,1)} %constant_dynamic-update-slice_fusion.refs_0_, bf16[8,256,128]{2,1,0:T(8,128)(2,1)S(1)} %copy-done.4, bf16[8,256,128]{2,1,0:T(8,128)(2,1)S(1)} %collective-permute-done.10.refs_2_, ...), custom_call_target="tpu_custom_call" | custom-call | flops 1610612736 | bytes 16777216 | tf_op jit(solution)/shard_map/pallas_call | solution.py:216
  70.7 3.7 %shard_map.124.mine_ref = f32[256,512]{1,0:T(8,128)S(1)} custom-call(s32[385]{0:T(512)S(1)} %pad_add_fusion.2.maps_ref, f32[256,512]{1,0:T(8,128)S(1)} %shard_map.123.refs_0_, bf16[8,256,128]{2,1,0:T(8,128)(2,1)} %collective-permute-done.17.refs_1_, bf16[8,256,128]{2,1,0:T(8,128)(2,1)} %collective-permute-done.18.refs_2_, bf16[64,128,128]{2,1,0:T(8,128)(2,1)S(1)} %copy-done, ...), custom_call_target="tpu_custom_call" | custom-call | flops 536870912 | bytes 16777216 | tf_op jit(solution)/shard_map/pallas_call | solution.py:216
  74.5 5.9 %collective-permute-start.19 = (f32[256,512]{1,0:T(8,128)S(1)}, f32[256,512]{1,0:T(8,128)S(1)}, u32[]{:S(2)}, u32[]{:S(2)}) collective-permute-start(f32[256,512]{1,0:T(8,128)S(1)} %shard_map.124.mine_ref), channel_id=1, source_target_pairs={{0,2},{2,0},{4,6},{6,4},{8,10},{10,8},{12,14},{14,12},{16,18},{18,... | collective-permute-start | bytes 1572872 | tf_op jit(solution)/shard_map/ppermute | solution.py:32
  80.4 1.5 %collective-permute-done.19.theirs_ref = f32[256,512]{1,0:T(8,128)S(1)} collective-permute-done((f32[256,512]{1,0:T(8,128)S(1)}, f32[256,512]{1,0:T(8,128)S(1)}, u32[]{:S(2)}, u32[]{:S(2)}) %collective-permute-start.19) | collective-permute-done | bytes 524320 | tf_op jit(solution)/shard_map/ppermute | solution.py:32
  81.9 5.3 %shard_map.125 = (f32[8,256,128]{2,1,0:T(8,128)S(1)}, f32[8,256,128]{2,1,0:T(8,128)S(1)}, f32[8,256,128]{2,1,0:T(8,128)S(1)}, f32[8,256,128]{2,1,0:T(8,128)S(1)}...) custom-call(s32[385]{0:T(512)S(1)} %pad_add_fusion.2.maps_ref, ...), custom_call_target="tpu_custom_call" | custom-call | flops 2147483648 | bytes 16777216 | tf_op jit(solution)/shard_map/pallas_call | solution.py:216
  87.4 2.6 %collective-permute-start.22 = (bf16[8,256,128]{2,1,0:T(8,128)(2,1)S(1)}, bf16[8,256,128]{2,1,0:T(8,128)(2,1)S(1)}, u32[]{:S(2)}, u32[]{:S(2)}) collective-permute-start(bf16[8,256,128]{2,1,0:T(8,128)(2,1)S(1)} %get-tuple-element.14), channel_id=1, source_target_pairs={{0,28},{2,194},{4,0},{6,198},{8,4},{10,202},{12,8},{14,206},{16,12... | collective-permute-start | bytes 1572872 | tf_op jit(solution)/shard_map/ppermute | solution.py:32
  89.9 0.3 collective-permute-start.28
  90.2 6.4 %collective-permute-done.20 = bf16[8,256,128]{2,1,0:T(8,128)(2,1)S(1)} collective-permute-done((bf16[8,256,128]{2,1,0:T(8,128)(2,1)S(1)}, bf16[8,256,128]{2,1,0:T(8,128)(2,1)S(1)}, u32[]{:S(2)}, u32[]{:S(2)}) %collective-permute-start.20) | collective-permute-done | bytes 524320 | tf_op jit(solution)/shard_map/ppermute | solution.py:32
  96.6 0.3 fusion.3
  96.9 0.3 collective-permute-start.27
  97.4 2.7 %collective-permute-start.23 = (bf16[8,256,128]{2,1,0:T(8,128)(2,1)S(1)}, bf16[8,256,128]{2,1,0:T(8,128)(2,1)S(1)}, u32[]{:S(2)}, u32[]{:S(2)}) collective-permute-start(bf16[8,256,128]{2,1,0:T(8,128)(2,1)S(1)} %add_convert_fusion), channel_id=1, source_target_pairs={{0,28},{2,194},{4,0},{6,198},{8,4},{10,202},{12,8},{14,206},{16,12... | collective-permute-start | bytes 1572872 | tf_op jit(solution)/shard_map/ppermute | solution.py:32
  100.2 1.5 %collective-permute-done.28 = bf16[8,256,128]{2,1,0:T(8,128)(2,1)S(1)} collective-permute-done((bf16[8,256,128]{2,1,0:T(8,128)(2,1)S(1)}, bf16[8,256,128]{2,1,0:T(8,128)(2,1)S(1)}, u32[]{:S(2)}, u32[]{:S(2)}) %collective-permute-start.28) | collective-permute-done | bytes 524320 | tf_op jit(solution)/shard_map/ppermute | solution.py:32
  101.7 5.0 %collective-permute-done.27 = bf16[8,256,128]{2,1,0:T(8,128)(2,1)S(1)} collective-permute-done((bf16[8,256,128]{2,1,0:T(8,128)(2,1)S(1)}, bf16[8,256,128]{2,1,0:T(8,128)(2,1)S(1)}, u32[]{:S(2)}, u32[]{:S(2)}) %collective-permute-start.27) | collective-permute-done | bytes 524320 | tf_op jit(solution)/shard_map/ppermute | solution.py:32
  106.7 0.2 fusion.18
  107.0 5.3 %collective-permute-done.21 = bf16[8,256,128]{2,1,0:T(8,128)(2,1)S(1)} collective-permute-done((bf16[8,256,128]{2,1,0:T(8,128)(2,1)S(1)}, bf16[8,256,128]{2,1,0:T(8,128)(2,1)S(1)}, u32[]{:S(2)}, u32[]{:S(2)}) %collective-permute-start.21) | collective-permute-done | bytes 524320 | tf_op jit(solution)/shard_map/ppermute | solution.py:32
  112.3 0.2 fusion.17
  112.6 2.7 %collective-permute-start.25 = (bf16[2,256,128]{2,1,0:T(8,128)(2,1)S(1)}, bf16[2,256,128]{2,1,0:T(8,128)(2,1)S(1)}, u32[]{:S(2)}, u32[]{:S(2)}) collective-permute-start(bf16[2,256,128]{2,1,0:T(8,128)(2,1)S(1)} %get-tuple-element.23), channel_id=1, source_target_pairs={{0,192},{2,30},{4,196},{6,2},{8,200},{10,6},{12,204},{14,10},{16,2... | collective-permute-start | bytes 393224 | tf_op jit(solution)/shard_map/ppermute | solution.py:32
  115.4 2.8 %collective-permute-start.31 = (bf16[2,256,128]{2,1,0:T(8,128)(2,1)S(1)}, bf16[2,256,128]{2,1,0:T(8,128)(2,1)S(1)}, u32[]{:S(2)}, u32[]{:S(2)}) collective-permute-start(bf16[2,256,128]{2,1,0:T(8,128)(2,1)S(1)} %fusion.4), channel_id=1, source_target_pairs={{0,192},{2,30},{4,196},{6,2},{8,200},{10,6},{12,204},{14,10},{16,2... | collective-permute-start | bytes 393224 | tf_op jit(solution)/shard_map/ppermute | solution.py:32
  118.2 2.3 %collective-permute-start.26 = (bf16[2,256,128]{2,1,0:T(8,128)(2,1)S(1)}, bf16[2,256,128]{2,1,0:T(8,128)(2,1)S(1)}, u32[]{:S(2)}, u32[]{:S(2)}) collective-permute-start(bf16[2,256,128]{2,1,0:T(8,128)(2,1)S(1)} %fusion.7), channel_id=1, source_target_pairs={{0,192},{2,30},{4,196},{6,2},{8,200},{10,6},{12,204},{14,10},{16,2... | collective-permute-start | bytes 393224 | tf_op jit(solution)/shard_map/ppermute | solution.py:32
  120.5 3.1 %collective-permute-start.32 = (bf16[2,256,128]{2,1,0:T(8,128)(2,1)S(1)}, bf16[2,256,128]{2,1,0:T(8,128)(2,1)S(1)}, u32[]{:S(2)}, u32[]{:S(2)}) collective-permute-start(bf16[2,256,128]{2,1,0:T(8,128)(2,1)S(1)} %fusion.6), channel_id=1, source_target_pairs={{0,16},{2,18},{4,20},{6,22},{8,24},{10,26},{12,28},{14,30},{16,0},... | collective-permute-start | bytes 393224 | tf_op jit(solution)/shard_map/ppermute | solution.py:32
  123.6 6.5 %collective-permute-done.32 = bf16[2,256,128]{2,1,0:T(8,128)(2,1)S(1)} collective-permute-done((bf16[2,256,128]{2,1,0:T(8,128)(2,1)S(1)}, bf16[2,256,128]{2,1,0:T(8,128)(2,1)S(1)}, u32[]{:S(2)}, u32[]{:S(2)}) %collective-permute-start.32) | collective-permute-done | bytes 131104 | tf_op jit(solution)/shard_map/ppermute | solution.py:32
  130.2 1.3 collective-permute-start.33
  131.5 1.9 %collective-permute-done.33 = bf16[256,128]{1,0:T(8,128)(2,1)S(1)} collective-permute-done((bf16[256,128]{1,0:T(8,128)(2,1)S(1)}, bf16[256,128]{1,0:T(8,128)(2,1)S(1)}, u32[]{:S(2)}, u32[]{:S(2)}) %collective-permute-start.33) | collective-permute-done | bytes 65568 | tf_op jit(solution)/shard_map/ppermute | solution.py:32
  133.5 4.8 %collective-permute-start.34 = (bf16[64,256]{1,0:T(8,128)(2,1)S(1)}, bf16[64,256]{1,0:T(8,128)(2,1)S(1)}, u32[]{:S(2)}, u32[]{:S(2)}) collective-permute-start(bf16[64,256]{1,0:T(8,128)(2,1)S(1)} %broadcast_select_fusion.2), channel_id=1, source_target_pairs={{0,2},{2,0},{4,6},{6,4},{8,10},{10,8},{12,14},{14,12},{16,18},{18,... | collective-permute-start | bytes 98312 | tf_op jit(solution)/shard_map/ppermute | solution.py:32
  138.3 0.9 collective-permute-done.34
  139.2 0.6 select_bitcast_fusion
  (71 shorter events, 2.0 us)
Async XLA Ops:
  0.6 43.8 %copy-start.7 = (s32[1,64]{1,0:T(1,128)S(1)}, s32[1,64]{1,0:T(1,128)}, u32[]{:S(2)}) copy-start(s32[1,64]{1,0:T(1,128)} %param.20) | copy-start | bytes 772
  0.6 43.8 %copy-start.8 = (s32[1,64]{1,0:T(1,128)S(1)}, s32[1,64]{1,0:T(1,128)}, u32[]{:S(2)}) copy-start(s32[1,64]{1,0:T(1,128)} %param.17) | copy-start | bytes 772
  0.7 43.8 %copy-start.9 = (s32[1,64]{1,0:T(1,128)S(1)}, s32[1,64]{1,0:T(1,128)}, u32[]{:S(2)}) copy-start(s32[1,64]{1,0:T(1,128)} %param.14) | copy-start | bytes 772
  1.4 5.4 %collective-permute-start.1 = (bf16[64,256]{1,0:T(8,128)(2,1)S(1)}, bf16[64,256]{1,0:T(8,128)(2,1)S(1)}, u32[]{:S(2)}, u32[]{:S(2)}) collective-permute-start(bf16[64,256]{1,0:T(8,128)(2,1)S(1)} %select_bitcast_fusion.2), channel_id=1, source_target_pairs={{0,2},{2,0},{4,6},{6,4},{8,10},{10,8},{12,14},{14,12},{16,18},{18,... | collective-permute-start | bytes 98312 | tf_op jit(solution)/shard_map/ppermute | solution.py:32
  7.6 53.6 %copy-start = (bf16[64,128,128]{2,1,0:T(8,128)(2,1)S(1)}, bf16[64,128,128]{2,1,0:T(8,128)(2,1)}, u32[]{:S(2)}) copy-start(bf16[64,128,128]{2,1,0:T(8,128)(2,1)} %g0.1) | copy-start | bytes 6291460
  7.7 3.8 %collective-permute-start.2 = (bf16[1,256,128]{2,1,0:T(8,128)(2,1)S(1)}, bf16[1,256,128]{2,1,0:T(8,128)(2,1)S(1)}, u32[]{:S(2)}, u32[]{:S(2)}) collective-permute-start(bf16[1,256,128]{2,1,0:T(8,128)(2,1)S(1)} %bitcast.24), channel_id=1, source_target_pairs={{0,32},{2,34},{4,36},{6,38},{8,40},{10,42},{12,44},{14,46},{16,48}... | collective-permute-start | bytes 196616 | tf_op jit(solution)/shard_map/ppermute | solution.py:32
  8.7 12.0 %collective-permute-start = (s32[3,65]{1,0:T(4,128)S(1)}, s32[3,65]{1,0:T(4,128)S(1)}, u32[]{:S(2)}, u32[]{:S(2)}) collective-permute-start(s32[3,65]{1,0:T(4,128)S(1)} %pad_add_fusion.1), channel_id=1, source_target_pairs={{0,2},{2,0},{4,6},{6,4},{8,10},{10,8},{12,14},{14,12},{16,18},{18,... | collective-permute-start | bytes 2348 | tf_op jit(solution)/shard_map/ppermute | solution.py:32
  8.7 52.5 %collective-permute-start.14 = (bf16[64,128,128]{2,1,0:T(8,128)(2,1)}, bf16[64,128,128]{2,1,0:T(8,128)(2,1)}, u32[]{:S(2)}, u32[]{:S(2)}) collective-permute-start(bf16[64,128,128]{2,1,0:T(8,128)(2,1)} %g0.1), channel_id=1, source_target_pairs={{0,2},{2,0},{4,6},{6,4},{8,10},{10,8},{12,14},{14,12},{16,18},{18,... | collective-permute-start | bytes 6291464 | tf_op jit(solution)/shard_map/ppermute | solution.py:32
  11.5 10.8 %collective-permute-start.4 = (bf16[2,256,128]{2,1,0:T(8,128)(2,1)S(1)}, bf16[2,256,128]{2,1,0:T(8,128)(2,1)S(1)}, u32[]{:S(2)}, u32[]{:S(2)}) collective-permute-start(bf16[2,256,128]{2,1,0:T(8,128)(2,1)S(1)} %pad_maximum_fusion), channel_id=1, source_target_pairs={{0,64},{2,6},{4,68},{6,10},{8,72},{10,14},{12,76},{14,18},{16,80},... | collective-permute-start | bytes 393224 | tf_op jit(solution)/shard_map/ppermute | solution.py:32
  11.6 10.8 %collective-permute-start.3 = (bf16[2,256,128]{2,1,0:T(8,128)(2,1)S(1)}, bf16[2,256,128]{2,1,0:T(8,128)(2,1)S(1)}, u32[]{:S(2)}, u32[]{:S(2)}) collective-permute-start(bf16[2,256,128]{2,1,0:T(8,128)(2,1)S(1)} %pad_maximum_fusion), channel_id=1, source_target_pairs={{0,192},{2,30},{4,196},{6,2},{8,200},{10,6},{12,204},{14,10},{16,2... | collective-permute-start | bytes 393224 | tf_op jit(solution)/shard_map/ppermute | solution.py:32
  16.1 10.4 %collective-permute-start.6 = (bf16[2,256,128]{2,1,0:T(8,128)(2,1)S(1)}, bf16[2,256,128]{2,1,0:T(8,128)(2,1)S(1)}, u32[]{:S(2)}, u32[]{:S(2)}) collective-permute-start(bf16[2,256,128]{2,1,0:T(8,128)(2,1)S(1)} %pad_maximum_fusion), channel_id=1, source_target_pairs={{0,16},{2,18},{4,20},{6,22},{8,24},{10,26},{12,28},{14,30},{16,0},... | collective-permute-start | bytes 393224 | tf_op jit(solution)/shard_map/ppermute | solution.py:32
  20.7 40.5 %collective-permute-start.15 = (bf16[64,128,128]{2,1,0:T(8,128)(2,1)}, bf16[64,128,128]{2,1,0:T(8,128)(2,1)}, u32[]{:S(2)}, u32[]{:S(2)}) collective-permute-start(bf16[64,128,128]{2,1,0:T(8,128)(2,1)} %u0.1), channel_id=1, source_target_pairs={{0,2},{2,0},{4,6},{6,4},{8,10},{10,8},{12,14},{14,12},{16,18},{18,... | collective-permute-start | bytes 6291464 | tf_op jit(solution)/shard_map/ppermute | solution.py:32
  22.3 38.9 %collective-permute-start.16 = (bf16[64,128,128]{2,1,0:T(8,128)(2,1)}, bf16[64,128,128]{2,1,0:T(8,128)(2,1)}, u32[]{:S(2)}, u32[]{:S(2)}) collective-permute-start(bf16[64,128,128]{2,1,0:T(8,128)(2,1)} %d0.1), channel_id=1, source_target_pairs={{0,2},{2,0},{4,6},{6,4},{8,10},{10,8},{12,14},{14,12},{16,18},{18,... | collective-permute-start | bytes 6291464 | tf_op jit(solution)/shard_map/ppermute | solution.py:32
  22.4 6.2 %collective-permute-start.5 = (bf16[2,256,128]{2,1,0:T(8,128)(2,1)S(1)}, bf16[2,256,128]{2,1,0:T(8,128)(2,1)S(1)}, u32[]{:S(2)}, u32[]{:S(2)}) collective-permute-start(bf16[2,256,128]{2,1,0:T(8,128)(2,1)S(1)} %collective-permute-done.4), channel_id=1, source_target_pairs={{0,64},{2,6},{4,68},{6,10},{8,72},{10,14},{12,76},{14,18},{16,80},... | collective-permute-start | bytes 393224 | tf_op jit(solution)/shard_map/ppermute | solution.py:32
  26.5 5.0 %collective-permute-start.8 = (bf16[2,256,128]{2,1,0:T(8,128)(2,1)S(1)}, bf16[2,256,128]{2,1,0:T(8,128)(2,1)S(1)}, u32[]{:S(2)}, u32[]{:S(2)}) collective-permute-start(bf16[2,256,128]{2,1,0:T(8,128)(2,1)S(1)} %collective-permute-done.6), channel_id=1, source_target_pairs={{0,64},{2,6},{4,68},{6,10},{8,72},{10,14},{12,76},{14,18},{16,80},... | collective-permute-start | bytes 393224 | tf_op jit(solution)/shard_map/ppermute | solution.py:32
  28.6 4.4 %collective-permute-start.7 = (bf16[2,256,128]{2,1,0:T(8,128)(2,1)S(1)}, bf16[2,256,128]{2,1,0:T(8,128)(2,1)S(1)}, u32[]{:S(2)}, u32[]{:S(2)}) collective-permute-start(bf16[2,256,128]{2,1,0:T(8,128)(2,1)S(1)} %collective-permute-done.6), channel_id=1, source_target_pairs={{0,192},{2,30},{4,196},{6,2},{8,200},{10,6},{12,204},{14,10},{16,2... | collective-permute-start | bytes 393224 | tf_op jit(solution)/shard_map/ppermute | solution.py:32
  31.5 11.5 %collective-permute-start.12 = (bf16[8,256,128]{2,1,0:T(8,128)(2,1)}, bf16[8,256,128]{2,1,0:T(8,128)(2,1)}, u32[]{:S(2)}, u32[]{:S(2)}) collective-permute-start(bf16[8,256,128]{2,1,0:T(8,128)(2,1)} %constant_dynamic-update-slice_fusion.refs_0_), channel_id=1, source_target_pairs={{0,4},{2,66},{4,8},{6,70},{8,12},{10,74},{12,16},{14,78},{16,20},{... | collective-permute-start | bytes 1572872 | tf_op jit(solution)/shard_map/ppermute | solution.py:32
  33.0 5.0 %collective-permute-start.9 = (bf16[2,256,128]{2,1,0:T(8,128)(2,1)S(1)}, bf16[2,256,128]{2,1,0:T(8,128)(2,1)S(1)}, u32[]{:S(2)}, u32[]{:S(2)}) collective-permute-start(bf16[2,256,128]{2,1,0:T(8,128)(2,1)S(1)} %collective-permute-done.8), channel_id=1, source_target_pairs={{0,64},{2,6},{4,68},{6,10},{8,72},{10,14},{12,76},{14,18},{16,80},... | collective-permute-start | bytes 393224 | tf_op jit(solution)/shard_map/ppermute | solution.py:32
  38.0 10.6 %collective-permute-start.10 = (bf16[8,256,128]{2,1,0:T(8,128)(2,1)}, bf16[8,256,128]{2,1,0:T(8,128)(2,1)S(1)}, u32[]{:S(2)}, u32[]{:S(2)}) collective-permute-start(bf16[8,256,128]{2,1,0:T(8,128)(2,1)} %constant_dynamic-update-slice_fusion.refs_0_), channel_id=1, source_target_pairs={{0,28},{2,194},{4,0},{6,198},{8,4},{10,202},{12,8},{14,206},{16,12... | collective-permute-start | bytes 1572872 | tf_op jit(solution)/shard_map/ppermute | solution.py:32
  43.0 11.2 %collective-permute-start.11 = (bf16[8,256,128]{2,1,0:T(8,128)(2,1)S(1)}, bf16[8,256,128]{2,1,0:T(8,128)(2,1)S(1)}, u32[]{:S(2)}, u32[]{:S(2)}) collective-permute-start(bf16[8,256,128]{2,1,0:T(8,128)(2,1)S(1)} %constant_dynamic-update-slice_fusion.5.refs_1_), channel_id=1, source_target_pairs={{0,28},{2,194},{4,0},{6,198},{8,4},{10,202},{12,8},{14,206},{16,12... | collective-permute-start | bytes 1572872 | tf_op jit(solution)/shard_map/ppermute | solution.py:32
  48.6 9.9 %collective-permute-start.13 = (bf16[8,256,128]{2,1,0:T(8,128)(2,1)S(1)}, bf16[8,256,128]{2,1,0:T(8,128)(2,1)S(1)}, u32[]{:S(2)}, u32[]{:S(2)}) collective-permute-start(bf16[8,256,128]{2,1,0:T(8,128)(2,1)S(1)} %constant_dynamic-update-slice_fusion.5.refs_1_), channel_id=1, source_target_pairs={{0,4},{2,66},{4,8},{6,70},{8,12},{10,74},{12,16},{14,78},{16,20},{... | collective-permute-start | bytes 1572872 | tf_op jit(solution)/shard_map/ppermute | solution.py:32
  49.6 0.8 copy-start.3
  54.2 16.6 %collective-permute-start.17 = (bf16[8,256,128]{2,1,0:T(8,128)(2,1)}, bf16[8,256,128]{2,1,0:T(8,128)(2,1)}, u32[]{:S(2)}, u32[]{:S(2)}) collective-permute-start(bf16[8,256,128]{2,1,0:T(8,128)(2,1)} %collective-permute-done.12.refs_4_), channel_id=1, source_target_pairs={{0,4},{2,66},{4,8},{6,70},{8,12},{10,74},{12,16},{14,78},{16,20},{... | collective-permute-start | bytes 1572872 | tf_op jit(solution)/shard_map/ppermute | solution.py:32
  58.5 0.8 copy-start.5
  59.3 11.4 %collective-permute-start.18 = (bf16[8,256,128]{2,1,0:T(8,128)(2,1)}, bf16[8,256,128]{2,1,0:T(8,128)(2,1)}, u32[]{:S(2)}, u32[]{:S(2)}) collective-permute-start(bf16[8,256,128]{2,1,0:T(8,128)(2,1)} %broadcast_select_fusion), channel_id=1, source_target_pairs={{0,28},{2,194},{4,0},{6,198},{8,4},{10,202},{12,8},{14,206},{16,12... | collective-permute-start | bytes 1572872 | tf_op jit(solution)/shard_map/ppermute | solution.py:32
  61.2 1.6 %copy-start.1 = (bf16[64,128,128]{2,1,0:T(8,128)(2,1)S(1)}, bf16[64,128,128]{2,1,0:T(8,128)(2,1)}, u32[]{:S(2)}) copy-start(bf16[64,128,128]{2,1,0:T(8,128)(2,1)} %u0.1) | copy-start | bytes 6291460
  62.8 1.6 %copy-start.2 = (bf16[64,128,128]{2,1,0:T(8,128)(2,1)S(1)}, bf16[64,128,128]{2,1,0:T(8,128)(2,1)}, u32[]{:S(2)}) copy-start(bf16[64,128,128]{2,1,0:T(8,128)(2,1)} %d0.1) | copy-start | bytes 6291460
  64.4 1.0 copy-start.4
  65.4 1.0 copy-start.6
  74.5 7.4 %collective-permute-start.19 = (f32[256,512]{1,0:T(8,128)S(1)}, f32[256,512]{1,0:T(8,128)S(1)}, u32[]{:S(2)}, u32[]{:S(2)}) collective-permute-start(f32[256,512]{1,0:T(8,128)S(1)} %shard_map.124.mine_ref), channel_id=1, source_target_pairs={{0,2},{2,0},{4,6},{6,4},{8,10},{10,8},{12,14},{14,12},{16,18},{18,... | collective-permute-start | bytes 1572872 | tf_op jit(solution)/shard_map/ppermute | solution.py:32
  87.2 9.4 %collective-permute-start.20 = (bf16[8,256,128]{2,1,0:T(8,128)(2,1)S(1)}, bf16[8,256,128]{2,1,0:T(8,128)(2,1)S(1)}, u32[]{:S(2)}, u32[]{:S(2)}) collective-permute-start(bf16[8,256,128]{2,1,0:T(8,128)(2,1)S(1)} %get-tuple-element.12), channel_id=1, source_target_pairs={{0,4},{2,66},{4,8},{6,70},{8,12},{10,74},{12,16},{14,78},{16,20},{... | collective-permute-start | bytes 1572872 | tf_op jit(solution)/shard_map/ppermute | solution.py:32
  87.4 9.9 %collective-permute-start.22 = (bf16[8,256,128]{2,1,0:T(8,128)(2,1)S(1)}, bf16[8,256,128]{2,1,0:T(8,128)(2,1)S(1)}, u32[]{:S(2)}, u32[]{:S(2)}) collective-permute-start(bf16[8,256,128]{2,1,0:T(8,128)(2,1)S(1)} %get-tuple-element.14), channel_id=1, source_target_pairs={{0,28},{2,194},{4,0},{6,198},{8,4},{10,202},{12,8},{14,206},{16,12... | collective-permute-start | bytes 1572872 | tf_op jit(solution)/shard_map/ppermute | solution.py:32
  89.9 11.7 %collective-permute-start.28 = (bf16[8,256,128]{2,1,0:T(8,128)(2,1)S(1)}, bf16[8,256,128]{2,1,0:T(8,128)(2,1)S(1)}, u32[]{:S(2)}, u32[]{:S(2)}) collective-permute-start(bf16[8,256,128]{2,1,0:T(8,128)(2,1)S(1)} %get-tuple-element.17), channel_id=1, source_target_pairs={{0,28},{2,194},{4,0},{6,198},{8,4},{10,202},{12,8},{14,206},{16,12... | collective-permute-start | bytes 1572872 | tf_op jit(solution)/shard_map/ppermute | solution.py:32
  96.9 9.8 %collective-permute-start.27 = (bf16[8,256,128]{2,1,0:T(8,128)(2,1)S(1)}, bf16[8,256,128]{2,1,0:T(8,128)(2,1)S(1)}, u32[]{:S(2)}, u32[]{:S(2)}) collective-permute-start(bf16[8,256,128]{2,1,0:T(8,128)(2,1)S(1)} %get-tuple-element.26), channel_id=1, source_target_pairs={{0,4},{2,66},{4,8},{6,70},{8,12},{10,74},{12,16},{14,78},{16,20},{... | collective-permute-start | bytes 1572872 | tf_op jit(solution)/shard_map/ppermute | solution.py:32
  97.2 15.1 %collective-permute-start.21 = (bf16[8,256,128]{2,1,0:T(8,128)(2,1)S(1)}, bf16[8,256,128]{2,1,0:T(8,128)(2,1)S(1)}, u32[]{:S(2)}, u32[]{:S(2)}) collective-permute-start(bf16[8,256,128]{2,1,0:T(8,128)(2,1)S(1)} %get-tuple-element.27), channel_id=1, source_target_pairs={{0,4},{2,66},{4,8},{6,70},{8,12},{10,74},{12,16},{14,78},{16,20},{... | collective-permute-start | bytes 1572872 | tf_op jit(solution)/shard_map/ppermute | solution.py:32
  97.4 14.9 %collective-permute-start.23 = (bf16[8,256,128]{2,1,0:T(8,128)(2,1)S(1)}, bf16[8,256,128]{2,1,0:T(8,128)(2,1)S(1)}, u32[]{:S(2)}, u32[]{:S(2)}) collective-permute-start(bf16[8,256,128]{2,1,0:T(8,128)(2,1)S(1)} %add_convert_fusion), channel_id=1, source_target_pairs={{0,28},{2,194},{4,0},{6,198},{8,4},{10,202},{12,8},{14,206},{16,12... | collective-permute-start | bytes 1572872 | tf_op jit(solution)/shard_map/ppermute | solution.py:32
  106.9 8.4 %collective-permute-start.30 = (bf16[2,256,128]{2,1,0:T(8,128)(2,1)S(1)}, bf16[2,256,128]{2,1,0:T(8,128)(2,1)S(1)}, u32[]{:S(2)}, u32[]{:S(2)}) collective-permute-start(bf16[2,256,128]{2,1,0:T(8,128)(2,1)S(1)} %get-tuple-element.25), channel_id=1, source_target_pairs={{0,192},{2,30},{4,196},{6,2},{8,200},{10,6},{12,204},{14,10},{16,2... | collective-permute-start | bytes 393224 | tf_op jit(solution)/shard_map/ppermute | solution.py:32
  112.6 11.0 %collective-permute-start.24 = (bf16[2,256,128]{2,1,0:T(8,128)(2,1)S(1)}, bf16[2,256,128]{2,1,0:T(8,128)(2,1)S(1)}, u32[]{:S(2)}, u32[]{:S(2)}) collective-permute-start(bf16[2,256,128]{2,1,0:T(8,128)(2,1)S(1)} %get-tuple-element.22), channel_id=1, source_target_pairs={{0,64},{2,6},{4,68},{6,10},{8,72},{10,14},{12,76},{14,18},{16,80},... | collective-permute-start | bytes 393224 | tf_op jit(solution)/shard_map/ppermute | solution.py:32
  112.6 5.5 %collective-permute-start.25 = (bf16[2,256,128]{2,1,0:T(8,128)(2,1)S(1)}, bf16[2,256,128]{2,1,0:T(8,128)(2,1)S(1)}, u32[]{:S(2)}, u32[]{:S(2)}) collective-permute-start(bf16[2,256,128]{2,1,0:T(8,128)(2,1)S(1)} %get-tuple-element.23), channel_id=1, source_target_pairs={{0,192},{2,30},{4,196},{6,2},{8,200},{10,6},{12,204},{14,10},{16,2... | collective-permute-start | bytes 393224 | tf_op jit(solution)/shard_map/ppermute | solution.py:32
  115.3 5.2 %collective-permute-start.29 = (bf16[2,256,128]{2,1,0:T(8,128)(2,1)S(1)}, bf16[2,256,128]{2,1,0:T(8,128)(2,1)S(1)}, u32[]{:S(2)}, u32[]{:S(2)}) collective-permute-start(bf16[2,256,128]{2,1,0:T(8,128)(2,1)S(1)} %get-tuple-element.24), channel_id=1, source_target_pairs={{0,64},{2,6},{4,68},{6,10},{8,72},{10,14},{12,76},{14,18},{16,80},... | collective-permute-start | bytes 393224 | tf_op jit(solution)/shard_map/ppermute | solution.py:32
  115.4 5.1 %collective-permute-start.31 = (bf16[2,256,128]{2,1,0:T(8,128)(2,1)S(1)}, bf16[2,256,128]{2,1,0:T(8,128)(2,1)S(1)}, u32[]{:S(2)}, u32[]{:S(2)}) collective-permute-start(bf16[2,256,128]{2,1,0:T(8,128)(2,1)S(1)} %fusion.4), channel_id=1, source_target_pairs={{0,192},{2,30},{4,196},{6,2},{8,200},{10,6},{12,204},{14,10},{16,2... | collective-permute-start | bytes 393224 | tf_op jit(solution)/shard_map/ppermute | solution.py:32
  118.2 5.5 %collective-permute-start.26 = (bf16[2,256,128]{2,1,0:T(8,128)(2,1)S(1)}, bf16[2,256,128]{2,1,0:T(8,128)(2,1)S(1)}, u32[]{:S(2)}, u32[]{:S(2)}) collective-permute-start(bf16[2,256,128]{2,1,0:T(8,128)(2,1)S(1)} %fusion.7), channel_id=1, source_target_pairs={{0,192},{2,30},{4,196},{6,2},{8,200},{10,6},{12,204},{14,10},{16,2... | collective-permute-start | bytes 393224 | tf_op jit(solution)/shard_map/ppermute | solution.py:32
  120.5 9.6 %collective-permute-start.32 = (bf16[2,256,128]{2,1,0:T(8,128)(2,1)S(1)}, bf16[2,256,128]{2,1,0:T(8,128)(2,1)S(1)}, u32[]{:S(2)}, u32[]{:S(2)}) collective-permute-start(bf16[2,256,128]{2,1,0:T(8,128)(2,1)S(1)} %fusion.6), channel_id=1, source_target_pairs={{0,16},{2,18},{4,20},{6,22},{8,24},{10,26},{12,28},{14,30},{16,0},... | collective-permute-start | bytes 393224 | tf_op jit(solution)/shard_map/ppermute | solution.py:32
  130.2 3.2 %collective-permute-start.33 = (bf16[256,128]{1,0:T(8,128)(2,1)S(1)}, bf16[256,128]{1,0:T(8,128)(2,1)S(1)}, u32[]{:S(2)}, u32[]{:S(2)}) collective-permute-start(bf16[256,128]{1,0:T(8,128)(2,1)S(1)} %fusion.12), channel_id=1, source_target_pairs={{0,32},{2,34},{4,36},{6,38},{8,40},{10,42},{12,44},{14,46},{16,48}... | collective-permute-start | bytes 196616 | tf_op jit(solution)/shard_map/ppermute | solution.py:32
  133.5 5.6 %collective-permute-start.34 = (bf16[64,256]{1,0:T(8,128)(2,1)S(1)}, bf16[64,256]{1,0:T(8,128)(2,1)S(1)}, u32[]{:S(2)}, u32[]{:S(2)}) collective-permute-start(bf16[64,256]{1,0:T(8,128)(2,1)S(1)} %broadcast_select_fusion.2), channel_id=1, source_target_pairs={{0,2},{2,0},{4,6},{6,4},{8,10},{10,8},{12,14},{14,12},{16,18},{18,... | collective-permute-start | bytes 98312 | tf_op jit(solution)/shard_map/ppermute | solution.py:32

commit v4 on v2

--- a/solution.py
+++ b/solution.py
@@ -111,15 +111,33 @@
     return lax.dot_general(left, right, (((1,), (1,)), ((), ())), preferred_element_type=F32)
 
 
+LOADS = ((0, 1, 2, 3, 4, 5), (4, 5, 0, 1, 2, 3))
+
+
 def inner_kernel(base, maps_ref, *refs):
-    *piece_refs, g0, u0, g1, u1, d0, d1, sums_ref = refs
     core = maps_ref[6 * SLOTS]
     wide = 2 * BLOCK
     if base:
-        start_ref, *piece_refs = piece_refs
+        start_ref, *piece_refs, held_ref, sums_ref = refs
         sums_ref[...] = start_ref[...]
     else:
+        *refs, sums_ref, held_ref, sems = refs
+        piece_refs, weight_refs = refs[:-6], refs[-6:]
+        copies = [pltpu.make_async_copy(ref, held_ref.at[n], sems.at[n]) for n, ref in enumerate(weight_refs)]
+        for k in range(NC):
+
+            @pl.when(core == k)
+            def _(k=k):
+                for n in LOADS[k]:
+                    copies[n].start()
+
         sums_ref[...] = jnp.zeros_like(sums_ref)
+    g0, u0, g1, u1, d0, d1 = (held_ref.at[n] for n in range(6))
+
+    def arrived(ranks):
+        if not base:
+            for n in ranks:
+                copies[n].wait()
 
     def groups():
         for rank, ref in enumerate(piece_refs):
@@ -129,6 +147,7 @@
 
     @pl.when(core == 0)
     def _():
+        arrived(LOADS[0][:4])
         for spots, left in groups():
             for n, pair in enumerate((((0, g0), (1, u0)), ((3, g1), (4, u1)))):
                 right = jnp.concatenate(
@@ -139,9 +158,11 @@
                     axis=0,
                 )
                 sums_ref[:, pl.ds(n * wide, wide)] += jnp.dot(left, right, preferred_element_type=F32)
+        arrived(LOADS[0][4:])
 
     @pl.when(core == 1)
     def _():
+        arrived(LOADS[1][:2])
         for spots, left in groups():
             right = jnp.concatenate(
                 [
@@ -151,10 +172,12 @@
                 axis=0,
             )
             sums_ref[:, pl.ds(0, wide)] += contract_last(left, right)
-
-
-def outer_kernel(maps_ref, mine_ref, theirs_ref, g0, u0, g1, u1, d0, d1, *part_refs):
+        arrived(LOADS[1][2:])
+
+
+def outer_kernel(maps_ref, mine_ref, theirs_ref, held_ref, *part_refs):
     core = maps_ref[6 * SLOTS]
+    g0, u0, g1, u1, d0, d1 = (held_ref.at[n] for n in range(6))
 
     def columns(ref, n):
         return ref[:, pl.ds(n * BLOCK, BLOCK)]
@@ -230,16 +253,19 @@
     )(block)
 
 
-def call(kernel, outs, flops, maps, *inputs):
+def call(kernel, outs, flops, maps, *inputs, weights=()):
     vmem = pl.BlockSpec(memory_space=pltpu.VMEM)
     return pl.pallas_call(
         kernel,
         out_shape=outs,
-        in_specs=[pl.BlockSpec(memory_space=pltpu.SMEM)] + [vmem] * len(inputs),
+        in_specs=[pl.BlockSpec(memory_space=pltpu.SMEM)]
+        + [vmem] * len(inputs)
+        + [pl.BlockSpec(memory_space=pltpu.HBM)] * len(weights),
         out_specs=jax.tree.map(lambda _: vmem, outs),
+        scratch_shapes=[pltpu.SemaphoreType.DMA((len(weights),))] if weights else [],
         cost_estimate=pl.CostEstimate(flops=flops, bytes_accessed=1 << 24, transcendentals=1 << 15),
         compiler_params=pltpu.CompilerParams(vmem_limit_bytes=21 << 20),
-    )(maps, *inputs)
+    )(maps, *inputs, *(pltpu.with_memory_space_constraint(w, pltpu.HBM) for w in weights))
 
 
 def body(
@@ -293,11 +319,14 @@
     weights += (down_blocks, shift(down_blocks, "c", 1))
     flops = NC * SLOTS * BLOCK * BLOCK * batch
     sums = jax.ShapeDtypeStruct((batch, 4 * BLOCK), F32)
-    mine = call(functools.partial(inner_kernel, 0), sums, 3 * flops, maps, *pieces[:6], *weights)
-    mine = call(functools.partial(inner_kernel, 6), sums, flops, maps, mine, *pieces[6:], *weights)
+    held = jax.ShapeDtypeStruct((6, SLOTS, BLOCK, BLOCK), BF16)
+    mine, held = call(
+        functools.partial(inner_kernel, 0), (sums, held), 3 * flops, maps, *pieces[:6], weights=weights
+    )
+    mine = call(functools.partial(inner_kernel, 6), sums, flops, maps, mine, *pieces[6:], held)
     theirs = shift(mine, "c", 1)
     parts = tuple(jax.ShapeDtypeStruct((PART, batch, BLOCK), BF16 if sent else F32) for sent in SENT)
-    parts = call(outer_kernel, parts, 4 * flops, maps, mine, theirs, *weights)
+    parts = call(outer_kernel, parts, 4 * flops, maps, mine, theirs, held)
     total = near_reduce(small_reduce(*large_reduce(parts, "zy"), "yz"))
     total = transpose(total).astype(BF16)
     low, high = jnp.split(total, 2)

time: 138 us -> 131 us (0.949)
  local copies, waits for them, and re-layouts: 6.52 us -> 0.6 us
  Pallas kernels: 13.6 us -> 10.2 us
  waiting for transfers between devices: 58.1 us -> 60 us
    unnamed x20 -> x12, local copies, waits for them, and re-layouts: 5.12 us -> 0.1 us
    pallas_call x3, Pallas kernels: 13.4 us -> 10 us  [call(): pl.pallas_call(kernel, out_shape=outs, in_specs=[pl.BlockSpec(memory_spac...]
    ppermute x33, waiting for transfers between devices: 58.1 us -> 60 us  [permute(): return lax.ppermute(value, 'tp', pairs)]
  transfers between devices with their start and end apart: 33 -> 33, of which waited for: 18 -> 20; matrix products, arithmetic and copies ran while one was open for 4% -> 3% of each run, Pallas kernels for 3% -> 4%
where the time goes in v4:
time: 131 us
  waiting for transfers between devices  60 us (46%)
  starting transfers between devices  52.8 us (40%)
  Pallas kernels  10.2 us (8%)
  other arithmetic  4.3 us (3%)
  between operations  2.89 us (2%)
    ppermute x33, waiting for transfers between devices, permute(): return lax.ppermute(value, 'tp', pairs)  60 us
    ppermute x33, starting transfers between devices, permute(): return lax.ppermute(value, 'tp', pairs)  52.8 us
    pallas_call x3, Pallas kernels, call(): pl.pallas_call(kernel, out_shape=outs, in_specs=[pl.BlockSpec(memory_spac...  10 us
  transfers between devices with their start and end apart: 33, of which 20 were waited for; matrix products, arithmetic and copies ran while one was open for 3% of the time, Pallas kernels for 4%

profile of v4, /device:TPU:1, one launch (start us, length us, event | category | flops | bytes accessed | tf_op | source)
XLA Modules:
  0.0 130.7 jit_solution(13819954409957937424)
XLA Ops:
  0.7 0.8 select_bitcast_fusion.2
  1.4 3.2 %collective-permute-start.1 = (bf16[64,256]{1,0:T(8,128)(2,1)S(1)}, bf16[64,256]{1,0:T(8,128)(2,1)S(1)}, u32[]{:S(2)}, u32[]{:S(2)}) collective-permute-start(bf16[64,256]{1,0:T(8,128)(2,1)S(1)} %select_bitcast_fusion.2), channel_id=1, source_target_pairs={{0,2},{2,0},{4,6},{6,4},{8,10},{10,8},{12,14},{14,12},{16,18},{18,... | collective-permute-start | bytes 98312 | tf_op jit(solution)/shard_map/ppermute | solution.py:32
  4.7 0.1 collective-permute-start.13
  4.8 0.4 collective-permute-start.14
  7.2 0.1 copy.14
  7.3 0.8 bitcast_select_fusion.1
  8.2 5.3 %collective-permute-start.2 = (bf16[1,256,128]{2,1,0:T(8,128)(2,1)S(1)}, bf16[1,256,128]{2,1,0:T(8,128)(2,1)S(1)}, u32[]{:S(2)}, u32[]{:S(2)}) collective-permute-start(bf16[1,256,128]{2,1,0:T(8,128)(2,1)S(1)} %bitcast.32), channel_id=1, source_target_pairs={{0,16},{2,18},{4,20},{6,22},{8,24},{10,26},{12,28},{14,30},{16,0},... | collective-permute-start | bytes 196616 | tf_op jit(solution)/shard_map/ppermute | solution.py:32
  13.5 1.2 collective-permute-start.3
  14.7 0.2 collective-permute-start.4
  14.8 0.8 pad_add_fusion.1
  15.6 0.2 collective-permute-done.2
  15.8 1.0 collective-permute-start.15
  16.8 7.0 %collective-permute-done.4 = bf16[1,256,128]{2,1,0:T(8,128)(2,1)S(1)} collective-permute-done((bf16[1,256,128]{2,1,0:T(8,128)(2,1)S(1)}, bf16[1,256,128]{2,1,0:T(8,128)(2,1)S(1)}, u32[]{:S(2)}, u32[]{:S(2)}) %collective-permute-start.4) | collective-permute-done | bytes 65568 | tf_op jit(solution)/shard_map/ppermute | solution.py:32
  24.0 2.7 %collective-permute-start.5 = (bf16[4,256,128]{2,1,0:T(8,128)(2,1)S(1)}, bf16[4,256,128]{2,1,0:T(8,128)(2,1)S(1)}, u32[]{:S(2)}, u32[]{:S(2)}) collective-permute-start(bf16[4,256,128]{2,1,0:T(8,128)(2,1)S(1)} %pad_maximum_fusion), channel_id=1, source_target_pairs={{0,192},{2,30},{4,196},{6,2},{8,200},{10,6},{12,204},{14,10},{16,2... | collective-permute-start | bytes 786440 | tf_op jit(solution)/shard_map/ppermute | solution.py:32
  26.7 4.0 %collective-permute-done.6 = bf16[4,256,128]{2,1,0:T(8,128)(2,1)S(1)} collective-permute-done((bf16[4,256,128]{2,1,0:T(8,128)(2,1)S(1)}, bf16[4,256,128]{2,1,0:T(8,128)(2,1)S(1)}, u32[]{:S(2)}, u32[]{:S(2)}) %collective-permute-start.6) | collective-permute-done | bytes 262176 | tf_op jit(solution)/shard_map/ppermute | solution.py:32
  30.7 1.8 %collective-permute-start = (s32[3,65]{1,0:T(4,128)S(1)}, s32[3,65]{1,0:T(4,128)S(1)}, u32[]{:S(2)}, u32[]{:S(2)}) collective-permute-start(s32[3,65]{1,0:T(4,128)S(1)} %pad_add_fusion.1), channel_id=1, source_target_pairs={{0,2},{2,0},{4,6},{6,4},{8,10},{10,8},{12,14},{14,12},{16,18},{18,... | collective-permute-start | bytes 2348 | tf_op jit(solution)/shard_map/ppermute | solution.py:32
  32.5 0.6 collective-permute-start.7
  33.1 0.2 collective-permute-done
  33.3 2.1 %collective-permute-start.8 = (bf16[2,256,128]{2,1,0:T(8,128)(2,1)S(1)}, bf16[2,256,128]{2,1,0:T(8,128)(2,1)S(1)}, u32[]{:S(2)}, u32[]{:S(2)}) collective-permute-start(bf16[2,256,128]{2,1,0:T(8,128)(2,1)S(1)} %slice.65), channel_id=1, source_target_pairs={{0,192},{2,30},{4,196},{6,2},{8,200},{10,6},{12,204},{14,10},{16,2... | collective-permute-start | bytes 393224 | tf_op jit(solution)/shard_map/ppermute | solution.py:32
  35.4 2.5 %collective-permute-done.7 = bf16[2,256,128]{2,1,0:T(8,128)(2,1)S(1)} collective-permute-done((bf16[2,256,128]{2,1,0:T(8,128)(2,1)S(1)}, bf16[2,256,128]{2,1,0:T(8,128)(2,1)S(1)}, u32[]{:S(2)}, u32[]{:S(2)}) %collective-permute-start.7) | collective-permute-done | bytes 131104 | tf_op jit(solution)/shard_map/ppermute | solution.py:32
  37.9 2.7 %collective-permute-start.9 = (bf16[8,256,128]{2,1,0:T(8,128)(2,1)S(1)}, bf16[8,256,128]{2,1,0:T(8,128)(2,1)S(1)}, u32[]{:S(2)}, u32[]{:S(2)}) collective-permute-start(bf16[8,256,128]{2,1,0:T(8,128)(2,1)S(1)} %constant_dynamic-update-slice_fusion.refs_0_), channel_id=1, source_target_pairs={{0,28},{2,194},{4,0},{6,198},{8,4},{10,202},{12,8},{14,206},{16,12... | collective-permute-start | bytes 1572872 | tf_op jit(solution)/shard_map/ppermute | solution.py:32
  40.7 6.8 %collective-permute-done.11.refs_4_ = bf16[8,256,128]{2,1,0:T(8,128)(2,1)S(1)} collective-permute-done((bf16[8,256,128]{2,1,0:T(8,128)(2,1)S(1)}, bf16[8,256,128]{2,1,0:T(8,128)(2,1)S(1)}, u32[]{:S(2)}, u32[]{:S(2)}) %collective-permute-start.11) | collective-permute-done | bytes 524320 | tf_op jit(solution)/shard_map/ppermute | solution.py:32
  47.5 1.4 %collective-permute-start.12 = (bf16[8,256,128]{2,1,0:T(8,128)(2,1)S(1)}, bf16[8,256,128]{2,1,0:T(8,128)(2,1)S(1)}, u32[]{:S(2)}, u32[]{:S(2)}) collective-permute-start(bf16[8,256,128]{2,1,0:T(8,128)(2,1)S(1)} %constant_dynamic-update-slice_fusion.5.refs_1_), channel_id=1, source_target_pairs={{0,4},{2,66},{4,8},{6,70},{8,12},{10,74},{12,16},{14,78},{16,20},{... | collective-permute-start | bytes 1572872 | tf_op jit(solution)/shard_map/ppermute | solution.py:32
  49.0 0.2 slice_reduce_fusion
  49.2 6.6 %collective-permute-done.10.refs_3_ = bf16[8,256,128]{2,1,0:T(8,128)(2,1)S(1)} collective-permute-done((bf16[8,256,128]{2,1,0:T(8,128)(2,1)S(1)}, bf16[8,256,128]{2,1,0:T(8,128)(2,1)S(1)}, u32[]{:S(2)}, u32[]{:S(2)}) %collective-permute-start.10) | collective-permute-done | bytes 524320 | tf_op jit(solution)/shard_map/ppermute | solution.py:32
  55.8 1.2 collective-permute-done.12.refs_5_
  57.0 1.4 %collective-permute-start.17 = (bf16[8,256,128]{2,1,0:T(8,128)(2,1)S(1)}, bf16[8,256,128]{2,1,0:T(8,128)(2,1)}, u32[]{:S(2)}, u32[]{:S(2)}) collective-permute-start(bf16[8,256,128]{2,1,0:T(8,128)(2,1)S(1)} %collective-permute-done.10.refs_3_), channel_id=1, source_target_pairs={{0,28},{2,194},{4,0},{6,198},{8,4},{10,202},{12,8},{14,206},{16,12... | collective-permute-start | bytes 1572872 | tf_op jit(solution)/shard_map/ppermute | solution.py:32
  58.5 0.3 select_reduce_fusion
  58.8 5.3 %shard_map.123 = (f32[256,512]{1,0:T(8,128)S(1)}, bf16[6,64,128,128]{3,2,1,0:T(8,128)(2,1)S(1)}) custom-call(s32[385]{0:T(512)S(1)} %pad_add_fusion.2.maps_ref, bf16[8,256,128]{2,1,0:T(8,128)(2,1)S(1)} %constant_dynamic-update-slice_fusion.refs_0_, bf16[8,256,128]{2,1,0:T(8,128)(2,1)S(1)} %constant_dynamic-update-slice_fusion.5.refs_1_, ...), custom_call_target="tpu_custom_call" | custom-call | flops 1610612736 | bytes 16777216 | tf_op jit(solution)/shard_map/pallas_call | solution.py:258
  64.1 1.3 collective-permute-done.16.refs_1_
  65.4 1.7 %shard_map.124.mine_ref = f32[256,512]{1,0:T(8,128)S(1)} custom-call(s32[385]{0:T(512)S(1)} %pad_add_fusion.2.maps_ref, f32[256,512]{1,0:T(8,128)S(1)} %get-tuple-element.12.refs_0_, bf16[8,256,128]{2,1,0:T(8,128)(2,1)} %collective-permute-done.16.refs_1_, bf16[8,256,128]{2,1,0:T(8,128)(2,1)} %collective-permute-done.17.refs_2_, ...), custom_call_target="tpu_custom_call" | custom-call | flops 536870912 | bytes 16777216 | tf_op jit(solution)/shard_map/pallas_call | solution.py:258
  67.2 4.0 %collective-permute-start.18 = (f32[256,512]{1,0:T(8,128)S(1)}, f32[256,512]{1,0:T(8,128)S(1)}, u32[]{:S(2)}, u32[]{:S(2)}) collective-permute-start(f32[256,512]{1,0:T(8,128)S(1)} %shard_map.124.mine_ref), channel_id=1, source_target_pairs={{0,2},{2,0},{4,6},{6,4},{8,10},{10,8},{12,14},{14,12},{16,18},{18,... | collective-permute-start | bytes 1572872 | tf_op jit(solution)/shard_map/ppermute | solution.py:32
  71.2 1.5 %collective-permute-done.18.theirs_ref = f32[256,512]{1,0:T(8,128)S(1)} collective-permute-done((f32[256,512]{1,0:T(8,128)S(1)}, f32[256,512]{1,0:T(8,128)S(1)}, u32[]{:S(2)}, u32[]{:S(2)}) %collective-permute-start.18) | collective-permute-done | bytes 524320 | tf_op jit(solution)/shard_map/ppermute | solution.py:32
  72.7 3.0 %shard_map.125 = (f32[8,256,128]{2,1,0:T(8,128)S(1)}, f32[8,256,128]{2,1,0:T(8,128)S(1)}, bf16[8,256,128]{2,1,0:T(8,128)(2,1)S(1)}, f32[8,256,128]{2,1,0:T(8,128...) custom-call(s32[385]{0:T(512)S(1)} %pad_add_fusion.2.maps_ref, ...), custom_call_target="tpu_custom_call" | custom-call | flops 2147483648 | bytes 16777216 | tf_op jit(solution)/shard_map/pallas_call | solution.py:258
  75.7 0.3 collective-permute-start.22
  76.0 2.4 %collective-permute-start.20 = (bf16[8,256,128]{2,1,0:T(8,128)(2,1)S(1)}, bf16[8,256,128]{2,1,0:T(8,128)(2,1)S(1)}, u32[]{:S(2)}, u32[]{:S(2)}) collective-permute-start(bf16[8,256,128]{2,1,0:T(8,128)(2,1)S(1)} %get-tuple-element.17), channel_id=1, source_target_pairs={{0,28},{2,194},{4,0},{6,198},{8,4},{10,202},{12,8},{14,206},{16,12... | collective-permute-start | bytes 1572872 | tf_op jit(solution)/shard_map/ppermute | solution.py:32
  78.5 0.6 collective-permute-start.24
  79.1 6.0 %collective-permute-done.22 = bf16[8,256,128]{2,1,0:T(8,128)(2,1)S(1)} collective-permute-done((bf16[8,256,128]{2,1,0:T(8,128)(2,1)S(1)}, bf16[8,256,128]{2,1,0:T(8,128)(2,1)S(1)}, u32[]{:S(2)}, u32[]{:S(2)}) %collective-permute-start.22) | collective-permute-done | bytes 524320 | tf_op jit(solution)/shard_map/ppermute | solution.py:32
  85.1 0.1 add_convert_fusion
  85.3 0.1 collective-permute-start.23
  85.3 0.4 collective-permute-start.19
  85.7 0.1 add_convert_fusion.1
  85.9 2.7 %collective-permute-start.21 = (bf16[8,256,128]{2,1,0:T(8,128)(2,1)S(1)}, bf16[8,256,128]{2,1,0:T(8,128)(2,1)S(1)}, u32[]{:S(2)}, u32[]{:S(2)}) collective-permute-start(bf16[8,256,128]{2,1,0:T(8,128)(2,1)S(1)} %add_convert_fusion.1), channel_id=1, source_target_pairs={{0,28},{2,194},{4,0},{6,198},{8,4},{10,202},{12,8},{14,206},{16,12... | collective-permute-start | bytes 1572872 | tf_op jit(solution)/shard_map/ppermute | solution.py:32
  88.5 1.7 %collective-permute-done.24 = bf16[8,256,128]{2,1,0:T(8,128)(2,1)S(1)} collective-permute-done((bf16[8,256,128]{2,1,0:T(8,128)(2,1)S(1)}, bf16[8,256,128]{2,1,0:T(8,128)(2,1)S(1)}, u32[]{:S(2)}, u32[]{:S(2)}) %collective-permute-start.24) | collective-permute-done | bytes 524320 | tf_op jit(solution)/shard_map/ppermute | solution.py:32
  90.2 4.7 %collective-permute-done.23 = bf16[8,256,128]{2,1,0:T(8,128)(2,1)S(1)} collective-permute-done((bf16[8,256,128]{2,1,0:T(8,128)(2,1)S(1)}, bf16[8,256,128]{2,1,0:T(8,128)(2,1)S(1)}, u32[]{:S(2)}, u32[]{:S(2)}) %collective-permute-start.23) | collective-permute-done | bytes 524320 | tf_op jit(solution)/shard_map/ppermute | solution.py:32
  94.9 0.2 fusion.10
  95.1 0.2 collective-permute-start.25
  95.4 5.1 %collective-permute-done.19 = bf16[8,256,128]{2,1,0:T(8,128)(2,1)S(1)} collective-permute-done((bf16[8,256,128]{2,1,0:T(8,128)(2,1)S(1)}, bf16[8,256,128]{2,1,0:T(8,128)(2,1)S(1)}, u32[]{:S(2)}, u32[]{:S(2)}) %collective-permute-start.19) | collective-permute-done | bytes 524320 | tf_op jit(solution)/shard_map/ppermute | solution.py:32
  100.5 0.1 convert_add_fusion.1
  100.7 4.3 %collective-permute-start.27 = (bf16[2,256,128]{2,1,0:T(8,128)(2,1)S(1)}, bf16[2,256,128]{2,1,0:T(8,128)(2,1)S(1)}, u32[]{:S(2)}, u32[]{:S(2)}) collective-permute-start(bf16[2,256,128]{2,1,0:T(8,128)(2,1)S(1)} %get-tuple-element.28), channel_id=1, source_target_pairs={{0,192},{2,30},{4,196},{6,2},{8,200},{10,6},{12,204},{14,10},{16,2... | collective-permute-start | bytes 393224 | tf_op jit(solution)/shard_map/ppermute | solution.py:32
  105.2 1.8 %collective-permute-done.27 = bf16[2,256,128]{2,1,0:T(8,128)(2,1)S(1)} collective-permute-done((bf16[2,256,128]{2,1,0:T(8,128)(2,1)S(1)}, bf16[2,256,128]{2,1,0:T(8,128)(2,1)S(1)}, u32[]{:S(2)}, u32[]{:S(2)}) %collective-permute-start.27) | collective-permute-done | bytes 131104 | tf_op jit(solution)/shard_map/ppermute | solution.py:32
  107.0 3.5 %collective-permute-start.28 = (bf16[4,256,128]{2,1,0:T(8,128)(2,1)S(1)}, bf16[4,256,128]{2,1,0:T(8,128)(2,1)S(1)}, u32[]{:S(2)}, u32[]{:S(2)}) collective-permute-start(bf16[4,256,128]{2,1,0:T(8,128)(2,1)S(1)} %pad_maximum_fusion.2), channel_id=1, source_target_pairs={{0,192},{2,30},{4,196},{6,2},{8,200},{10,6},{12,204},{14,10},{16,2... | collective-permute-start | bytes 786440 | tf_op jit(solution)/shard_map/ppermute | solution.py:32
  110.5 1.4 %collective-permute-done.26 = bf16[4,256,128]{2,1,0:T(8,128)(2,1)S(1)} collective-permute-done((bf16[4,256,128]{2,1,0:T(8,128)(2,1)S(1)}, bf16[4,256,128]{2,1,0:T(8,128)(2,1)S(1)}, u32[]{:S(2)}, u32[]{:S(2)}) %collective-permute-start.26) | collective-permute-done | bytes 262176 | tf_op jit(solution)/shard_map/ppermute | solution.py:32
  111.9 1.9 %collective-permute-done.28 = bf16[4,256,128]{2,1,0:T(8,128)(2,1)S(1)} collective-permute-done((bf16[4,256,128]{2,1,0:T(8,128)(2,1)S(1)}, bf16[4,256,128]{2,1,0:T(8,128)(2,1)S(1)}, u32[]{:S(2)}, u32[]{:S(2)}) %collective-permute-start.28) | collective-permute-done | bytes 262176 | tf_op jit(solution)/shard_map/ppermute | solution.py:32
  113.8 0.1 fusion.8
  113.9 1.7 %collective-permute-start.29 = (bf16[256,128]{1,0:T(8,128)(2,1)S(1)}, bf16[256,128]{1,0:T(8,128)(2,1)S(1)}, u32[]{:S(2)}, u32[]{:S(2)}) collective-permute-start(bf16[256,128]{1,0:T(8,128)(2,1)S(1)} %get-tuple-element.29), channel_id=1, source_target_pairs={{0,16},{2,18},{4,20},{6,22},{8,24},{10,26},{12,28},{14,30},{16,0},... | collective-permute-start | bytes 196616 | tf_op jit(solution)/shard_map/ppermute | solution.py:32
  115.6 0.3 collective-permute-start.30
  115.9 4.7 %collective-permute-start.31 = (bf16[256,128]{1,0:T(8,128)(2,1)S(1)}, bf16[256,128]{1,0:T(8,128)(2,1)S(1)}, u32[]{:S(2)}, u32[]{:S(2)}) collective-permute-start(bf16[256,128]{1,0:T(8,128)(2,1)S(1)} %get-tuple-element.30), channel_id=1, source_target_pairs={{0,48},{2,50},{4,52},{6,54},{8,56},{10,58},{12,60},{14,62},{16,32}... | collective-permute-start | bytes 196616 | tf_op jit(solution)/shard_map/ppermute | solution.py:32
  120.6 0.5 collective-permute-done.29
  121.0 4.6 %collective-permute-done.31 = bf16[256,128]{1,0:T(8,128)(2,1)S(1)} collective-permute-done((bf16[256,128]{1,0:T(8,128)(2,1)S(1)}, bf16[256,128]{1,0:T(8,128)(2,1)S(1)}, u32[]{:S(2)}, u32[]{:S(2)}) %collective-permute-start.31) | collective-permute-done | bytes 65568 | tf_op jit(solution)/shard_map/ppermute | solution.py:32
  125.7 0.1 shard_map.126
  125.9 3.4 %collective-permute-start.32 = (bf16[64,256]{1,0:T(8,128)(2,1)S(1)}, bf16[64,256]{1,0:T(8,128)(2,1)S(1)}, u32[]{:S(2)}, u32[]{:S(2)}) collective-permute-start(bf16[64,256]{1,0:T(8,128)(2,1)S(1)} %broadcast_select_fusion.1), channel_id=1, source_target_pairs={{0,2},{2,0},{4,6},{6,4},{8,10},{10,8},{12,14},{14,12},{16,18},{18,... | collective-permute-start | bytes 98312 | tf_op jit(solution)/shard_map/ppermute | solution.py:32
  129.2 0.9 collective-permute-done.32
  130.1 0.6 select_bitcast_fusion
  (54 shorter events, 1.0 us)
Async XLA Ops:
  0.6 48.3 %copy-start.2 = (s32[1,64]{1,0:T(1,128)S(1)}, s32[1,64]{1,0:T(1,128)}, u32[]{:S(2)}) copy-start(s32[1,64]{1,0:T(1,128)} %param.14) | copy-start | bytes 772
  0.6 48.3 %copy-start.1 = (s32[1,64]{1,0:T(1,128)S(1)}, s32[1,64]{1,0:T(1,128)}, u32[]{:S(2)}) copy-start(s32[1,64]{1,0:T(1,128)} %param.17) | copy-start | bytes 772
  0.7 48.3 %copy-start = (s32[1,64]{1,0:T(1,128)S(1)}, s32[1,64]{1,0:T(1,128)}, u32[]{:S(2)}) copy-start(s32[1,64]{1,0:T(1,128)} %param.20) | copy-start | bytes 772
  1.4 5.9 %collective-permute-start.1 = (bf16[64,256]{1,0:T(8,128)(2,1)S(1)}, bf16[64,256]{1,0:T(8,128)(2,1)S(1)}, u32[]{:S(2)}, u32[]{:S(2)}) collective-permute-start(bf16[64,256]{1,0:T(8,128)(2,1)S(1)} %select_bitcast_fusion.2), channel_id=1, source_target_pairs={{0,2},{2,0},{4,6},{6,4},{8,10},{10,8},{12,14},{14,12},{16,18},{18,... | collective-permute-start | bytes 98312 | tf_op jit(solution)/shard_map/ppermute | solution.py:32
  4.7 54.1 %collective-permute-start.13 = (bf16[64,128,128]{2,1,0:T(8,128)(2,1)}, bf16[64,128,128]{2,1,0:T(8,128)(2,1)}, u32[]{:S(2)}, u32[]{:S(2)}) collective-permute-start(bf16[64,128,128]{2,1,0:T(8,128)(2,1)} %refs_6_.1), channel_id=1, source_target_pairs={{0,2},{2,0},{4,6},{6,4},{8,10},{10,8},{12,14},{14,12},{16,18},{18,... | collective-permute-start | bytes 6291464 | tf_op jit(solution)/shard_map/ppermute | solution.py:32
  4.8 54.0 %collective-permute-start.14 = (bf16[64,128,128]{2,1,0:T(8,128)(2,1)}, bf16[64,128,128]{2,1,0:T(8,128)(2,1)}, u32[]{:S(2)}, u32[]{:S(2)}) collective-permute-start(bf16[64,128,128]{2,1,0:T(8,128)(2,1)} %refs_7_.1), channel_id=1, source_target_pairs={{0,2},{2,0},{4,6},{6,4},{8,10},{10,8},{12,14},{14,12},{16,18},{18,... | collective-permute-start | bytes 6291464 | tf_op jit(solution)/shard_map/ppermute | solution.py:32
  8.2 7.7 %collective-permute-start.2 = (bf16[1,256,128]{2,1,0:T(8,128)(2,1)S(1)}, bf16[1,256,128]{2,1,0:T(8,128)(2,1)S(1)}, u32[]{:S(2)}, u32[]{:S(2)}) collective-permute-start(bf16[1,256,128]{2,1,0:T(8,128)(2,1)S(1)} %bitcast.32), channel_id=1, source_target_pairs={{0,16},{2,18},{4,20},{6,22},{8,24},{10,26},{12,28},{14,30},{16,0},... | collective-permute-start | bytes 196616 | tf_op jit(solution)/shard_map/ppermute | solution.py:32
  13.5 3.3 %collective-permute-start.3 = (bf16[1,256,128]{2,1,0:T(8,128)(2,1)S(1)}, bf16[1,256,128]{2,1,0:T(8,128)(2,1)S(1)}, u32[]{:S(2)}, u32[]{:S(2)}) collective-permute-start(bf16[1,256,128]{2,1,0:T(8,128)(2,1)S(1)} %bitcast.33), channel_id=1, source_target_pairs={{0,32},{2,34},{4,36},{6,38},{8,40},{10,42},{12,44},{14,46},{16,48}... | collective-permute-start | bytes 196616 | tf_op jit(solution)/shard_map/ppermute | solution.py:32
  14.7 9.2 %collective-permute-start.4 = (bf16[1,256,128]{2,1,0:T(8,128)(2,1)S(1)}, bf16[1,256,128]{2,1,0:T(8,128)(2,1)S(1)}, u32[]{:S(2)}, u32[]{:S(2)}) collective-permute-start(bf16[1,256,128]{2,1,0:T(8,128)(2,1)S(1)} %bitcast.34), channel_id=1, source_target_pairs={{0,48},{2,50},{4,52},{6,54},{8,56},{10,58},{12,60},{14,62},{16,32}... | collective-permute-start | bytes 196616 | tf_op jit(solution)/shard_map/ppermute | solution.py:32
  15.8 43.0 %collective-permute-start.15 = (bf16[64,128,128]{2,1,0:T(8,128)(2,1)}, bf16[64,128,128]{2,1,0:T(8,128)(2,1)}, u32[]{:S(2)}, u32[]{:S(2)}) collective-permute-start(bf16[64,128,128]{2,1,0:T(8,128)(2,1)} %refs_10_.1), channel_id=1, source_target_pairs={{0,2},{2,0},{4,6},{6,4},{8,10},{10,8},{12,14},{14,12},{16,18},{18,... | collective-permute-start | bytes 6291464 | tf_op jit(solution)/shard_map/ppermute | solution.py:32
  23.9 6.8 %collective-permute-start.6 = (bf16[4,256,128]{2,1,0:T(8,128)(2,1)S(1)}, bf16[4,256,128]{2,1,0:T(8,128)(2,1)S(1)}, u32[]{:S(2)}, u32[]{:S(2)}) collective-permute-start(bf16[4,256,128]{2,1,0:T(8,128)(2,1)S(1)} %pad_maximum_fusion), channel_id=1, source_target_pairs={{0,64},{2,6},{4,68},{6,10},{8,72},{10,14},{12,76},{14,18},{16,80},... | collective-permute-start | bytes 786440 | tf_op jit(solution)/shard_map/ppermute | solution.py:32
  24.0 8.5 %collective-permute-start.5 = (bf16[4,256,128]{2,1,0:T(8,128)(2,1)S(1)}, bf16[4,256,128]{2,1,0:T(8,128)(2,1)S(1)}, u32[]{:S(2)}, u32[]{:S(2)}) collective-permute-start(bf16[4,256,128]{2,1,0:T(8,128)(2,1)S(1)} %pad_maximum_fusion), channel_id=1, source_target_pairs={{0,192},{2,30},{4,196},{6,2},{8,200},{10,6},{12,204},{14,10},{16,2... | collective-permute-start | bytes 786440 | tf_op jit(solution)/shard_map/ppermute | solution.py:32
  30.7 2.6 %collective-permute-start = (s32[3,65]{1,0:T(4,128)S(1)}, s32[3,65]{1,0:T(4,128)S(1)}, u32[]{:S(2)}, u32[]{:S(2)}) collective-permute-start(s32[3,65]{1,0:T(4,128)S(1)} %pad_add_fusion.1), channel_id=1, source_target_pairs={{0,2},{2,0},{4,6},{6,4},{8,10},{10,8},{12,14},{14,12},{16,18},{18,... | collective-permute-start | bytes 2348 | tf_op jit(solution)/shard_map/ppermute | solution.py:32
  32.5 5.4 %collective-permute-start.7 = (bf16[2,256,128]{2,1,0:T(8,128)(2,1)S(1)}, bf16[2,256,128]{2,1,0:T(8,128)(2,1)S(1)}, u32[]{:S(2)}, u32[]{:S(2)}) collective-permute-start(bf16[2,256,128]{2,1,0:T(8,128)(2,1)S(1)} %slice.64), channel_id=1, source_target_pairs={{0,64},{2,6},{4,68},{6,10},{8,72},{10,14},{12,76},{14,18},{16,80},... | collective-permute-start | bytes 393224 | tf_op jit(solution)/shard_map/ppermute | solution.py:32
  33.3 4.6 %collective-permute-start.8 = (bf16[2,256,128]{2,1,0:T(8,128)(2,1)S(1)}, bf16[2,256,128]{2,1,0:T(8,128)(2,1)S(1)}, u32[]{:S(2)}, u32[]{:S(2)}) collective-permute-start(bf16[2,256,128]{2,1,0:T(8,128)(2,1)S(1)} %slice.65), channel_id=1, source_target_pairs={{0,192},{2,30},{4,196},{6,2},{8,200},{10,6},{12,204},{14,10},{16,2... | collective-permute-start | bytes 393224 | tf_op jit(solution)/shard_map/ppermute | solution.py:32
  37.9 9.5 %collective-permute-start.11 = (bf16[8,256,128]{2,1,0:T(8,128)(2,1)S(1)}, bf16[8,256,128]{2,1,0:T(8,128)(2,1)S(1)}, u32[]{:S(2)}, u32[]{:S(2)}) collective-permute-start(bf16[8,256,128]{2,1,0:T(8,128)(2,1)S(1)} %constant_dynamic-update-slice_fusion.refs_0_), channel_id=1, source_target_pairs={{0,4},{2,66},{4,8},{6,70},{8,12},{10,74},{12,16},{14,78},{16,20},{... | collective-permute-start | bytes 1572872 | tf_op jit(solution)/shard_map/ppermute | solution.py:32
  37.9 9.6 %collective-permute-start.9 = (bf16[8,256,128]{2,1,0:T(8,128)(2,1)S(1)}, bf16[8,256,128]{2,1,0:T(8,128)(2,1)S(1)}, u32[]{:S(2)}, u32[]{:S(2)}) collective-permute-start(bf16[8,256,128]{2,1,0:T(8,128)(2,1)S(1)} %constant_dynamic-update-slice_fusion.refs_0_), channel_id=1, source_target_pairs={{0,28},{2,194},{4,0},{6,198},{8,4},{10,202},{12,8},{14,206},{16,12... | collective-permute-start | bytes 1572872 | tf_op jit(solution)/shard_map/ppermute | solution.py:32
  47.4 8.3 %collective-permute-start.10 = (bf16[8,256,128]{2,1,0:T(8,128)(2,1)S(1)}, bf16[8,256,128]{2,1,0:T(8,128)(2,1)S(1)}, u32[]{:S(2)}, u32[]{:S(2)}) collective-permute-start(bf16[8,256,128]{2,1,0:T(8,128)(2,1)S(1)} %constant_dynamic-update-slice_fusion.5.refs_1_), channel_id=1, source_target_pairs={{0,28},{2,194},{4,0},{6,198},{8,4},{10,202},{12,8},{14,206},{16,12... | collective-permute-start | bytes 1572872 | tf_op jit(solution)/shard_map/ppermute | solution.py:32
  47.5 9.5 %collective-permute-start.12 = (bf16[8,256,128]{2,1,0:T(8,128)(2,1)S(1)}, bf16[8,256,128]{2,1,0:T(8,128)(2,1)S(1)}, u32[]{:S(2)}, u32[]{:S(2)}) collective-permute-start(bf16[8,256,128]{2,1,0:T(8,128)(2,1)S(1)} %constant_dynamic-update-slice_fusion.5.refs_1_), channel_id=1, source_target_pairs={{0,4},{2,66},{4,8},{6,70},{8,12},{10,74},{12,16},{14,78},{16,20},{... | collective-permute-start | bytes 1572872 | tf_op jit(solution)/shard_map/ppermute | solution.py:32
  55.8 9.6 %collective-permute-start.16 = (bf16[8,256,128]{2,1,0:T(8,128)(2,1)S(1)}, bf16[8,256,128]{2,1,0:T(8,128)(2,1)}, u32[]{:S(2)}, u32[]{:S(2)}) collective-permute-start(bf16[8,256,128]{2,1,0:T(8,128)(2,1)S(1)} %collective-permute-done.11.refs_4_), channel_id=1, source_target_pairs={{0,4},{2,66},{4,8},{6,70},{8,12},{10,74},{12,16},{14,78},{16,20},{... | collective-permute-start | bytes 1572872 | tf_op jit(solution)/shard_map/ppermute | solution.py:32
  57.0 8.4 %collective-permute-start.17 = (bf16[8,256,128]{2,1,0:T(8,128)(2,1)S(1)}, bf16[8,256,128]{2,1,0:T(8,128)(2,1)}, u32[]{:S(2)}, u32[]{:S(2)}) collective-permute-start(bf16[8,256,128]{2,1,0:T(8,128)(2,1)S(1)} %collective-permute-done.10.refs_3_), channel_id=1, source_target_pairs={{0,28},{2,194},{4,0},{6,198},{8,4},{10,202},{12,8},{14,206},{16,12... | collective-permute-start | bytes 1572872 | tf_op jit(solution)/shard_map/ppermute | solution.py:32
  67.2 5.5 %collective-permute-start.18 = (f32[256,512]{1,0:T(8,128)S(1)}, f32[256,512]{1,0:T(8,128)S(1)}, u32[]{:S(2)}, u32[]{:S(2)}) collective-permute-start(f32[256,512]{1,0:T(8,128)S(1)} %shard_map.124.mine_ref), channel_id=1, source_target_pairs={{0,2},{2,0},{4,6},{6,4},{8,10},{10,8},{12,14},{14,12},{16,18},{18,... | collective-permute-start | bytes 1572872 | tf_op jit(solution)/shard_map/ppermute | solution.py:32
  75.7 9.4 %collective-permute-start.22 = (bf16[8,256,128]{2,1,0:T(8,128)(2,1)S(1)}, bf16[8,256,128]{2,1,0:T(8,128)(2,1)S(1)}, u32[]{:S(2)}, u32[]{:S(2)}) collective-permute-start(bf16[8,256,128]{2,1,0:T(8,128)(2,1)S(1)} %get-tuple-element.20), channel_id=1, source_target_pairs={{0,4},{2,66},{4,8},{6,70},{8,12},{10,74},{12,16},{14,78},{16,20},{... | collective-permute-start | bytes 1572872 | tf_op jit(solution)/shard_map/ppermute | solution.py:32
  76.0 9.7 %collective-permute-start.20 = (bf16[8,256,128]{2,1,0:T(8,128)(2,1)S(1)}, bf16[8,256,128]{2,1,0:T(8,128)(2,1)S(1)}, u32[]{:S(2)}, u32[]{:S(2)}) collective-permute-start(bf16[8,256,128]{2,1,0:T(8,128)(2,1)S(1)} %get-tuple-element.17), channel_id=1, source_target_pairs={{0,28},{2,194},{4,0},{6,198},{8,4},{10,202},{12,8},{14,206},{16,12... | collective-permute-start | bytes 1572872 | tf_op jit(solution)/shard_map/ppermute | solution.py:32
  78.5 11.7 %collective-permute-start.24 = (bf16[8,256,128]{2,1,0:T(8,128)(2,1)S(1)}, bf16[8,256,128]{2,1,0:T(8,128)(2,1)S(1)}, u32[]{:S(2)}, u32[]{:S(2)}) collective-permute-start(bf16[8,256,128]{2,1,0:T(8,128)(2,1)S(1)} %get-tuple-element.21), channel_id=1, source_target_pairs={{0,28},{2,194},{4,0},{6,198},{8,4},{10,202},{12,8},{14,206},{16,12... | collective-permute-start | bytes 1572872 | tf_op jit(solution)/shard_map/ppermute | solution.py:32
  85.3 9.6 %collective-permute-start.23 = (bf16[8,256,128]{2,1,0:T(8,128)(2,1)S(1)}, bf16[8,256,128]{2,1,0:T(8,128)(2,1)S(1)}, u32[]{:S(2)}, u32[]{:S(2)}) collective-permute-start(bf16[8,256,128]{2,1,0:T(8,128)(2,1)S(1)} %add_convert_fusion), channel_id=1, source_target_pairs={{0,4},{2,66},{4,8},{6,70},{8,12},{10,74},{12,16},{14,78},{16,20},{... | collective-permute-start | bytes 1572872 | tf_op jit(solution)/shard_map/ppermute | solution.py:32
  85.3 15.1 %collective-permute-start.19 = (bf16[8,256,128]{2,1,0:T(8,128)(2,1)S(1)}, bf16[8,256,128]{2,1,0:T(8,128)(2,1)S(1)}, u32[]{:S(2)}, u32[]{:S(2)}) collective-permute-start(bf16[8,256,128]{2,1,0:T(8,128)(2,1)S(1)} %get-tuple-element.15), channel_id=1, source_target_pairs={{0,4},{2,66},{4,8},{6,70},{8,12},{10,74},{12,16},{14,78},{16,20},{... | collective-permute-start | bytes 1572872 | tf_op jit(solution)/shard_map/ppermute | solution.py:32
  85.9 14.6 %collective-permute-start.21 = (bf16[8,256,128]{2,1,0:T(8,128)(2,1)S(1)}, bf16[8,256,128]{2,1,0:T(8,128)(2,1)S(1)}, u32[]{:S(2)}, u32[]{:S(2)}) collective-permute-start(bf16[8,256,128]{2,1,0:T(8,128)(2,1)S(1)} %add_convert_fusion.1), channel_id=1, source_target_pairs={{0,28},{2,194},{4,0},{6,198},{8,4},{10,202},{12,8},{14,206},{16,12... | collective-permute-start | bytes 1572872 | tf_op jit(solution)/shard_map/ppermute | solution.py:32
  95.1 9.9 %collective-permute-start.25 = (bf16[2,256,128]{2,1,0:T(8,128)(2,1)S(1)}, bf16[2,256,128]{2,1,0:T(8,128)(2,1)S(1)}, u32[]{:S(2)}, u32[]{:S(2)}) collective-permute-start(bf16[2,256,128]{2,1,0:T(8,128)(2,1)S(1)} %get-tuple-element.26), channel_id=1, source_target_pairs={{0,64},{2,6},{4,68},{6,10},{8,72},{10,14},{12,76},{14,18},{16,80},... | collective-permute-start | bytes 393224 | tf_op jit(solution)/shard_map/ppermute | solution.py:32
  100.7 6.3 %collective-permute-start.27 = (bf16[2,256,128]{2,1,0:T(8,128)(2,1)S(1)}, bf16[2,256,128]{2,1,0:T(8,128)(2,1)S(1)}, u32[]{:S(2)}, u32[]{:S(2)}) collective-permute-start(bf16[2,256,128]{2,1,0:T(8,128)(2,1)S(1)} %get-tuple-element.28), channel_id=1, source_target_pairs={{0,192},{2,30},{4,196},{6,2},{8,200},{10,6},{12,204},{14,10},{16,2... | collective-permute-start | bytes 393224 | tf_op jit(solution)/shard_map/ppermute | solution.py:32
  105.1 6.8 %collective-permute-start.26 = (bf16[4,256,128]{2,1,0:T(8,128)(2,1)S(1)}, bf16[4,256,128]{2,1,0:T(8,128)(2,1)S(1)}, u32[]{:S(2)}, u32[]{:S(2)}) collective-permute-start(bf16[4,256,128]{2,1,0:T(8,128)(2,1)S(1)} %pad_maximum_fusion.1), channel_id=1, source_target_pairs={{0,64},{2,6},{4,68},{6,10},{8,72},{10,14},{12,76},{14,18},{16,80},... | collective-permute-start | bytes 786440 | tf_op jit(solution)/shard_map/ppermute | solution.py:32
  107.0 6.8 %collective-permute-start.28 = (bf16[4,256,128]{2,1,0:T(8,128)(2,1)S(1)}, bf16[4,256,128]{2,1,0:T(8,128)(2,1)S(1)}, u32[]{:S(2)}, u32[]{:S(2)}) collective-permute-start(bf16[4,256,128]{2,1,0:T(8,128)(2,1)S(1)} %pad_maximum_fusion.2), channel_id=1, source_target_pairs={{0,192},{2,30},{4,196},{6,2},{8,200},{10,6},{12,204},{14,10},{16,2... | collective-permute-start | bytes 786440 | tf_op jit(solution)/shard_map/ppermute | solution.py:32
  113.9 7.1 %collective-permute-start.29 = (bf16[256,128]{1,0:T(8,128)(2,1)S(1)}, bf16[256,128]{1,0:T(8,128)(2,1)S(1)}, u32[]{:S(2)}, u32[]{:S(2)}) collective-permute-start(bf16[256,128]{1,0:T(8,128)(2,1)S(1)} %get-tuple-element.29), channel_id=1, source_target_pairs={{0,16},{2,18},{4,20},{6,22},{8,24},{10,26},{12,28},{14,30},{16,0},... | collective-permute-start | bytes 196616 | tf_op jit(solution)/shard_map/ppermute | solution.py:32
  115.6 5.4 %collective-permute-start.30 = (bf16[256,128]{1,0:T(8,128)(2,1)S(1)}, bf16[256,128]{1,0:T(8,128)(2,1)S(1)}, u32[]{:S(2)}, u32[]{:S(2)}) collective-permute-start(bf16[256,128]{1,0:T(8,128)(2,1)S(1)} %get-tuple-element.31), channel_id=1, source_target_pairs={{0,32},{2,34},{4,36},{6,38},{8,40},{10,42},{12,44},{14,46},{16,48}... | collective-permute-start | bytes 196616 | tf_op jit(solution)/shard_map/ppermute | solution.py:32
  115.9 9.8 %collective-permute-start.31 = (bf16[256,128]{1,0:T(8,128)(2,1)S(1)}, bf16[256,128]{1,0:T(8,128)(2,1)S(1)}, u32[]{:S(2)}, u32[]{:S(2)}) collective-permute-start(bf16[256,128]{1,0:T(8,128)(2,1)S(1)} %get-tuple-element.30), channel_id=1, source_target_pairs={{0,48},{2,50},{4,52},{6,54},{8,56},{10,58},{12,60},{14,62},{16,32}... | collective-permute-start | bytes 196616 | tf_op jit(solution)/shard_map/ppermute | solution.py:32
  125.9 4.2 %collective-permute-start.32 = (bf16[64,256]{1,0:T(8,128)(2,1)S(1)}, bf16[64,256]{1,0:T(8,128)(2,1)S(1)}, u32[]{:S(2)}, u32[]{:S(2)}) collective-permute-start(bf16[64,256]{1,0:T(8,128)(2,1)S(1)} %broadcast_select_fusion.1), channel_id=1, source_target_pairs={{0,2},{2,0},{4,6},{6,4},{8,10},{10,8},{12,14},{14,12},{16,18},{18,... | collective-permute-start | bytes 98312 | tf_op jit(solution)/shard_map/ppermute | solution.py:32

commit v5 on v4

--- a/solution.py
+++ b/solution.py
@@ -63,17 +63,14 @@
 
 
 def small_gather(value, axes):
+    up, down = turn(value, axes, 1), turn(value, axes, -1)
+    return jnp.concatenate([value, down, up, turn(up, axes, 1)])
+
+
+def large_gather(value, axes):
     half = value.shape[0] // 2
-    down, up = turn(value, axes, -1), turn(value, axes, 1)
-    far_up, far_down = turn(up[:half], axes, 1), turn(down[half:], axes, -1)
-    return jnp.concatenate([value, down]), jnp.concatenate([up, far_up, far_down])
-
-
-def large_gather(first, second, axes):
-    first_up, first_down = turn(first, axes, 1), turn(first, axes, -1)
-    second_down, second_up = turn(second, axes, -1), turn(second, axes, 1)
-    first_far, second_far = turn(first_up, axes, 1), turn(second_down, axes, -1)
-    return first, second, first_down, second_down, first_up, second_up, first_far, second_far
+    up, down = turn(value, axes, 1), turn(value, axes, -1)
+    return value, down, up, turn(up[:half], axes, 1), turn(down[half:], axes, -1)
 
 
 SENT = (False, False, True, False, False, True, True, True)
@@ -93,12 +90,9 @@
 def small_reduce(first, second, axes):
     here, ahead = jnp.split(first, 2)
     behind, far = jnp.split(second, 2)
-    half = here.shape[0] // 2
-    far = far.astype(BF16)
-    down, up = turn(far[:half], axes, -1), turn(far[half:], axes, 1)
-    behind = jnp.concatenate([behind[:half] + down.astype(F32), behind[half:]])
-    ahead = jnp.concatenate([ahead[:half], ahead[half:] + up.astype(F32)])
-    ahead, behind = turn(ahead.astype(BF16), axes, 1), turn(behind.astype(BF16), axes, -1)
+    far = turn(far.astype(BF16), axes, -1)
+    ahead = turn(ahead.astype(BF16), axes, 1)
+    behind = turn((behind + far.astype(F32)).astype(BF16), axes, -1)
     return here + ahead.astype(F32) + behind.astype(F32)
 
 
@@ -140,10 +134,12 @@
                 copies[n].wait()
 
     def groups():
-        for rank, ref in enumerate(piece_refs):
-            for i in range(0, PART, GROUP):
-                spots = [(base + rank) * PART + i + j for j in range(GROUP)]
+        at = base
+        for ref in piece_refs:
+            for i in range(0, ref.shape[0], GROUP):
+                spots = [at + i + j for j in range(GROUP)]
                 yield spots, jnp.concatenate([ref[i + j] for j in range(GROUP)], axis=1)
+            at += ref.shape[0]
 
     @pl.when(core == 0)
     def _():
@@ -291,7 +287,7 @@
     other = shift(other, "c", 1)
     block = jnp.concatenate([jnp.where(first, own, other), jnp.where(first, other, own)])
     block = transpose(block).reshape(1, batch, BLOCK)
-    pieces = large_gather(*small_gather(near(block), "yz"), "zy")
+    pieces = large_gather(small_gather(near(block), "yz"), "zy")
 
     lists = jnp.concatenate([gate_index, up_index, down_index])
     counts = jnp.stack([gate_count, up_count, down_count])
@@ -305,7 +301,7 @@
         return jnp.where(k >= 2, 5 - k, k)
 
     y_rank, z_rank = ranked(y), ranked(low)
-    from_ahead = jnp.where(first, y_rank >= 2, x == 1)
+    from_ahead = first & (y_rank >= 2)
     flipped = (low == 3) | ((low == 2) & jnp.logical_not(from_ahead))
     high = jnp.where(flipped, 1 - high, high)
     position = jnp.where(first, z_rank * RING + y_rank, y_rank * RING + z_rank) * 4 + x * 2 + high
@@ -321,9 +317,9 @@
     sums = jax.ShapeDtypeStruct((batch, 4 * BLOCK), F32)
     held = jax.ShapeDtypeStruct((6, SLOTS, BLOCK, BLOCK), BF16)
     mine, held = call(
-        functools.partial(inner_kernel, 0), (sums, held), 3 * flops, maps, *pieces[:6], weights=weights
+        functools.partial(inner_kernel, 0), (sums, held), 3 * flops, maps, *pieces[:3], weights=weights
     )
-    mine = call(functools.partial(inner_kernel, 6), sums, flops, maps, mine, *pieces[6:], held)
+    mine = call(functools.partial(inner_kernel, 6 * PART), sums, flops, maps, mine, *pieces[3:], held)
     theirs = shift(mine, "c", 1)
     parts = tuple(jax.ShapeDtypeStruct((PART, batch, BLOCK), BF16 if sent else F32) for sent in SENT)
     parts = call(outer_kernel, parts, 4 * flops, maps, mine, theirs, held)

time: 131 us -> 124 us (0.947)
  waiting for transfers between devices: 60 us -> 54.8 us
  starting transfers between devices: 52.8 us -> 49.8 us
  local copies, waits for them, and re-layouts: 0.6 us -> 2.32 us
    ppermute x33 -> x29, waiting for transfers between devices: 60 us -> 54.8 us  [permute(): return lax.ppermute(value, 'tp', pairs)]
    ppermute x33 -> x29, starting transfers between devices: 52.8 us -> 49.8 us  [permute(): return lax.ppermute(value, 'tp', pairs)]
    slice x4 -> x2, local copies, waits for them, and re-layouts: 0.07 us -> 1.7 us  [the longest x1 0.88 us: large_gather(): down[half:]]
  transfers between devices with their start and end apart: 33 -> 29, of which waited for: 20 -> 17; matrix products, arithmetic and copies ran while one was open for 3% -> 4% of each run, Pallas kernels for 4% -> 4%
where the time goes in v5:
time: 124 us
  waiting for transfers between devices  54.8 us (44%)
  starting transfers between devices  49.8 us (40%)
  Pallas kernels  10.2 us (8%)
  other arithmetic  4.23 us (3%)
  between operations  2.87 us (2%)
  local copies, waits for them, and re-layouts  2.32 us (2%)
    ppermute x29, waiting for transfers between devices, permute(): return lax.ppermute(value, 'tp', pairs)  54.8 us
    ppermute x29, starting transfers between devices, permute(): return lax.ppermute(value, 'tp', pairs)  49.8 us
    pallas_call x3, Pallas kernels, call(): pl.pallas_call(kernel, out_shape=outs, in_specs=[pl.BlockSpec(memory_spac...  10 us
  transfers between devices with their start and end apart: 29, of which 17 were waited for; matrix products, arithmetic and copies ran while one was open for 4% of the time, Pallas kernels for 4%

profile of v5, /device:TPU:1, one launch (start us, length us, event | category | flops | bytes accessed | tf_op | source)
XLA Modules:
  0.0 124.2 jit_solution(3514229037632827352)
XLA Ops:
  0.7 0.8 select_bitcast_fusion.2
  1.4 3.2 %collective-permute-start.1 = (bf16[64,256]{1,0:T(8,128)(2,1)S(1)}, bf16[64,256]{1,0:T(8,128)(2,1)S(1)}, u32[]{:S(2)}, u32[]{:S(2)}) collective-permute-start(bf16[64,256]{1,0:T(8,128)(2,1)S(1)} %select_bitcast_fusion.2), channel_id=1, source_target_pairs={{0,2},{2,0},{4,6},{6,4},{8,10},{10,8},{12,14},{14,12},{16,18},{18,... | collective-permute-start | bytes 98312 | tf_op jit(solution)/shard_map/ppermute | solution.py:32
  4.7 0.1 collective-permute-start.10
  4.8 0.4 collective-permute-start.11
  7.1 0.1 pad_add_fusion.3
  7.2 0.1 copy.14
  7.3 0.8 bitcast_select_fusion.1
  8.1 0.1 shard_map.122
  8.2 5.3 %collective-permute-start.2 = (bf16[1,256,128]{2,1,0:T(8,128)(2,1)S(1)}, bf16[1,256,128]{2,1,0:T(8,128)(2,1)S(1)}, u32[]{:S(2)}, u32[]{:S(2)}) collective-permute-start(bf16[1,256,128]{2,1,0:T(8,128)(2,1)S(1)} %bitcast.32), channel_id=1, source_target_pairs={{0,16},{2,18},{4,20},{6,22},{8,24},{10,26},{12,28},{14,30},{16,0},... | collective-permute-start | bytes 196616 | tf_op jit(solution)/shard_map/ppermute | solution.py:32
  13.5 1.2 collective-permute-start.3
  14.7 0.2 collective-permute-start.4
  14.8 0.8 pad_add_fusion.1
  15.6 0.2 collective-permute-done.2
  15.8 1.0 collective-permute-start.12
  16.8 7.0 %collective-permute-done.4 = bf16[1,256,128]{2,1,0:T(8,128)(2,1)S(1)} collective-permute-done((bf16[1,256,128]{2,1,0:T(8,128)(2,1)S(1)}, bf16[1,256,128]{2,1,0:T(8,128)(2,1)S(1)}, u32[]{:S(2)}, u32[]{:S(2)}) %collective-permute-start.4) | collective-permute-done | bytes 65568 | tf_op jit(solution)/shard_map/ppermute | solution.py:32
  23.9 0.1 collective-permute-start.6
  24.0 2.7 %collective-permute-start.5 = (bf16[4,256,128]{2,1,0:T(8,128)(2,1)S(1)}, bf16[4,256,128]{2,1,0:T(8,128)(2,1)S(1)}, u32[]{:S(2)}, u32[]{:S(2)}) collective-permute-start(bf16[4,256,128]{2,1,0:T(8,128)(2,1)S(1)} %pad_maximum_fusion), channel_id=1, source_target_pairs={{0,192},{2,30},{4,196},{6,2},{8,200},{10,6},{12,204},{14,10},{16,2... | collective-permute-start | bytes 786440 | tf_op jit(solution)/shard_map/ppermute | solution.py:32
  26.7 4.0 %collective-permute-done.6 = bf16[4,256,128]{2,1,0:T(8,128)(2,1)S(1)} collective-permute-done((bf16[4,256,128]{2,1,0:T(8,128)(2,1)S(1)}, bf16[4,256,128]{2,1,0:T(8,128)(2,1)S(1)}, u32[]{:S(2)}, u32[]{:S(2)}) %collective-permute-start.6) | collective-permute-done | bytes 262176 | tf_op jit(solution)/shard_map/ppermute | solution.py:32
  30.7 2.2 %collective-permute-start = (s32[3,65]{1,0:T(4,128)S(1)}, s32[3,65]{1,0:T(4,128)S(1)}, u32[]{:S(2)}, u32[]{:S(2)}) collective-permute-start(s32[3,65]{1,0:T(4,128)S(1)} %pad_add_fusion.1), channel_id=1, source_target_pairs={{0,2},{2,0},{4,6},{6,4},{8,10},{10,8},{12,14},{14,12},{16,18},{18,... | collective-permute-start | bytes 2348 | tf_op jit(solution)/shard_map/ppermute | solution.py:32
  33.0 4.4 %collective-permute-done.7 = bf16[4,256,128]{2,1,0:T(8,128)(2,1)S(1)} collective-permute-done((bf16[4,256,128]{2,1,0:T(8,128)(2,1)S(1)}, bf16[4,256,128]{2,1,0:T(8,128)(2,1)S(1)}, u32[]{:S(2)}, u32[]{:S(2)}) %collective-permute-start.7) | collective-permute-done | bytes 262176 | tf_op jit(solution)/shard_map/ppermute | solution.py:32
  37.5 0.8 collective-permute-start.9
  38.2 2.0 %collective-permute-start.8 = (bf16[16,256,128]{2,1,0:T(8,128)(2,1)S(1)}, bf16[16,256,128]{2,1,0:T(8,128)(2,1)S(1)}, u32[]{:S(2)}, u32[]{:S(2)}) collective-permute-start(bf16[16,256,128]{2,1,0:T(8,128)(2,1)S(1)} %constant_dynamic-update-slice_fusion.refs_0_), channel_id=1, source_target_pairs={{0,28},{2,194},{4,0},{6,198},{8,4},{10,202},{12,8},{14,206},{16,12... | collective-permute-start | bytes 3145736 | tf_op jit(solution)/shard_map/ppermute | solution.py:32
  40.2 0.1 pad_add_fusion
  40.3 0.2 slice_reduce_fusion
  40.5 12.2 %collective-permute-done.9.refs_2_ = bf16[16,256,128]{2,1,0:T(8,128)(2,1)S(1)} collective-permute-done((bf16[16,256,128]{2,1,0:T(8,128)(2,1)S(1)}, bf16[16,256,128]{2,1,0:T(8,128)(2,1)S(1)}, u32[]{:S(2)}, u32[]{:S(2)}) %collective-permute-start.9) | collective-permute-done | bytes 1048608 | tf_op jit(solution)/shard_map/ppermute | solution.py:32
  52.7 0.8 slice.32
  53.5 0.9 slice.33
  54.4 2.7 %collective-permute-start.14 = (bf16[8,256,128]{2,1,0:T(8,128)(2,1)}, bf16[8,256,128]{2,1,0:T(8,128)(2,1)}, u32[]{:S(2)}, u32[]{:S(2)}) collective-permute-start(bf16[8,256,128]{2,1,0:T(8,128)(2,1)} %slice.33), channel_id=1, source_target_pairs={{0,28},{2,194},{4,0},{6,198},{8,4},{10,202},{12,8},{14,206},{16,12... | collective-permute-start | bytes 1572872 | tf_op jit(solution)/shard_map/ppermute | solution.py:32
  57.1 0.3 select_reduce_fusion
  57.3 0.1 sub.34
  57.5 5.3 %shard_map.123 = (f32[256,512]{1,0:T(8,128)S(1)}, bf16[6,64,128,128]{3,2,1,0:T(8,128)(2,1)S(1)}) custom-call(s32[385]{0:T(512)S(1)} %pad_add_fusion.2.maps_ref, bf16[16,256,128]{2,1,0:T(8,128)(2,1)S(1)} %constant_dynamic-update-slice_fusion.refs_0_, bf16[16,256,128]{2,1,0:T(8,128)(2,1)S(1)} %collective-permute-done.8.refs_1_, ...), custom_call_target="tpu_custom_call" | custom-call | flops 1610612736 | bytes 16777216 | tf_op jit(solution)/shard_map/pallas_call | solution.py:254
  62.7 0.6 collective-permute-done.13.refs_1_
  63.4 0.2 collective-permute-done.14.refs_2_
  63.5 1.7 %shard_map.124.mine_ref = f32[256,512]{1,0:T(8,128)S(1)} custom-call(s32[385]{0:T(512)S(1)} %pad_add_fusion.2.maps_ref, f32[256,512]{1,0:T(8,128)S(1)} %get-tuple-element.12.refs_0_, bf16[8,256,128]{2,1,0:T(8,128)(2,1)} %collective-permute-done.13.refs_1_, bf16[8,256,128]{2,1,0:T(8,128)(2,1)} %collective-permute-done.14.refs_2_, ...), custom_call_target="tpu_custom_call" | custom-call | flops 536870912 | bytes 16777216 | tf_op jit(solution)/shard_map/pallas_call | solution.py:254
  65.3 6.6 %collective-permute-start.15 = (f32[256,512]{1,0:T(8,128)S(1)}, f32[256,512]{1,0:T(8,128)S(1)}, u32[]{:S(2)}, u32[]{:S(2)}) collective-permute-start(f32[256,512]{1,0:T(8,128)S(1)} %shard_map.124.mine_ref), channel_id=1, source_target_pairs={{0,2},{2,0},{4,6},{6,4},{8,10},{10,8},{12,14},{14,12},{16,18},{18,... | collective-permute-start | bytes 1572872 | tf_op jit(solution)/shard_map/ppermute | solution.py:32
  71.8 1.5 %collective-permute-done.15.theirs_ref = f32[256,512]{1,0:T(8,128)S(1)} collective-permute-done((f32[256,512]{1,0:T(8,128)S(1)}, f32[256,512]{1,0:T(8,128)S(1)}, u32[]{:S(2)}, u32[]{:S(2)}) %collective-permute-start.15) | collective-permute-done | bytes 524320 | tf_op jit(solution)/shard_map/ppermute | solution.py:32
  73.4 3.0 %shard_map.125 = (f32[8,256,128]{2,1,0:T(8,128)S(1)}, f32[8,256,128]{2,1,0:T(8,128)S(1)}, bf16[8,256,128]{2,1,0:T(8,128)(2,1)S(1)}, f32[8,256,128]{2,1,0:T(8,128...) custom-call(s32[385]{0:T(512)S(1)} %pad_add_fusion.2.maps_ref, ...), custom_call_target="tpu_custom_call" | custom-call | flops 2147483648 | bytes 16777216 | tf_op jit(solution)/shard_map/pallas_call | solution.py:254
  76.4 0.1 collective-permute-start.20
  76.5 2.7 %collective-permute-start.17 = (bf16[8,256,128]{2,1,0:T(8,128)(2,1)S(1)}, bf16[8,256,128]{2,1,0:T(8,128)(2,1)S(1)}, u32[]{:S(2)}, u32[]{:S(2)}) collective-permute-start(bf16[8,256,128]{2,1,0:T(8,128)(2,1)S(1)} %get-tuple-element.17), channel_id=1, source_target_pairs={{0,28},{2,194},{4,0},{6,198},{8,4},{10,202},{12,8},{14,206},{16,12... | collective-permute-start | bytes 1572872 | tf_op jit(solution)/shard_map/ppermute | solution.py:32
  79.2 6.6 %collective-permute-done.20 = bf16[8,256,128]{2,1,0:T(8,128)(2,1)S(1)} collective-permute-done((bf16[8,256,128]{2,1,0:T(8,128)(2,1)S(1)}, bf16[8,256,128]{2,1,0:T(8,128)(2,1)S(1)}, u32[]{:S(2)}, u32[]{:S(2)}) %collective-permute-start.20) | collective-permute-done | bytes 524320 | tf_op jit(solution)/shard_map/ppermute | solution.py:32
  85.8 0.1 add_convert_fusion
  85.9 0.1 collective-permute-start.21
  86.0 0.1 collective-permute-start.16
  86.1 0.1 add_convert_fusion.1
  86.3 3.0 %collective-permute-start.18 = (bf16[8,256,128]{2,1,0:T(8,128)(2,1)S(1)}, bf16[8,256,128]{2,1,0:T(8,128)(2,1)S(1)}, u32[]{:S(2)}, u32[]{:S(2)}) collective-permute-start(bf16[8,256,128]{2,1,0:T(8,128)(2,1)S(1)} %add_convert_fusion.1), channel_id=1, source_target_pairs={{0,28},{2,194},{4,0},{6,198},{8,4},{10,202},{12,8},{14,206},{16,12... | collective-permute-start | bytes 1572872 | tf_op jit(solution)/shard_map/ppermute | solution.py:32
  89.2 1.7 %collective-permute-done.22 = bf16[8,256,128]{2,1,0:T(8,128)(2,1)S(1)} collective-permute-done((bf16[8,256,128]{2,1,0:T(8,128)(2,1)S(1)}, bf16[8,256,128]{2,1,0:T(8,128)(2,1)S(1)}, u32[]{:S(2)}, u32[]{:S(2)}) %collective-permute-start.22) | collective-permute-done | bytes 524320 | tf_op jit(solution)/shard_map/ppermute | solution.py:32
  90.9 4.7 %collective-permute-done.21 = bf16[8,256,128]{2,1,0:T(8,128)(2,1)S(1)} collective-permute-done((bf16[8,256,128]{2,1,0:T(8,128)(2,1)S(1)}, bf16[8,256,128]{2,1,0:T(8,128)(2,1)S(1)}, u32[]{:S(2)}, u32[]{:S(2)}) %collective-permute-start.21) | collective-permute-done | bytes 524320 | tf_op jit(solution)/shard_map/ppermute | solution.py:32
  95.5 0.2 convert_add_fusion
  95.8 2.1 %collective-permute-start.23 = (bf16[4,256,128]{2,1,0:T(8,128)(2,1)S(1)}, bf16[4,256,128]{2,1,0:T(8,128)(2,1)S(1)}, u32[]{:S(2)}, u32[]{:S(2)}) collective-permute-start(bf16[4,256,128]{2,1,0:T(8,128)(2,1)S(1)} %split.52), channel_id=1, source_target_pairs={{0,192},{2,30},{4,196},{6,2},{8,200},{10,6},{12,204},{14,10},{16,2... | collective-permute-start | bytes 786440 | tf_op jit(solution)/shard_map/ppermute | solution.py:32
  97.9 3.3 %collective-permute-done.16 = bf16[8,256,128]{2,1,0:T(8,128)(2,1)S(1)} collective-permute-done((bf16[8,256,128]{2,1,0:T(8,128)(2,1)S(1)}, bf16[8,256,128]{2,1,0:T(8,128)(2,1)S(1)}, u32[]{:S(2)}, u32[]{:S(2)}) %collective-permute-start.16) | collective-permute-done | bytes 524320 | tf_op jit(solution)/shard_map/ppermute | solution.py:32
  101.2 0.1 convert_add_fusion.1
  101.4 1.4 %collective-permute-start.19 = (bf16[4,256,128]{2,1,0:T(8,128)(2,1)S(1)}, bf16[4,256,128]{2,1,0:T(8,128)(2,1)S(1)}, u32[]{:S(2)}, u32[]{:S(2)}) collective-permute-start(bf16[4,256,128]{2,1,0:T(8,128)(2,1)S(1)} %split.53), channel_id=1, source_target_pairs={{0,64},{2,6},{4,68},{6,10},{8,72},{10,14},{12,76},{14,18},{16,80},... | collective-permute-start | bytes 786440 | tf_op jit(solution)/shard_map/ppermute | solution.py:32
  102.9 1.6 %collective-permute-start.24 = (bf16[4,256,128]{2,1,0:T(8,128)(2,1)S(1)}, bf16[4,256,128]{2,1,0:T(8,128)(2,1)S(1)}, u32[]{:S(2)}, u32[]{:S(2)}) collective-permute-start(bf16[4,256,128]{2,1,0:T(8,128)(2,1)S(1)} %fusion), channel_id=1, source_target_pairs={{0,192},{2,30},{4,196},{6,2},{8,200},{10,6},{12,204},{14,10},{16,2... | collective-permute-start | bytes 786440 | tf_op jit(solution)/shard_map/ppermute | solution.py:32
  104.4 3.7 %collective-permute-done.19 = bf16[4,256,128]{2,1,0:T(8,128)(2,1)S(1)} collective-permute-done((bf16[4,256,128]{2,1,0:T(8,128)(2,1)S(1)}, bf16[4,256,128]{2,1,0:T(8,128)(2,1)S(1)}, u32[]{:S(2)}, u32[]{:S(2)}) %collective-permute-start.19) | collective-permute-done | bytes 262176 | tf_op jit(solution)/shard_map/ppermute | solution.py:32
  108.2 0.3 collective-permute-done.24
  108.5 0.1 fusion.13
  108.6 1.8 %collective-permute-start.25 = (bf16[256,128]{1,0:T(8,128)(2,1)S(1)}, bf16[256,128]{1,0:T(8,128)(2,1)S(1)}, u32[]{:S(2)}, u32[]{:S(2)}) collective-permute-start(bf16[256,128]{1,0:T(8,128)(2,1)S(1)} %get-tuple-element.24), channel_id=1, source_target_pairs={{0,16},{2,18},{4,20},{6,22},{8,24},{10,26},{12,28},{14,30},{16,0},... | collective-permute-start | bytes 196616 | tf_op jit(solution)/shard_map/ppermute | solution.py:32
  110.4 4.8 %collective-permute-start.27 = (bf16[256,128]{1,0:T(8,128)(2,1)S(1)}, bf16[256,128]{1,0:T(8,128)(2,1)S(1)}, u32[]{:S(2)}, u32[]{:S(2)}) collective-permute-start(bf16[256,128]{1,0:T(8,128)(2,1)S(1)} %get-tuple-element.25), channel_id=1, source_target_pairs={{0,48},{2,50},{4,52},{6,54},{8,56},{10,58},{12,60},{14,62},{16,32}... | collective-permute-start | bytes 196616 | tf_op jit(solution)/shard_map/ppermute | solution.py:32
  115.2 1.7 %collective-permute-done.25 = bf16[256,128]{1,0:T(8,128)(2,1)S(1)} collective-permute-done((bf16[256,128]{1,0:T(8,128)(2,1)S(1)}, bf16[256,128]{1,0:T(8,128)(2,1)S(1)}, u32[]{:S(2)}, u32[]{:S(2)}) %collective-permute-start.25) | collective-permute-done | bytes 65568 | tf_op jit(solution)/shard_map/ppermute | solution.py:32
  116.9 1.8 %collective-permute-done.27 = bf16[256,128]{1,0:T(8,128)(2,1)S(1)} collective-permute-done((bf16[256,128]{1,0:T(8,128)(2,1)S(1)}, bf16[256,128]{1,0:T(8,128)(2,1)S(1)}, u32[]{:S(2)}, u32[]{:S(2)}) %collective-permute-start.27) | collective-permute-done | bytes 65568 | tf_op jit(solution)/shard_map/ppermute | solution.py:32
  118.7 0.1 shard_map.126
  118.9 3.9 %collective-permute-start.28 = (bf16[64,256]{1,0:T(8,128)(2,1)S(1)}, bf16[64,256]{1,0:T(8,128)(2,1)S(1)}, u32[]{:S(2)}, u32[]{:S(2)}) collective-permute-start(bf16[64,256]{1,0:T(8,128)(2,1)S(1)} %broadcast_select_fusion.1), channel_id=1, source_target_pairs={{0,2},{2,0},{4,6},{6,4},{8,10},{10,8},{12,14},{14,12},{16,18},{18,... | collective-permute-start | bytes 98312 | tf_op jit(solution)/shard_map/ppermute | solution.py:32
  122.7 0.9 collective-permute-done.28
  123.6 0.6 select_bitcast_fusion
  (42 shorter events, 0.5 us)
Async XLA Ops:
  0.6 39.6 %copy-start.2 = (s32[1,64]{1,0:T(1,128)S(1)}, s32[1,64]{1,0:T(1,128)}, u32[]{:S(2)}) copy-start(s32[1,64]{1,0:T(1,128)} %param.14) | copy-start | bytes 772
  0.6 39.6 %copy-start.1 = (s32[1,64]{1,0:T(1,128)S(1)}, s32[1,64]{1,0:T(1,128)}, u32[]{:S(2)}) copy-start(s32[1,64]{1,0:T(1,128)} %param.17) | copy-start | bytes 772
  0.7 39.6 %copy-start = (s32[1,64]{1,0:T(1,128)S(1)}, s32[1,64]{1,0:T(1,128)}, u32[]{:S(2)}) copy-start(s32[1,64]{1,0:T(1,128)} %param.20) | copy-start | bytes 772
  1.4 5.9 %collective-permute-start.1 = (bf16[64,256]{1,0:T(8,128)(2,1)S(1)}, bf16[64,256]{1,0:T(8,128)(2,1)S(1)}, u32[]{:S(2)}, u32[]{:S(2)}) collective-permute-start(bf16[64,256]{1,0:T(8,128)(2,1)S(1)} %select_bitcast_fusion.2), channel_id=1, source_target_pairs={{0,2},{2,0},{4,6},{6,4},{8,10},{10,8},{12,14},{14,12},{16,18},{18,... | collective-permute-start | bytes 98312 | tf_op jit(solution)/shard_map/ppermute | solution.py:32
  4.7 52.7 %collective-permute-start.10 = (bf16[64,128,128]{2,1,0:T(8,128)(2,1)}, bf16[64,128,128]{2,1,0:T(8,128)(2,1)}, u32[]{:S(2)}, u32[]{:S(2)}) collective-permute-start(bf16[64,128,128]{2,1,0:T(8,128)(2,1)} %refs_3_.1), channel_id=1, source_target_pairs={{0,2},{2,0},{4,6},{6,4},{8,10},{10,8},{12,14},{14,12},{16,18},{18,... | collective-permute-start | bytes 6291464 | tf_op jit(solution)/shard_map/ppermute | solution.py:32
  4.8 52.6 %collective-permute-start.11 = (bf16[64,128,128]{2,1,0:T(8,128)(2,1)}, bf16[64,128,128]{2,1,0:T(8,128)(2,1)}, u32[]{:S(2)}, u32[]{:S(2)}) collective-permute-start(bf16[64,128,128]{2,1,0:T(8,128)(2,1)} %refs_4_.1), channel_id=1, source_target_pairs={{0,2},{2,0},{4,6},{6,4},{8,10},{10,8},{12,14},{14,12},{16,18},{18,... | collective-permute-start | bytes 6291464 | tf_op jit(solution)/shard_map/ppermute | solution.py:32
  8.2 7.7 %collective-permute-start.2 = (bf16[1,256,128]{2,1,0:T(8,128)(2,1)S(1)}, bf16[1,256,128]{2,1,0:T(8,128)(2,1)S(1)}, u32[]{:S(2)}, u32[]{:S(2)}) collective-permute-start(bf16[1,256,128]{2,1,0:T(8,128)(2,1)S(1)} %bitcast.32), channel_id=1, source_target_pairs={{0,16},{2,18},{4,20},{6,22},{8,24},{10,26},{12,28},{14,30},{16,0},... | collective-permute-start | bytes 196616 | tf_op jit(solution)/shard_map/ppermute | solution.py:32
  13.5 3.3 %collective-permute-start.3 = (bf16[1,256,128]{2,1,0:T(8,128)(2,1)S(1)}, bf16[1,256,128]{2,1,0:T(8,128)(2,1)S(1)}, u32[]{:S(2)}, u32[]{:S(2)}) collective-permute-start(bf16[1,256,128]{2,1,0:T(8,128)(2,1)S(1)} %bitcast.33), channel_id=1, source_target_pairs={{0,32},{2,34},{4,36},{6,38},{8,40},{10,42},{12,44},{14,46},{16,48}... | collective-permute-start | bytes 196616 | tf_op jit(solution)/shard_map/ppermute | solution.py:32
  14.7 9.2 %collective-permute-start.4 = (bf16[1,256,128]{2,1,0:T(8,128)(2,1)S(1)}, bf16[1,256,128]{2,1,0:T(8,128)(2,1)S(1)}, u32[]{:S(2)}, u32[]{:S(2)}) collective-permute-start(bf16[1,256,128]{2,1,0:T(8,128)(2,1)S(1)} %bitcast.34), channel_id=1, source_target_pairs={{0,48},{2,50},{4,52},{6,54},{8,56},{10,58},{12,60},{14,62},{16,32}... | collective-permute-start | bytes 196616 | tf_op jit(solution)/shard_map/ppermute | solution.py:32
  15.8 41.6 %collective-permute-start.12 = (bf16[64,128,128]{2,1,0:T(8,128)(2,1)}, bf16[64,128,128]{2,1,0:T(8,128)(2,1)}, u32[]{:S(2)}, u32[]{:S(2)}) collective-permute-start(bf16[64,128,128]{2,1,0:T(8,128)(2,1)} %refs_7_.1), channel_id=1, source_target_pairs={{0,2},{2,0},{4,6},{6,4},{8,10},{10,8},{12,14},{14,12},{16,18},{18,... | collective-permute-start | bytes 6291464 | tf_op jit(solution)/shard_map/ppermute | solution.py:32
  23.9 6.8 %collective-permute-start.6 = (bf16[4,256,128]{2,1,0:T(8,128)(2,1)S(1)}, bf16[4,256,128]{2,1,0:T(8,128)(2,1)S(1)}, u32[]{:S(2)}, u32[]{:S(2)}) collective-permute-start(bf16[4,256,128]{2,1,0:T(8,128)(2,1)S(1)} %pad_maximum_fusion), channel_id=1, source_target_pairs={{0,64},{2,6},{4,68},{6,10},{8,72},{10,14},{12,76},{14,18},{16,80},... | collective-permute-start | bytes 786440 | tf_op jit(solution)/shard_map/ppermute | solution.py:32
  24.0 6.7 %collective-permute-start.5 = (bf16[4,256,128]{2,1,0:T(8,128)(2,1)S(1)}, bf16[4,256,128]{2,1,0:T(8,128)(2,1)S(1)}, u32[]{:S(2)}, u32[]{:S(2)}) collective-permute-start(bf16[4,256,128]{2,1,0:T(8,128)(2,1)S(1)} %pad_maximum_fusion), channel_id=1, source_target_pairs={{0,192},{2,30},{4,196},{6,2},{8,200},{10,6},{12,204},{14,10},{16,2... | collective-permute-start | bytes 786440 | tf_op jit(solution)/shard_map/ppermute | solution.py:32
  30.7 6.7 %collective-permute-start.7 = (bf16[4,256,128]{2,1,0:T(8,128)(2,1)S(1)}, bf16[4,256,128]{2,1,0:T(8,128)(2,1)S(1)}, u32[]{:S(2)}, u32[]{:S(2)}) collective-permute-start(bf16[4,256,128]{2,1,0:T(8,128)(2,1)S(1)} %collective-permute-done.6), channel_id=1, source_target_pairs={{0,64},{2,6},{4,68},{6,10},{8,72},{10,14},{12,76},{14,18},{16,80},... | collective-permute-start | bytes 786440 | tf_op jit(solution)/shard_map/ppermute | solution.py:32
  30.7 7.5 %collective-permute-start = (s32[3,65]{1,0:T(4,128)S(1)}, s32[3,65]{1,0:T(4,128)S(1)}, u32[]{:S(2)}, u32[]{:S(2)}) collective-permute-start(s32[3,65]{1,0:T(4,128)S(1)} %pad_add_fusion.1), channel_id=1, source_target_pairs={{0,2},{2,0},{4,6},{6,4},{8,10},{10,8},{12,14},{14,12},{16,18},{18,... | collective-permute-start | bytes 2348 | tf_op jit(solution)/shard_map/ppermute | solution.py:32
  37.5 15.2 %collective-permute-start.9 = (bf16[16,256,128]{2,1,0:T(8,128)(2,1)S(1)}, bf16[16,256,128]{2,1,0:T(8,128)(2,1)S(1)}, u32[]{:S(2)}, u32[]{:S(2)}) collective-permute-start(bf16[16,256,128]{2,1,0:T(8,128)(2,1)S(1)} %constant_dynamic-update-slice_fusion.refs_0_), channel_id=1, source_target_pairs={{0,4},{2,66},{4,8},{6,70},{8,12},{10,74},{12,16},{14,78},{16,20},{... | collective-permute-start | bytes 3145736 | tf_op jit(solution)/shard_map/ppermute | solution.py:32
  38.2 15.3 %collective-permute-start.8 = (bf16[16,256,128]{2,1,0:T(8,128)(2,1)S(1)}, bf16[16,256,128]{2,1,0:T(8,128)(2,1)S(1)}, u32[]{:S(2)}, u32[]{:S(2)}) collective-permute-start(bf16[16,256,128]{2,1,0:T(8,128)(2,1)S(1)} %constant_dynamic-update-slice_fusion.refs_0_), channel_id=1, source_target_pairs={{0,28},{2,194},{4,0},{6,198},{8,4},{10,202},{12,8},{14,206},{16,12... | collective-permute-start | bytes 3145736 | tf_op jit(solution)/shard_map/ppermute | solution.py:32
  53.5 9.9 %collective-permute-start.13 = (bf16[8,256,128]{2,1,0:T(8,128)(2,1)}, bf16[8,256,128]{2,1,0:T(8,128)(2,1)}, u32[]{:S(2)}, u32[]{:S(2)}) collective-permute-start(bf16[8,256,128]{2,1,0:T(8,128)(2,1)} %slice.32), channel_id=1, source_target_pairs={{0,4},{2,66},{4,8},{6,70},{8,12},{10,74},{12,16},{14,78},{16,20},{... | collective-permute-start | bytes 1572872 | tf_op jit(solution)/shard_map/ppermute | solution.py:32
  54.4 9.1 %collective-permute-start.14 = (bf16[8,256,128]{2,1,0:T(8,128)(2,1)}, bf16[8,256,128]{2,1,0:T(8,128)(2,1)}, u32[]{:S(2)}, u32[]{:S(2)}) collective-permute-start(bf16[8,256,128]{2,1,0:T(8,128)(2,1)} %slice.33), channel_id=1, source_target_pairs={{0,28},{2,194},{4,0},{6,198},{8,4},{10,202},{12,8},{14,206},{16,12... | collective-permute-start | bytes 1572872 | tf_op jit(solution)/shard_map/ppermute | solution.py:32
  65.3 8.1 %collective-permute-start.15 = (f32[256,512]{1,0:T(8,128)S(1)}, f32[256,512]{1,0:T(8,128)S(1)}, u32[]{:S(2)}, u32[]{:S(2)}) collective-permute-start(f32[256,512]{1,0:T(8,128)S(1)} %shard_map.124.mine_ref), channel_id=1, source_target_pairs={{0,2},{2,0},{4,6},{6,4},{8,10},{10,8},{12,14},{14,12},{16,18},{18,... | collective-permute-start | bytes 1572872 | tf_op jit(solution)/shard_map/ppermute | solution.py:32
  76.4 9.4 %collective-permute-start.20 = (bf16[8,256,128]{2,1,0:T(8,128)(2,1)S(1)}, bf16[8,256,128]{2,1,0:T(8,128)(2,1)S(1)}, u32[]{:S(2)}, u32[]{:S(2)}) collective-permute-start(bf16[8,256,128]{2,1,0:T(8,128)(2,1)S(1)} %get-tuple-element.20), channel_id=1, source_target_pairs={{0,4},{2,66},{4,8},{6,70},{8,12},{10,74},{12,16},{14,78},{16,20},{... | collective-permute-start | bytes 1572872 | tf_op jit(solution)/shard_map/ppermute | solution.py:32
  76.5 9.6 %collective-permute-start.17 = (bf16[8,256,128]{2,1,0:T(8,128)(2,1)S(1)}, bf16[8,256,128]{2,1,0:T(8,128)(2,1)S(1)}, u32[]{:S(2)}, u32[]{:S(2)}) collective-permute-start(bf16[8,256,128]{2,1,0:T(8,128)(2,1)S(1)} %get-tuple-element.17), channel_id=1, source_target_pairs={{0,28},{2,194},{4,0},{6,198},{8,4},{10,202},{12,8},{14,206},{16,12... | collective-permute-start | bytes 1572872 | tf_op jit(solution)/shard_map/ppermute | solution.py:32
  79.1 11.7 %collective-permute-start.22 = (bf16[8,256,128]{2,1,0:T(8,128)(2,1)S(1)}, bf16[8,256,128]{2,1,0:T(8,128)(2,1)S(1)}, u32[]{:S(2)}, u32[]{:S(2)}) collective-permute-start(bf16[8,256,128]{2,1,0:T(8,128)(2,1)S(1)} %get-tuple-element.21), channel_id=1, source_target_pairs={{0,28},{2,194},{4,0},{6,198},{8,4},{10,202},{12,8},{14,206},{16,12... | collective-permute-start | bytes 1572872 | tf_op jit(solution)/shard_map/ppermute | solution.py:32
  85.9 9.6 %collective-permute-start.21 = (bf16[8,256,128]{2,1,0:T(8,128)(2,1)S(1)}, bf16[8,256,128]{2,1,0:T(8,128)(2,1)S(1)}, u32[]{:S(2)}, u32[]{:S(2)}) collective-permute-start(bf16[8,256,128]{2,1,0:T(8,128)(2,1)S(1)} %add_convert_fusion), channel_id=1, source_target_pairs={{0,4},{2,66},{4,8},{6,70},{8,12},{10,74},{12,16},{14,78},{16,20},{... | collective-permute-start | bytes 1572872 | tf_op jit(solution)/shard_map/ppermute | solution.py:32
  86.0 15.1 %collective-permute-start.16 = (bf16[8,256,128]{2,1,0:T(8,128)(2,1)S(1)}, bf16[8,256,128]{2,1,0:T(8,128)(2,1)S(1)}, u32[]{:S(2)}, u32[]{:S(2)}) collective-permute-start(bf16[8,256,128]{2,1,0:T(8,128)(2,1)S(1)} %get-tuple-element.15), channel_id=1, source_target_pairs={{0,4},{2,66},{4,8},{6,70},{8,12},{10,74},{12,16},{14,78},{16,20},{... | collective-permute-start | bytes 1572872 | tf_op jit(solution)/shard_map/ppermute | solution.py:32
  86.3 14.9 %collective-permute-start.18 = (bf16[8,256,128]{2,1,0:T(8,128)(2,1)S(1)}, bf16[8,256,128]{2,1,0:T(8,128)(2,1)S(1)}, u32[]{:S(2)}, u32[]{:S(2)}) collective-permute-start(bf16[8,256,128]{2,1,0:T(8,128)(2,1)S(1)} %add_convert_fusion.1), channel_id=1, source_target_pairs={{0,28},{2,194},{4,0},{6,198},{8,4},{10,202},{12,8},{14,206},{16,12... | collective-permute-start | bytes 1572872 | tf_op jit(solution)/shard_map/ppermute | solution.py:32
  95.8 7.0 %collective-permute-start.23 = (bf16[4,256,128]{2,1,0:T(8,128)(2,1)S(1)}, bf16[4,256,128]{2,1,0:T(8,128)(2,1)S(1)}, u32[]{:S(2)}, u32[]{:S(2)}) collective-permute-start(bf16[4,256,128]{2,1,0:T(8,128)(2,1)S(1)} %split.52), channel_id=1, source_target_pairs={{0,192},{2,30},{4,196},{6,2},{8,200},{10,6},{12,204},{14,10},{16,2... | collective-permute-start | bytes 786440 | tf_op jit(solution)/shard_map/ppermute | solution.py:32
  101.4 6.8 %collective-permute-start.19 = (bf16[4,256,128]{2,1,0:T(8,128)(2,1)S(1)}, bf16[4,256,128]{2,1,0:T(8,128)(2,1)S(1)}, u32[]{:S(2)}, u32[]{:S(2)}) collective-permute-start(bf16[4,256,128]{2,1,0:T(8,128)(2,1)S(1)} %split.53), channel_id=1, source_target_pairs={{0,64},{2,6},{4,68},{6,10},{8,72},{10,14},{12,76},{14,18},{16,80},... | collective-permute-start | bytes 786440 | tf_op jit(solution)/shard_map/ppermute | solution.py:32
  102.9 5.6 %collective-permute-start.24 = (bf16[4,256,128]{2,1,0:T(8,128)(2,1)S(1)}, bf16[4,256,128]{2,1,0:T(8,128)(2,1)S(1)}, u32[]{:S(2)}, u32[]{:S(2)}) collective-permute-start(bf16[4,256,128]{2,1,0:T(8,128)(2,1)S(1)} %fusion), channel_id=1, source_target_pairs={{0,192},{2,30},{4,196},{6,2},{8,200},{10,6},{12,204},{14,10},{16,2... | collective-permute-start | bytes 786440 | tf_op jit(solution)/shard_map/ppermute | solution.py:32
  108.6 8.3 %collective-permute-start.25 = (bf16[256,128]{1,0:T(8,128)(2,1)S(1)}, bf16[256,128]{1,0:T(8,128)(2,1)S(1)}, u32[]{:S(2)}, u32[]{:S(2)}) collective-permute-start(bf16[256,128]{1,0:T(8,128)(2,1)S(1)} %get-tuple-element.24), channel_id=1, source_target_pairs={{0,16},{2,18},{4,20},{6,22},{8,24},{10,26},{12,28},{14,30},{16,0},... | collective-permute-start | bytes 196616 | tf_op jit(solution)/shard_map/ppermute | solution.py:32
  110.4 6.5 %collective-permute-start.26 = (bf16[256,128]{1,0:T(8,128)(2,1)S(1)}, bf16[256,128]{1,0:T(8,128)(2,1)S(1)}, u32[]{:S(2)}, u32[]{:S(2)}) collective-permute-start(bf16[256,128]{1,0:T(8,128)(2,1)S(1)} %get-tuple-element.26), channel_id=1, source_target_pairs={{0,32},{2,34},{4,36},{6,38},{8,40},{10,42},{12,44},{14,46},{16,48}... | collective-permute-start | bytes 196616 | tf_op jit(solution)/shard_map/ppermute | solution.py:32
  110.4 8.3 %collective-permute-start.27 = (bf16[256,128]{1,0:T(8,128)(2,1)S(1)}, bf16[256,128]{1,0:T(8,128)(2,1)S(1)}, u32[]{:S(2)}, u32[]{:S(2)}) collective-permute-start(bf16[256,128]{1,0:T(8,128)(2,1)S(1)} %get-tuple-element.25), channel_id=1, source_target_pairs={{0,48},{2,50},{4,52},{6,54},{8,56},{10,58},{12,60},{14,62},{16,32}... | collective-permute-start | bytes 196616 | tf_op jit(solution)/shard_map/ppermute | solution.py:32
  118.9 4.7 %collective-permute-start.28 = (bf16[64,256]{1,0:T(8,128)(2,1)S(1)}, bf16[64,256]{1,0:T(8,128)(2,1)S(1)}, u32[]{:S(2)}, u32[]{:S(2)}) collective-permute-start(bf16[64,256]{1,0:T(8,128)(2,1)S(1)} %broadcast_select_fusion.1), channel_id=1, source_target_pairs={{0,2},{2,0},{4,6},{6,4},{8,10},{10,8},{12,14},{14,12},{16,18},{18,... | collective-permute-start | bytes 98312 | tf_op jit(solution)/shard_map/ppermute | solution.py:32

commit v6 on v5

--- a/solution.py
+++ b/solution.py
@@ -50,16 +50,13 @@
 
 
 def near(value):
-    far = permute(value, lambda at: at | {"x": 1 - at["x"], "z": (at["z"] + 4) % NZ})
-    ahead, beside = shift(value, "z", 4), shift(value, "x", 1)
-    return jnp.concatenate([value, ahead, beside, far])
+    value = jnp.concatenate([value, shift(value, "z", 4)])
+    return jnp.concatenate([value, shift(value, "x", 1)])
 
 
 def near_reduce(total):
-    sent = total.astype(BF16)
-    far = permute(sent[3], lambda at: at | {"x": 1 - at["x"], "z": (at["z"] + 4) % NZ})
-    ahead, beside = shift(sent[1], "z", 4), shift(sent[2], "x", 1)
-    return total[0] + ahead.astype(F32) + beside.astype(F32) + far.astype(F32)
+    total = total[:2] + shift(total[2:].astype(BF16), "x", 1).astype(F32)
+    return total[0] + shift(total[1].astype(BF16), "z", 4).astype(F32)
 
 
 def small_gather(value, axes):
@@ -171,7 +168,7 @@
         arrived(LOADS[1][2:])
 
 
-def outer_kernel(maps_ref, mine_ref, theirs_ref, held_ref, *part_refs):
+def outer_kernel(ranks, maps_ref, mine_ref, theirs_ref, held_ref, *part_refs):
     core = maps_ref[6 * SLOTS]
     g0, u0, g1, u1, d0, d1 = (held_ref.at[n] for n in range(6))
 
@@ -179,7 +176,7 @@
         return ref[:, pl.ds(n * BLOCK, BLOCK)]
 
     def emit(product):
-        for rank, part_ref in enumerate(part_refs):
+        for rank, part_ref in zip(ranks, part_refs, strict=True):
 
             def step(i, carry, rank=rank, part_ref=part_ref):
                 spots = [i * 2 + j for j in range(2)]
@@ -321,8 +318,12 @@
     )
     mine = call(functools.partial(inner_kernel, 6 * PART), sums, flops, maps, mine, *pieces[3:], held)
     theirs = shift(mine, "c", 1)
-    parts = tuple(jax.ShapeDtypeStruct((PART, batch, BLOCK), BF16 if sent else F32) for sent in SENT)
-    parts = call(outer_kernel, parts, 4 * flops, maps, mine, theirs, held)
+    parts = [None] * PIECES
+    for ranks in ([5, 6, 7], [0, 1, 2, 3, 4]):
+        outs = tuple(jax.ShapeDtypeStruct((PART, batch, BLOCK), BF16 if SENT[rank] else F32) for rank in ranks)
+        made = call(functools.partial(outer_kernel, ranks), outs, len(ranks) * flops // 2, maps, mine, theirs, held)
+        for rank, part in zip(ranks, made, strict=True):
+            parts[rank] = part
     total = near_reduce(small_reduce(*large_reduce(parts, "zy"), "yz"))
     total = transpose(total).astype(BF16)
     low, high = jnp.split(total, 2)

time: 124 us -> 127 us (1.024)
  starting transfers between devices: 49.8 us -> 54.7 us
  waiting for transfers between devices: 54.8 us -> 51.6 us
    ppermute x29 -> x27, starting transfers between devices: 49.8 us -> 54.7 us  [permute(): return lax.ppermute(value, 'tp', pairs)]
    ppermute x29 -> x27, waiting for transfers between devices: 54.8 us -> 51.6 us  [permute(): return lax.ppermute(value, 'tp', pairs)]
    pallas_call x3 -> x4, Pallas kernels: 10 us -> 10.8 us  [call(): pl.pallas_call(kernel, out_shape=outs, in_specs=[pl.BlockSpec(memory_spac...]
  transfers between devices with their start and end apart: 29 -> 27, of which waited for: 17 -> 18; matrix products, arithmetic and copies ran while one was open for 4% -> 3% of each run, Pallas kernels for 4% -> 6%
where the time goes in v6:
time: 127 us
  starting transfers between devices  54.7 us (43%)
  waiting for transfers between devices  51.6 us (41%)
  Pallas kernels  11 us (9%)
  other arithmetic  4.16 us (3%)
  between operations  2.9 us (2%)
  local copies, waits for them, and re-layouts  2.35 us (2%)
    ppermute x27, starting transfers between devices, permute(): return lax.ppermute(value, 'tp', pairs)  54.7 us
    ppermute x27, waiting for transfers between devices, permute(): return lax.ppermute(value, 'tp', pairs)  51.6 us
    pallas_call x4, Pallas kernels, call(): pl.pallas_call(kernel, out_shape=outs, in_specs=[pl.BlockSpec(memory_spac...  10.8 us
  transfers between devices with their start and end apart: 27, of which 18 were waited for; matrix products, arithmetic and copies ran while one was open for 3% of the time, Pallas kernels for 6%

profile of v6, /device:TPU:1, one launch (start us, length us, event | category | flops | bytes accessed | tf_op | source)
XLA Modules:
  0.0 126.6 jit_solution(16667897008108499163)
XLA Ops:
  0.7 0.8 select_bitcast_fusion.2
  1.4 3.2 %collective-permute-start.1 = (bf16[64,256]{1,0:T(8,128)(2,1)S(1)}, bf16[64,256]{1,0:T(8,128)(2,1)S(1)}, u32[]{:S(2)}, u32[]{:S(2)}) collective-permute-start(bf16[64,256]{1,0:T(8,128)(2,1)S(1)} %select_bitcast_fusion.2), channel_id=1, source_target_pairs={{0,2},{2,0},{4,6},{6,4},{8,10},{10,8},{12,14},{14,12},{16,18},{18,... | collective-permute-start | bytes 98312 | tf_op jit(solution)/shard_map/ppermute | solution.py:32
  4.7 0.9 collective-permute-done.1
  5.5 0.8 bitcast_select_fusion.1
  6.3 0.1 shard_map.122
  6.4 5.3 %collective-permute-start.2 = (bf16[1,256,128]{2,1,0:T(8,128)(2,1)S(1)}, bf16[1,256,128]{2,1,0:T(8,128)(2,1)S(1)}, u32[]{:S(2)}, u32[]{:S(2)}) collective-permute-start(bf16[1,256,128]{2,1,0:T(8,128)(2,1)S(1)} %bitcast.24), channel_id=1, source_target_pairs={{0,16},{2,18},{4,20},{6,22},{8,24},{10,26},{12,28},{14,30},{16,0},... | collective-permute-start | bytes 196616 | tf_op jit(solution)/shard_map/ppermute | solution.py:32
  11.7 0.6 collective-permute-start.10
  12.3 0.5 collective-permute-start.9
  14.8 1.3 %collective-permute-start.3 = (bf16[2,256,128]{2,1,0:T(8,128)(2,1)S(1)}, bf16[2,256,128]{2,1,0:T(8,128)(2,1)S(1)}, u32[]{:S(2)}, u32[]{:S(2)}) collective-permute-start(bf16[2,256,128]{2,1,0:T(8,128)(2,1)S(1)} %pad_maximum_fusion.1), channel_id=1, source_target_pairs={{0,32},{2,34},{4,36},{6,38},{8,40},{10,42},{12,44},{14,46},{16,48}... | collective-permute-start | bytes 393224 | tf_op jit(solution)/shard_map/ppermute | solution.py:32
  16.1 0.1 pad_add_fusion.3
  16.2 0.1 copy.14
  16.3 0.8 pad_add_fusion.1
  17.0 2.7 %collective-permute-done.3 = bf16[2,256,128]{2,1,0:T(8,128)(2,1)S(1)} collective-permute-done((bf16[2,256,128]{2,1,0:T(8,128)(2,1)S(1)}, bf16[2,256,128]{2,1,0:T(8,128)(2,1)S(1)}, u32[]{:S(2)}, u32[]{:S(2)}) %collective-permute-start.3) | collective-permute-done | bytes 131104 | tf_op jit(solution)/shard_map/ppermute | solution.py:32
  19.8 2.3 %collective-permute-start.4 = (bf16[4,256,128]{2,1,0:T(8,128)(2,1)S(1)}, bf16[4,256,128]{2,1,0:T(8,128)(2,1)S(1)}, u32[]{:S(2)}, u32[]{:S(2)}) collective-permute-start(bf16[4,256,128]{2,1,0:T(8,128)(2,1)S(1)} %pad_maximum_fusion), channel_id=1, source_target_pairs={{0,192},{2,30},{4,196},{6,2},{8,200},{10,6},{12,204},{14,10},{16,2... | collective-permute-start | bytes 786440 | tf_op jit(solution)/shard_map/ppermute | solution.py:32
  22.1 6.7 %collective-permute-done.5 = bf16[4,256,128]{2,1,0:T(8,128)(2,1)S(1)} collective-permute-done((bf16[4,256,128]{2,1,0:T(8,128)(2,1)S(1)}, bf16[4,256,128]{2,1,0:T(8,128)(2,1)S(1)}, u32[]{:S(2)}, u32[]{:S(2)}) %collective-permute-start.5) | collective-permute-done | bytes 262176 | tf_op jit(solution)/shard_map/ppermute | solution.py:32
  28.8 2.8 %collective-permute-start = (s32[3,65]{1,0:T(4,128)S(1)}, s32[3,65]{1,0:T(4,128)S(1)}, u32[]{:S(2)}, u32[]{:S(2)}) collective-permute-start(s32[3,65]{1,0:T(4,128)S(1)} %pad_add_fusion.1), channel_id=1, source_target_pairs={{0,2},{2,0},{4,6},{6,4},{8,10},{10,8},{12,14},{14,12},{16,18},{18,... | collective-permute-start | bytes 2348 | tf_op jit(solution)/shard_map/ppermute | solution.py:32
  31.7 3.5 %collective-permute-done.6 = bf16[4,256,128]{2,1,0:T(8,128)(2,1)S(1)} collective-permute-done((bf16[4,256,128]{2,1,0:T(8,128)(2,1)S(1)}, bf16[4,256,128]{2,1,0:T(8,128)(2,1)S(1)}, u32[]{:S(2)}, u32[]{:S(2)}) %collective-permute-start.6) | collective-permute-done | bytes 262176 | tf_op jit(solution)/shard_map/ppermute | solution.py:32
  35.2 1.1 collective-permute-start.8
  36.3 1.7 %collective-permute-start.7 = (bf16[16,256,128]{2,1,0:T(8,128)(2,1)S(1)}, bf16[16,256,128]{2,1,0:T(8,128)(2,1)S(1)}, u32[]{:S(2)}, u32[]{:S(2)}) collective-permute-start(bf16[16,256,128]{2,1,0:T(8,128)(2,1)S(1)} %constant_dynamic-update-slice_fusion.refs_0_), channel_id=1, source_target_pairs={{0,28},{2,194},{4,0},{6,198},{8,4},{10,202},{12,8},{14,206},{16,12... | collective-permute-start | bytes 3145736 | tf_op jit(solution)/shard_map/ppermute | solution.py:32
  38.0 0.1 pad_add_fusion
  38.1 0.2 slice_reduce_fusion
  38.3 12.2 %collective-permute-done.8.refs_2_ = bf16[16,256,128]{2,1,0:T(8,128)(2,1)S(1)} collective-permute-done((bf16[16,256,128]{2,1,0:T(8,128)(2,1)S(1)}, bf16[16,256,128]{2,1,0:T(8,128)(2,1)S(1)}, u32[]{:S(2)}, u32[]{:S(2)}) %collective-permute-start.8) | collective-permute-done | bytes 1048608 | tf_op jit(solution)/shard_map/ppermute | solution.py:32
  50.5 0.8 slice.34
  51.3 0.9 slice.35
  52.2 2.7 %collective-permute-start.13 = (bf16[8,256,128]{2,1,0:T(8,128)(2,1)}, bf16[8,256,128]{2,1,0:T(8,128)(2,1)}, u32[]{:S(2)}, u32[]{:S(2)}) collective-permute-start(bf16[8,256,128]{2,1,0:T(8,128)(2,1)} %slice.35), channel_id=1, source_target_pairs={{0,28},{2,194},{4,0},{6,198},{8,4},{10,202},{12,8},{14,206},{16,12... | collective-permute-start | bytes 1572872 | tf_op jit(solution)/shard_map/ppermute | solution.py:32
  54.9 0.3 select_reduce_fusion
  55.1 0.1 sub.34
  55.3 5.3 %shard_map.123 = (f32[256,512]{1,0:T(8,128)S(1)}, bf16[6,64,128,128]{3,2,1,0:T(8,128)(2,1)S(1)}) custom-call(s32[385]{0:T(512)S(1)} %pad_add_fusion.2.maps_ref, bf16[16,256,128]{2,1,0:T(8,128)(2,1)S(1)} %constant_dynamic-update-slice_fusion.refs_0_, bf16[16,256,128]{2,1,0:T(8,128)(2,1)S(1)} %collective-permute-done.7.refs_1_, ...), custom_call_target="tpu_custom_call" | custom-call | flops 1610612736 | bytes 16777216 | tf_op jit(solution)/shard_map/pallas_call | solution.py:251
  60.5 0.3 collective-permute-done.12.refs_1_
  60.9 0.5 collective-permute-done.13.refs_2_
  61.3 1.7 %shard_map.124.mine_ref = f32[256,512]{1,0:T(8,128)S(1)} custom-call(s32[385]{0:T(512)S(1)} %pad_add_fusion.2.maps_ref, f32[256,512]{1,0:T(8,128)S(1)} %get-tuple-element.12.refs_0_, bf16[8,256,128]{2,1,0:T(8,128)(2,1)} %collective-permute-done.12.refs_1_, bf16[8,256,128]{2,1,0:T(8,128)(2,1)} %collective-permute-done.13.refs_2_, ...), custom_call_target="tpu_custom_call" | custom-call | flops 536870912 | bytes 16777216 | tf_op jit(solution)/shard_map/pallas_call | solution.py:251
  63.1 9.3 %collective-permute-start.14 = (f32[256,512]{1,0:T(8,128)S(1)}, f32[256,512]{1,0:T(8,128)S(1)}, u32[]{:S(2)}, u32[]{:S(2)}) collective-permute-start(f32[256,512]{1,0:T(8,128)S(1)} %shard_map.124.mine_ref), channel_id=1, source_target_pairs={{0,2},{2,0},{4,6},{6,4},{8,10},{10,8},{12,14},{14,12},{16,18},{18,... | collective-permute-start | bytes 1572872 | tf_op jit(solution)/shard_map/ppermute | solution.py:32
  72.3 1.5 %collective-permute-done.14.theirs_ref = f32[256,512]{1,0:T(8,128)S(1)} collective-permute-done((f32[256,512]{1,0:T(8,128)S(1)}, f32[256,512]{1,0:T(8,128)S(1)}, u32[]{:S(2)}, u32[]{:S(2)}) %collective-permute-start.14) | collective-permute-done | bytes 524320 | tf_op jit(solution)/shard_map/ppermute | solution.py:32
  73.9 1.6 %shard_map.126 = (bf16[8,256,128]{2,1,0:T(8,128)(2,1)S(1)}, bf16[8,256,128]{2,1,0:T(8,128)(2,1)S(1)}, bf16[8,256,128]{2,1,0:T(8,128)(2,1)S(1)}) custom-call(s32[385]{0:T(512)S(1)} %pad_add_fusion.2.maps_ref, f32[256,512]{1,0:T(8,128)S(1)} %shard_map.124.mine_ref, f32[256,512]{1,0:T(8,128)S(1)} %collective-permute-done.14.theirs_ref, ...), custom_call_target="tpu_custom_call" | custom-call | flops 805306368 | bytes 16777216 | tf_op jit(solution)/shard_map/pallas_call | solution.py:251
  75.5 0.1 collective-permute-start.19
  75.6 2.7 %collective-permute-start.16 = (bf16[8,256,128]{2,1,0:T(8,128)(2,1)S(1)}, bf16[8,256,128]{2,1,0:T(8,128)(2,1)S(1)}, u32[]{:S(2)}, u32[]{:S(2)}) collective-permute-start(bf16[8,256,128]{2,1,0:T(8,128)(2,1)S(1)} %get-tuple-element.17), channel_id=1, source_target_pairs={{0,28},{2,194},{4,0},{6,198},{8,4},{10,202},{12,8},{14,206},{16,12... | collective-permute-start | bytes 1572872 | tf_op jit(solution)/shard_map/ppermute | solution.py:32
  78.3 2.2 %shard_map.125 = (f32[8,256,128]{2,1,0:T(8,128)S(1)}, f32[8,256,128]{2,1,0:T(8,128)S(1)}, bf16[8,256,128]{2,1,0:T(8,128)(2,1)S(1)}, f32[8,256,128]{2,1,0:T(8,128)S(1)}, f32[8,256,128]{2,1,0:T(8,128)S(1)}) custom-call(s32[385]{0:T(512)S(1)} %pad_add_fusion.2.maps_ref, f32[256,512]{1,0:T(8,128)S(1)} %shard_map.124.mine_ref, ...), custom_call_target="tpu_custom_call" | custom-call | flops 1342177280 | bytes 16777216 | tf_op jit(solution)/shard_map/pallas_call | solution.py:251
  80.4 4.7 %collective-permute-done.19 = bf16[8,256,128]{2,1,0:T(8,128)(2,1)S(1)} collective-permute-done((bf16[8,256,128]{2,1,0:T(8,128)(2,1)S(1)}, bf16[8,256,128]{2,1,0:T(8,128)(2,1)S(1)}, u32[]{:S(2)}, u32[]{:S(2)}) %collective-permute-start.19) | collective-permute-done | bytes 524320 | tf_op jit(solution)/shard_map/ppermute | solution.py:32
  85.1 0.1 add_convert_fusion
  85.2 0.1 collective-permute-start.20
  85.3 0.1 collective-permute-start.15
  85.4 0.1 add_convert_fusion.1
  85.5 2.7 %collective-permute-start.17 = (bf16[8,256,128]{2,1,0:T(8,128)(2,1)S(1)}, bf16[8,256,128]{2,1,0:T(8,128)(2,1)S(1)}, u32[]{:S(2)}, u32[]{:S(2)}) collective-permute-start(bf16[8,256,128]{2,1,0:T(8,128)(2,1)S(1)} %add_convert_fusion.1), channel_id=1, source_target_pairs={{0,28},{2,194},{4,0},{6,198},{8,4},{10,202},{12,8},{14,206},{16,12... | collective-permute-start | bytes 1572872 | tf_op jit(solution)/shard_map/ppermute | solution.py:32
  88.2 1.7 %collective-permute-done.21 = bf16[8,256,128]{2,1,0:T(8,128)(2,1)S(1)} collective-permute-done((bf16[8,256,128]{2,1,0:T(8,128)(2,1)S(1)}, bf16[8,256,128]{2,1,0:T(8,128)(2,1)S(1)}, u32[]{:S(2)}, u32[]{:S(2)}) %collective-permute-start.21) | collective-permute-done | bytes 524320 | tf_op jit(solution)/shard_map/ppermute | solution.py:32
  90.0 4.8 %collective-permute-done.20 = bf16[8,256,128]{2,1,0:T(8,128)(2,1)S(1)} collective-permute-done((bf16[8,256,128]{2,1,0:T(8,128)(2,1)S(1)}, bf16[8,256,128]{2,1,0:T(8,128)(2,1)S(1)}, u32[]{:S(2)}, u32[]{:S(2)}) %collective-permute-start.20) | collective-permute-done | bytes 524320 | tf_op jit(solution)/shard_map/ppermute | solution.py:32
  94.8 0.2 convert_add_fusion
  95.0 3.7 %collective-permute-start.22 = (bf16[4,256,128]{2,1,0:T(8,128)(2,1)S(1)}, bf16[4,256,128]{2,1,0:T(8,128)(2,1)S(1)}, u32[]{:S(2)}, u32[]{:S(2)}) collective-permute-start(bf16[4,256,128]{2,1,0:T(8,128)(2,1)S(1)} %split.52), channel_id=1, source_target_pairs={{0,192},{2,30},{4,196},{6,2},{8,200},{10,6},{12,204},{14,10},{16,2... | collective-permute-start | bytes 786440 | tf_op jit(solution)/shard_map/ppermute | solution.py:32
  98.7 1.7 %collective-permute-done.15 = bf16[8,256,128]{2,1,0:T(8,128)(2,1)S(1)} collective-permute-done((bf16[8,256,128]{2,1,0:T(8,128)(2,1)S(1)}, bf16[8,256,128]{2,1,0:T(8,128)(2,1)S(1)}, u32[]{:S(2)}, u32[]{:S(2)}) %collective-permute-start.15) | collective-permute-done | bytes 524320 | tf_op jit(solution)/shard_map/ppermute | solution.py:32
  100.4 0.1 convert_add_fusion.1
  100.6 0.1 collective-permute-start.18
  100.7 1.3 %collective-permute-done.22 = bf16[4,256,128]{2,1,0:T(8,128)(2,1)S(1)} collective-permute-done((bf16[4,256,128]{2,1,0:T(8,128)(2,1)S(1)}, bf16[4,256,128]{2,1,0:T(8,128)(2,1)S(1)}, u32[]{:S(2)}, u32[]{:S(2)}) %collective-permute-start.22) | collective-permute-done | bytes 262176 | tf_op jit(solution)/shard_map/ppermute | solution.py:32
  102.1 0.1 fusion
  102.1 3.2 %collective-permute-start.23 = (bf16[4,256,128]{2,1,0:T(8,128)(2,1)S(1)}, bf16[4,256,128]{2,1,0:T(8,128)(2,1)S(1)}, u32[]{:S(2)}, u32[]{:S(2)}) collective-permute-start(bf16[4,256,128]{2,1,0:T(8,128)(2,1)S(1)} %fusion), channel_id=1, source_target_pairs={{0,192},{2,30},{4,196},{6,2},{8,200},{10,6},{12,204},{14,10},{16,2... | collective-permute-start | bytes 786440 | tf_op jit(solution)/shard_map/ppermute | solution.py:32
  105.3 2.6 %collective-permute-done.18 = bf16[4,256,128]{2,1,0:T(8,128)(2,1)S(1)} collective-permute-done((bf16[4,256,128]{2,1,0:T(8,128)(2,1)S(1)}, bf16[4,256,128]{2,1,0:T(8,128)(2,1)S(1)}, u32[]{:S(2)}, u32[]{:S(2)}) %collective-permute-start.18) | collective-permute-done | bytes 262176 | tf_op jit(solution)/shard_map/ppermute | solution.py:32
  107.9 0.8 collective-permute-done.23
  108.6 0.1 fusion.1
  108.8 1.3 %collective-permute-start.24 = (bf16[2,256,128]{2,1,0:T(8,128)(2,1)S(1)}, bf16[2,256,128]{2,1,0:T(8,128)(2,1)S(1)}, u32[]{:S(2)}, u32[]{:S(2)}) collective-permute-start(bf16[2,256,128]{2,1,0:T(8,128)(2,1)S(1)} %slice.50), channel_id=1, source_target_pairs={{0,32},{2,34},{4,36},{6,38},{8,40},{10,42},{12,44},{14,46},{16,48}... | collective-permute-start | bytes 393224 | tf_op jit(solution)/shard_map/ppermute | solution.py:32
  110.1 2.6 %collective-permute-done.24 = bf16[2,256,128]{2,1,0:T(8,128)(2,1)S(1)} collective-permute-done((bf16[2,256,128]{2,1,0:T(8,128)(2,1)S(1)}, bf16[2,256,128]{2,1,0:T(8,128)(2,1)S(1)}, u32[]{:S(2)}, u32[]{:S(2)}) %collective-permute-start.24) | collective-permute-done | bytes 131104 | tf_op jit(solution)/shard_map/ppermute | solution.py:32
  112.7 4.8 %collective-permute-start.25 = (bf16[256,128]{1,0:T(8,128)(2,1)S(1)}, bf16[256,128]{1,0:T(8,128)(2,1)S(1)}, u32[]{:S(2)}, u32[]{:S(2)}) collective-permute-start(bf16[256,128]{1,0:T(8,128)(2,1)S(1)} %fusion.4), channel_id=1, source_target_pairs={{0,16},{2,18},{4,20},{6,22},{8,24},{10,26},{12,28},{14,30},{16,0},... | collective-permute-start | bytes 196616 | tf_op jit(solution)/shard_map/ppermute | solution.py:32
  117.5 2.3 %collective-permute-done.25 = bf16[256,128]{1,0:T(8,128)(2,1)S(1)} collective-permute-done((bf16[256,128]{1,0:T(8,128)(2,1)S(1)}, bf16[256,128]{1,0:T(8,128)(2,1)S(1)}, u32[]{:S(2)}, u32[]{:S(2)}) %collective-permute-start.25) | collective-permute-done | bytes 65568 | tf_op jit(solution)/shard_map/ppermute | solution.py:32
  119.8 0.1 shard_map.127
  120.0 5.1 %collective-permute-start.26 = (bf16[64,256]{1,0:T(8,128)(2,1)S(1)}, bf16[64,256]{1,0:T(8,128)(2,1)S(1)}, u32[]{:S(2)}, u32[]{:S(2)}) collective-permute-start(bf16[64,256]{1,0:T(8,128)(2,1)S(1)} %broadcast_select_fusion.1), channel_id=1, source_target_pairs={{0,2},{2,0},{4,6},{6,4},{8,10},{10,8},{12,14},{14,12},{16,18},{18,... | collective-permute-start | bytes 98312 | tf_op jit(solution)/shard_map/ppermute | solution.py:32
  125.1 0.9 collective-permute-done.26
  126.0 0.6 select_bitcast_fusion
  (41 shorter events, 0.5 us)
Async XLA Ops:
  0.6 37.4 %copy-start.2 = (s32[1,64]{1,0:T(1,128)S(1)}, s32[1,64]{1,0:T(1,128)}, u32[]{:S(2)}) copy-start(s32[1,64]{1,0:T(1,128)} %param.14) | copy-start | bytes 772
  0.6 37.4 %copy-start.1 = (s32[1,64]{1,0:T(1,128)S(1)}, s32[1,64]{1,0:T(1,128)}, u32[]{:S(2)}) copy-start(s32[1,64]{1,0:T(1,128)} %param.17) | copy-start | bytes 772
  0.7 37.3 %copy-start = (s32[1,64]{1,0:T(1,128)S(1)}, s32[1,64]{1,0:T(1,128)}, u32[]{:S(2)}) copy-start(s32[1,64]{1,0:T(1,128)} %param.20) | copy-start | bytes 772
  1.4 4.1 %collective-permute-start.1 = (bf16[64,256]{1,0:T(8,128)(2,1)S(1)}, bf16[64,256]{1,0:T(8,128)(2,1)S(1)}, u32[]{:S(2)}, u32[]{:S(2)}) collective-permute-start(bf16[64,256]{1,0:T(8,128)(2,1)S(1)} %select_bitcast_fusion.2), channel_id=1, source_target_pairs={{0,2},{2,0},{4,6},{6,4},{8,10},{10,8},{12,14},{14,12},{16,18},{18,... | collective-permute-start | bytes 98312 | tf_op jit(solution)/shard_map/ppermute | solution.py:32
  6.4 8.4 %collective-permute-start.2 = (bf16[1,256,128]{2,1,0:T(8,128)(2,1)S(1)}, bf16[1,256,128]{2,1,0:T(8,128)(2,1)S(1)}, u32[]{:S(2)}, u32[]{:S(2)}) collective-permute-start(bf16[1,256,128]{2,1,0:T(8,128)(2,1)S(1)} %bitcast.24), channel_id=1, source_target_pairs={{0,16},{2,18},{4,20},{6,22},{8,24},{10,26},{12,28},{14,30},{16,0},... | collective-permute-start | bytes 196616 | tf_op jit(solution)/shard_map/ppermute | solution.py:32
  11.7 43.6 %collective-permute-start.10 = (bf16[64,128,128]{2,1,0:T(8,128)(2,1)}, bf16[64,128,128]{2,1,0:T(8,128)(2,1)}, u32[]{:S(2)}, u32[]{:S(2)}) collective-permute-start(bf16[64,128,128]{2,1,0:T(8,128)(2,1)} %refs_4_.1), channel_id=1, source_target_pairs={{0,2},{2,0},{4,6},{6,4},{8,10},{10,8},{12,14},{14,12},{16,18},{18,... | collective-permute-start | bytes 6291464 | tf_op jit(solution)/shard_map/ppermute | solution.py:32
  12.3 42.9 %collective-permute-start.11 = (bf16[64,128,128]{2,1,0:T(8,128)(2,1)}, bf16[64,128,128]{2,1,0:T(8,128)(2,1)}, u32[]{:S(2)}, u32[]{:S(2)}) collective-permute-start(bf16[64,128,128]{2,1,0:T(8,128)(2,1)} %refs_7_.1), channel_id=1, source_target_pairs={{0,2},{2,0},{4,6},{6,4},{8,10},{10,8},{12,14},{14,12},{16,18},{18,... | collective-permute-start | bytes 6291464 | tf_op jit(solution)/shard_map/ppermute | solution.py:32
  12.3 42.9 %collective-permute-start.9 = (bf16[64,128,128]{2,1,0:T(8,128)(2,1)}, bf16[64,128,128]{2,1,0:T(8,128)(2,1)}, u32[]{:S(2)}, u32[]{:S(2)}) collective-permute-start(bf16[64,128,128]{2,1,0:T(8,128)(2,1)} %refs_3_.1), channel_id=1, source_target_pairs={{0,2},{2,0},{4,6},{6,4},{8,10},{10,8},{12,14},{14,12},{16,18},{18,... | collective-permute-start | bytes 6291464 | tf_op jit(solution)/shard_map/ppermute | solution.py:32
  14.8 4.9 %collective-permute-start.3 = (bf16[2,256,128]{2,1,0:T(8,128)(2,1)S(1)}, bf16[2,256,128]{2,1,0:T(8,128)(2,1)S(1)}, u32[]{:S(2)}, u32[]{:S(2)}) collective-permute-start(bf16[2,256,128]{2,1,0:T(8,128)(2,1)S(1)} %pad_maximum_fusion.1), channel_id=1, source_target_pairs={{0,32},{2,34},{4,36},{6,38},{8,40},{10,42},{12,44},{14,46},{16,48}... | collective-permute-start | bytes 393224 | tf_op jit(solution)/shard_map/ppermute | solution.py:32
  19.8 9.0 %collective-permute-start.4 = (bf16[4,256,128]{2,1,0:T(8,128)(2,1)S(1)}, bf16[4,256,128]{2,1,0:T(8,128)(2,1)S(1)}, u32[]{:S(2)}, u32[]{:S(2)}) collective-permute-start(bf16[4,256,128]{2,1,0:T(8,128)(2,1)S(1)} %pad_maximum_fusion), channel_id=1, source_target_pairs={{0,192},{2,30},{4,196},{6,2},{8,200},{10,6},{12,204},{14,10},{16,2... | collective-permute-start | bytes 786440 | tf_op jit(solution)/shard_map/ppermute | solution.py:32
  22.0 6.7 %collective-permute-start.5 = (bf16[4,256,128]{2,1,0:T(8,128)(2,1)S(1)}, bf16[4,256,128]{2,1,0:T(8,128)(2,1)S(1)}, u32[]{:S(2)}, u32[]{:S(2)}) collective-permute-start(bf16[4,256,128]{2,1,0:T(8,128)(2,1)S(1)} %pad_maximum_fusion), channel_id=1, source_target_pairs={{0,64},{2,6},{4,68},{6,10},{8,72},{10,14},{12,76},{14,18},{16,80},... | collective-permute-start | bytes 786440 | tf_op jit(solution)/shard_map/ppermute | solution.py:32
  28.8 6.4 %collective-permute-start.6 = (bf16[4,256,128]{2,1,0:T(8,128)(2,1)S(1)}, bf16[4,256,128]{2,1,0:T(8,128)(2,1)S(1)}, u32[]{:S(2)}, u32[]{:S(2)}) collective-permute-start(bf16[4,256,128]{2,1,0:T(8,128)(2,1)S(1)} %collective-permute-done.5), channel_id=1, source_target_pairs={{0,64},{2,6},{4,68},{6,10},{8,72},{10,14},{12,76},{14,18},{16,80},... | collective-permute-start | bytes 786440 | tf_op jit(solution)/shard_map/ppermute | solution.py:32
  28.8 7.5 %collective-permute-start = (s32[3,65]{1,0:T(4,128)S(1)}, s32[3,65]{1,0:T(4,128)S(1)}, u32[]{:S(2)}, u32[]{:S(2)}) collective-permute-start(s32[3,65]{1,0:T(4,128)S(1)} %pad_add_fusion.1), channel_id=1, source_target_pairs={{0,2},{2,0},{4,6},{6,4},{8,10},{10,8},{12,14},{14,12},{16,18},{18,... | collective-permute-start | bytes 2348 | tf_op jit(solution)/shard_map/ppermute | solution.py:32
  35.2 15.2 %collective-permute-start.8 = (bf16[16,256,128]{2,1,0:T(8,128)(2,1)S(1)}, bf16[16,256,128]{2,1,0:T(8,128)(2,1)S(1)}, u32[]{:S(2)}, u32[]{:S(2)}) collective-permute-start(bf16[16,256,128]{2,1,0:T(8,128)(2,1)S(1)} %constant_dynamic-update-slice_fusion.refs_0_), channel_id=1, source_target_pairs={{0,4},{2,66},{4,8},{6,70},{8,12},{10,74},{12,16},{14,78},{16,20},{... | collective-permute-start | bytes 3145736 | tf_op jit(solution)/shard_map/ppermute | solution.py:32
  36.3 15.0 %collective-permute-start.7 = (bf16[16,256,128]{2,1,0:T(8,128)(2,1)S(1)}, bf16[16,256,128]{2,1,0:T(8,128)(2,1)S(1)}, u32[]{:S(2)}, u32[]{:S(2)}) collective-permute-start(bf16[16,256,128]{2,1,0:T(8,128)(2,1)S(1)} %constant_dynamic-update-slice_fusion.refs_0_), channel_id=1, source_target_pairs={{0,28},{2,194},{4,0},{6,198},{8,4},{10,202},{12,8},{14,206},{16,12... | collective-permute-start | bytes 3145736 | tf_op jit(solution)/shard_map/ppermute | solution.py:32
  51.3 9.6 %collective-permute-start.12 = (bf16[8,256,128]{2,1,0:T(8,128)(2,1)}, bf16[8,256,128]{2,1,0:T(8,128)(2,1)}, u32[]{:S(2)}, u32[]{:S(2)}) collective-permute-start(bf16[8,256,128]{2,1,0:T(8,128)(2,1)} %slice.34), channel_id=1, source_target_pairs={{0,4},{2,66},{4,8},{6,70},{8,12},{10,74},{12,16},{14,78},{16,20},{... | collective-permute-start | bytes 1572872 | tf_op jit(solution)/shard_map/ppermute | solution.py:32
  52.2 9.1 %collective-permute-start.13 = (bf16[8,256,128]{2,1,0:T(8,128)(2,1)}, bf16[8,256,128]{2,1,0:T(8,128)(2,1)}, u32[]{:S(2)}, u32[]{:S(2)}) collective-permute-start(bf16[8,256,128]{2,1,0:T(8,128)(2,1)} %slice.35), channel_id=1, source_target_pairs={{0,28},{2,194},{4,0},{6,198},{8,4},{10,202},{12,8},{14,206},{16,12... | collective-permute-start | bytes 1572872 | tf_op jit(solution)/shard_map/ppermute | solution.py:32
  63.1 10.8 %collective-permute-start.14 = (f32[256,512]{1,0:T(8,128)S(1)}, f32[256,512]{1,0:T(8,128)S(1)}, u32[]{:S(2)}, u32[]{:S(2)}) collective-permute-start(f32[256,512]{1,0:T(8,128)S(1)} %shard_map.124.mine_ref), channel_id=1, source_target_pairs={{0,2},{2,0},{4,6},{6,4},{8,10},{10,8},{12,14},{14,12},{16,18},{18,... | collective-permute-start | bytes 1572872 | tf_op jit(solution)/shard_map/ppermute | solution.py:32
  75.5 9.6 %collective-permute-start.19 = (bf16[8,256,128]{2,1,0:T(8,128)(2,1)S(1)}, bf16[8,256,128]{2,1,0:T(8,128)(2,1)S(1)}, u32[]{:S(2)}, u32[]{:S(2)}) collective-permute-start(bf16[8,256,128]{2,1,0:T(8,128)(2,1)S(1)} %get-tuple-element.20), channel_id=1, source_target_pairs={{0,4},{2,66},{4,8},{6,70},{8,12},{10,74},{12,16},{14,78},{16,20},{... | collective-permute-start | bytes 1572872 | tf_op jit(solution)/shard_map/ppermute | solution.py:32
  75.6 9.8 %collective-permute-start.16 = (bf16[8,256,128]{2,1,0:T(8,128)(2,1)S(1)}, bf16[8,256,128]{2,1,0:T(8,128)(2,1)S(1)}, u32[]{:S(2)}, u32[]{:S(2)}) collective-permute-start(bf16[8,256,128]{2,1,0:T(8,128)(2,1)S(1)} %get-tuple-element.17), channel_id=1, source_target_pairs={{0,28},{2,194},{4,0},{6,198},{8,4},{10,202},{12,8},{14,206},{16,12... | collective-permute-start | bytes 1572872 | tf_op jit(solution)/shard_map/ppermute | solution.py:32
  78.2 11.7 %collective-permute-start.21 = (bf16[8,256,128]{2,1,0:T(8,128)(2,1)S(1)}, bf16[8,256,128]{2,1,0:T(8,128)(2,1)S(1)}, u32[]{:S(2)}, u32[]{:S(2)}) collective-permute-start(bf16[8,256,128]{2,1,0:T(8,128)(2,1)S(1)} %get-tuple-element.21), channel_id=1, source_target_pairs={{0,28},{2,194},{4,0},{6,198},{8,4},{10,202},{12,8},{14,206},{16,12... | collective-permute-start | bytes 1572872 | tf_op jit(solution)/shard_map/ppermute | solution.py:32
  85.2 9.6 %collective-permute-start.20 = (bf16[8,256,128]{2,1,0:T(8,128)(2,1)S(1)}, bf16[8,256,128]{2,1,0:T(8,128)(2,1)S(1)}, u32[]{:S(2)}, u32[]{:S(2)}) collective-permute-start(bf16[8,256,128]{2,1,0:T(8,128)(2,1)S(1)} %add_convert_fusion), channel_id=1, source_target_pairs={{0,4},{2,66},{4,8},{6,70},{8,12},{10,74},{12,16},{14,78},{16,20},{... | collective-permute-start | bytes 1572872 | tf_op jit(solution)/shard_map/ppermute | solution.py:32
  85.3 15.1 %collective-permute-start.15 = (bf16[8,256,128]{2,1,0:T(8,128)(2,1)S(1)}, bf16[8,256,128]{2,1,0:T(8,128)(2,1)S(1)}, u32[]{:S(2)}, u32[]{:S(2)}) collective-permute-start(bf16[8,256,128]{2,1,0:T(8,128)(2,1)S(1)} %get-tuple-element.15), channel_id=1, source_target_pairs={{0,4},{2,66},{4,8},{6,70},{8,12},{10,74},{12,16},{14,78},{16,20},{... | collective-permute-start | bytes 1572872 | tf_op jit(solution)/shard_map/ppermute | solution.py:32
  85.5 14.9 %collective-permute-start.17 = (bf16[8,256,128]{2,1,0:T(8,128)(2,1)S(1)}, bf16[8,256,128]{2,1,0:T(8,128)(2,1)S(1)}, u32[]{:S(2)}, u32[]{:S(2)}) collective-permute-start(bf16[8,256,128]{2,1,0:T(8,128)(2,1)S(1)} %add_convert_fusion.1), channel_id=1, source_target_pairs={{0,28},{2,194},{4,0},{6,198},{8,4},{10,202},{12,8},{14,206},{16,12... | collective-permute-start | bytes 1572872 | tf_op jit(solution)/shard_map/ppermute | solution.py:32
  95.0 7.0 %collective-permute-start.22 = (bf16[4,256,128]{2,1,0:T(8,128)(2,1)S(1)}, bf16[4,256,128]{2,1,0:T(8,128)(2,1)S(1)}, u32[]{:S(2)}, u32[]{:S(2)}) collective-permute-start(bf16[4,256,128]{2,1,0:T(8,128)(2,1)S(1)} %split.52), channel_id=1, source_target_pairs={{0,192},{2,30},{4,196},{6,2},{8,200},{10,6},{12,204},{14,10},{16,2... | collective-permute-start | bytes 786440 | tf_op jit(solution)/shard_map/ppermute | solution.py:32
  100.6 7.2 %collective-permute-start.18 = (bf16[4,256,128]{2,1,0:T(8,128)(2,1)S(1)}, bf16[4,256,128]{2,1,0:T(8,128)(2,1)S(1)}, u32[]{:S(2)}, u32[]{:S(2)}) collective-permute-start(bf16[4,256,128]{2,1,0:T(8,128)(2,1)S(1)} %split.53), channel_id=1, source_target_pairs={{0,64},{2,6},{4,68},{6,10},{8,72},{10,14},{12,76},{14,18},{16,80},... | collective-permute-start | bytes 786440 | tf_op jit(solution)/shard_map/ppermute | solution.py:32
  102.1 6.5 %collective-permute-start.23 = (bf16[4,256,128]{2,1,0:T(8,128)(2,1)S(1)}, bf16[4,256,128]{2,1,0:T(8,128)(2,1)S(1)}, u32[]{:S(2)}, u32[]{:S(2)}) collective-permute-start(bf16[4,256,128]{2,1,0:T(8,128)(2,1)S(1)} %fusion), channel_id=1, source_target_pairs={{0,192},{2,30},{4,196},{6,2},{8,200},{10,6},{12,204},{14,10},{16,2... | collective-permute-start | bytes 786440 | tf_op jit(solution)/shard_map/ppermute | solution.py:32
  108.8 3.9 %collective-permute-start.24 = (bf16[2,256,128]{2,1,0:T(8,128)(2,1)S(1)}, bf16[2,256,128]{2,1,0:T(8,128)(2,1)S(1)}, u32[]{:S(2)}, u32[]{:S(2)}) collective-permute-start(bf16[2,256,128]{2,1,0:T(8,128)(2,1)S(1)} %slice.50), channel_id=1, source_target_pairs={{0,32},{2,34},{4,36},{6,38},{8,40},{10,42},{12,44},{14,46},{16,48}... | collective-permute-start | bytes 393224 | tf_op jit(solution)/shard_map/ppermute | solution.py:32
  112.7 7.1 %collective-permute-start.25 = (bf16[256,128]{1,0:T(8,128)(2,1)S(1)}, bf16[256,128]{1,0:T(8,128)(2,1)S(1)}, u32[]{:S(2)}, u32[]{:S(2)}) collective-permute-start(bf16[256,128]{1,0:T(8,128)(2,1)S(1)} %fusion.4), channel_id=1, source_target_pairs={{0,16},{2,18},{4,20},{6,22},{8,24},{10,26},{12,28},{14,30},{16,0},... | collective-permute-start | bytes 196616 | tf_op jit(solution)/shard_map/ppermute | solution.py:32
  120.0 6.0 %collective-permute-start.26 = (bf16[64,256]{1,0:T(8,128)(2,1)S(1)}, bf16[64,256]{1,0:T(8,128)(2,1)S(1)}, u32[]{:S(2)}, u32[]{:S(2)}) collective-permute-start(bf16[64,256]{1,0:T(8,128)(2,1)S(1)} %broadcast_select_fusion.1), channel_id=1, source_target_pairs={{0,2},{2,0},{4,6},{6,4},{8,10},{10,8},{12,14},{14,12},{16,18},{18,... | collective-permute-start | bytes 98312 | tf_op jit(solution)/shard_map/ppermute | solution.py:32

commit v7 on v5

--- a/solution.py
+++ b/solution.py
@@ -287,7 +287,7 @@
     other = shift(other, "c", 1)
     block = jnp.concatenate([jnp.where(first, own, other), jnp.where(first, other, own)])
     block = transpose(block).reshape(1, batch, BLOCK)
-    pieces = large_gather(small_gather(near(block), "yz"), "zy")
+    pieces = large_gather(small_gather(near(block), "zy"), "yz")
 
     lists = jnp.concatenate([gate_index, up_index, down_index])
     counts = jnp.stack([gate_count, up_count, down_count])
@@ -301,10 +301,11 @@
         return jnp.where(k >= 2, 5 - k, k)
 
     y_rank, z_rank = ranked(y), ranked(low)
-    from_ahead = first & (y_rank >= 2)
+    z_large = core == 1
+    from_ahead = z_large & (y_rank >= 2)
     flipped = (low == 3) | ((low == 2) & jnp.logical_not(from_ahead))
     high = jnp.where(flipped, 1 - high, high)
-    position = jnp.where(first, z_rank * RING + y_rank, y_rank * RING + z_rank) * 4 + x * 2 + high
+    position = jnp.where(z_large, z_rank * RING + y_rank, y_rank * RING + z_rank) * 4 + x * 2 + high
     number = lax.broadcasted_iota(jnp.int32, (6, SLOTS, SLOTS), 2)
     places = lax.broadcasted_iota(jnp.int32, (6, SLOTS, SLOTS), 1)
     here = (position[:, None, :] == places) & (number < counts[:, :, None])
@@ -323,7 +324,7 @@
     theirs = shift(mine, "c", 1)
     parts = tuple(jax.ShapeDtypeStruct((PART, batch, BLOCK), BF16 if sent else F32) for sent in SENT)
     parts = call(outer_kernel, parts, 4 * flops, maps, mine, theirs, held)
-    total = near_reduce(small_reduce(*large_reduce(parts, "zy"), "yz"))
+    total = near_reduce(small_reduce(*large_reduce(parts, "yz"), "zy"))
     total = transpose(total).astype(BF16)
     low, high = jnp.split(total, 2)
     own, other = jnp.where(first, low, high), jnp.where(first, high, low)

time: 124 us -> 123 us (level)
  transfers between devices with their start and end apart: 29 -> 29, of which waited for: 17 -> 18; matrix products, arithmetic and copies ran while one was open for 4% -> 4% of each run, Pallas kernels for 4% -> 4%
where the time goes in v7:
time: 123 us
  waiting for transfers between devices  54.8 us (45%)
  starting transfers between devices  48.6 us (40%)
  Pallas kernels  10.2 us (8%)
  other arithmetic  4.23 us (3%)
  between operations  2.85 us (2%)
  local copies, waits for them, and re-layouts  2.32 us (2%)
    ppermute x29, waiting for transfers between devices, permute(): return lax.ppermute(value, 'tp', pairs)  54.8 us
    ppermute x29, starting transfers between devices, permute(): return lax.ppermute(value, 'tp', pairs)  48.6 us
    pallas_call x3, Pallas kernels, call(): pl.pallas_call(kernel, out_shape=outs, in_specs=[pl.BlockSpec(memory_spac...  10 us
  transfers between devices with their start and end apart: 29, of which 18 were waited for; matrix products, arithmetic and copies ran while one was open for 4% of the time, Pallas kernels for 4%

profile of v7, /device:TPU:1, one launch (start us, length us, event | category | flops | bytes accessed | tf_op | source)
XLA Modules:
  0.0 123.0 jit_solution(5152035445294263587)
XLA Ops:
  0.7 0.8 select_bitcast_fusion.2
  1.5 3.2 %collective-permute-start.1 = (bf16[64,256]{1,0:T(8,128)(2,1)S(1)}, bf16[64,256]{1,0:T(8,128)(2,1)S(1)}, u32[]{:S(2)}, u32[]{:S(2)}) collective-permute-start(bf16[64,256]{1,0:T(8,128)(2,1)S(1)} %select_bitcast_fusion.2), channel_id=1, source_target_pairs={{0,2},{2,0},{4,6},{6,4},{8,10},{10,8},{12,14},{14,12},{16,18},{18,... | collective-permute-start | bytes 98312 | tf_op jit(solution)/shard_map/ppermute | solution.py:32
  4.7 0.1 collective-permute-start.10
  4.8 0.4 collective-permute-start.11
  7.2 0.1 copy.14
  7.3 0.8 bitcast_select_fusion.1
  8.2 5.3 %collective-permute-start.2 = (bf16[1,256,128]{2,1,0:T(8,128)(2,1)S(1)}, bf16[1,256,128]{2,1,0:T(8,128)(2,1)S(1)}, u32[]{:S(2)}, u32[]{:S(2)}) collective-permute-start(bf16[1,256,128]{2,1,0:T(8,128)(2,1)S(1)} %bitcast.32), channel_id=1, source_target_pairs={{0,16},{2,18},{4,20},{6,22},{8,24},{10,26},{12,28},{14,30},{16,0},... | collective-permute-start | bytes 196616 | tf_op jit(solution)/shard_map/ppermute | solution.py:32
  13.5 1.2 collective-permute-start.3
  14.7 0.2 collective-permute-start.4
  14.8 0.8 pad_add_fusion.1
  15.6 0.2 collective-permute-done.2
  15.8 1.0 collective-permute-start.12
  16.8 7.0 %collective-permute-done.4 = bf16[1,256,128]{2,1,0:T(8,128)(2,1)S(1)} collective-permute-done((bf16[1,256,128]{2,1,0:T(8,128)(2,1)S(1)}, bf16[1,256,128]{2,1,0:T(8,128)(2,1)S(1)}, u32[]{:S(2)}, u32[]{:S(2)}) %collective-permute-start.4) | collective-permute-done | bytes 65568 | tf_op jit(solution)/shard_map/ppermute | solution.py:32
  23.9 1.4 %collective-permute-start.6 = (bf16[4,256,128]{2,1,0:T(8,128)(2,1)S(1)}, bf16[4,256,128]{2,1,0:T(8,128)(2,1)S(1)}, u32[]{:S(2)}, u32[]{:S(2)}) collective-permute-start(bf16[4,256,128]{2,1,0:T(8,128)(2,1)S(1)} %pad_maximum_fusion), channel_id=1, source_target_pairs={{0,4},{2,66},{4,8},{6,70},{8,12},{10,74},{12,16},{14,78},{16,20},{... | collective-permute-start | bytes 786440 | tf_op jit(solution)/shard_map/ppermute | solution.py:32
  25.3 1.5 %collective-permute-start.5 = (bf16[4,256,128]{2,1,0:T(8,128)(2,1)S(1)}, bf16[4,256,128]{2,1,0:T(8,128)(2,1)S(1)}, u32[]{:S(2)}, u32[]{:S(2)}) collective-permute-start(bf16[4,256,128]{2,1,0:T(8,128)(2,1)S(1)} %pad_maximum_fusion), channel_id=1, source_target_pairs={{0,28},{2,194},{4,0},{6,198},{8,4},{10,202},{12,8},{14,206},{16,12... | collective-permute-start | bytes 786440 | tf_op jit(solution)/shard_map/ppermute | solution.py:32
  26.8 3.9 %collective-permute-done.6 = bf16[4,256,128]{2,1,0:T(8,128)(2,1)S(1)} collective-permute-done((bf16[4,256,128]{2,1,0:T(8,128)(2,1)S(1)}, bf16[4,256,128]{2,1,0:T(8,128)(2,1)S(1)}, u32[]{:S(2)}, u32[]{:S(2)}) %collective-permute-start.6) | collective-permute-done | bytes 262176 | tf_op jit(solution)/shard_map/ppermute | solution.py:32
  30.8 1.8 %collective-permute-start = (s32[3,65]{1,0:T(4,128)S(1)}, s32[3,65]{1,0:T(4,128)S(1)}, u32[]{:S(2)}, u32[]{:S(2)}) collective-permute-start(s32[3,65]{1,0:T(4,128)S(1)} %pad_add_fusion.1), channel_id=1, source_target_pairs={{0,2},{2,0},{4,6},{6,4},{8,10},{10,8},{12,14},{14,12},{16,18},{18,... | collective-permute-start | bytes 2348 | tf_op jit(solution)/shard_map/ppermute | solution.py:32
  32.7 4.8 %collective-permute-done.7 = bf16[4,256,128]{2,1,0:T(8,128)(2,1)S(1)} collective-permute-done((bf16[4,256,128]{2,1,0:T(8,128)(2,1)S(1)}, bf16[4,256,128]{2,1,0:T(8,128)(2,1)S(1)}, u32[]{:S(2)}, u32[]{:S(2)}) %collective-permute-start.7) | collective-permute-done | bytes 262176 | tf_op jit(solution)/shard_map/ppermute | solution.py:32
  37.5 0.1 collective-permute-start.9
  37.6 2.7 %collective-permute-start.8 = (bf16[16,256,128]{2,1,0:T(8,128)(2,1)S(1)}, bf16[16,256,128]{2,1,0:T(8,128)(2,1)S(1)}, u32[]{:S(2)}, u32[]{:S(2)}) collective-permute-start(bf16[16,256,128]{2,1,0:T(8,128)(2,1)S(1)} %constant_dynamic-update-slice_fusion.refs_0_), channel_id=1, source_target_pairs={{0,192},{2,30},{4,196},{6,2},{8,200},{10,6},{12,204},{14,10},{16,2... | collective-permute-start | bytes 3145736 | tf_op jit(solution)/shard_map/ppermute | solution.py:32
  40.3 0.1 pad_add_fusion
  40.4 0.2 slice_reduce_fusion
  40.6 12.2 %collective-permute-done.9.refs_2_ = bf16[16,256,128]{2,1,0:T(8,128)(2,1)S(1)} collective-permute-done((bf16[16,256,128]{2,1,0:T(8,128)(2,1)S(1)}, bf16[16,256,128]{2,1,0:T(8,128)(2,1)S(1)}, u32[]{:S(2)}, u32[]{:S(2)}) %collective-permute-start.9) | collective-permute-done | bytes 1048608 | tf_op jit(solution)/shard_map/ppermute | solution.py:32
  52.7 0.8 slice.32
  53.6 0.9 slice.33
  54.5 2.7 %collective-permute-start.14 = (bf16[8,256,128]{2,1,0:T(8,128)(2,1)}, bf16[8,256,128]{2,1,0:T(8,128)(2,1)}, u32[]{:S(2)}, u32[]{:S(2)}) collective-permute-start(bf16[8,256,128]{2,1,0:T(8,128)(2,1)} %slice.33), channel_id=1, source_target_pairs={{0,192},{2,30},{4,196},{6,2},{8,200},{10,6},{12,204},{14,10},{16,2... | collective-permute-start | bytes 1572872 | tf_op jit(solution)/shard_map/ppermute | solution.py:32
  57.1 0.3 select_reduce_fusion
  57.4 0.1 sub.34
  57.5 5.3 %shard_map.123 = (f32[256,512]{1,0:T(8,128)S(1)}, bf16[6,64,128,128]{3,2,1,0:T(8,128)(2,1)S(1)}) custom-call(s32[385]{0:T(512)S(1)} %pad_add_fusion.2.maps_ref, bf16[16,256,128]{2,1,0:T(8,128)(2,1)S(1)} %constant_dynamic-update-slice_fusion.refs_0_, bf16[16,256,128]{2,1,0:T(8,128)(2,1)S(1)} %collective-permute-done.8.refs_1_, ...), custom_call_target="tpu_custom_call" | custom-call | flops 1610612736 | bytes 16777216 | tf_op jit(solution)/shard_map/pallas_call | solution.py:254
  62.8 0.6 collective-permute-done.13.refs_1_
  63.4 0.2 collective-permute-done.14.refs_2_
  63.6 1.7 %shard_map.124.mine_ref = f32[256,512]{1,0:T(8,128)S(1)} custom-call(s32[385]{0:T(512)S(1)} %pad_add_fusion.2.maps_ref, f32[256,512]{1,0:T(8,128)S(1)} %get-tuple-element.12.refs_0_, bf16[8,256,128]{2,1,0:T(8,128)(2,1)} %collective-permute-done.13.refs_1_, bf16[8,256,128]{2,1,0:T(8,128)(2,1)} %collective-permute-done.14.refs_2_, ...), custom_call_target="tpu_custom_call" | custom-call | flops 536870912 | bytes 16777216 | tf_op jit(solution)/shard_map/pallas_call | solution.py:254
  65.3 5.5 %collective-permute-start.15 = (f32[256,512]{1,0:T(8,128)S(1)}, f32[256,512]{1,0:T(8,128)S(1)}, u32[]{:S(2)}, u32[]{:S(2)}) collective-permute-start(f32[256,512]{1,0:T(8,128)S(1)} %shard_map.124.mine_ref), channel_id=1, source_target_pairs={{0,2},{2,0},{4,6},{6,4},{8,10},{10,8},{12,14},{14,12},{16,18},{18,... | collective-permute-start | bytes 1572872 | tf_op jit(solution)/shard_map/ppermute | solution.py:32
  70.9 1.5 %collective-permute-done.15.theirs_ref = f32[256,512]{1,0:T(8,128)S(1)} collective-permute-done((f32[256,512]{1,0:T(8,128)S(1)}, f32[256,512]{1,0:T(8,128)S(1)}, u32[]{:S(2)}, u32[]{:S(2)}) %collective-permute-start.15) | collective-permute-done | bytes 524320 | tf_op jit(solution)/shard_map/ppermute | solution.py:32
  72.4 3.0 %shard_map.125 = (f32[8,256,128]{2,1,0:T(8,128)S(1)}, f32[8,256,128]{2,1,0:T(8,128)S(1)}, bf16[8,256,128]{2,1,0:T(8,128)(2,1)S(1)}, f32[8,256,128]{2,1,0:T(8,128...) custom-call(s32[385]{0:T(512)S(1)} %pad_add_fusion.2.maps_ref, ...), custom_call_target="tpu_custom_call" | custom-call | flops 2147483648 | bytes 16777216 | tf_op jit(solution)/shard_map/pallas_call | solution.py:254
  75.4 0.1 collective-permute-start.20
  75.5 2.7 %collective-permute-start.17 = (bf16[8,256,128]{2,1,0:T(8,128)(2,1)S(1)}, bf16[8,256,128]{2,1,0:T(8,128)(2,1)S(1)}, u32[]{:S(2)}, u32[]{:S(2)}) collective-permute-start(bf16[8,256,128]{2,1,0:T(8,128)(2,1)S(1)} %get-tuple-element.17), channel_id=1, source_target_pairs={{0,192},{2,30},{4,196},{6,2},{8,200},{10,6},{12,204},{14,10},{16,2... | collective-permute-start | bytes 1572872 | tf_op jit(solution)/shard_map/ppermute | solution.py:32
  78.2 6.8 %collective-permute-done.20 = bf16[8,256,128]{2,1,0:T(8,128)(2,1)S(1)} collective-permute-done((bf16[8,256,128]{2,1,0:T(8,128)(2,1)S(1)}, bf16[8,256,128]{2,1,0:T(8,128)(2,1)S(1)}, u32[]{:S(2)}, u32[]{:S(2)}) %collective-permute-start.20) | collective-permute-done | bytes 524320 | tf_op jit(solution)/shard_map/ppermute | solution.py:32
  85.0 0.1 add_convert_fusion
  85.2 0.1 collective-permute-start.21
  85.2 0.3 collective-permute-start.16
  85.6 0.1 add_convert_fusion.1
  85.7 2.8 %collective-permute-start.18 = (bf16[8,256,128]{2,1,0:T(8,128)(2,1)S(1)}, bf16[8,256,128]{2,1,0:T(8,128)(2,1)S(1)}, u32[]{:S(2)}, u32[]{:S(2)}) collective-permute-start(bf16[8,256,128]{2,1,0:T(8,128)(2,1)S(1)} %add_convert_fusion.1), channel_id=1, source_target_pairs={{0,192},{2,30},{4,196},{6,2},{8,200},{10,6},{12,204},{14,10},{16,2... | collective-permute-start | bytes 1572872 | tf_op jit(solution)/shard_map/ppermute | solution.py:32
  88.4 1.5 %collective-permute-done.22 = bf16[8,256,128]{2,1,0:T(8,128)(2,1)S(1)} collective-permute-done((bf16[8,256,128]{2,1,0:T(8,128)(2,1)S(1)}, bf16[8,256,128]{2,1,0:T(8,128)(2,1)S(1)}, u32[]{:S(2)}, u32[]{:S(2)}) %collective-permute-start.22) | collective-permute-done | bytes 524320 | tf_op jit(solution)/shard_map/ppermute | solution.py:32
  89.9 4.9 %collective-permute-done.21 = bf16[8,256,128]{2,1,0:T(8,128)(2,1)S(1)} collective-permute-done((bf16[8,256,128]{2,1,0:T(8,128)(2,1)S(1)}, bf16[8,256,128]{2,1,0:T(8,128)(2,1)S(1)}, u32[]{:S(2)}, u32[]{:S(2)}) %collective-permute-start.21) | collective-permute-done | bytes 524320 | tf_op jit(solution)/shard_map/ppermute | solution.py:32
  94.8 0.2 convert_add_fusion
  95.0 3.5 %collective-permute-start.23 = (bf16[4,256,128]{2,1,0:T(8,128)(2,1)S(1)}, bf16[4,256,128]{2,1,0:T(8,128)(2,1)S(1)}, u32[]{:S(2)}, u32[]{:S(2)}) collective-permute-start(bf16[4,256,128]{2,1,0:T(8,128)(2,1)S(1)} %split.52), channel_id=1, source_target_pairs={{0,28},{2,194},{4,0},{6,198},{8,4},{10,202},{12,8},{14,206},{16,12... | collective-permute-start | bytes 786440 | tf_op jit(solution)/shard_map/ppermute | solution.py:32
  98.5 1.9 %collective-permute-done.16 = bf16[8,256,128]{2,1,0:T(8,128)(2,1)S(1)} collective-permute-done((bf16[8,256,128]{2,1,0:T(8,128)(2,1)S(1)}, bf16[8,256,128]{2,1,0:T(8,128)(2,1)S(1)}, u32[]{:S(2)}, u32[]{:S(2)}) %collective-permute-start.16) | collective-permute-done | bytes 524320 | tf_op jit(solution)/shard_map/ppermute | solution.py:32
  100.4 0.1 convert_add_fusion.1
  100.6 0.6 collective-permute-start.19
  101.2 0.6 collective-permute-done.23
  101.9 3.2 %collective-permute-start.24 = (bf16[4,256,128]{2,1,0:T(8,128)(2,1)S(1)}, bf16[4,256,128]{2,1,0:T(8,128)(2,1)S(1)}, u32[]{:S(2)}, u32[]{:S(2)}) collective-permute-start(bf16[4,256,128]{2,1,0:T(8,128)(2,1)S(1)} %fusion), channel_id=1, source_target_pairs={{0,28},{2,194},{4,0},{6,198},{8,4},{10,202},{12,8},{14,206},{16,12... | collective-permute-start | bytes 786440 | tf_op jit(solution)/shard_map/ppermute | solution.py:32
  105.1 2.8 %collective-permute-done.19 = bf16[4,256,128]{2,1,0:T(8,128)(2,1)S(1)} collective-permute-done((bf16[4,256,128]{2,1,0:T(8,128)(2,1)S(1)}, bf16[4,256,128]{2,1,0:T(8,128)(2,1)S(1)}, u32[]{:S(2)}, u32[]{:S(2)}) %collective-permute-start.19) | collective-permute-done | bytes 262176 | tf_op jit(solution)/shard_map/ppermute | solution.py:32
  107.8 0.6 collective-permute-done.24
  108.4 0.1 fusion.13
  108.5 1.0 collective-permute-start.25
  109.5 0.3 collective-permute-start.26
  109.8 5.4 %collective-permute-start.27 = (bf16[256,128]{1,0:T(8,128)(2,1)S(1)}, bf16[256,128]{1,0:T(8,128)(2,1)S(1)}, u32[]{:S(2)}, u32[]{:S(2)}) collective-permute-start(bf16[256,128]{1,0:T(8,128)(2,1)S(1)} %get-tuple-element.25), channel_id=1, source_target_pairs={{0,48},{2,50},{4,52},{6,54},{8,56},{10,58},{12,60},{14,62},{16,32}... | collective-permute-start | bytes 196616 | tf_op jit(solution)/shard_map/ppermute | solution.py:32
  115.2 0.5 collective-permute-done.25
  115.7 4.0 %collective-permute-done.27 = bf16[256,128]{1,0:T(8,128)(2,1)S(1)} collective-permute-done((bf16[256,128]{1,0:T(8,128)(2,1)S(1)}, bf16[256,128]{1,0:T(8,128)(2,1)S(1)}, u32[]{:S(2)}, u32[]{:S(2)}) %collective-permute-start.27) | collective-permute-done | bytes 65568 | tf_op jit(solution)/shard_map/ppermute | solution.py:32
  119.7 0.1 shard_map.126
  119.8 1.7 %collective-permute-start.28 = (bf16[64,256]{1,0:T(8,128)(2,1)S(1)}, bf16[64,256]{1,0:T(8,128)(2,1)S(1)}, u32[]{:S(2)}, u32[]{:S(2)}) collective-permute-start(bf16[64,256]{1,0:T(8,128)(2,1)S(1)} %broadcast_select_fusion.1), channel_id=1, source_target_pairs={{0,2},{2,0},{4,6},{6,4},{8,10},{10,8},{12,14},{14,12},{16,18},{18,... | collective-permute-start | bytes 98312 | tf_op jit(solution)/shard_map/ppermute | solution.py:32
  121.5 0.9 collective-permute-done.28
  122.4 0.6 select_bitcast_fusion
  (42 shorter events, 0.7 us)
Async XLA Ops:
  0.6 39.7 %copy-start.2 = (s32[1,64]{1,0:T(1,128)S(1)}, s32[1,64]{1,0:T(1,128)}, u32[]{:S(2)}) copy-start(s32[1,64]{1,0:T(1,128)} %param.14) | copy-start | bytes 772
  0.6 39.6 %copy-start.1 = (s32[1,64]{1,0:T(1,128)S(1)}, s32[1,64]{1,0:T(1,128)}, u32[]{:S(2)}) copy-start(s32[1,64]{1,0:T(1,128)} %param.17) | copy-start | bytes 772
  0.7 39.6 %copy-start = (s32[1,64]{1,0:T(1,128)S(1)}, s32[1,64]{1,0:T(1,128)}, u32[]{:S(2)}) copy-start(s32[1,64]{1,0:T(1,128)} %param.20) | copy-start | bytes 772
  1.5 5.9 %collective-permute-start.1 = (bf16[64,256]{1,0:T(8,128)(2,1)S(1)}, bf16[64,256]{1,0:T(8,128)(2,1)S(1)}, u32[]{:S(2)}, u32[]{:S(2)}) collective-permute-start(bf16[64,256]{1,0:T(8,128)(2,1)S(1)} %select_bitcast_fusion.2), channel_id=1, source_target_pairs={{0,2},{2,0},{4,6},{6,4},{8,10},{10,8},{12,14},{14,12},{16,18},{18,... | collective-permute-start | bytes 98312 | tf_op jit(solution)/shard_map/ppermute | solution.py:32
  4.7 52.8 %collective-permute-start.10 = (bf16[64,128,128]{2,1,0:T(8,128)(2,1)}, bf16[64,128,128]{2,1,0:T(8,128)(2,1)}, u32[]{:S(2)}, u32[]{:S(2)}) collective-permute-start(bf16[64,128,128]{2,1,0:T(8,128)(2,1)} %refs_3_.1), channel_id=1, source_target_pairs={{0,2},{2,0},{4,6},{6,4},{8,10},{10,8},{12,14},{14,12},{16,18},{18,... | collective-permute-start | bytes 6291464 | tf_op jit(solution)/shard_map/ppermute | solution.py:32
  4.8 52.7 %collective-permute-start.11 = (bf16[64,128,128]{2,1,0:T(8,128)(2,1)}, bf16[64,128,128]{2,1,0:T(8,128)(2,1)}, u32[]{:S(2)}, u32[]{:S(2)}) collective-permute-start(bf16[64,128,128]{2,1,0:T(8,128)(2,1)} %refs_4_.1), channel_id=1, source_target_pairs={{0,2},{2,0},{4,6},{6,4},{8,10},{10,8},{12,14},{14,12},{16,18},{18,... | collective-permute-start | bytes 6291464 | tf_op jit(solution)/shard_map/ppermute | solution.py:32
  8.2 7.7 %collective-permute-start.2 = (bf16[1,256,128]{2,1,0:T(8,128)(2,1)S(1)}, bf16[1,256,128]{2,1,0:T(8,128)(2,1)S(1)}, u32[]{:S(2)}, u32[]{:S(2)}) collective-permute-start(bf16[1,256,128]{2,1,0:T(8,128)(2,1)S(1)} %bitcast.32), channel_id=1, source_target_pairs={{0,16},{2,18},{4,20},{6,22},{8,24},{10,26},{12,28},{14,30},{16,0},... | collective-permute-start | bytes 196616 | tf_op jit(solution)/shard_map/ppermute | solution.py:32
  13.5 3.3 %collective-permute-start.3 = (bf16[1,256,128]{2,1,0:T(8,128)(2,1)S(1)}, bf16[1,256,128]{2,1,0:T(8,128)(2,1)S(1)}, u32[]{:S(2)}, u32[]{:S(2)}) collective-permute-start(bf16[1,256,128]{2,1,0:T(8,128)(2,1)S(1)} %bitcast.33), channel_id=1, source_target_pairs={{0,32},{2,34},{4,36},{6,38},{8,40},{10,42},{12,44},{14,46},{16,48}... | collective-permute-start | bytes 196616 | tf_op jit(solution)/shard_map/ppermute | solution.py:32
  14.7 9.2 %collective-permute-start.4 = (bf16[1,256,128]{2,1,0:T(8,128)(2,1)S(1)}, bf16[1,256,128]{2,1,0:T(8,128)(2,1)S(1)}, u32[]{:S(2)}, u32[]{:S(2)}) collective-permute-start(bf16[1,256,128]{2,1,0:T(8,128)(2,1)S(1)} %bitcast.34), channel_id=1, source_target_pairs={{0,48},{2,50},{4,52},{6,54},{8,56},{10,58},{12,60},{14,62},{16,32}... | collective-permute-start | bytes 196616 | tf_op jit(solution)/shard_map/ppermute | solution.py:32
  15.8 41.7 %collective-permute-start.12 = (bf16[64,128,128]{2,1,0:T(8,128)(2,1)}, bf16[64,128,128]{2,1,0:T(8,128)(2,1)}, u32[]{:S(2)}, u32[]{:S(2)}) collective-permute-start(bf16[64,128,128]{2,1,0:T(8,128)(2,1)} %refs_7_.1), channel_id=1, source_target_pairs={{0,2},{2,0},{4,6},{6,4},{8,10},{10,8},{12,14},{14,12},{16,18},{18,... | collective-permute-start | bytes 6291464 | tf_op jit(solution)/shard_map/ppermute | solution.py:32
  23.9 6.9 %collective-permute-start.6 = (bf16[4,256,128]{2,1,0:T(8,128)(2,1)S(1)}, bf16[4,256,128]{2,1,0:T(8,128)(2,1)S(1)}, u32[]{:S(2)}, u32[]{:S(2)}) collective-permute-start(bf16[4,256,128]{2,1,0:T(8,128)(2,1)S(1)} %pad_maximum_fusion), channel_id=1, source_target_pairs={{0,4},{2,66},{4,8},{6,70},{8,12},{10,74},{12,16},{14,78},{16,20},{... | collective-permute-start | bytes 786440 | tf_op jit(solution)/shard_map/ppermute | solution.py:32
  25.3 5.5 %collective-permute-start.5 = (bf16[4,256,128]{2,1,0:T(8,128)(2,1)S(1)}, bf16[4,256,128]{2,1,0:T(8,128)(2,1)S(1)}, u32[]{:S(2)}, u32[]{:S(2)}) collective-permute-start(bf16[4,256,128]{2,1,0:T(8,128)(2,1)S(1)} %pad_maximum_fusion), channel_id=1, source_target_pairs={{0,28},{2,194},{4,0},{6,198},{8,4},{10,202},{12,8},{14,206},{16,12... | collective-permute-start | bytes 786440 | tf_op jit(solution)/shard_map/ppermute | solution.py:32
  30.7 6.7 %collective-permute-start.7 = (bf16[4,256,128]{2,1,0:T(8,128)(2,1)S(1)}, bf16[4,256,128]{2,1,0:T(8,128)(2,1)S(1)}, u32[]{:S(2)}, u32[]{:S(2)}) collective-permute-start(bf16[4,256,128]{2,1,0:T(8,128)(2,1)S(1)} %collective-permute-done.6), channel_id=1, source_target_pairs={{0,4},{2,66},{4,8},{6,70},{8,12},{10,74},{12,16},{14,78},{16,20},{... | collective-permute-start | bytes 786440 | tf_op jit(solution)/shard_map/ppermute | solution.py:32
  30.8 6.8 %collective-permute-start = (s32[3,65]{1,0:T(4,128)S(1)}, s32[3,65]{1,0:T(4,128)S(1)}, u32[]{:S(2)}, u32[]{:S(2)}) collective-permute-start(s32[3,65]{1,0:T(4,128)S(1)} %pad_add_fusion.1), channel_id=1, source_target_pairs={{0,2},{2,0},{4,6},{6,4},{8,10},{10,8},{12,14},{14,12},{16,18},{18,... | collective-permute-start | bytes 2348 | tf_op jit(solution)/shard_map/ppermute | solution.py:32
  37.5 15.2 %collective-permute-start.9 = (bf16[16,256,128]{2,1,0:T(8,128)(2,1)S(1)}, bf16[16,256,128]{2,1,0:T(8,128)(2,1)S(1)}, u32[]{:S(2)}, u32[]{:S(2)}) collective-permute-start(bf16[16,256,128]{2,1,0:T(8,128)(2,1)S(1)} %constant_dynamic-update-slice_fusion.refs_0_), channel_id=1, source_target_pairs={{0,64},{2,6},{4,68},{6,10},{8,72},{10,14},{12,76},{14,18},{16,80},... | collective-permute-start | bytes 3145736 | tf_op jit(solution)/shard_map/ppermute | solution.py:32
  37.6 16.0 %collective-permute-start.8 = (bf16[16,256,128]{2,1,0:T(8,128)(2,1)S(1)}, bf16[16,256,128]{2,1,0:T(8,128)(2,1)S(1)}, u32[]{:S(2)}, u32[]{:S(2)}) collective-permute-start(bf16[16,256,128]{2,1,0:T(8,128)(2,1)S(1)} %constant_dynamic-update-slice_fusion.refs_0_), channel_id=1, source_target_pairs={{0,192},{2,30},{4,196},{6,2},{8,200},{10,6},{12,204},{14,10},{16,2... | collective-permute-start | bytes 3145736 | tf_op jit(solution)/shard_map/ppermute | solution.py:32
  53.6 9.9 %collective-permute-start.13 = (bf16[8,256,128]{2,1,0:T(8,128)(2,1)}, bf16[8,256,128]{2,1,0:T(8,128)(2,1)}, u32[]{:S(2)}, u32[]{:S(2)}) collective-permute-start(bf16[8,256,128]{2,1,0:T(8,128)(2,1)} %slice.32), channel_id=1, source_target_pairs={{0,64},{2,6},{4,68},{6,10},{8,72},{10,14},{12,76},{14,18},{16,80},... | collective-permute-start | bytes 1572872 | tf_op jit(solution)/shard_map/ppermute | solution.py:32
  54.5 9.1 %collective-permute-start.14 = (bf16[8,256,128]{2,1,0:T(8,128)(2,1)}, bf16[8,256,128]{2,1,0:T(8,128)(2,1)}, u32[]{:S(2)}, u32[]{:S(2)}) collective-permute-start(bf16[8,256,128]{2,1,0:T(8,128)(2,1)} %slice.33), channel_id=1, source_target_pairs={{0,192},{2,30},{4,196},{6,2},{8,200},{10,6},{12,204},{14,10},{16,2... | collective-permute-start | bytes 1572872 | tf_op jit(solution)/shard_map/ppermute | solution.py:32
  65.3 7.1 %collective-permute-start.15 = (f32[256,512]{1,0:T(8,128)S(1)}, f32[256,512]{1,0:T(8,128)S(1)}, u32[]{:S(2)}, u32[]{:S(2)}) collective-permute-start(f32[256,512]{1,0:T(8,128)S(1)} %shard_map.124.mine_ref), channel_id=1, source_target_pairs={{0,2},{2,0},{4,6},{6,4},{8,10},{10,8},{12,14},{14,12},{16,18},{18,... | collective-permute-start | bytes 1572872 | tf_op jit(solution)/shard_map/ppermute | solution.py:32
  75.4 9.6 %collective-permute-start.20 = (bf16[8,256,128]{2,1,0:T(8,128)(2,1)S(1)}, bf16[8,256,128]{2,1,0:T(8,128)(2,1)S(1)}, u32[]{:S(2)}, u32[]{:S(2)}) collective-permute-start(bf16[8,256,128]{2,1,0:T(8,128)(2,1)S(1)} %get-tuple-element.20), channel_id=1, source_target_pairs={{0,64},{2,6},{4,68},{6,10},{8,72},{10,14},{12,76},{14,18},{16,80},... | collective-permute-start | bytes 1572872 | tf_op jit(solution)/shard_map/ppermute | solution.py:32
  75.5 10.1 %collective-permute-start.17 = (bf16[8,256,128]{2,1,0:T(8,128)(2,1)S(1)}, bf16[8,256,128]{2,1,0:T(8,128)(2,1)S(1)}, u32[]{:S(2)}, u32[]{:S(2)}) collective-permute-start(bf16[8,256,128]{2,1,0:T(8,128)(2,1)S(1)} %get-tuple-element.17), channel_id=1, source_target_pairs={{0,192},{2,30},{4,196},{6,2},{8,200},{10,6},{12,204},{14,10},{16,2... | collective-permute-start | bytes 1572872 | tf_op jit(solution)/shard_map/ppermute | solution.py:32
  78.2 11.7 %collective-permute-start.22 = (bf16[8,256,128]{2,1,0:T(8,128)(2,1)S(1)}, bf16[8,256,128]{2,1,0:T(8,128)(2,1)S(1)}, u32[]{:S(2)}, u32[]{:S(2)}) collective-permute-start(bf16[8,256,128]{2,1,0:T(8,128)(2,1)S(1)} %get-tuple-element.21), channel_id=1, source_target_pairs={{0,192},{2,30},{4,196},{6,2},{8,200},{10,6},{12,204},{14,10},{16,2... | collective-permute-start | bytes 1572872 | tf_op jit(solution)/shard_map/ppermute | solution.py:32
  85.2 9.6 %collective-permute-start.21 = (bf16[8,256,128]{2,1,0:T(8,128)(2,1)S(1)}, bf16[8,256,128]{2,1,0:T(8,128)(2,1)S(1)}, u32[]{:S(2)}, u32[]{:S(2)}) collective-permute-start(bf16[8,256,128]{2,1,0:T(8,128)(2,1)S(1)} %add_convert_fusion), channel_id=1, source_target_pairs={{0,64},{2,6},{4,68},{6,10},{8,72},{10,14},{12,76},{14,18},{16,80},... | collective-permute-start | bytes 1572872 | tf_op jit(solution)/shard_map/ppermute | solution.py:32
  85.2 15.1 %collective-permute-start.16 = (bf16[8,256,128]{2,1,0:T(8,128)(2,1)S(1)}, bf16[8,256,128]{2,1,0:T(8,128)(2,1)S(1)}, u32[]{:S(2)}, u32[]{:S(2)}) collective-permute-start(bf16[8,256,128]{2,1,0:T(8,128)(2,1)S(1)} %get-tuple-element.15), channel_id=1, source_target_pairs={{0,64},{2,6},{4,68},{6,10},{8,72},{10,14},{12,76},{14,18},{16,80},... | collective-permute-start | bytes 1572872 | tf_op jit(solution)/shard_map/ppermute | solution.py:32
  85.7 14.7 %collective-permute-start.18 = (bf16[8,256,128]{2,1,0:T(8,128)(2,1)S(1)}, bf16[8,256,128]{2,1,0:T(8,128)(2,1)S(1)}, u32[]{:S(2)}, u32[]{:S(2)}) collective-permute-start(bf16[8,256,128]{2,1,0:T(8,128)(2,1)S(1)} %add_convert_fusion.1), channel_id=1, source_target_pairs={{0,192},{2,30},{4,196},{6,2},{8,200},{10,6},{12,204},{14,10},{16,2... | collective-permute-start | bytes 1572872 | tf_op jit(solution)/shard_map/ppermute | solution.py:32
  95.0 6.8 %collective-permute-start.23 = (bf16[4,256,128]{2,1,0:T(8,128)(2,1)S(1)}, bf16[4,256,128]{2,1,0:T(8,128)(2,1)S(1)}, u32[]{:S(2)}, u32[]{:S(2)}) collective-permute-start(bf16[4,256,128]{2,1,0:T(8,128)(2,1)S(1)} %split.52), channel_id=1, source_target_pairs={{0,28},{2,194},{4,0},{6,198},{8,4},{10,202},{12,8},{14,206},{16,12... | collective-permute-start | bytes 786440 | tf_op jit(solution)/shard_map/ppermute | solution.py:32
  100.6 7.3 %collective-permute-start.19 = (bf16[4,256,128]{2,1,0:T(8,128)(2,1)S(1)}, bf16[4,256,128]{2,1,0:T(8,128)(2,1)S(1)}, u32[]{:S(2)}, u32[]{:S(2)}) collective-permute-start(bf16[4,256,128]{2,1,0:T(8,128)(2,1)S(1)} %split.53), channel_id=1, source_target_pairs={{0,4},{2,66},{4,8},{6,70},{8,12},{10,74},{12,16},{14,78},{16,20},{... | collective-permute-start | bytes 786440 | tf_op jit(solution)/shard_map/ppermute | solution.py:32
  101.9 6.5 %collective-permute-start.24 = (bf16[4,256,128]{2,1,0:T(8,128)(2,1)S(1)}, bf16[4,256,128]{2,1,0:T(8,128)(2,1)S(1)}, u32[]{:S(2)}, u32[]{:S(2)}) collective-permute-start(bf16[4,256,128]{2,1,0:T(8,128)(2,1)S(1)} %fusion), channel_id=1, source_target_pairs={{0,28},{2,194},{4,0},{6,198},{8,4},{10,202},{12,8},{14,206},{16,12... | collective-permute-start | bytes 786440 | tf_op jit(solution)/shard_map/ppermute | solution.py:32
  108.5 7.1 %collective-permute-start.25 = (bf16[256,128]{1,0:T(8,128)(2,1)S(1)}, bf16[256,128]{1,0:T(8,128)(2,1)S(1)}, u32[]{:S(2)}, u32[]{:S(2)}) collective-permute-start(bf16[256,128]{1,0:T(8,128)(2,1)S(1)} %get-tuple-element.24), channel_id=1, source_target_pairs={{0,16},{2,18},{4,20},{6,22},{8,24},{10,26},{12,28},{14,30},{16,0},... | collective-permute-start | bytes 196616 | tf_op jit(solution)/shard_map/ppermute | solution.py:32
  109.5 6.2 %collective-permute-start.26 = (bf16[256,128]{1,0:T(8,128)(2,1)S(1)}, bf16[256,128]{1,0:T(8,128)(2,1)S(1)}, u32[]{:S(2)}, u32[]{:S(2)}) collective-permute-start(bf16[256,128]{1,0:T(8,128)(2,1)S(1)} %get-tuple-element.26), channel_id=1, source_target_pairs={{0,32},{2,34},{4,36},{6,38},{8,40},{10,42},{12,44},{14,46},{16,48}... | collective-permute-start | bytes 196616 | tf_op jit(solution)/shard_map/ppermute | solution.py:32
  109.8 9.9 %collective-permute-start.27 = (bf16[256,128]{1,0:T(8,128)(2,1)S(1)}, bf16[256,128]{1,0:T(8,128)(2,1)S(1)}, u32[]{:S(2)}, u32[]{:S(2)}) collective-permute-start(bf16[256,128]{1,0:T(8,128)(2,1)S(1)} %get-tuple-element.25), channel_id=1, source_target_pairs={{0,48},{2,50},{4,52},{6,54},{8,56},{10,58},{12,60},{14,62},{16,32}... | collective-permute-start | bytes 196616 | tf_op jit(solution)/shard_map/ppermute | solution.py:32
  119.8 2.6 %collective-permute-start.28 = (bf16[64,256]{1,0:T(8,128)(2,1)S(1)}, bf16[64,256]{1,0:T(8,128)(2,1)S(1)}, u32[]{:S(2)}, u32[]{:S(2)}) collective-permute-start(bf16[64,256]{1,0:T(8,128)(2,1)S(1)} %broadcast_select_fusion.1), channel_id=1, source_target_pairs={{0,2},{2,0},{4,6},{6,4},{8,10},{10,8},{12,14},{14,12},{16,18},{18,... | collective-permute-start | bytes 98312 | tf_op jit(solution)/shard_map/ppermute | solution.py:32

commit v8 on v7

--- a/solution.py
+++ b/solution.py
@@ -283,7 +283,8 @@
     batch = tokens.shape[0]
 
     tokens, grad_out = tokens.T, grad_out.T
-    own, other = jnp.where(first, tokens, grad_out), jnp.where(first, grad_out, tokens)
+    forward = core == 1
+    own, other = jnp.where(forward, tokens, grad_out), jnp.where(forward, grad_out, tokens)
     other = shift(other, "c", 1)
     block = jnp.concatenate([jnp.where(first, own, other), jnp.where(first, other, own)])
     block = transpose(block).reshape(1, batch, BLOCK)
@@ -310,7 +311,7 @@
     places = lax.broadcasted_iota(jnp.int32, (6, SLOTS, SLOTS), 1)
     here = (position[:, None, :] == places) & (number < counts[:, :, None])
     maps = jnp.sum(jnp.where(here, number + 1, 0), axis=2) - 1
-    maps = jnp.concatenate([maps.reshape(6 * SLOTS), core[None]])
+    maps = jnp.concatenate([maps.reshape(6 * SLOTS), (1 - core)[None]])
 
     weights = (gate_blocks, up_blocks, shift(gate_blocks, "c", 1), shift(up_blocks, "c", 1))
     weights += (down_blocks, shift(down_blocks, "c", 1))
@@ -329,7 +330,7 @@
     low, high = jnp.split(total, 2)
     own, other = jnp.where(first, low, high), jnp.where(first, high, low)
     other = shift(other, "c", 1)
-    return jnp.where(first, own, other).T, jnp.where(first, other, own).T
+    return jnp.where(forward, own, other).T, jnp.where(forward, other, own).T
 
 
 def solution(mesh):

time: 123 us -> 125 us (1.016); the launches traced: 123 us -> 124 us
  starting transfers between devices: 48.6 us -> 52.1 us
  waiting for transfers between devices: 54.8 us -> 52.1 us
    ppermute x29, starting transfers between devices: 48.6 us -> 52.1 us  [permute(): return lax.ppermute(value, 'tp', pairs)]
    ppermute x29, waiting for transfers between devices: 54.8 us -> 52.1 us  [permute(): return lax.ppermute(value, 'tp', pairs)]
  transfers between devices with their start and end apart: 29 -> 29, of which waited for: 18 -> 16; matrix products, arithmetic and copies ran while one was open for 4% -> 4% of each run, Pallas kernels for 4% -> 5%
where the time goes in v8:
time: 125 us; the launch traced here: 124 us
  starting transfers between devices  52.1 us (42%)
  waiting for transfers between devices  52.1 us (42%)
  Pallas kernels  10.1 us (8%)
  other arithmetic  4.23 us (3%)
  between operations  2.86 us (2%)
  local copies, waits for them, and re-layouts  2.32 us (2%)
    ppermute x29, waiting for transfers between devices, permute(): return lax.ppermute(value, 'tp', pairs)  52.1 us
    ppermute x29, starting transfers between devices, permute(): return lax.ppermute(value, 'tp', pairs)  52.1 us
    pallas_call x3, Pallas kernels, call(): pl.pallas_call(kernel, out_shape=outs, in_specs=[pl.BlockSpec(memory_spac...  9.95 us
  transfers between devices with their start and end apart: 29, of which 16 were waited for; matrix products, arithmetic and copies ran while one was open for 4% of the time, Pallas kernels for 5%

profile of v8, /device:TPU:1, one launch (start us, length us, event | category | flops | bytes accessed | tf_op | source)
XLA Modules:
  0.0 123.7 jit_solution(5634585706624430859)
XLA Ops:
  0.7 0.8 select_bitcast_fusion.2
  1.4 3.2 %collective-permute-start.1 = (bf16[64,256]{1,0:T(8,128)(2,1)S(1)}, bf16[64,256]{1,0:T(8,128)(2,1)S(1)}, u32[]{:S(2)}, u32[]{:S(2)}) collective-permute-start(bf16[64,256]{1,0:T(8,128)(2,1)S(1)} %select_bitcast_fusion.2), channel_id=1, source_target_pairs={{0,2},{2,0},{4,6},{6,4},{8,10},{10,8},{12,14},{14,12},{16,18},{18,... | collective-permute-start | bytes 98312 | tf_op jit(solution)/shard_map/ppermute | solution.py:32
  4.7 0.1 collective-permute-start.10
  4.8 0.4 collective-permute-start.11
  7.1 0.1 pad_add_fusion.3
  7.2 0.1 copy.14
  7.3 0.8 bitcast_select_fusion.1
  8.1 0.1 shard_map.122
  8.2 5.3 %collective-permute-start.2 = (bf16[1,256,128]{2,1,0:T(8,128)(2,1)S(1)}, bf16[1,256,128]{2,1,0:T(8,128)(2,1)S(1)}, u32[]{:S(2)}, u32[]{:S(2)}) collective-permute-start(bf16[1,256,128]{2,1,0:T(8,128)(2,1)S(1)} %bitcast.32), channel_id=1, source_target_pairs={{0,16},{2,18},{4,20},{6,22},{8,24},{10,26},{12,28},{14,30},{16,0},... | collective-permute-start | bytes 196616 | tf_op jit(solution)/shard_map/ppermute | solution.py:32
  13.5 1.2 collective-permute-start.3
  14.7 0.2 collective-permute-start.4
  14.8 0.8 pad_add_fusion.1
  15.6 0.2 collective-permute-done.2
  15.8 1.0 collective-permute-start.12
  16.8 7.0 %collective-permute-done.4 = bf16[1,256,128]{2,1,0:T(8,128)(2,1)S(1)} collective-permute-done((bf16[1,256,128]{2,1,0:T(8,128)(2,1)S(1)}, bf16[1,256,128]{2,1,0:T(8,128)(2,1)S(1)}, u32[]{:S(2)}, u32[]{:S(2)}) %collective-permute-start.4) | collective-permute-done | bytes 65568 | tf_op jit(solution)/shard_map/ppermute | solution.py:32
  23.9 1.4 %collective-permute-start.6 = (bf16[4,256,128]{2,1,0:T(8,128)(2,1)S(1)}, bf16[4,256,128]{2,1,0:T(8,128)(2,1)S(1)}, u32[]{:S(2)}, u32[]{:S(2)}) collective-permute-start(bf16[4,256,128]{2,1,0:T(8,128)(2,1)S(1)} %pad_maximum_fusion), channel_id=1, source_target_pairs={{0,4},{2,66},{4,8},{6,70},{8,12},{10,74},{12,16},{14,78},{16,20},{... | collective-permute-start | bytes 786440 | tf_op jit(solution)/shard_map/ppermute | solution.py:32
  25.3 1.5 %collective-permute-start.5 = (bf16[4,256,128]{2,1,0:T(8,128)(2,1)S(1)}, bf16[4,256,128]{2,1,0:T(8,128)(2,1)S(1)}, u32[]{:S(2)}, u32[]{:S(2)}) collective-permute-start(bf16[4,256,128]{2,1,0:T(8,128)(2,1)S(1)} %pad_maximum_fusion), channel_id=1, source_target_pairs={{0,28},{2,194},{4,0},{6,198},{8,4},{10,202},{12,8},{14,206},{16,12... | collective-permute-start | bytes 786440 | tf_op jit(solution)/shard_map/ppermute | solution.py:32
  26.8 3.9 %collective-permute-done.6 = bf16[4,256,128]{2,1,0:T(8,128)(2,1)S(1)} collective-permute-done((bf16[4,256,128]{2,1,0:T(8,128)(2,1)S(1)}, bf16[4,256,128]{2,1,0:T(8,128)(2,1)S(1)}, u32[]{:S(2)}, u32[]{:S(2)}) %collective-permute-start.6) | collective-permute-done | bytes 262176 | tf_op jit(solution)/shard_map/ppermute | solution.py:32
  30.8 1.8 %collective-permute-start = (s32[3,65]{1,0:T(4,128)S(1)}, s32[3,65]{1,0:T(4,128)S(1)}, u32[]{:S(2)}, u32[]{:S(2)}) collective-permute-start(s32[3,65]{1,0:T(4,128)S(1)} %pad_add_fusion.1), channel_id=1, source_target_pairs={{0,2},{2,0},{4,6},{6,4},{8,10},{10,8},{12,14},{14,12},{16,18},{18,... | collective-permute-start | bytes 2348 | tf_op jit(solution)/shard_map/ppermute | solution.py:32
  32.7 4.8 %collective-permute-done.7 = bf16[4,256,128]{2,1,0:T(8,128)(2,1)S(1)} collective-permute-done((bf16[4,256,128]{2,1,0:T(8,128)(2,1)S(1)}, bf16[4,256,128]{2,1,0:T(8,128)(2,1)S(1)}, u32[]{:S(2)}, u32[]{:S(2)}) %collective-permute-start.7) | collective-permute-done | bytes 262176 | tf_op jit(solution)/shard_map/ppermute | solution.py:32
  37.5 0.1 collective-permute-start.9
  37.6 2.7 %collective-permute-start.8 = (bf16[16,256,128]{2,1,0:T(8,128)(2,1)S(1)}, bf16[16,256,128]{2,1,0:T(8,128)(2,1)S(1)}, u32[]{:S(2)}, u32[]{:S(2)}) collective-permute-start(bf16[16,256,128]{2,1,0:T(8,128)(2,1)S(1)} %constant_dynamic-update-slice_fusion.refs_0_), channel_id=1, source_target_pairs={{0,192},{2,30},{4,196},{6,2},{8,200},{10,6},{12,204},{14,10},{16,2... | collective-permute-start | bytes 3145736 | tf_op jit(solution)/shard_map/ppermute | solution.py:32
  40.3 0.1 pad_add_fusion
  40.4 0.2 slice_reduce_fusion
  40.6 12.2 %collective-permute-done.9.refs_2_ = bf16[16,256,128]{2,1,0:T(8,128)(2,1)S(1)} collective-permute-done((bf16[16,256,128]{2,1,0:T(8,128)(2,1)S(1)}, bf16[16,256,128]{2,1,0:T(8,128)(2,1)S(1)}, u32[]{:S(2)}, u32[]{:S(2)}) %collective-permute-start.9) | collective-permute-done | bytes 1048608 | tf_op jit(solution)/shard_map/ppermute | solution.py:32
  52.7 0.8 slice.32
  53.6 0.9 slice.33
  54.5 2.7 %collective-permute-start.14 = (bf16[8,256,128]{2,1,0:T(8,128)(2,1)}, bf16[8,256,128]{2,1,0:T(8,128)(2,1)}, u32[]{:S(2)}, u32[]{:S(2)}) collective-permute-start(bf16[8,256,128]{2,1,0:T(8,128)(2,1)} %slice.33), channel_id=1, source_target_pairs={{0,192},{2,30},{4,196},{6,2},{8,200},{10,6},{12,204},{14,10},{16,2... | collective-permute-start | bytes 1572872 | tf_op jit(solution)/shard_map/ppermute | solution.py:32
  57.1 0.3 select_reduce_fusion
  57.4 0.1 sub.37
  57.5 6.0 %shard_map.123 = (f32[256,512]{1,0:T(8,128)S(1)}, bf16[6,64,128,128]{3,2,1,0:T(8,128)(2,1)S(1)}) custom-call(s32[385]{0:T(512)S(1)} %pad_add_fusion.2.maps_ref, bf16[16,256,128]{2,1,0:T(8,128)(2,1)S(1)} %constant_dynamic-update-slice_fusion.refs_0_, bf16[16,256,128]{2,1,0:T(8,128)(2,1)S(1)} %collective-permute-done.8.refs_1_, ...), custom_call_target="tpu_custom_call" | custom-call | flops 1610612736 | bytes 16777216 | tf_op jit(solution)/shard_map/pallas_call | solution.py:254
  63.6 2.0 %shard_map.124.mine_ref = f32[256,512]{1,0:T(8,128)S(1)} custom-call(s32[385]{0:T(512)S(1)} %pad_add_fusion.2.maps_ref, f32[256,512]{1,0:T(8,128)S(1)} %get-tuple-element.12.refs_0_, bf16[8,256,128]{2,1,0:T(8,128)(2,1)} %collective-permute-done.13.refs_1_, bf16[8,256,128]{2,1,0:T(8,128)(2,1)} %collective-permute-done.14.refs_2_, ...), custom_call_target="tpu_custom_call" | custom-call | flops 536870912 | bytes 16777216 | tf_op jit(solution)/shard_map/pallas_call | solution.py:254
  65.6 5.0 %collective-permute-start.15 = (f32[256,512]{1,0:T(8,128)S(1)}, f32[256,512]{1,0:T(8,128)S(1)}, u32[]{:S(2)}, u32[]{:S(2)}) collective-permute-start(f32[256,512]{1,0:T(8,128)S(1)} %shard_map.124.mine_ref), channel_id=1, source_target_pairs={{0,2},{2,0},{4,6},{6,4},{8,10},{10,8},{12,14},{14,12},{16,18},{18,... | collective-permute-start | bytes 1572872 | tf_op jit(solution)/shard_map/ppermute | solution.py:32
  70.6 1.5 %collective-permute-done.15.theirs_ref = f32[256,512]{1,0:T(8,128)S(1)} collective-permute-done((f32[256,512]{1,0:T(8,128)S(1)}, f32[256,512]{1,0:T(8,128)S(1)}, u32[]{:S(2)}, u32[]{:S(2)}) %collective-permute-start.15) | collective-permute-done | bytes 524320 | tf_op jit(solution)/shard_map/ppermute | solution.py:32
  72.1 1.9 %shard_map.125 = (f32[8,256,128]{2,1,0:T(8,128)S(1)}, f32[8,256,128]{2,1,0:T(8,128)S(1)}, bf16[8,256,128]{2,1,0:T(8,128)(2,1)S(1)}, f32[8,256,128]{2,1,0:T(8,128...) custom-call(s32[385]{0:T(512)S(1)} %pad_add_fusion.2.maps_ref, ...), custom_call_target="tpu_custom_call" | custom-call | flops 2147483648 | bytes 16777216 | tf_op jit(solution)/shard_map/pallas_call | solution.py:254
  74.1 0.1 collective-permute-start.20
  74.2 2.7 %collective-permute-start.17 = (bf16[8,256,128]{2,1,0:T(8,128)(2,1)S(1)}, bf16[8,256,128]{2,1,0:T(8,128)(2,1)S(1)}, u32[]{:S(2)}, u32[]{:S(2)}) collective-permute-start(bf16[8,256,128]{2,1,0:T(8,128)(2,1)S(1)} %get-tuple-element.17), channel_id=1, source_target_pairs={{0,192},{2,30},{4,196},{6,2},{8,200},{10,6},{12,204},{14,10},{16,2... | collective-permute-start | bytes 1572872 | tf_op jit(solution)/shard_map/ppermute | solution.py:32
  76.9 6.8 %collective-permute-done.20 = bf16[8,256,128]{2,1,0:T(8,128)(2,1)S(1)} collective-permute-done((bf16[8,256,128]{2,1,0:T(8,128)(2,1)S(1)}, bf16[8,256,128]{2,1,0:T(8,128)(2,1)S(1)}, u32[]{:S(2)}, u32[]{:S(2)}) %collective-permute-start.20) | collective-permute-done | bytes 524320 | tf_op jit(solution)/shard_map/ppermute | solution.py:32
  83.7 0.1 add_convert_fusion
  83.8 0.1 collective-permute-start.21
  83.9 0.3 collective-permute-start.16
  84.2 0.1 add_convert_fusion.1
  84.4 2.8 %collective-permute-start.18 = (bf16[8,256,128]{2,1,0:T(8,128)(2,1)S(1)}, bf16[8,256,128]{2,1,0:T(8,128)(2,1)S(1)}, u32[]{:S(2)}, u32[]{:S(2)}) collective-permute-start(bf16[8,256,128]{2,1,0:T(8,128)(2,1)S(1)} %add_convert_fusion.1), channel_id=1, source_target_pairs={{0,192},{2,30},{4,196},{6,2},{8,200},{10,6},{12,204},{14,10},{16,2... | collective-permute-start | bytes 1572872 | tf_op jit(solution)/shard_map/ppermute | solution.py:32
  87.1 1.5 %collective-permute-done.22 = bf16[8,256,128]{2,1,0:T(8,128)(2,1)S(1)} collective-permute-done((bf16[8,256,128]{2,1,0:T(8,128)(2,1)S(1)}, bf16[8,256,128]{2,1,0:T(8,128)(2,1)S(1)}, u32[]{:S(2)}, u32[]{:S(2)}) %collective-permute-start.22) | collective-permute-done | bytes 524320 | tf_op jit(solution)/shard_map/ppermute | solution.py:32
  88.6 4.9 %collective-permute-done.21 = bf16[8,256,128]{2,1,0:T(8,128)(2,1)S(1)} collective-permute-done((bf16[8,256,128]{2,1,0:T(8,128)(2,1)S(1)}, bf16[8,256,128]{2,1,0:T(8,128)(2,1)S(1)}, u32[]{:S(2)}, u32[]{:S(2)}) %collective-permute-start.21) | collective-permute-done | bytes 524320 | tf_op jit(solution)/shard_map/ppermute | solution.py:32
  93.5 0.2 convert_add_fusion
  93.7 3.5 %collective-permute-start.23 = (bf16[4,256,128]{2,1,0:T(8,128)(2,1)S(1)}, bf16[4,256,128]{2,1,0:T(8,128)(2,1)S(1)}, u32[]{:S(2)}, u32[]{:S(2)}) collective-permute-start(bf16[4,256,128]{2,1,0:T(8,128)(2,1)S(1)} %split.52), channel_id=1, source_target_pairs={{0,28},{2,194},{4,0},{6,198},{8,4},{10,202},{12,8},{14,206},{16,12... | collective-permute-start | bytes 786440 | tf_op jit(solution)/shard_map/ppermute | solution.py:32
  97.2 1.9 %collective-permute-done.16 = bf16[8,256,128]{2,1,0:T(8,128)(2,1)S(1)} collective-permute-done((bf16[8,256,128]{2,1,0:T(8,128)(2,1)S(1)}, bf16[8,256,128]{2,1,0:T(8,128)(2,1)S(1)}, u32[]{:S(2)}, u32[]{:S(2)}) %collective-permute-start.16) | collective-permute-done | bytes 524320 | tf_op jit(solution)/shard_map/ppermute | solution.py:32
  99.1 0.1 convert_add_fusion.1
  99.3 0.6 collective-permute-start.19
  99.9 0.6 collective-permute-done.23
  100.6 3.2 %collective-permute-start.24 = (bf16[4,256,128]{2,1,0:T(8,128)(2,1)S(1)}, bf16[4,256,128]{2,1,0:T(8,128)(2,1)S(1)}, u32[]{:S(2)}, u32[]{:S(2)}) collective-permute-start(bf16[4,256,128]{2,1,0:T(8,128)(2,1)S(1)} %fusion), channel_id=1, source_target_pairs={{0,28},{2,194},{4,0},{6,198},{8,4},{10,202},{12,8},{14,206},{16,12... | collective-permute-start | bytes 786440 | tf_op jit(solution)/shard_map/ppermute | solution.py:32
  103.8 2.5 %collective-permute-done.19 = bf16[4,256,128]{2,1,0:T(8,128)(2,1)S(1)} collective-permute-done((bf16[4,256,128]{2,1,0:T(8,128)(2,1)S(1)}, bf16[4,256,128]{2,1,0:T(8,128)(2,1)S(1)}, u32[]{:S(2)}, u32[]{:S(2)}) %collective-permute-start.19) | collective-permute-done | bytes 262176 | tf_op jit(solution)/shard_map/ppermute | solution.py:32
  106.2 0.8 collective-permute-done.24
  107.1 0.1 fusion.13
  107.2 1.0 collective-permute-start.25
  108.2 0.3 collective-permute-start.26
  108.4 5.4 %collective-permute-start.27 = (bf16[256,128]{1,0:T(8,128)(2,1)S(1)}, bf16[256,128]{1,0:T(8,128)(2,1)S(1)}, u32[]{:S(2)}, u32[]{:S(2)}) collective-permute-start(bf16[256,128]{1,0:T(8,128)(2,1)S(1)} %get-tuple-element.25), channel_id=1, source_target_pairs={{0,48},{2,50},{4,52},{6,54},{8,56},{10,58},{12,60},{14,62},{16,32}... | collective-permute-start | bytes 196616 | tf_op jit(solution)/shard_map/ppermute | solution.py:32
  113.8 0.6 collective-permute-done.25
  114.4 1.9 %collective-permute-done.27 = bf16[256,128]{1,0:T(8,128)(2,1)S(1)} collective-permute-done((bf16[256,128]{1,0:T(8,128)(2,1)S(1)}, bf16[256,128]{1,0:T(8,128)(2,1)S(1)}, u32[]{:S(2)}, u32[]{:S(2)}) %collective-permute-start.27) | collective-permute-done | bytes 65568 | tf_op jit(solution)/shard_map/ppermute | solution.py:32
  116.4 0.1 shard_map.126
  116.5 5.7 %collective-permute-start.28 = (bf16[64,256]{1,0:T(8,128)(2,1)S(1)}, bf16[64,256]{1,0:T(8,128)(2,1)S(1)}, u32[]{:S(2)}, u32[]{:S(2)}) collective-permute-start(bf16[64,256]{1,0:T(8,128)(2,1)S(1)} %broadcast_select_fusion.1), channel_id=1, source_target_pairs={{0,2},{2,0},{4,6},{6,4},{8,10},{10,8},{12,14},{14,12},{16,18},{18,... | collective-permute-start | bytes 98312 | tf_op jit(solution)/shard_map/ppermute | solution.py:32
  122.2 0.9 collective-permute-done.28
  123.1 0.6 select_bitcast_fusion
  (42 shorter events, 0.6 us)
Async XLA Ops:
  0.6 39.7 %copy-start.2 = (s32[1,64]{1,0:T(1,128)S(1)}, s32[1,64]{1,0:T(1,128)}, u32[]{:S(2)}) copy-start(s32[1,64]{1,0:T(1,128)} %param.14) | copy-start | bytes 772
  0.6 39.6 %copy-start.1 = (s32[1,64]{1,0:T(1,128)S(1)}, s32[1,64]{1,0:T(1,128)}, u32[]{:S(2)}) copy-start(s32[1,64]{1,0:T(1,128)} %param.17) | copy-start | bytes 772
  0.7 39.6 %copy-start = (s32[1,64]{1,0:T(1,128)S(1)}, s32[1,64]{1,0:T(1,128)}, u32[]{:S(2)}) copy-start(s32[1,64]{1,0:T(1,128)} %param.20) | copy-start | bytes 772
  1.4 5.9 %collective-permute-start.1 = (bf16[64,256]{1,0:T(8,128)(2,1)S(1)}, bf16[64,256]{1,0:T(8,128)(2,1)S(1)}, u32[]{:S(2)}, u32[]{:S(2)}) collective-permute-start(bf16[64,256]{1,0:T(8,128)(2,1)S(1)} %select_bitcast_fusion.2), channel_id=1, source_target_pairs={{0,2},{2,0},{4,6},{6,4},{8,10},{10,8},{12,14},{14,12},{16,18},{18,... | collective-permute-start | bytes 98312 | tf_op jit(solution)/shard_map/ppermute | solution.py:32
  4.7 52.8 %collective-permute-start.10 = (bf16[64,128,128]{2,1,0:T(8,128)(2,1)}, bf16[64,128,128]{2,1,0:T(8,128)(2,1)}, u32[]{:S(2)}, u32[]{:S(2)}) collective-permute-start(bf16[64,128,128]{2,1,0:T(8,128)(2,1)} %refs_3_.1), channel_id=1, source_target_pairs={{0,2},{2,0},{4,6},{6,4},{8,10},{10,8},{12,14},{14,12},{16,18},{18,... | collective-permute-start | bytes 6291464 | tf_op jit(solution)/shard_map/ppermute | solution.py:32
  4.8 52.7 %collective-permute-start.11 = (bf16[64,128,128]{2,1,0:T(8,128)(2,1)}, bf16[64,128,128]{2,1,0:T(8,128)(2,1)}, u32[]{:S(2)}, u32[]{:S(2)}) collective-permute-start(bf16[64,128,128]{2,1,0:T(8,128)(2,1)} %refs_4_.1), channel_id=1, source_target_pairs={{0,2},{2,0},{4,6},{6,4},{8,10},{10,8},{12,14},{14,12},{16,18},{18,... | collective-permute-start | bytes 6291464 | tf_op jit(solution)/shard_map/ppermute | solution.py:32
  8.2 7.7 %collective-permute-start.2 = (bf16[1,256,128]{2,1,0:T(8,128)(2,1)S(1)}, bf16[1,256,128]{2,1,0:T(8,128)(2,1)S(1)}, u32[]{:S(2)}, u32[]{:S(2)}) collective-permute-start(bf16[1,256,128]{2,1,0:T(8,128)(2,1)S(1)} %bitcast.32), channel_id=1, source_target_pairs={{0,16},{2,18},{4,20},{6,22},{8,24},{10,26},{12,28},{14,30},{16,0},... | collective-permute-start | bytes 196616 | tf_op jit(solution)/shard_map/ppermute | solution.py:32
  13.5 3.3 %collective-permute-start.3 = (bf16[1,256,128]{2,1,0:T(8,128)(2,1)S(1)}, bf16[1,256,128]{2,1,0:T(8,128)(2,1)S(1)}, u32[]{:S(2)}, u32[]{:S(2)}) collective-permute-start(bf16[1,256,128]{2,1,0:T(8,128)(2,1)S(1)} %bitcast.33), channel_id=1, source_target_pairs={{0,32},{2,34},{4,36},{6,38},{8,40},{10,42},{12,44},{14,46},{16,48}... | collective-permute-start | bytes 196616 | tf_op jit(solution)/shard_map/ppermute | solution.py:32
  14.7 9.2 %collective-permute-start.4 = (bf16[1,256,128]{2,1,0:T(8,128)(2,1)S(1)}, bf16[1,256,128]{2,1,0:T(8,128)(2,1)S(1)}, u32[]{:S(2)}, u32[]{:S(2)}) collective-permute-start(bf16[1,256,128]{2,1,0:T(8,128)(2,1)S(1)} %bitcast.34), channel_id=1, source_target_pairs={{0,48},{2,50},{4,52},{6,54},{8,56},{10,58},{12,60},{14,62},{16,32}... | collective-permute-start | bytes 196616 | tf_op jit(solution)/shard_map/ppermute | solution.py:32
  15.8 41.7 %collective-permute-start.12 = (bf16[64,128,128]{2,1,0:T(8,128)(2,1)}, bf16[64,128,128]{2,1,0:T(8,128)(2,1)}, u32[]{:S(2)}, u32[]{:S(2)}) collective-permute-start(bf16[64,128,128]{2,1,0:T(8,128)(2,1)} %refs_7_.1), channel_id=1, source_target_pairs={{0,2},{2,0},{4,6},{6,4},{8,10},{10,8},{12,14},{14,12},{16,18},{18,... | collective-permute-start | bytes 6291464 | tf_op jit(solution)/shard_map/ppermute | solution.py:32
  23.9 6.9 %collective-permute-start.6 = (bf16[4,256,128]{2,1,0:T(8,128)(2,1)S(1)}, bf16[4,256,128]{2,1,0:T(8,128)(2,1)S(1)}, u32[]{:S(2)}, u32[]{:S(2)}) collective-permute-start(bf16[4,256,128]{2,1,0:T(8,128)(2,1)S(1)} %pad_maximum_fusion), channel_id=1, source_target_pairs={{0,4},{2,66},{4,8},{6,70},{8,12},{10,74},{12,16},{14,78},{16,20},{... | collective-permute-start | bytes 786440 | tf_op jit(solution)/shard_map/ppermute | solution.py:32
  25.3 5.5 %collective-permute-start.5 = (bf16[4,256,128]{2,1,0:T(8,128)(2,1)S(1)}, bf16[4,256,128]{2,1,0:T(8,128)(2,1)S(1)}, u32[]{:S(2)}, u32[]{:S(2)}) collective-permute-start(bf16[4,256,128]{2,1,0:T(8,128)(2,1)S(1)} %pad_maximum_fusion), channel_id=1, source_target_pairs={{0,28},{2,194},{4,0},{6,198},{8,4},{10,202},{12,8},{14,206},{16,12... | collective-permute-start | bytes 786440 | tf_op jit(solution)/shard_map/ppermute | solution.py:32
  30.7 6.7 %collective-permute-start.7 = (bf16[4,256,128]{2,1,0:T(8,128)(2,1)S(1)}, bf16[4,256,128]{2,1,0:T(8,128)(2,1)S(1)}, u32[]{:S(2)}, u32[]{:S(2)}) collective-permute-start(bf16[4,256,128]{2,1,0:T(8,128)(2,1)S(1)} %collective-permute-done.6), channel_id=1, source_target_pairs={{0,4},{2,66},{4,8},{6,70},{8,12},{10,74},{12,16},{14,78},{16,20},{... | collective-permute-start | bytes 786440 | tf_op jit(solution)/shard_map/ppermute | solution.py:32
  30.8 6.8 %collective-permute-start = (s32[3,65]{1,0:T(4,128)S(1)}, s32[3,65]{1,0:T(4,128)S(1)}, u32[]{:S(2)}, u32[]{:S(2)}) collective-permute-start(s32[3,65]{1,0:T(4,128)S(1)} %pad_add_fusion.1), channel_id=1, source_target_pairs={{0,2},{2,0},{4,6},{6,4},{8,10},{10,8},{12,14},{14,12},{16,18},{18,... | collective-permute-start | bytes 2348 | tf_op jit(solution)/shard_map/ppermute | solution.py:32
  37.5 15.2 %collective-permute-start.9 = (bf16[16,256,128]{2,1,0:T(8,128)(2,1)S(1)}, bf16[16,256,128]{2,1,0:T(8,128)(2,1)S(1)}, u32[]{:S(2)}, u32[]{:S(2)}) collective-permute-start(bf16[16,256,128]{2,1,0:T(8,128)(2,1)S(1)} %constant_dynamic-update-slice_fusion.refs_0_), channel_id=1, source_target_pairs={{0,64},{2,6},{4,68},{6,10},{8,72},{10,14},{12,76},{14,18},{16,80},... | collective-permute-start | bytes 3145736 | tf_op jit(solution)/shard_map/ppermute | solution.py:32
  37.6 16.0 %collective-permute-start.8 = (bf16[16,256,128]{2,1,0:T(8,128)(2,1)S(1)}, bf16[16,256,128]{2,1,0:T(8,128)(2,1)S(1)}, u32[]{:S(2)}, u32[]{:S(2)}) collective-permute-start(bf16[16,256,128]{2,1,0:T(8,128)(2,1)S(1)} %constant_dynamic-update-slice_fusion.refs_0_), channel_id=1, source_target_pairs={{0,192},{2,30},{4,196},{6,2},{8,200},{10,6},{12,204},{14,10},{16,2... | collective-permute-start | bytes 3145736 | tf_op jit(solution)/shard_map/ppermute | solution.py:32
  53.6 10.0 %collective-permute-start.13 = (bf16[8,256,128]{2,1,0:T(8,128)(2,1)}, bf16[8,256,128]{2,1,0:T(8,128)(2,1)}, u32[]{:S(2)}, u32[]{:S(2)}) collective-permute-start(bf16[8,256,128]{2,1,0:T(8,128)(2,1)} %slice.32), channel_id=1, source_target_pairs={{0,64},{2,6},{4,68},{6,10},{8,72},{10,14},{12,76},{14,18},{16,80},... | collective-permute-start | bytes 1572872 | tf_op jit(solution)/shard_map/ppermute | solution.py:32
  54.5 9.1 %collective-permute-start.14 = (bf16[8,256,128]{2,1,0:T(8,128)(2,1)}, bf16[8,256,128]{2,1,0:T(8,128)(2,1)}, u32[]{:S(2)}, u32[]{:S(2)}) collective-permute-start(bf16[8,256,128]{2,1,0:T(8,128)(2,1)} %slice.33), channel_id=1, source_target_pairs={{0,192},{2,30},{4,196},{6,2},{8,200},{10,6},{12,204},{14,10},{16,2... | collective-permute-start | bytes 1572872 | tf_op jit(solution)/shard_map/ppermute | solution.py:32
  65.6 6.6 %collective-permute-start.15 = (f32[256,512]{1,0:T(8,128)S(1)}, f32[256,512]{1,0:T(8,128)S(1)}, u32[]{:S(2)}, u32[]{:S(2)}) collective-permute-start(f32[256,512]{1,0:T(8,128)S(1)} %shard_map.124.mine_ref), channel_id=1, source_target_pairs={{0,2},{2,0},{4,6},{6,4},{8,10},{10,8},{12,14},{14,12},{16,18},{18,... | collective-permute-start | bytes 1572872 | tf_op jit(solution)/shard_map/ppermute | solution.py:32
  74.1 9.6 %collective-permute-start.20 = (bf16[8,256,128]{2,1,0:T(8,128)(2,1)S(1)}, bf16[8,256,128]{2,1,0:T(8,128)(2,1)S(1)}, u32[]{:S(2)}, u32[]{:S(2)}) collective-permute-start(bf16[8,256,128]{2,1,0:T(8,128)(2,1)S(1)} %get-tuple-element.20), channel_id=1, source_target_pairs={{0,64},{2,6},{4,68},{6,10},{8,72},{10,14},{12,76},{14,18},{16,80},... | collective-permute-start | bytes 1572872 | tf_op jit(solution)/shard_map/ppermute | solution.py:32
  74.2 10.0 %collective-permute-start.17 = (bf16[8,256,128]{2,1,0:T(8,128)(2,1)S(1)}, bf16[8,256,128]{2,1,0:T(8,128)(2,1)S(1)}, u32[]{:S(2)}, u32[]{:S(2)}) collective-permute-start(bf16[8,256,128]{2,1,0:T(8,128)(2,1)S(1)} %get-tuple-element.17), channel_id=1, source_target_pairs={{0,192},{2,30},{4,196},{6,2},{8,200},{10,6},{12,204},{14,10},{16,2... | collective-permute-start | bytes 1572872 | tf_op jit(solution)/shard_map/ppermute | solution.py:32
  76.8 11.7 %collective-permute-start.22 = (bf16[8,256,128]{2,1,0:T(8,128)(2,1)S(1)}, bf16[8,256,128]{2,1,0:T(8,128)(2,1)S(1)}, u32[]{:S(2)}, u32[]{:S(2)}) collective-permute-start(bf16[8,256,128]{2,1,0:T(8,128)(2,1)S(1)} %get-tuple-element.21), channel_id=1, source_target_pairs={{0,192},{2,30},{4,196},{6,2},{8,200},{10,6},{12,204},{14,10},{16,2... | collective-permute-start | bytes 1572872 | tf_op jit(solution)/shard_map/ppermute | solution.py:32
  83.8 9.6 %collective-permute-start.21 = (bf16[8,256,128]{2,1,0:T(8,128)(2,1)S(1)}, bf16[8,256,128]{2,1,0:T(8,128)(2,1)S(1)}, u32[]{:S(2)}, u32[]{:S(2)}) collective-permute-start(bf16[8,256,128]{2,1,0:T(8,128)(2,1)S(1)} %add_convert_fusion), channel_id=1, source_target_pairs={{0,64},{2,6},{4,68},{6,10},{8,72},{10,14},{12,76},{14,18},{16,80},... | collective-permute-start | bytes 1572872 | tf_op jit(solution)/shard_map/ppermute | solution.py:32
  83.9 15.1 %collective-permute-start.16 = (bf16[8,256,128]{2,1,0:T(8,128)(2,1)S(1)}, bf16[8,256,128]{2,1,0:T(8,128)(2,1)S(1)}, u32[]{:S(2)}, u32[]{:S(2)}) collective-permute-start(bf16[8,256,128]{2,1,0:T(8,128)(2,1)S(1)} %get-tuple-element.15), channel_id=1, source_target_pairs={{0,64},{2,6},{4,68},{6,10},{8,72},{10,14},{12,76},{14,18},{16,80},... | collective-permute-start | bytes 1572872 | tf_op jit(solution)/shard_map/ppermute | solution.py:32
  84.4 14.7 %collective-permute-start.18 = (bf16[8,256,128]{2,1,0:T(8,128)(2,1)S(1)}, bf16[8,256,128]{2,1,0:T(8,128)(2,1)S(1)}, u32[]{:S(2)}, u32[]{:S(2)}) collective-permute-start(bf16[8,256,128]{2,1,0:T(8,128)(2,1)S(1)} %add_convert_fusion.1), channel_id=1, source_target_pairs={{0,192},{2,30},{4,196},{6,2},{8,200},{10,6},{12,204},{14,10},{16,2... | collective-permute-start | bytes 1572872 | tf_op jit(solution)/shard_map/ppermute | solution.py:32
  93.7 6.8 %collective-permute-start.23 = (bf16[4,256,128]{2,1,0:T(8,128)(2,1)S(1)}, bf16[4,256,128]{2,1,0:T(8,128)(2,1)S(1)}, u32[]{:S(2)}, u32[]{:S(2)}) collective-permute-start(bf16[4,256,128]{2,1,0:T(8,128)(2,1)S(1)} %split.52), channel_id=1, source_target_pairs={{0,28},{2,194},{4,0},{6,198},{8,4},{10,202},{12,8},{14,206},{16,12... | collective-permute-start | bytes 786440 | tf_op jit(solution)/shard_map/ppermute | solution.py:32
  99.3 7.0 %collective-permute-start.19 = (bf16[4,256,128]{2,1,0:T(8,128)(2,1)S(1)}, bf16[4,256,128]{2,1,0:T(8,128)(2,1)S(1)}, u32[]{:S(2)}, u32[]{:S(2)}) collective-permute-start(bf16[4,256,128]{2,1,0:T(8,128)(2,1)S(1)} %split.53), channel_id=1, source_target_pairs={{0,4},{2,66},{4,8},{6,70},{8,12},{10,74},{12,16},{14,78},{16,20},{... | collective-permute-start | bytes 786440 | tf_op jit(solution)/shard_map/ppermute | solution.py:32
  100.6 6.5 %collective-permute-start.24 = (bf16[4,256,128]{2,1,0:T(8,128)(2,1)S(1)}, bf16[4,256,128]{2,1,0:T(8,128)(2,1)S(1)}, u32[]{:S(2)}, u32[]{:S(2)}) collective-permute-start(bf16[4,256,128]{2,1,0:T(8,128)(2,1)S(1)} %fusion), channel_id=1, source_target_pairs={{0,28},{2,194},{4,0},{6,198},{8,4},{10,202},{12,8},{14,206},{16,12... | collective-permute-start | bytes 786440 | tf_op jit(solution)/shard_map/ppermute | solution.py:32
  107.2 7.2 %collective-permute-start.25 = (bf16[256,128]{1,0:T(8,128)(2,1)S(1)}, bf16[256,128]{1,0:T(8,128)(2,1)S(1)}, u32[]{:S(2)}, u32[]{:S(2)}) collective-permute-start(bf16[256,128]{1,0:T(8,128)(2,1)S(1)} %get-tuple-element.24), channel_id=1, source_target_pairs={{0,16},{2,18},{4,20},{6,22},{8,24},{10,26},{12,28},{14,30},{16,0},... | collective-permute-start | bytes 196616 | tf_op jit(solution)/shard_map/ppermute | solution.py:32
  108.2 6.3 %collective-permute-start.26 = (bf16[256,128]{1,0:T(8,128)(2,1)S(1)}, bf16[256,128]{1,0:T(8,128)(2,1)S(1)}, u32[]{:S(2)}, u32[]{:S(2)}) collective-permute-start(bf16[256,128]{1,0:T(8,128)(2,1)S(1)} %get-tuple-element.26), channel_id=1, source_target_pairs={{0,32},{2,34},{4,36},{6,38},{8,40},{10,42},{12,44},{14,46},{16,48}... | collective-permute-start | bytes 196616 | tf_op jit(solution)/shard_map/ppermute | solution.py:32
  108.4 7.9 %collective-permute-start.27 = (bf16[256,128]{1,0:T(8,128)(2,1)S(1)}, bf16[256,128]{1,0:T(8,128)(2,1)S(1)}, u32[]{:S(2)}, u32[]{:S(2)}) collective-permute-start(bf16[256,128]{1,0:T(8,128)(2,1)S(1)} %get-tuple-element.25), channel_id=1, source_target_pairs={{0,48},{2,50},{4,52},{6,54},{8,56},{10,58},{12,60},{14,62},{16,32}... | collective-permute-start | bytes 196616 | tf_op jit(solution)/shard_map/ppermute | solution.py:32
  116.5 6.5 %collective-permute-start.28 = (bf16[64,256]{1,0:T(8,128)(2,1)S(1)}, bf16[64,256]{1,0:T(8,128)(2,1)S(1)}, u32[]{:S(2)}, u32[]{:S(2)}) collective-permute-start(bf16[64,256]{1,0:T(8,128)(2,1)S(1)} %broadcast_select_fusion.1), channel_id=1, source_target_pairs={{0,2},{2,0},{4,6},{6,4},{8,10},{10,8},{12,14},{14,12},{16,18},{18,... | collective-permute-start | bytes 98312 | tf_op jit(solution)/shard_map/ppermute | solution.py:32

commit v9 on v7

--- a/solution.py
+++ b/solution.py
@@ -70,7 +70,18 @@
 def large_gather(value, axes):
     half = value.shape[0] // 2
     up, down = turn(value, axes, 1), turn(value, axes, -1)
-    return value, down, up, turn(up[:half], axes, 1), turn(down[half:], axes, -1)
+    return value, down, up, turn(pick(up, 0, half), axes, 1), turn(pick(down, half, half), axes, -1)
+
+
+def pick(blocks, start, count):
+    def kernel(blocks_ref, picked_ref):
+        picked_ref[...] = blocks_ref[start : start + count]
+
+    return pl.pallas_call(
+        kernel,
+        out_shape=jax.ShapeDtypeStruct((count, *blocks.shape[1:]), blocks.dtype),
+        compiler_params=pltpu.CompilerParams(vmem_limit_bytes=4 << 20),
+    )(blocks)
 
 
 SENT = (False, False, True, False, False, True, True, True)

time: 123 us -> 123 us (level)
  Pallas kernels: 10.2 us -> 11.9 us
  local copies, waits for them, and re-layouts: 2.32 us -> 0.62 us
    slice x2 -> x0, local copies, waits for them, and re-layouts: 1.7 us -> none  [the longest x1 0.88 us: large_gather(): down[half:]]
    pallas_call x0 -> x2, Pallas kernels: none -> 1.7 us  [pick(): pl.pallas_call(kernel, out_shape=jax.ShapeDtypeStruct((count, *blocks.sha...]
  transfers between devices with their start and end apart: 29 -> 29, of which waited for: 18 -> 18; matrix products, arithmetic and copies ran while one was open for 4% -> 3% of each run, Pallas kernels for 4% -> 6%
where the time goes in v9:
time: 123 us
  waiting for transfers between devices  54.8 us (45%)
  starting transfers between devices  48.6 us (40%)
  Pallas kernels  11.9 us (10%)
  other arithmetic  4.23 us (3%)
  between operations  2.85 us (2%)
    ppermute x29, waiting for transfers between devices, permute(): return lax.ppermute(value, 'tp', pairs)  54.8 us
    ppermute x29, starting transfers between devices, permute(): return lax.ppermute(value, 'tp', pairs)  48.6 us
    pallas_call x3, Pallas kernels, call(): pl.pallas_call(kernel, out_shape=outs, in_specs=[pl.BlockSpec(memory_spac...  10 us
  transfers between devices with their start and end apart: 29, of which 18 were waited for; matrix products, arithmetic and copies ran while one was open for 3% of the time, Pallas kernels for 6%

profile of v9, /device:TPU:1, one launch (start us, length us, event | category | flops | bytes accessed | tf_op | source)
XLA Modules:
  0.0 123.0 jit_solution(11448776499979287811)
XLA Ops:
  0.7 0.8 select_bitcast_fusion.2
  1.5 3.2 %collective-permute-start.1 = (bf16[64,256]{1,0:T(8,128)(2,1)S(1)}, bf16[64,256]{1,0:T(8,128)(2,1)S(1)}, u32[]{:S(2)}, u32[]{:S(2)}) collective-permute-start(bf16[64,256]{1,0:T(8,128)(2,1)S(1)} %select_bitcast_fusion.2), channel_id=1, source_target_pairs={{0,2},{2,0},{4,6},{6,4},{8,10},{10,8},{12,14},{14,12},{16,18},{18,... | collective-permute-start | bytes 98312 | tf_op jit(solution)/shard_map/ppermute | solution.py:32
  4.7 0.1 collective-permute-start.10
  4.8 0.4 collective-permute-start.11
  7.2 0.1 copy.14
  7.3 0.8 bitcast_select_fusion.1
  8.2 5.3 %collective-permute-start.2 = (bf16[1,256,128]{2,1,0:T(8,128)(2,1)S(1)}, bf16[1,256,128]{2,1,0:T(8,128)(2,1)S(1)}, u32[]{:S(2)}, u32[]{:S(2)}) collective-permute-start(bf16[1,256,128]{2,1,0:T(8,128)(2,1)S(1)} %bitcast.32), channel_id=1, source_target_pairs={{0,16},{2,18},{4,20},{6,22},{8,24},{10,26},{12,28},{14,30},{16,0},... | collective-permute-start | bytes 196616 | tf_op jit(solution)/shard_map/ppermute | solution.py:32
  13.5 1.2 collective-permute-start.3
  14.7 0.2 collective-permute-start.4
  14.8 0.8 pad_add_fusion.1
  15.6 0.2 collective-permute-done.2
  15.8 1.0 collective-permute-start.12
  16.8 7.0 %collective-permute-done.4 = bf16[1,256,128]{2,1,0:T(8,128)(2,1)S(1)} collective-permute-done((bf16[1,256,128]{2,1,0:T(8,128)(2,1)S(1)}, bf16[1,256,128]{2,1,0:T(8,128)(2,1)S(1)}, u32[]{:S(2)}, u32[]{:S(2)}) %collective-permute-start.4) | collective-permute-done | bytes 65568 | tf_op jit(solution)/shard_map/ppermute | solution.py:32
  23.9 1.4 %collective-permute-start.6 = (bf16[4,256,128]{2,1,0:T(8,128)(2,1)S(1)}, bf16[4,256,128]{2,1,0:T(8,128)(2,1)S(1)}, u32[]{:S(2)}, u32[]{:S(2)}) collective-permute-start(bf16[4,256,128]{2,1,0:T(8,128)(2,1)S(1)} %pad_maximum_fusion), channel_id=1, source_target_pairs={{0,4},{2,66},{4,8},{6,70},{8,12},{10,74},{12,16},{14,78},{16,20},{... | collective-permute-start | bytes 786440 | tf_op jit(solution)/shard_map/ppermute | solution.py:32
  25.3 1.5 %collective-permute-start.5 = (bf16[4,256,128]{2,1,0:T(8,128)(2,1)S(1)}, bf16[4,256,128]{2,1,0:T(8,128)(2,1)S(1)}, u32[]{:S(2)}, u32[]{:S(2)}) collective-permute-start(bf16[4,256,128]{2,1,0:T(8,128)(2,1)S(1)} %pad_maximum_fusion), channel_id=1, source_target_pairs={{0,28},{2,194},{4,0},{6,198},{8,4},{10,202},{12,8},{14,206},{16,12... | collective-permute-start | bytes 786440 | tf_op jit(solution)/shard_map/ppermute | solution.py:32
  26.8 3.9 %collective-permute-done.6 = bf16[4,256,128]{2,1,0:T(8,128)(2,1)S(1)} collective-permute-done((bf16[4,256,128]{2,1,0:T(8,128)(2,1)S(1)}, bf16[4,256,128]{2,1,0:T(8,128)(2,1)S(1)}, u32[]{:S(2)}, u32[]{:S(2)}) %collective-permute-start.6) | collective-permute-done | bytes 262176 | tf_op jit(solution)/shard_map/ppermute | solution.py:32
  30.8 1.8 %collective-permute-start = (s32[3,65]{1,0:T(4,128)S(1)}, s32[3,65]{1,0:T(4,128)S(1)}, u32[]{:S(2)}, u32[]{:S(2)}) collective-permute-start(s32[3,65]{1,0:T(4,128)S(1)} %pad_add_fusion.1), channel_id=1, source_target_pairs={{0,2},{2,0},{4,6},{6,4},{8,10},{10,8},{12,14},{14,12},{16,18},{18,... | collective-permute-start | bytes 2348 | tf_op jit(solution)/shard_map/ppermute | solution.py:32
  32.7 4.8 %collective-permute-done.7 = bf16[4,256,128]{2,1,0:T(8,128)(2,1)S(1)} collective-permute-done((bf16[4,256,128]{2,1,0:T(8,128)(2,1)S(1)}, bf16[4,256,128]{2,1,0:T(8,128)(2,1)S(1)}, u32[]{:S(2)}, u32[]{:S(2)}) %collective-permute-start.7) | collective-permute-done | bytes 262176 | tf_op jit(solution)/shard_map/ppermute | solution.py:32
  37.5 0.1 collective-permute-start.9
  37.6 2.7 %collective-permute-start.8 = (bf16[16,256,128]{2,1,0:T(8,128)(2,1)S(1)}, bf16[16,256,128]{2,1,0:T(8,128)(2,1)S(1)}, u32[]{:S(2)}, u32[]{:S(2)}) collective-permute-start(bf16[16,256,128]{2,1,0:T(8,128)(2,1)S(1)} %constant_dynamic-update-slice_fusion.refs_0_), channel_id=1, source_target_pairs={{0,192},{2,30},{4,196},{6,2},{8,200},{10,6},{12,204},{14,10},{16,2... | collective-permute-start | bytes 3145736 | tf_op jit(solution)/shard_map/ppermute | solution.py:32
  40.3 0.1 pad_add_fusion
  40.4 0.2 slice_reduce_fusion
  40.6 12.2 %collective-permute-done.9.refs_2_.blocks_ref = bf16[16,256,128]{2,1,0:T(8,128)(2,1)S(1)} collective-permute-done((bf16[16,256,128]{2,1,0:T(8,128)(2,1)S(1)}, bf16[16,256,128]{2,1,0:T(8,128)(2,1)S(1)}, u32[]{:S(2)}, u32[]{:S(2)}) %collective-permute-start.9) | collective-permute-done | bytes 1048608 | tf_op jit(solution)/shard_map/ppermute | solution.py:32
  52.7 0.8 shard_map.124
  53.6 0.9 shard_map.125
  54.5 2.7 %collective-permute-start.14 = (bf16[8,256,128]{2,1,0:T(8,128)(2,1)}, bf16[8,256,128]{2,1,0:T(8,128)(2,1)}, u32[]{:S(2)}, u32[]{:S(2)}) collective-permute-start(bf16[8,256,128]{2,1,0:T(8,128)(2,1)} %shard_map.125), channel_id=1, source_target_pairs={{0,192},{2,30},{4,196},{6,2},{8,200},{10,6},{12,204},{14,10},{16,2... | collective-permute-start | bytes 1572872 | tf_op jit(solution)/shard_map/ppermute | solution.py:32
  57.1 0.3 select_reduce_fusion
  57.4 0.1 sub.34
  57.5 5.3 %shard_map.123 = (f32[256,512]{1,0:T(8,128)S(1)}, bf16[6,64,128,128]{3,2,1,0:T(8,128)(2,1)S(1)}) custom-call(s32[385]{0:T(512)S(1)} %pad_add_fusion.2.maps_ref, bf16[16,256,128]{2,1,0:T(8,128)(2,1)S(1)} %constant_dynamic-update-slice_fusion.refs_0_, bf16[16,256,128]{2,1,0:T(8,128)(2,1)S(1)} %collective-permute-done.8.refs_1_.blocks_ref, ...), custom_call_target="tpu_custom_call" | custom-call | flops 1610612736 | bytes 16777216 | tf_op jit(solution)/shard_map/pallas_call | solution.py:265
  62.8 0.6 collective-permute-done.13.refs_1_
  63.4 0.1 collective-permute-done.14.refs_2_
  63.6 1.7 %shard_map.126.mine_ref = f32[256,512]{1,0:T(8,128)S(1)} custom-call(s32[385]{0:T(512)S(1)} %pad_add_fusion.2.maps_ref, f32[256,512]{1,0:T(8,128)S(1)} %get-tuple-element.12.refs_0_, bf16[8,256,128]{2,1,0:T(8,128)(2,1)} %collective-permute-done.13.refs_1_, bf16[8,256,128]{2,1,0:T(8,128)(2,1)} %collective-permute-done.14.refs_2_, ...), custom_call_target="tpu_custom_call" | custom-call | flops 536870912 | bytes 16777216 | tf_op jit(solution)/shard_map/pallas_call | solution.py:265
  65.3 5.5 %collective-permute-start.15 = (f32[256,512]{1,0:T(8,128)S(1)}, f32[256,512]{1,0:T(8,128)S(1)}, u32[]{:S(2)}, u32[]{:S(2)}) collective-permute-start(f32[256,512]{1,0:T(8,128)S(1)} %shard_map.126.mine_ref), channel_id=1, source_target_pairs={{0,2},{2,0},{4,6},{6,4},{8,10},{10,8},{12,14},{14,12},{16,18},{18,... | collective-permute-start | bytes 1572872 | tf_op jit(solution)/shard_map/ppermute | solution.py:32
  70.9 1.5 %collective-permute-done.15.theirs_ref = f32[256,512]{1,0:T(8,128)S(1)} collective-permute-done((f32[256,512]{1,0:T(8,128)S(1)}, f32[256,512]{1,0:T(8,128)S(1)}, u32[]{:S(2)}, u32[]{:S(2)}) %collective-permute-start.15) | collective-permute-done | bytes 524320 | tf_op jit(solution)/shard_map/ppermute | solution.py:32
  72.4 3.0 %shard_map.127 = (f32[8,256,128]{2,1,0:T(8,128)S(1)}, f32[8,256,128]{2,1,0:T(8,128)S(1)}, bf16[8,256,128]{2,1,0:T(8,128)(2,1)S(1)}, f32[8,256,128]{2,1,0:T(8,128...) custom-call(s32[385]{0:T(512)S(1)} %pad_add_fusion.2.maps_ref, ...), custom_call_target="tpu_custom_call" | custom-call | flops 2147483648 | bytes 16777216 | tf_op jit(solution)/shard_map/pallas_call | solution.py:265
  75.4 0.1 collective-permute-start.20
  75.5 2.7 %collective-permute-start.17 = (bf16[8,256,128]{2,1,0:T(8,128)(2,1)S(1)}, bf16[8,256,128]{2,1,0:T(8,128)(2,1)S(1)}, u32[]{:S(2)}, u32[]{:S(2)}) collective-permute-start(bf16[8,256,128]{2,1,0:T(8,128)(2,1)S(1)} %get-tuple-element.17), channel_id=1, source_target_pairs={{0,192},{2,30},{4,196},{6,2},{8,200},{10,6},{12,204},{14,10},{16,2... | collective-permute-start | bytes 1572872 | tf_op jit(solution)/shard_map/ppermute | solution.py:32
  78.2 6.8 %collective-permute-done.20 = bf16[8,256,128]{2,1,0:T(8,128)(2,1)S(1)} collective-permute-done((bf16[8,256,128]{2,1,0:T(8,128)(2,1)S(1)}, bf16[8,256,128]{2,1,0:T(8,128)(2,1)S(1)}, u32[]{:S(2)}, u32[]{:S(2)}) %collective-permute-start.20) | collective-permute-done | bytes 524320 | tf_op jit(solution)/shard_map/ppermute | solution.py:32
  85.0 0.1 add_convert_fusion
  85.1 0.1 collective-permute-start.21
  85.2 0.3 collective-permute-start.16
  85.5 0.1 add_convert_fusion.1
  85.7 2.8 %collective-permute-start.18 = (bf16[8,256,128]{2,1,0:T(8,128)(2,1)S(1)}, bf16[8,256,128]{2,1,0:T(8,128)(2,1)S(1)}, u32[]{:S(2)}, u32[]{:S(2)}) collective-permute-start(bf16[8,256,128]{2,1,0:T(8,128)(2,1)S(1)} %add_convert_fusion.1), channel_id=1, source_target_pairs={{0,192},{2,30},{4,196},{6,2},{8,200},{10,6},{12,204},{14,10},{16,2... | collective-permute-start | bytes 1572872 | tf_op jit(solution)/shard_map/ppermute | solution.py:32
  88.4 1.5 %collective-permute-done.22 = bf16[8,256,128]{2,1,0:T(8,128)(2,1)S(1)} collective-permute-done((bf16[8,256,128]{2,1,0:T(8,128)(2,1)S(1)}, bf16[8,256,128]{2,1,0:T(8,128)(2,1)S(1)}, u32[]{:S(2)}, u32[]{:S(2)}) %collective-permute-start.22) | collective-permute-done | bytes 524320 | tf_op jit(solution)/shard_map/ppermute | solution.py:32
  89.9 4.9 %collective-permute-done.21 = bf16[8,256,128]{2,1,0:T(8,128)(2,1)S(1)} collective-permute-done((bf16[8,256,128]{2,1,0:T(8,128)(2,1)S(1)}, bf16[8,256,128]{2,1,0:T(8,128)(2,1)S(1)}, u32[]{:S(2)}, u32[]{:S(2)}) %collective-permute-start.21) | collective-permute-done | bytes 524320 | tf_op jit(solution)/shard_map/ppermute | solution.py:32
  94.8 0.2 convert_add_fusion
  95.0 3.5 %collective-permute-start.23 = (bf16[4,256,128]{2,1,0:T(8,128)(2,1)S(1)}, bf16[4,256,128]{2,1,0:T(8,128)(2,1)S(1)}, u32[]{:S(2)}, u32[]{:S(2)}) collective-permute-start(bf16[4,256,128]{2,1,0:T(8,128)(2,1)S(1)} %split.52), channel_id=1, source_target_pairs={{0,28},{2,194},{4,0},{6,198},{8,4},{10,202},{12,8},{14,206},{16,12... | collective-permute-start | bytes 786440 | tf_op jit(solution)/shard_map/ppermute | solution.py:32
  98.5 1.9 %collective-permute-done.16 = bf16[8,256,128]{2,1,0:T(8,128)(2,1)S(1)} collective-permute-done((bf16[8,256,128]{2,1,0:T(8,128)(2,1)S(1)}, bf16[8,256,128]{2,1,0:T(8,128)(2,1)S(1)}, u32[]{:S(2)}, u32[]{:S(2)}) %collective-permute-start.16) | collective-permute-done | bytes 524320 | tf_op jit(solution)/shard_map/ppermute | solution.py:32
  100.4 0.1 convert_add_fusion.1
  100.6 0.6 collective-permute-start.19
  101.2 0.6 collective-permute-done.23
  101.9 3.2 %collective-permute-start.24 = (bf16[4,256,128]{2,1,0:T(8,128)(2,1)S(1)}, bf16[4,256,128]{2,1,0:T(8,128)(2,1)S(1)}, u32[]{:S(2)}, u32[]{:S(2)}) collective-permute-start(bf16[4,256,128]{2,1,0:T(8,128)(2,1)S(1)} %fusion), channel_id=1, source_target_pairs={{0,28},{2,194},{4,0},{6,198},{8,4},{10,202},{12,8},{14,206},{16,12... | collective-permute-start | bytes 786440 | tf_op jit(solution)/shard_map/ppermute | solution.py:32
  105.1 2.8 %collective-permute-done.19 = bf16[4,256,128]{2,1,0:T(8,128)(2,1)S(1)} collective-permute-done((bf16[4,256,128]{2,1,0:T(8,128)(2,1)S(1)}, bf16[4,256,128]{2,1,0:T(8,128)(2,1)S(1)}, u32[]{:S(2)}, u32[]{:S(2)}) %collective-permute-start.19) | collective-permute-done | bytes 262176 | tf_op jit(solution)/shard_map/ppermute | solution.py:32
  107.8 0.6 collective-permute-done.24
  108.4 0.1 fusion.13
  108.5 1.0 collective-permute-start.25
  109.5 0.3 collective-permute-start.26
  109.8 5.4 %collective-permute-start.27 = (bf16[256,128]{1,0:T(8,128)(2,1)S(1)}, bf16[256,128]{1,0:T(8,128)(2,1)S(1)}, u32[]{:S(2)}, u32[]{:S(2)}) collective-permute-start(bf16[256,128]{1,0:T(8,128)(2,1)S(1)} %get-tuple-element.25), channel_id=1, source_target_pairs={{0,48},{2,50},{4,52},{6,54},{8,56},{10,58},{12,60},{14,62},{16,32}... | collective-permute-start | bytes 196616 | tf_op jit(solution)/shard_map/ppermute | solution.py:32
  115.2 0.5 collective-permute-done.25
  115.7 4.0 %collective-permute-done.27 = bf16[256,128]{1,0:T(8,128)(2,1)S(1)} collective-permute-done((bf16[256,128]{1,0:T(8,128)(2,1)S(1)}, bf16[256,128]{1,0:T(8,128)(2,1)S(1)}, u32[]{:S(2)}, u32[]{:S(2)}) %collective-permute-start.27) | collective-permute-done | bytes 65568 | tf_op jit(solution)/shard_map/ppermute | solution.py:32
  119.7 0.1 shard_map.128
  119.8 1.7 %collective-permute-start.28 = (bf16[64,256]{1,0:T(8,128)(2,1)S(1)}, bf16[64,256]{1,0:T(8,128)(2,1)S(1)}, u32[]{:S(2)}, u32[]{:S(2)}) collective-permute-start(bf16[64,256]{1,0:T(8,128)(2,1)S(1)} %broadcast_select_fusion.1), channel_id=1, source_target_pairs={{0,2},{2,0},{4,6},{6,4},{8,10},{10,8},{12,14},{14,12},{16,18},{18,... | collective-permute-start | bytes 98312 | tf_op jit(solution)/shard_map/ppermute | solution.py:32
  121.5 0.9 collective-permute-done.28
  122.4 0.6 select_bitcast_fusion
  (42 shorter events, 0.7 us)
Async XLA Ops:
  0.6 39.7 %copy-start.2 = (s32[1,64]{1,0:T(1,128)S(1)}, s32[1,64]{1,0:T(1,128)}, u32[]{:S(2)}) copy-start(s32[1,64]{1,0:T(1,128)} %param.14) | copy-start | bytes 772
  0.6 39.6 %copy-start.1 = (s32[1,64]{1,0:T(1,128)S(1)}, s32[1,64]{1,0:T(1,128)}, u32[]{:S(2)}) copy-start(s32[1,64]{1,0:T(1,128)} %param.17) | copy-start | bytes 772
  0.7 39.6 %copy-start = (s32[1,64]{1,0:T(1,128)S(1)}, s32[1,64]{1,0:T(1,128)}, u32[]{:S(2)}) copy-start(s32[1,64]{1,0:T(1,128)} %param.20) | copy-start | bytes 772
  1.5 5.9 %collective-permute-start.1 = (bf16[64,256]{1,0:T(8,128)(2,1)S(1)}, bf16[64,256]{1,0:T(8,128)(2,1)S(1)}, u32[]{:S(2)}, u32[]{:S(2)}) collective-permute-start(bf16[64,256]{1,0:T(8,128)(2,1)S(1)} %select_bitcast_fusion.2), channel_id=1, source_target_pairs={{0,2},{2,0},{4,6},{6,4},{8,10},{10,8},{12,14},{14,12},{16,18},{18,... | collective-permute-start | bytes 98312 | tf_op jit(solution)/shard_map/ppermute | solution.py:32
  4.7 52.8 %collective-permute-start.10 = (bf16[64,128,128]{2,1,0:T(8,128)(2,1)}, bf16[64,128,128]{2,1,0:T(8,128)(2,1)}, u32[]{:S(2)}, u32[]{:S(2)}) collective-permute-start(bf16[64,128,128]{2,1,0:T(8,128)(2,1)} %refs_3_.1), channel_id=1, source_target_pairs={{0,2},{2,0},{4,6},{6,4},{8,10},{10,8},{12,14},{14,12},{16,18},{18,... | collective-permute-start | bytes 6291464 | tf_op jit(solution)/shard_map/ppermute | solution.py:32
  4.8 52.7 %collective-permute-start.11 = (bf16[64,128,128]{2,1,0:T(8,128)(2,1)}, bf16[64,128,128]{2,1,0:T(8,128)(2,1)}, u32[]{:S(2)}, u32[]{:S(2)}) collective-permute-start(bf16[64,128,128]{2,1,0:T(8,128)(2,1)} %refs_4_.1), channel_id=1, source_target_pairs={{0,2},{2,0},{4,6},{6,4},{8,10},{10,8},{12,14},{14,12},{16,18},{18,... | collective-permute-start | bytes 6291464 | tf_op jit(solution)/shard_map/ppermute | solution.py:32
  8.2 7.7 %collective-permute-start.2 = (bf16[1,256,128]{2,1,0:T(8,128)(2,1)S(1)}, bf16[1,256,128]{2,1,0:T(8,128)(2,1)S(1)}, u32[]{:S(2)}, u32[]{:S(2)}) collective-permute-start(bf16[1,256,128]{2,1,0:T(8,128)(2,1)S(1)} %bitcast.32), channel_id=1, source_target_pairs={{0,16},{2,18},{4,20},{6,22},{8,24},{10,26},{12,28},{14,30},{16,0},... | collective-permute-start | bytes 196616 | tf_op jit(solution)/shard_map/ppermute | solution.py:32
  13.5 3.3 %collective-permute-start.3 = (bf16[1,256,128]{2,1,0:T(8,128)(2,1)S(1)}, bf16[1,256,128]{2,1,0:T(8,128)(2,1)S(1)}, u32[]{:S(2)}, u32[]{:S(2)}) collective-permute-start(bf16[1,256,128]{2,1,0:T(8,128)(2,1)S(1)} %bitcast.33), channel_id=1, source_target_pairs={{0,32},{2,34},{4,36},{6,38},{8,40},{10,42},{12,44},{14,46},{16,48}... | collective-permute-start | bytes 196616 | tf_op jit(solution)/shard_map/ppermute | solution.py:32
  14.7 9.2 %collective-permute-start.4 = (bf16[1,256,128]{2,1,0:T(8,128)(2,1)S(1)}, bf16[1,256,128]{2,1,0:T(8,128)(2,1)S(1)}, u32[]{:S(2)}, u32[]{:S(2)}) collective-permute-start(bf16[1,256,128]{2,1,0:T(8,128)(2,1)S(1)} %bitcast.34), channel_id=1, source_target_pairs={{0,48},{2,50},{4,52},{6,54},{8,56},{10,58},{12,60},{14,62},{16,32}... | collective-permute-start | bytes 196616 | tf_op jit(solution)/shard_map/ppermute | solution.py:32
  15.8 41.7 %collective-permute-start.12 = (bf16[64,128,128]{2,1,0:T(8,128)(2,1)}, bf16[64,128,128]{2,1,0:T(8,128)(2,1)}, u32[]{:S(2)}, u32[]{:S(2)}) collective-permute-start(bf16[64,128,128]{2,1,0:T(8,128)(2,1)} %refs_7_.1), channel_id=1, source_target_pairs={{0,2},{2,0},{4,6},{6,4},{8,10},{10,8},{12,14},{14,12},{16,18},{18,... | collective-permute-start | bytes 6291464 | tf_op jit(solution)/shard_map/ppermute | solution.py:32
  23.9 6.9 %collective-permute-start.6 = (bf16[4,256,128]{2,1,0:T(8,128)(2,1)S(1)}, bf16[4,256,128]{2,1,0:T(8,128)(2,1)S(1)}, u32[]{:S(2)}, u32[]{:S(2)}) collective-permute-start(bf16[4,256,128]{2,1,0:T(8,128)(2,1)S(1)} %pad_maximum_fusion), channel_id=1, source_target_pairs={{0,4},{2,66},{4,8},{6,70},{8,12},{10,74},{12,16},{14,78},{16,20},{... | collective-permute-start | bytes 786440 | tf_op jit(solution)/shard_map/ppermute | solution.py:32
  25.3 5.5 %collective-permute-start.5 = (bf16[4,256,128]{2,1,0:T(8,128)(2,1)S(1)}, bf16[4,256,128]{2,1,0:T(8,128)(2,1)S(1)}, u32[]{:S(2)}, u32[]{:S(2)}) collective-permute-start(bf16[4,256,128]{2,1,0:T(8,128)(2,1)S(1)} %pad_maximum_fusion), channel_id=1, source_target_pairs={{0,28},{2,194},{4,0},{6,198},{8,4},{10,202},{12,8},{14,206},{16,12... | collective-permute-start | bytes 786440 | tf_op jit(solution)/shard_map/ppermute | solution.py:32
  30.7 6.7 %collective-permute-start.7 = (bf16[4,256,128]{2,1,0:T(8,128)(2,1)S(1)}, bf16[4,256,128]{2,1,0:T(8,128)(2,1)S(1)}, u32[]{:S(2)}, u32[]{:S(2)}) collective-permute-start(bf16[4,256,128]{2,1,0:T(8,128)(2,1)S(1)} %collective-permute-done.6), channel_id=1, source_target_pairs={{0,4},{2,66},{4,8},{6,70},{8,12},{10,74},{12,16},{14,78},{16,20},{... | collective-permute-start | bytes 786440 | tf_op jit(solution)/shard_map/ppermute | solution.py:32
  30.8 6.8 %collective-permute-start = (s32[3,65]{1,0:T(4,128)S(1)}, s32[3,65]{1,0:T(4,128)S(1)}, u32[]{:S(2)}, u32[]{:S(2)}) collective-permute-start(s32[3,65]{1,0:T(4,128)S(1)} %pad_add_fusion.1), channel_id=1, source_target_pairs={{0,2},{2,0},{4,6},{6,4},{8,10},{10,8},{12,14},{14,12},{16,18},{18,... | collective-permute-start | bytes 2348 | tf_op jit(solution)/shard_map/ppermute | solution.py:32
  37.5 15.2 %collective-permute-start.9 = (bf16[16,256,128]{2,1,0:T(8,128)(2,1)S(1)}, bf16[16,256,128]{2,1,0:T(8,128)(2,1)S(1)}, u32[]{:S(2)}, u32[]{:S(2)}) collective-permute-start(bf16[16,256,128]{2,1,0:T(8,128)(2,1)S(1)} %constant_dynamic-update-slice_fusion.refs_0_), channel_id=1, source_target_pairs={{0,64},{2,6},{4,68},{6,10},{8,72},{10,14},{12,76},{14,18},{16,80},... | collective-permute-start | bytes 3145736 | tf_op jit(solution)/shard_map/ppermute | solution.py:32
  37.6 16.0 %collective-permute-start.8 = (bf16[16,256,128]{2,1,0:T(8,128)(2,1)S(1)}, bf16[16,256,128]{2,1,0:T(8,128)(2,1)S(1)}, u32[]{:S(2)}, u32[]{:S(2)}) collective-permute-start(bf16[16,256,128]{2,1,0:T(8,128)(2,1)S(1)} %constant_dynamic-update-slice_fusion.refs_0_), channel_id=1, source_target_pairs={{0,192},{2,30},{4,196},{6,2},{8,200},{10,6},{12,204},{14,10},{16,2... | collective-permute-start | bytes 3145736 | tf_op jit(solution)/shard_map/ppermute | solution.py:32
  53.6 9.9 %collective-permute-start.13 = (bf16[8,256,128]{2,1,0:T(8,128)(2,1)}, bf16[8,256,128]{2,1,0:T(8,128)(2,1)}, u32[]{:S(2)}, u32[]{:S(2)}) collective-permute-start(bf16[8,256,128]{2,1,0:T(8,128)(2,1)} %shard_map.124), channel_id=1, source_target_pairs={{0,64},{2,6},{4,68},{6,10},{8,72},{10,14},{12,76},{14,18},{16,80},... | collective-permute-start | bytes 1572872 | tf_op jit(solution)/shard_map/ppermute | solution.py:32
  54.5 9.1 %collective-permute-start.14 = (bf16[8,256,128]{2,1,0:T(8,128)(2,1)}, bf16[8,256,128]{2,1,0:T(8,128)(2,1)}, u32[]{:S(2)}, u32[]{:S(2)}) collective-permute-start(bf16[8,256,128]{2,1,0:T(8,128)(2,1)} %shard_map.125), channel_id=1, source_target_pairs={{0,192},{2,30},{4,196},{6,2},{8,200},{10,6},{12,204},{14,10},{16,2... | collective-permute-start | bytes 1572872 | tf_op jit(solution)/shard_map/ppermute | solution.py:32
  65.3 7.1 %collective-permute-start.15 = (f32[256,512]{1,0:T(8,128)S(1)}, f32[256,512]{1,0:T(8,128)S(1)}, u32[]{:S(2)}, u32[]{:S(2)}) collective-permute-start(f32[256,512]{1,0:T(8,128)S(1)} %shard_map.126.mine_ref), channel_id=1, source_target_pairs={{0,2},{2,0},{4,6},{6,4},{8,10},{10,8},{12,14},{14,12},{16,18},{18,... | collective-permute-start | bytes 1572872 | tf_op jit(solution)/shard_map/ppermute | solution.py:32
  75.4 9.6 %collective-permute-start.20 = (bf16[8,256,128]{2,1,0:T(8,128)(2,1)S(1)}, bf16[8,256,128]{2,1,0:T(8,128)(2,1)S(1)}, u32[]{:S(2)}, u32[]{:S(2)}) collective-permute-start(bf16[8,256,128]{2,1,0:T(8,128)(2,1)S(1)} %get-tuple-element.20), channel_id=1, source_target_pairs={{0,64},{2,6},{4,68},{6,10},{8,72},{10,14},{12,76},{14,18},{16,80},... | collective-permute-start | bytes 1572872 | tf_op jit(solution)/shard_map/ppermute | solution.py:32
  75.5 10.1 %collective-permute-start.17 = (bf16[8,256,128]{2,1,0:T(8,128)(2,1)S(1)}, bf16[8,256,128]{2,1,0:T(8,128)(2,1)S(1)}, u32[]{:S(2)}, u32[]{:S(2)}) collective-permute-start(bf16[8,256,128]{2,1,0:T(8,128)(2,1)S(1)} %get-tuple-element.17), channel_id=1, source_target_pairs={{0,192},{2,30},{4,196},{6,2},{8,200},{10,6},{12,204},{14,10},{16,2... | collective-permute-start | bytes 1572872 | tf_op jit(solution)/shard_map/ppermute | solution.py:32
  78.1 11.7 %collective-permute-start.22 = (bf16[8,256,128]{2,1,0:T(8,128)(2,1)S(1)}, bf16[8,256,128]{2,1,0:T(8,128)(2,1)S(1)}, u32[]{:S(2)}, u32[]{:S(2)}) collective-permute-start(bf16[8,256,128]{2,1,0:T(8,128)(2,1)S(1)} %get-tuple-element.21), channel_id=1, source_target_pairs={{0,192},{2,30},{4,196},{6,2},{8,200},{10,6},{12,204},{14,10},{16,2... | collective-permute-start | bytes 1572872 | tf_op jit(solution)/shard_map/ppermute | solution.py:32
  85.1 9.6 %collective-permute-start.21 = (bf16[8,256,128]{2,1,0:T(8,128)(2,1)S(1)}, bf16[8,256,128]{2,1,0:T(8,128)(2,1)S(1)}, u32[]{:S(2)}, u32[]{:S(2)}) collective-permute-start(bf16[8,256,128]{2,1,0:T(8,128)(2,1)S(1)} %add_convert_fusion), channel_id=1, source_target_pairs={{0,64},{2,6},{4,68},{6,10},{8,72},{10,14},{12,76},{14,18},{16,80},... | collective-permute-start | bytes 1572872 | tf_op jit(solution)/shard_map/ppermute | solution.py:32
  85.2 15.1 %collective-permute-start.16 = (bf16[8,256,128]{2,1,0:T(8,128)(2,1)S(1)}, bf16[8,256,128]{2,1,0:T(8,128)(2,1)S(1)}, u32[]{:S(2)}, u32[]{:S(2)}) collective-permute-start(bf16[8,256,128]{2,1,0:T(8,128)(2,1)S(1)} %get-tuple-element.15), channel_id=1, source_target_pairs={{0,64},{2,6},{4,68},{6,10},{8,72},{10,14},{12,76},{14,18},{16,80},... | collective-permute-start | bytes 1572872 | tf_op jit(solution)/shard_map/ppermute | solution.py:32
  85.7 14.7 %collective-permute-start.18 = (bf16[8,256,128]{2,1,0:T(8,128)(2,1)S(1)}, bf16[8,256,128]{2,1,0:T(8,128)(2,1)S(1)}, u32[]{:S(2)}, u32[]{:S(2)}) collective-permute-start(bf16[8,256,128]{2,1,0:T(8,128)(2,1)S(1)} %add_convert_fusion.1), channel_id=1, source_target_pairs={{0,192},{2,30},{4,196},{6,2},{8,200},{10,6},{12,204},{14,10},{16,2... | collective-permute-start | bytes 1572872 | tf_op jit(solution)/shard_map/ppermute | solution.py:32
  95.0 6.8 %collective-permute-start.23 = (bf16[4,256,128]{2,1,0:T(8,128)(2,1)S(1)}, bf16[4,256,128]{2,1,0:T(8,128)(2,1)S(1)}, u32[]{:S(2)}, u32[]{:S(2)}) collective-permute-start(bf16[4,256,128]{2,1,0:T(8,128)(2,1)S(1)} %split.52), channel_id=1, source_target_pairs={{0,28},{2,194},{4,0},{6,198},{8,4},{10,202},{12,8},{14,206},{16,12... | collective-permute-start | bytes 786440 | tf_op jit(solution)/shard_map/ppermute | solution.py:32
  100.6 7.3 %collective-permute-start.19 = (bf16[4,256,128]{2,1,0:T(8,128)(2,1)S(1)}, bf16[4,256,128]{2,1,0:T(8,128)(2,1)S(1)}, u32[]{:S(2)}, u32[]{:S(2)}) collective-permute-start(bf16[4,256,128]{2,1,0:T(8,128)(2,1)S(1)} %split.53), channel_id=1, source_target_pairs={{0,4},{2,66},{4,8},{6,70},{8,12},{10,74},{12,16},{14,78},{16,20},{... | collective-permute-start | bytes 786440 | tf_op jit(solution)/shard_map/ppermute | solution.py:32
  101.9 6.5 %collective-permute-start.24 = (bf16[4,256,128]{2,1,0:T(8,128)(2,1)S(1)}, bf16[4,256,128]{2,1,0:T(8,128)(2,1)S(1)}, u32[]{:S(2)}, u32[]{:S(2)}) collective-permute-start(bf16[4,256,128]{2,1,0:T(8,128)(2,1)S(1)} %fusion), channel_id=1, source_target_pairs={{0,28},{2,194},{4,0},{6,198},{8,4},{10,202},{12,8},{14,206},{16,12... | collective-permute-start | bytes 786440 | tf_op jit(solution)/shard_map/ppermute | solution.py:32
  108.5 7.1 %collective-permute-start.25 = (bf16[256,128]{1,0:T(8,128)(2,1)S(1)}, bf16[256,128]{1,0:T(8,128)(2,1)S(1)}, u32[]{:S(2)}, u32[]{:S(2)}) collective-permute-start(bf16[256,128]{1,0:T(8,128)(2,1)S(1)} %get-tuple-element.24), channel_id=1, source_target_pairs={{0,16},{2,18},{4,20},{6,22},{8,24},{10,26},{12,28},{14,30},{16,0},... | collective-permute-start | bytes 196616 | tf_op jit(solution)/shard_map/ppermute | solution.py:32
  109.5 6.2 %collective-permute-start.26 = (bf16[256,128]{1,0:T(8,128)(2,1)S(1)}, bf16[256,128]{1,0:T(8,128)(2,1)S(1)}, u32[]{:S(2)}, u32[]{:S(2)}) collective-permute-start(bf16[256,128]{1,0:T(8,128)(2,1)S(1)} %get-tuple-element.26), channel_id=1, source_target_pairs={{0,32},{2,34},{4,36},{6,38},{8,40},{10,42},{12,44},{14,46},{16,48}... | collective-permute-start | bytes 196616 | tf_op jit(solution)/shard_map/ppermute | solution.py:32
  109.8 9.9 %collective-permute-start.27 = (bf16[256,128]{1,0:T(8,128)(2,1)S(1)}, bf16[256,128]{1,0:T(8,128)(2,1)S(1)}, u32[]{:S(2)}, u32[]{:S(2)}) collective-permute-start(bf16[256,128]{1,0:T(8,128)(2,1)S(1)} %get-tuple-element.25), channel_id=1, source_target_pairs={{0,48},{2,50},{4,52},{6,54},{8,56},{10,58},{12,60},{14,62},{16,32}... | collective-permute-start | bytes 196616 | tf_op jit(solution)/shard_map/ppermute | solution.py:32
  119.8 2.6 %collective-permute-start.28 = (bf16[64,256]{1,0:T(8,128)(2,1)S(1)}, bf16[64,256]{1,0:T(8,128)(2,1)S(1)}, u32[]{:S(2)}, u32[]{:S(2)}) collective-permute-start(bf16[64,256]{1,0:T(8,128)(2,1)S(1)} %broadcast_select_fusion.1), channel_id=1, source_target_pairs={{0,2},{2,0},{4,6},{6,4},{8,10},{10,8},{12,14},{14,12},{16,18},{18,... | collective-permute-start | bytes 98312 | tf_op jit(solution)/shard_map/ppermute | solution.py:32
